TPU v7x, 768 devices: a whole 4x8x12 slice. The times are simulated.
768 devices in a mesh: group: 16 (over y, core), dom: 48 (over z, x).
Axes of the slice: x: 4, y: 8, z: 12, core: 2. Of those that a mesh axis runs over, the one named last changes fastest.
Arguments:
- prior: bfloat16 [294912, 1000], P(('group', 'dom')), may hold values from 0.019897461 to 2
- seed_labels: int32 [294912], P(('group', 'dom')), may hold values from 0 to 3999
- degree: int32 [294912], P(('group', 'dom')), may hold values from 42 to 85
- tiles: bfloat16 [2304, 8, 128, 128], P(('group', 'dom')), may hold values from 0 to 1, as said below
- tile_source: int32 [2304, 8], P(('group', 'dom')), may hold values from 0 to 8, as said below
- tile_count: int32 [768], P(('group', 'dom')), may hold values from 8 to 24
- send_list: int32 [768, 6], P(('group', 'dom')), may hold values from 0 to 2
Outputs:
- labels: float32 [294912, 1000], P(('group', 'dom'))
Inputs may be any that keep to these rules, and one draw needn't show every extreme that they name: `seed_labels`: a value below 1000 seeds that class; larger values leave the node unseeded. Only the first tile_count slots of a device, row block after row block, hold live tiles. `tiles`: nonnegative edge weights, most of them zero. `tile_source`: index of a source slot.
All inputs are finite; a program needn't handle non-finite values.
Results may differ from a plain program's by a relative error of at most 0.00032.
Values may be sent and summed in bfloat16 or wider, within the bound.
No kernel may reach another device: no remote copies, remote signals or barrier semaphores. Data moves between devices by JAX's collectives and lax.ppermute only.
A program may use at most 32 MiB of HBM per device.

v0:
```python
import jax
import jax.numpy as jnp
from jax import lax
from jax.sharding import PartitionSpec as P

ITERS = 3


def with_halo(x, sides, width):
    for axis, dim in sides:
        count, length = (lax.axis_size(axis), x.shape[dim])
        up = [(i, (i + 1) % count) for i in range(count - 1)]
        down = [(j, i) for i, j in up]
        last = lax.slice_in_dim(x, length - width, length, axis=dim)
        first = lax.slice_in_dim(x, 0, width, axis=dim)
        before = lax.ppermute(last, axis, up)
        after = lax.ppermute(first, axis, down)
        x = jnp.concatenate([before, x, after], axis=dim)
    return x


def shifted(block, axis, distance):
    devices = range(lax.axis_size(axis))
    route = [(i - distance, i) for i in devices if i - distance in devices]
    return lax.ppermute(block, axis, route)


def receive_blocks(sends):
    near = with_halo(jnp.stack([sends[0], sends[1]]), (("dom", 0),), 1)
    from_up = shifted(sends[3], "dom", 2)
    from_down = shifted(sends[2], "dom", -2)
    below, above = (near[0], near[3])
    across = with_halo(jnp.stack([sends[4], sends[5]]), (("group", 0),), 1)
    return jnp.stack([below, above, from_up, from_down, across[0], across[3]])


def on_device(prior, seed_labels, degree, tiles, tile_source, tile_count, send_list):
    row_blocks, per_row, block_rows = (tiles.shape[0], tiles.shape[1], tiles.shape[2])
    classes = prior.shape[1]
    sources_all = row_blocks + 6
    onehot = (seed_labels[:, None] == jnp.arange(classes)[None, :]).astype(jnp.float32)
    start = jnp.where(seed_labels[:, None] < classes, onehot, prior.astype(jnp.float32))
    inv_root = 1.0 / jnp.sqrt(degree.astype(jnp.float32))
    count = tile_count[0]
    live = jnp.arange(row_blocks * per_row).reshape(row_blocks, per_row) < count
    weights = jnp.where(live[:, :, None, None], tiles, jnp.zeros_like(tiles))
    select = (tile_source[:, :, None] == jnp.arange(sources_all)[None, None, :]).astype(
        jnp.bfloat16
    )
    combined = jnp.einsum("rtij,rts->risj", weights, select, preferred_element_type=jnp.float32)
    combined = combined.astype(jnp.bfloat16).reshape(
        row_blocks, block_rows, sources_all * block_rows
    )
    picker = (send_list[0][:, None] == jnp.arange(row_blocks)[None, :]).astype(jnp.bfloat16)
    labels = start
    for step in range(ITERS):
        scaled = (inv_root[:, None] * labels).astype(jnp.bfloat16)
        blocks = scaled.reshape(row_blocks, block_rows, classes)
        sends = jnp.einsum(
            "kr,rjc->kjc", picker, blocks, preferred_element_type=jnp.float32
        ).astype(jnp.bfloat16)
        sources = jnp.concatenate([blocks, receive_blocks(sends)], axis=0)
        flat_sources = sources.reshape(sources_all * block_rows, classes)
        totals = jnp.einsum(
            "rik,kc->ric", combined, flat_sources, preferred_element_type=jnp.float32
        )
        product = totals.reshape(row_blocks * block_rows, classes)
        labels = 0.9 * inv_root[:, None] * product + 0.1 * start
    return labels


def solution(mesh):
    return jax.shard_map(
        on_device,
        mesh=mesh,
        in_specs=(
            P(("group", "dom"), None),
            P(("group", "dom")),
            P(("group", "dom")),
            P(("group", "dom"), None, None, None),
            P(("group", "dom"), None),
            P(("group", "dom")),
            P(("group", "dom"), None),
        ),
        out_specs=P(("group", "dom"), None),
        check_vma=False,
    )
```

profile of v0, /device:TPU:512, one launch (start us, length us, event | category | flops | bytes accessed | tf_op | source)
XLA Modules:
  0.0 156.7 jit_solution(7441018792749985906)
XLA Ops:
  1.4 1.5 multiply_convert_fusion.2
  3.2 1.3 copy.18
  5.6 3.4 %fusion.17 = (bf16[1,128,1000]{1,0,2:T(2,128)(2,1)S(1)}, bf16[1,128,1000]{1,0,2:T(2,128)(2,1)}, bf16[1,128,1000]{1,0,2:T(2,128)(2,1)S(1)}, bf16[1,128,1000]{1,0,...) fusion(bf16[6,128,1000]{1,0,2:T(8,128)(2,1)S(1)} %convolution_convert_fusion.2), kind=kLoop, calls=%fused_computation.51 | loop fusion | bytes 3072000 | tf_op jit(solution)/shard_map/slice | solution.py:33
  8.9 1.3 copy.43
  10.3 4.9 %collective-permute-start.2 = (bf16[128,1000]{1,0:T(8,128)(2,1)}, bf16[128,1000]{1,0:T(8,128)(2,1)}, u32[]{:S(2)}, u32[]{:S(2)}) collective-permute-start(bf16[128,1000]{1,0:T(8,128)(2,1)} %bitcast.7), channel_id=1, source_target_pairs={{0,2},{1,3},{2,4},{3,5},{4,6},{5,7},{6,8},{7,9},{8,10},{9,11},{10,... | collective-permute-start | bytes 768008 | tf_op jit(solution)/shard_map/ppermute | solution.py:25
  15.2 1.4 copy.44
  16.6 4.5 %collective-permute-start.3 = (bf16[128,1000]{1,0:T(8,128)(2,1)}, bf16[128,1000]{1,0:T(8,128)(2,1)}, u32[]{:S(2)}, u32[]{:S(2)}) collective-permute-start(bf16[128,1000]{1,0:T(8,128)(2,1)} %bitcast.9), channel_id=1, source_target_pairs={{2,0},{3,1},{4,2},{5,3},{6,4},{7,5},{8,6},{9,7},{10,8},{11,9},{12,... | collective-permute-start | bytes 768008 | tf_op jit(solution)/shard_map/ppermute | solution.py:25
  21.1 2.1 %collective-permute-start.4 = (bf16[1,128,1000]{1,0,2:T(2,128)(2,1)}, bf16[1,128,1000]{1,0,2:T(2,128)(2,1)}, u32[]{:S(2)}, u32[]{:S(2)}) collective-permute-start(bf16[1,128,1000]{1,0,2:T(2,128)(2,1)} %get-tuple-element.18), channel_id=1, source_target_pairs={{0,48},{48,96},{96,144},{144,192},{192,240},{240,288},{288,336},{3... | collective-permute-start | bytes 768008 | tf_op jit(solution)/shard_map/ppermute | solution.py:16
  23.2 3.7 %collective-permute-start.1 = (bf16[1,128,1000]{1,0,2:T(2,128)(2,1)}, bf16[1,128,1000]{1,0,2:T(2,128)(2,1)S(1)}, u32[]{:S(2)}, u32[]{:S(2)}) collective-permute-start(bf16[1,128,1000]{1,0,2:T(2,128)(2,1)} %get-tuple-element.21), channel_id=1, source_target_pairs={{1,0},{2,1},{3,2},{4,3},{5,4},{6,5},{7,6},{8,7},{9,8},{10,9},{11,1... | collective-permute-start | bytes 768008 | tf_op jit(solution)/shard_map/ppermute | solution.py:17
  26.9 2.1 %collective-permute-start = (bf16[1,128,1000]{1,0,2:T(2,128)(2,1)}, bf16[1,128,1000]{1,0,2:T(2,128)(2,1)}, u32[]{:S(2)}, u32[]{:S(2)}) collective-permute-start(bf16[1,128,1000]{1,0,2:T(2,128)(2,1)} %get-tuple-element.22), channel_id=1, source_target_pairs={{0,1},{1,2},{2,3},{3,4},{4,5},{5,6},{6,7},{7,8},{8,9},{9,10},{10,1... | collective-permute-start | bytes 768008 | tf_op jit(solution)/shard_map/ppermute | solution.py:16
  31.6 7.7 %collective-permute-done.1 = bf16[1,128,1000]{1,0,2:T(2,128)(2,1)S(1)} collective-permute-done((bf16[1,128,1000]{1,0,2:T(2,128)(2,1)}, bf16[1,128,1000]{1,0,2:T(2,128)(2,1)S(1)}, u32[]{:S(2)}, u32[]{:S(2)}) %collective-permute-start.1) | collective-permute-done | bytes 256032 | tf_op jit(solution)/shard_map/ppermute | solution.py:17
  40.1 1.3 collective-permute-start.5
  41.4 1.3 copy.22
  42.6 4.1 %collective-permute-done = bf16[1,128,1000]{1,0,2:T(2,128)(2,1)} collective-permute-done((bf16[1,128,1000]{1,0,2:T(2,128)(2,1)}, bf16[1,128,1000]{1,0,2:T(2,128)(2,1)}, u32[]{:S(2)}, u32[]{:S(2)}) %collective-permute-start) | collective-permute-done | bytes 256032 | tf_op jit(solution)/shard_map/ppermute | solution.py:16
  49.4 1.2 copy.23
  50.7 1.7 %bitcast_dynamic-update-slice_fusion.5 = bf16[9,128,1000]{2,1,0:T(8,128)(2,1)} fusion(bf16[9,128,1000]{2,1,0:T(8,128)(2,1)} %constant_dynamic-update-slice_fusion.2, bf16[128,1000]{1,0:T(8,128)(2,1)} %collective-permute-done.2), kind=kLoop, calls=%fused_computation.21 | loop fusion | bytes 524288
  52.4 1.7 %bitcast_dynamic-update-slice_fusion.4 = bf16[9,128,1000]{2,1,0:T(8,128)(2,1)} fusion(bf16[9,128,1000]{2,1,0:T(8,128)(2,1)} %bitcast_dynamic-update-slice_fusion.5, bf16[128,1000]{1,0:T(8,128)(2,1)} %collective-permute-done.3), kind=kLoop, calls=%fused_computation.20 | loop fusion | bytes 524288
  56.8 3.4 %multiply_convert_fusion.1 = bf16[384,1000]{0,1:T(8,128)(2,1)S(1)} fusion(bf16[384,1000]{0,1:T(8,128)(2,1)S(1)} %copy-done.1, bf16[1152,1000]{1,0:T(8,128)(2,1)} %bitcast.66, s32[384]{0:T(512)S(1)} %copy-done.5, f32[384]{0:T(512)S(1)} %get-tuple-element.24, f32[384]{0:T(512)S(1)} %get-tuple-element.23, pred[384]{0:T(512)(128)(4,1)S(1)} %broadcast_compare_fusion, ...), kind=kOutput, calls=%fused_computation.6 | convolution fusion | flops 888192000 | bytes 4729728 | tf_op jit(solution)/shard_map/rik,kc->ric/dot_general | solution.py:64
  60.4 1.3 copy.26
  62.8 3.3 %fusion.16 = (bf16[1,128,1000]{1,0,2:T(2,128)(2,1)}, bf16[1,128,1000]{1,0,2:T(2,128)(2,1)}, bf16[1,128,1000]{1,0,2:T(2,128)(2,1)S(1)}, bf16[1,128,1000]{1,0,2:T(...) fusion(bf16[6,128,1000]{1,0,2:T(8,128)(2,1)S(1)} %convolution_convert_fusion.1), kind=kLoop, calls=%fused_computation.50 | loop fusion | bytes 3072000 | tf_op jit(solution)/shard_map/slice | solution.py:33
  66.1 3.0 %collective-permute-start.7 = (bf16[1,128,1000]{1,0,2:T(2,128)(2,1)}, bf16[1,128,1000]{1,0,2:T(2,128)(2,1)}, u32[]{:S(2)}, u32[]{:S(2)}) collective-permute-start(bf16[1,128,1000]{1,0,2:T(2,128)(2,1)} %get-tuple-element.15), channel_id=1, source_target_pairs={{1,0},{2,1},{3,2},{4,3},{5,4},{6,5},{7,6},{8,7},{9,8},{10,9},{11,1... | collective-permute-start | bytes 768008 | tf_op jit(solution)/shard_map/ppermute | solution.py:17
  69.1 2.8 %collective-permute-start.6 = (bf16[1,128,1000]{1,0,2:T(2,128)(2,1)}, bf16[1,128,1000]{1,0,2:T(2,128)(2,1)}, u32[]{:S(2)}, u32[]{:S(2)}) collective-permute-start(bf16[1,128,1000]{1,0,2:T(2,128)(2,1)} %get-tuple-element.16), channel_id=1, source_target_pairs={{0,1},{1,2},{2,3},{3,4},{4,5},{5,6},{6,7},{7,8},{8,9},{9,10},{10,1... | collective-permute-start | bytes 768008 | tf_op jit(solution)/shard_map/ppermute | solution.py:16
  71.9 1.4 copy.45
  73.3 1.9 %collective-permute-start.8 = (bf16[128,1000]{1,0:T(8,128)(2,1)}, bf16[128,1000]{1,0:T(8,128)(2,1)}, u32[]{:S(2)}, u32[]{:S(2)}) collective-permute-start(bf16[128,1000]{1,0:T(8,128)(2,1)} %bitcast.62), channel_id=1, source_target_pairs={{0,2},{1,3},{2,4},{3,5},{4,6},{5,7},{6,8},{7,9},{8,10},{9,11},{10,... | collective-permute-start | bytes 768008 | tf_op jit(solution)/shard_map/ppermute | solution.py:25
  75.2 2.7 %collective-permute-start.10 = (bf16[1,128,1000]{1,0,2:T(2,128)(2,1)}, bf16[1,128,1000]{1,0,2:T(2,128)(2,1)}, u32[]{:S(2)}, u32[]{:S(2)}) collective-permute-start(bf16[1,128,1000]{1,0,2:T(2,128)(2,1)} %get-tuple-element.12), channel_id=1, source_target_pairs={{0,48},{48,96},{96,144},{144,192},{192,240},{240,288},{288,336},{3... | collective-permute-start | bytes 768008 | tf_op jit(solution)/shard_map/ppermute | solution.py:16
  78.8 1.3 copy.46
  80.1 7.2 %collective-permute-start.9 = (bf16[128,1000]{1,0:T(8,128)(2,1)}, bf16[128,1000]{1,0:T(8,128)(2,1)}, u32[]{:S(2)}, u32[]{:S(2)}) collective-permute-start(bf16[128,1000]{1,0:T(8,128)(2,1)} %bitcast.15), channel_id=1, source_target_pairs={{2,0},{3,1},{4,2},{5,3},{6,4},{7,5},{8,6},{9,7},{10,8},{11,9},{12,... | collective-permute-start | bytes 768008 | tf_op jit(solution)/shard_map/ppermute | solution.py:25
  87.4 1.5 collective-permute-start.11
  88.9 1.3 copy.30
  90.1 5.4 %collective-permute-done.6 = bf16[1,128,1000]{1,0,2:T(2,128)(2,1)} collective-permute-done((bf16[1,128,1000]{1,0,2:T(2,128)(2,1)}, bf16[1,128,1000]{1,0,2:T(2,128)(2,1)}, u32[]{:S(2)}, u32[]{:S(2)}) %collective-permute-start.6) | collective-permute-done | bytes 256032 | tf_op jit(solution)/shard_map/ppermute | solution.py:16
  99.5 1.7 %bitcast_dynamic-update-slice_fusion.3 = bf16[9,128,1000]{2,1,0:T(8,128)(2,1)} fusion(bf16[9,128,1000]{2,1,0:T(8,128)(2,1)} %constant_dynamic-update-slice_fusion.7, bf16[128,1000]{1,0:T(8,128)(2,1)} %collective-permute-done.8), kind=kLoop, calls=%fused_computation.19 | loop fusion | bytes 524288
  101.1 1.7 %bitcast_dynamic-update-slice_fusion.2 = bf16[9,128,1000]{2,1,0:T(8,128)(2,1)} fusion(bf16[9,128,1000]{2,1,0:T(8,128)(2,1)} %bitcast_dynamic-update-slice_fusion.3, bf16[128,1000]{1,0:T(8,128)(2,1)} %collective-permute-done.9), kind=kLoop, calls=%fused_computation.18 | loop fusion | bytes 524288
  104.9 3.4 %multiply_convert_fusion = bf16[384,1000]{0,1:T(8,128)(2,1)S(1)} fusion(bf16[384,1000]{0,1:T(8,128)(2,1)S(1)} %copy-done.2, bf16[1152,1000]{1,0:T(8,128)(2,1)} %bitcast.64, s32[384]{0:T(512)S(1)} %copy-done.5, f32[384]{0:T(512)S(1)} %get-tuple-element.24, f32[384]{0:T(512)S(1)} %get-tuple-element.23, pred[384]{0:T(512)(128)(4,1)S(1)} %broadcast_compare_fusion, ...), kind=kOutput, calls=%fused_computation.5 | convolution fusion | flops 888192000 | bytes 4729728 | tf_op jit(solution)/shard_map/rik,kc->ric/dot_general | solution.py:64
  108.6 1.3 copy.34
  111.0 3.3 %fusion.15 = (bf16[1,128,1000]{1,0,2:T(2,128)(2,1)}, bf16[1,128,1000]{1,0,2:T(2,128)(2,1)}, bf16[1,128,1000]{1,0,2:T(2,128)(2,1)S(1)}, bf16[1,128,1000]{1,0,2:T(...) fusion(bf16[6,128,1000]{1,0,2:T(8,128)(2,1)S(1)} %convolution_convert_fusion), kind=kLoop, calls=%fused_computation.49 | loop fusion | bytes 3072000 | tf_op jit(solution)/shard_map/slice | solution.py:33
  114.3 3.0 %collective-permute-start.13 = (bf16[1,128,1000]{1,0,2:T(2,128)(2,1)}, bf16[1,128,1000]{1,0,2:T(2,128)(2,1)}, u32[]{:S(2)}, u32[]{:S(2)}) collective-permute-start(bf16[1,128,1000]{1,0,2:T(2,128)(2,1)} %get-tuple-element.9), channel_id=1, source_target_pairs={{1,0},{2,1},{3,2},{4,3},{5,4},{6,5},{7,6},{8,7},{9,8},{10,9},{11,1... | collective-permute-start | bytes 768008 | tf_op jit(solution)/shard_map/ppermute | solution.py:17
  117.3 2.8 %collective-permute-start.12 = (bf16[1,128,1000]{1,0,2:T(2,128)(2,1)}, bf16[1,128,1000]{1,0,2:T(2,128)(2,1)}, u32[]{:S(2)}, u32[]{:S(2)}) collective-permute-start(bf16[1,128,1000]{1,0,2:T(2,128)(2,1)} %get-tuple-element.10), channel_id=1, source_target_pairs={{0,1},{1,2},{2,3},{3,4},{4,5},{5,6},{6,7},{7,8},{8,9},{9,10},{10,1... | collective-permute-start | bytes 768008 | tf_op jit(solution)/shard_map/ppermute | solution.py:16
  120.1 1.4 copy.47
  121.5 2.8 %collective-permute-start.14 = (bf16[128,1000]{1,0:T(8,128)(2,1)}, bf16[128,1000]{1,0:T(8,128)(2,1)}, u32[]{:S(2)}, u32[]{:S(2)}) collective-permute-start(bf16[128,1000]{1,0:T(8,128)(2,1)} %bitcast.63), channel_id=1, source_target_pairs={{0,2},{1,3},{2,4},{3,5},{4,6},{5,7},{6,8},{7,9},{8,10},{9,11},{10,... | collective-permute-start | bytes 768008 | tf_op jit(solution)/shard_map/ppermute | solution.py:25
  124.3 2.1 %collective-permute-start.16 = (bf16[1,128,1000]{1,0,2:T(2,128)(2,1)}, bf16[1,128,1000]{1,0,2:T(2,128)(2,1)}, u32[]{:S(2)}, u32[]{:S(2)}) collective-permute-start(bf16[1,128,1000]{1,0,2:T(2,128)(2,1)} %get-tuple-element.6), channel_id=1, source_target_pairs={{0,48},{48,96},{96,144},{144,192},{192,240},{240,288},{288,336},{3... | collective-permute-start | bytes 768008 | tf_op jit(solution)/shard_map/ppermute | solution.py:16
  127.3 1.3 copy.48
  128.6 6.6 %collective-permute-start.15 = (bf16[128,1000]{1,0:T(8,128)(2,1)}, bf16[128,1000]{1,0:T(8,128)(2,1)}, u32[]{:S(2)}, u32[]{:S(2)}) collective-permute-start(bf16[128,1000]{1,0:T(8,128)(2,1)} %bitcast.21), channel_id=1, source_target_pairs={{2,0},{3,1},{4,2},{5,3},{6,4},{7,5},{8,6},{9,7},{10,8},{11,9},{12,... | collective-permute-start | bytes 768008 | tf_op jit(solution)/shard_map/ppermute | solution.py:25
  135.3 1.3 collective-permute-start.17
  136.6 1.3 copy.38
  137.8 5.0 %collective-permute-done.12 = bf16[1,128,1000]{1,0,2:T(2,128)(2,1)} collective-permute-done((bf16[1,128,1000]{1,0,2:T(2,128)(2,1)}, bf16[1,128,1000]{1,0,2:T(2,128)(2,1)}, u32[]{:S(2)}, u32[]{:S(2)}) %collective-permute-start.12) | collective-permute-done | bytes 256032 | tf_op jit(solution)/shard_map/ppermute | solution.py:16
  146.8 1.7 %bitcast_dynamic-update-slice_fusion.1 = bf16[9,128,1000]{2,1,0:T(8,128)(2,1)} fusion(bf16[9,128,1000]{2,1,0:T(8,128)(2,1)} %constant_dynamic-update-slice_fusion.12, bf16[128,1000]{1,0:T(8,128)(2,1)} %collective-permute-done.14), kind=kLoop, calls=%fused_computation.17 | loop fusion | bytes 524288
  148.5 1.7 %bitcast_dynamic-update-slice_fusion = bf16[9,128,1000]{2,1,0:T(8,128)(2,1)} fusion(bf16[9,128,1000]{2,1,0:T(8,128)(2,1)} %bitcast_dynamic-update-slice_fusion.1, bf16[128,1000]{1,0:T(8,128)(2,1)} %collective-permute-done.15), kind=kLoop, calls=%fused_computation.16 | loop fusion | bytes 524288
  152.3 4.4 %multiply_add_fusion = f32[384,1000]{0,1:T(8,128)} fusion(bf16[384,1000]{0,1:T(8,128)(2,1)S(1)} %copy-done.3, bf16[1152,1000]{1,0:T(8,128)(2,1)} %bitcast.65, s32[384]{0:T(512)S(1)} %copy-done.5, f32[384]{0:T(512)S(1)} %get-tuple-element.23, pred[384]{0:T(512)(128)(4,1)S(1)} %broadcast_compare_fusion, bf16[48,8,9,128]{3,2,1,0:T(8,128)(2,1)S(1)} %bitcast.61), kind=kOutput, calls=%fused_computation.4 | convolution fusion | flops 887424000 | bytes 5496192 | tf_op jit(solution)/shard_map/rik,kc->ric/dot_general | solution.py:64
  (64 shorter events, 27.5 us)
Async XLA Ops:
  1.4 3.1 %copy-start.6 = (s32[1,6]{1,0:T(1,128)S(1)}, s32[1,6]{1,0:T(1,128)}, u32[]{:S(2)}) copy-start(s32[1,6]{1,0:T(1,128)} %param.13) | copy-start | bytes 76
  5.6 24.1 %copy-start = (bf16[3,8,128,128]{3,2,1,0:T(8,128)(2,1)S(1)}, bf16[3,8,128,128]{3,2,1,0:T(8,128)(2,1)}, u32[]{:S(2)}) copy-start(bf16[3,8,128,128]{3,2,1,0:T(8,128)(2,1)} %param.10) | copy-start | bytes 2359300
  8.9 20.9 %copy-start.7 = (s32[3,8]{1,0:T(4,128)S(1)}, s32[3,8]{1,0:T(4,128)}, u32[]{:S(2)}) copy-start(s32[3,8]{1,0:T(4,128)} %param.11) | copy-start | bytes 292
  10.3 40.4 %collective-permute-start.2 = (bf16[128,1000]{1,0:T(8,128)(2,1)}, bf16[128,1000]{1,0:T(8,128)(2,1)}, u32[]{:S(2)}, u32[]{:S(2)}) collective-permute-start(bf16[128,1000]{1,0:T(8,128)(2,1)} %bitcast.7), channel_id=1, source_target_pairs={{0,2},{1,3},{2,4},{3,5},{4,6},{5,7},{6,8},{7,9},{8,10},{9,11},{10,... | collective-permute-start | bytes 768008 | tf_op jit(solution)/shard_map/ppermute | solution.py:25
  16.6 35.8 %collective-permute-start.3 = (bf16[128,1000]{1,0:T(8,128)(2,1)}, bf16[128,1000]{1,0:T(8,128)(2,1)}, u32[]{:S(2)}, u32[]{:S(2)}) collective-permute-start(bf16[128,1000]{1,0:T(8,128)(2,1)} %bitcast.9), channel_id=1, source_target_pairs={{2,0},{3,1},{4,2},{5,3},{6,4},{7,5},{8,6},{9,7},{10,8},{11,9},{12,... | collective-permute-start | bytes 768008 | tf_op jit(solution)/shard_map/ppermute | solution.py:25
  21.1 28.4 %collective-permute-start.4 = (bf16[1,128,1000]{1,0,2:T(2,128)(2,1)}, bf16[1,128,1000]{1,0,2:T(2,128)(2,1)}, u32[]{:S(2)}, u32[]{:S(2)}) collective-permute-start(bf16[1,128,1000]{1,0,2:T(2,128)(2,1)} %get-tuple-element.18), channel_id=1, source_target_pairs={{0,48},{48,96},{96,144},{144,192},{192,240},{240,288},{288,336},{3... | collective-permute-start | bytes 768008 | tf_op jit(solution)/shard_map/ppermute | solution.py:16
  23.2 16.1 %collective-permute-start.1 = (bf16[1,128,1000]{1,0,2:T(2,128)(2,1)}, bf16[1,128,1000]{1,0,2:T(2,128)(2,1)S(1)}, u32[]{:S(2)}, u32[]{:S(2)}) collective-permute-start(bf16[1,128,1000]{1,0,2:T(2,128)(2,1)} %get-tuple-element.21), channel_id=1, source_target_pairs={{1,0},{2,1},{3,2},{4,3},{5,4},{6,5},{7,6},{8,7},{9,8},{10,9},{11,1... | collective-permute-start | bytes 768008 | tf_op jit(solution)/shard_map/ppermute | solution.py:17
  26.9 19.8 %collective-permute-start = (bf16[1,128,1000]{1,0,2:T(2,128)(2,1)}, bf16[1,128,1000]{1,0,2:T(2,128)(2,1)}, u32[]{:S(2)}, u32[]{:S(2)}) collective-permute-start(bf16[1,128,1000]{1,0,2:T(2,128)(2,1)} %get-tuple-element.22), channel_id=1, source_target_pairs={{0,1},{1,2},{2,3},{3,4},{4,5},{5,6},{6,7},{7,8},{8,9},{9,10},{10,1... | collective-permute-start | bytes 768008 | tf_op jit(solution)/shard_map/ppermute | solution.py:16
  39.3 0.8 copy-start.4
  40.1 14.7 %collective-permute-start.5 = (bf16[1,128,1000]{1,0,2:T(2,128)(2,1)S(1)}, bf16[1,128,1000]{1,0,2:T(2,128)(2,1)}, u32[]{:S(2)}, u32[]{:S(2)}) collective-permute-start(bf16[1,128,1000]{1,0,2:T(2,128)(2,1)S(1)} %get-tuple-element.17), channel_id=1, source_target_pairs={{48,0},{96,48},{144,96},{192,144},{240,192},{288,240},{336,288},{3... | collective-permute-start | bytes 768008 | tf_op jit(solution)/shard_map/ppermute | solution.py:17
  48.0 8.8 %copy-start.1 = (bf16[384,1000]{0,1:T(8,128)(2,1)S(1)}, bf16[384,1000]{0,1:T(8,128)(2,1)}, u32[]{:S(2)}) copy-start(bf16[384,1000]{0,1:T(8,128)(2,1)} %param.7) | copy-start | bytes 2304004
  48.0 8.8 %copy-start.5 = (s32[384]{0:T(512)S(1)}, s32[384]{0:T(512)}, u32[]{:S(2)}) copy-start(s32[384]{0:T(512)} %param.8) | copy-start | bytes 4612
  66.1 21.3 %collective-permute-start.7 = (bf16[1,128,1000]{1,0,2:T(2,128)(2,1)}, bf16[1,128,1000]{1,0,2:T(2,128)(2,1)}, u32[]{:S(2)}, u32[]{:S(2)}) collective-permute-start(bf16[1,128,1000]{1,0,2:T(2,128)(2,1)} %get-tuple-element.15), channel_id=1, source_target_pairs={{1,0},{2,1},{3,2},{4,3},{5,4},{6,5},{7,6},{8,7},{9,8},{10,9},{11,1... | collective-permute-start | bytes 768008 | tf_op jit(solution)/shard_map/ppermute | solution.py:17
  69.1 26.4 %collective-permute-start.6 = (bf16[1,128,1000]{1,0,2:T(2,128)(2,1)}, bf16[1,128,1000]{1,0,2:T(2,128)(2,1)}, u32[]{:S(2)}, u32[]{:S(2)}) collective-permute-start(bf16[1,128,1000]{1,0,2:T(2,128)(2,1)} %get-tuple-element.16), channel_id=1, source_target_pairs={{0,1},{1,2},{2,3},{3,4},{4,5},{5,6},{6,7},{7,8},{8,9},{9,10},{10,1... | collective-permute-start | bytes 768008 | tf_op jit(solution)/shard_map/ppermute | solution.py:16
  73.3 26.2 %collective-permute-start.8 = (bf16[128,1000]{1,0:T(8,128)(2,1)}, bf16[128,1000]{1,0:T(8,128)(2,1)}, u32[]{:S(2)}, u32[]{:S(2)}) collective-permute-start(bf16[128,1000]{1,0:T(8,128)(2,1)} %bitcast.62), channel_id=1, source_target_pairs={{0,2},{1,3},{2,4},{3,5},{4,6},{5,7},{6,8},{7,9},{8,10},{9,11},{10,... | collective-permute-start | bytes 768008 | tf_op jit(solution)/shard_map/ppermute | solution.py:25
  75.2 23.0 %collective-permute-start.10 = (bf16[1,128,1000]{1,0,2:T(2,128)(2,1)}, bf16[1,128,1000]{1,0,2:T(2,128)(2,1)}, u32[]{:S(2)}, u32[]{:S(2)}) collective-permute-start(bf16[1,128,1000]{1,0,2:T(2,128)(2,1)} %get-tuple-element.12), channel_id=1, source_target_pairs={{0,48},{48,96},{96,144},{144,192},{192,240},{240,288},{288,336},{3... | collective-permute-start | bytes 768008 | tf_op jit(solution)/shard_map/ppermute | solution.py:16
  80.1 21.0 %collective-permute-start.9 = (bf16[128,1000]{1,0:T(8,128)(2,1)}, bf16[128,1000]{1,0:T(8,128)(2,1)}, u32[]{:S(2)}, u32[]{:S(2)}) collective-permute-start(bf16[128,1000]{1,0:T(8,128)(2,1)} %bitcast.15), channel_id=1, source_target_pairs={{2,0},{3,1},{4,2},{5,3},{6,4},{7,5},{8,6},{9,7},{10,8},{11,9},{12,... | collective-permute-start | bytes 768008 | tf_op jit(solution)/shard_map/ppermute | solution.py:25
  87.4 16.2 %collective-permute-start.11 = (bf16[1,128,1000]{1,0,2:T(2,128)(2,1)}, bf16[1,128,1000]{1,0,2:T(2,128)(2,1)S(1)}, u32[]{:S(2)}, u32[]{:S(2)}) collective-permute-start(bf16[1,128,1000]{1,0,2:T(2,128)(2,1)} %get-tuple-element.11), channel_id=1, source_target_pairs={{48,0},{96,48},{144,96},{192,144},{240,192},{288,240},{336,288},{3... | collective-permute-start | bytes 768008 | tf_op jit(solution)/shard_map/ppermute | solution.py:17
  96.7 8.2 %copy-start.2 = (bf16[384,1000]{0,1:T(8,128)(2,1)S(1)}, bf16[384,1000]{0,1:T(8,128)(2,1)}, u32[]{:S(2)}) copy-start(bf16[384,1000]{0,1:T(8,128)(2,1)} %param.7) | copy-start | bytes 2304004
  114.3 21.0 %collective-permute-start.13 = (bf16[1,128,1000]{1,0,2:T(2,128)(2,1)}, bf16[1,128,1000]{1,0,2:T(2,128)(2,1)}, u32[]{:S(2)}, u32[]{:S(2)}) collective-permute-start(bf16[1,128,1000]{1,0,2:T(2,128)(2,1)} %get-tuple-element.9), channel_id=1, source_target_pairs={{1,0},{2,1},{3,2},{4,3},{5,4},{6,5},{7,6},{8,7},{9,8},{10,9},{11,1... | collective-permute-start | bytes 768008 | tf_op jit(solution)/shard_map/ppermute | solution.py:17
  117.3 25.5 %collective-permute-start.12 = (bf16[1,128,1000]{1,0,2:T(2,128)(2,1)}, bf16[1,128,1000]{1,0,2:T(2,128)(2,1)}, u32[]{:S(2)}, u32[]{:S(2)}) collective-permute-start(bf16[1,128,1000]{1,0,2:T(2,128)(2,1)} %get-tuple-element.10), channel_id=1, source_target_pairs={{0,1},{1,2},{2,3},{3,4},{4,5},{5,6},{6,7},{7,8},{8,9},{9,10},{10,1... | collective-permute-start | bytes 768008 | tf_op jit(solution)/shard_map/ppermute | solution.py:16
  121.5 25.3 %collective-permute-start.14 = (bf16[128,1000]{1,0:T(8,128)(2,1)}, bf16[128,1000]{1,0:T(8,128)(2,1)}, u32[]{:S(2)}, u32[]{:S(2)}) collective-permute-start(bf16[128,1000]{1,0:T(8,128)(2,1)} %bitcast.63), channel_id=1, source_target_pairs={{0,2},{1,3},{2,4},{3,5},{4,6},{5,7},{6,8},{7,9},{8,10},{9,11},{10,... | collective-permute-start | bytes 768008 | tf_op jit(solution)/shard_map/ppermute | solution.py:25
  124.3 21.3 %collective-permute-start.16 = (bf16[1,128,1000]{1,0,2:T(2,128)(2,1)}, bf16[1,128,1000]{1,0,2:T(2,128)(2,1)}, u32[]{:S(2)}, u32[]{:S(2)}) collective-permute-start(bf16[1,128,1000]{1,0,2:T(2,128)(2,1)} %get-tuple-element.6), channel_id=1, source_target_pairs={{0,48},{48,96},{96,144},{144,192},{192,240},{240,288},{288,336},{3... | collective-permute-start | bytes 768008 | tf_op jit(solution)/shard_map/ppermute | solution.py:16
  128.6 19.8 %collective-permute-start.15 = (bf16[128,1000]{1,0:T(8,128)(2,1)}, bf16[128,1000]{1,0:T(8,128)(2,1)}, u32[]{:S(2)}, u32[]{:S(2)}) collective-permute-start(bf16[128,1000]{1,0:T(8,128)(2,1)} %bitcast.21), channel_id=1, source_target_pairs={{2,0},{3,1},{4,2},{5,3},{6,4},{7,5},{8,6},{9,7},{10,8},{11,9},{12,... | collective-permute-start | bytes 768008 | tf_op jit(solution)/shard_map/ppermute | solution.py:25
  135.3 15.6 %collective-permute-start.17 = (bf16[1,128,1000]{1,0,2:T(2,128)(2,1)}, bf16[1,128,1000]{1,0,2:T(2,128)(2,1)S(1)}, u32[]{:S(2)}, u32[]{:S(2)}) collective-permute-start(bf16[1,128,1000]{1,0,2:T(2,128)(2,1)} %get-tuple-element.5), channel_id=1, source_target_pairs={{48,0},{96,48},{144,96},{192,144},{240,192},{288,240},{336,288},{3... | collective-permute-start | bytes 768008 | tf_op jit(solution)/shard_map/ppermute | solution.py:17
  144.1 8.2 %copy-start.3 = (bf16[384,1000]{0,1:T(8,128)(2,1)S(1)}, bf16[384,1000]{0,1:T(8,128)(2,1)}, u32[]{:S(2)}) copy-start(bf16[384,1000]{0,1:T(8,128)(2,1)} %param.7) | copy-start | bytes 2304004
where the time goes:
time: 158 us; the launch traced here: 157 us
  local copies, waits for them, and re-layouts  58.9 us (37%)
  starting transfers between devices  56.4 us (36%)
  waiting for transfers between devices  22.1 us (14%)
  matrix products  15.1 us (10%)
  other arithmetic  3.02 us (2%)
    ppermute x6, starting transfers between devices, shifted(): return lax.ppermute(block, axis, route)  28 us
    unnamed x34, local copies, waits for them, and re-layouts  20.2 us
    ppermute x6, starting transfers between devices, with_halo(): before = lax.ppermute(last, axis, up)  14.5 us
    ppermute x6, waiting for transfers between devices, with_halo(): before = lax.ppermute(last, axis, up)  14.4 us
    ppermute x6, starting transfers between devices, with_halo(): after = lax.ppermute(first, axis, down)  13.9 us
    dot_general x3, matrix products, on_device(): jnp.einsum('rik,kc->ric', combined, flat_sources, preferred_element_type=...  11.1 us
    slice x3, local copies, waits for them, and re-layouts, receive_blocks(): across = with_halo(jnp.stack([sends[4], sends[5]]), (('group', 0),), 1)  9.99 us
    ppermute x6, waiting for transfers between devices, with_halo(): after = lax.ppermute(first, axis, down)  7.72 us
  transfers between devices with their start and end apart: 18, of which 4 were waited for; matrix products, arithmetic and copies ran while one was open for 24% of the time, Pallas kernels for 0%

commit v1 on v0

v1 whole, which is shorter than its diff:
```python
import functools

import jax
import jax.numpy as jnp
from jax import lax
from jax.experimental import pallas as pl
from jax.experimental.pallas import tpu as pltpu
from jax.sharding import PartitionSpec as P

ITERS = 3
ROWS = 256
SMEM = pl.BlockSpec(memory_space=pltpu.SMEM)

SWAPS = (
    ("dom", 2, 0),
    ("dom", 2, 1),
    ("dom", 1, 0),
    ("dom", 1, 1),
    ("group", 1, 1),
    ("group", 1, 0),
)
UP_COLUMN = {("dom", 1): 1, ("dom", 2): 3, ("group", 1): 5}
DOWN_COLUMN = {("dom", 1): 0, ("dom", 2): 2, ("group", 1): 4}
FROM_DOWN = {("dom", 1): 0, ("dom", 2): 2, ("group", 1): 4}
FROM_UP = {("dom", 1): 1, ("dom", 2): 3, ("group", 1): 5}


def is_lower(swap):
    axis, distance, phase = swap
    return (lax.axis_index(axis) // distance) % 2 == phase


def exchange(block, swap):
    axis, distance, phase = swap
    count = lax.axis_size(axis)
    lower = [i for i in range(count - distance) if (i // distance) % 2 == phase]
    pairs = [(i, i + distance) for i in lower] + [(i + distance, i) for i in lower]
    return lax.ppermute(block, axis, pairs)


def first_labels(prior, seeds, row0):
    rows, nodes = prior.shape
    label = lax.broadcasted_iota(jnp.int32, (rows, nodes), 0) + row0
    onehot = jnp.where(label == seeds, 1.0, 0.0)
    return onehot, prior.astype(jnp.float32)


def start_of(prior_ref, seeds_ref, classes):
    seeds = seeds_ref[...]
    onehot, soft = first_labels(prior_ref[...], seeds, pl.program_id(0) * prior_ref.shape[0])
    return jnp.where(seeds < classes, onehot, soft)


def put_scaled(scaled, which_ref, own_ref, send_refs):
    own_ref[...] = scaled
    for k, ref in enumerate(send_refs):
        ref[...] = own_ref[:, pl.ds(pl.multiple_of(which_ref[k] * 128, 128), 128)]


def prepare_kernel(classes, which_ref, prior_ref, seeds_ref, degree_ref, own_ref, *send_refs):
    inv_root = 1.0 / jnp.sqrt(degree_ref[...].astype(jnp.float32))
    start = start_of(prior_ref, seeds_ref, classes)
    put_scaled((inv_root * start).astype(jnp.bfloat16), which_ref, own_ref, send_refs)


def step_kernel(
    classes, last, which_ref, prior_ref, seeds_ref, degree_ref, weight_ref, own_ref, *refs
):
    received, outs = refs[: len(SWAPS)], refs[len(SWAPS) :]
    inv_root = 1.0 / jnp.sqrt(degree_ref[...].astype(jnp.float32))
    sources = jnp.concatenate([own_ref[...]] + [ref[...] for ref in received], axis=1)
    product = jnp.dot(sources, weight_ref[...], preferred_element_type=jnp.float32)
    start = start_of(prior_ref, seeds_ref, classes)
    labels = 0.9 * inv_root * product + 0.1 * start
    if last:
        outs[0][...] = labels
    else:
        put_scaled((inv_root * labels).astype(jnp.bfloat16), which_ref, outs[0], outs[1:])


def weight_kernel(place_ref, source_ref, count_ref, tiles_ref, weight_ref, total_ref):
    row_blocks, per_row, side, _ = tiles_ref.shape
    slots = weight_ref.shape[0] // side
    for r in range(row_blocks):
        total_ref[...] = jnp.zeros_like(total_ref)
        for t in range(per_row):
            place = place_ref[source_ref[r, t]]
            live = r * per_row + t < count_ref[0]

            @pl.when(live)
            def _():
                total_ref[place] += tiles_ref[r, t].astype(jnp.float32)

        for s in range(slots):
            weight_ref[pl.ds(s * side, side), pl.ds(r * side, side)] = total_ref[s].T.astype(
                weight_ref.dtype
            )


def on_device(prior, seed_labels, degree, tiles, tile_source, tile_count, send_list):
    row_blocks, per_row, side, _ = tiles.shape
    nodes, classes = prior.shape
    slots = row_blocks + len(SWAPS)
    prior_t = prior.T
    seeds = seed_labels[None, :]
    degrees = degree[None, :]

    which, place = [], list(range(row_blocks)) + [0] * len(SWAPS)
    for k, swap in enumerate(SWAPS):
        lower, kind = is_lower(swap), swap[:2]
        which.append(jnp.where(lower, send_list[0, UP_COLUMN[kind]], send_list[0, DOWN_COLUMN[kind]]))
        mate = [other for other in SWAPS if other[:2] == kind and other != swap][0]
        other = SWAPS.index(mate)
        place[row_blocks + FROM_UP[kind]] = jnp.where(lower, row_blocks + k, row_blocks + other)
        place[row_blocks + FROM_DOWN[kind]] = jnp.where(lower, row_blocks + other, row_blocks + k)
    which = jnp.stack(which).astype(jnp.int32)
    place = jnp.stack([jnp.asarray(p, jnp.int32) for p in place])

    grid = (pl.cdiv(classes, ROWS),)
    wide = pl.BlockSpec((ROWS, nodes), lambda i: (i, 0))
    narrow = pl.BlockSpec((ROWS, side), lambda i: (i, 0))
    lanes = pl.BlockSpec((1, nodes), lambda i: (0, 0))
    weights = pl.BlockSpec((slots * side, nodes), lambda i: (0, 0))
    scaled_shapes = [jax.ShapeDtypeStruct((classes, nodes), jnp.bfloat16)] + [
        jax.ShapeDtypeStruct((classes, side), jnp.bfloat16)
    ] * len(SWAPS)
    params = pltpu.CompilerParams(vmem_limit_bytes=40 * 1024 * 1024)

    own, *sends = pl.pallas_call(
        functools.partial(prepare_kernel, classes),
        grid=grid,
        in_specs=[SMEM, wide, lanes, lanes],
        out_specs=[wide] + [narrow] * len(SWAPS),
        out_shape=scaled_shapes,
        compiler_params=params,
    )(which, prior_t, seeds, degrees)
    weight = pl.pallas_call(
        weight_kernel,
        in_specs=[SMEM, SMEM, SMEM, pl.BlockSpec(memory_space=pltpu.VMEM)],
        out_specs=pl.BlockSpec(memory_space=pltpu.VMEM),
        out_shape=jax.ShapeDtypeStruct((slots * side, nodes), jnp.bfloat16),
        scratch_shapes=[pltpu.VMEM((slots, side, side), jnp.float32)],
        compiler_params=params,
        cost_estimate=pl.CostEstimate(flops=0, bytes_accessed=8_000_000, transcendentals=0),
    )(place, tile_source, tile_count, tiles)
    for step in range(ITERS):
        last = step == ITERS - 1
        received = [exchange(block, swap) for block, swap in zip(sends, SWAPS)]
        outs = pl.pallas_call(
            functools.partial(step_kernel, classes, last),
            grid=grid,
            in_specs=[SMEM, wide, lanes, lanes, weights, wide] + [narrow] * len(SWAPS),
            out_specs=[wide] if last else [wide] + [narrow] * len(SWAPS),
            out_shape=[jax.ShapeDtypeStruct((classes, nodes), jnp.float32)] if last else scaled_shapes,
            compiler_params=params,
        )(which, prior_t, seeds, degrees, weight, own, *received)
        own, sends = outs[0], outs[1:]
    return own.T


def solution(mesh):
    return jax.shard_map(
        on_device,
        mesh=mesh,
        in_specs=(
            P(("group", "dom"), None),
            P(("group", "dom")),
            P(("group", "dom")),
            P(("group", "dom"), None, None, None),
            P(("group", "dom"), None),
            P(("group", "dom")),
            P(("group", "dom"), None),
        ),
        out_specs=P(("group", "dom"), None),
        check_vma=False,
    )
```

time: 158 us -> 104 us (0.66)
  the two profiles are of different devices: /device:TPU:512 before, /device:TPU:155 now
where the time goes in v1:
time: 104 us; the launch traced here: 103 us
  starting transfers between devices  66.4 us (64%)
  Pallas kernels  17.9 us (17%)
  between operations  8.86 us (9%)
  local copies, waits for them, and re-layouts  6.04 us (6%)
  waiting for transfers between devices  4.06 us (4%)
    ppermute x18, starting transfers between devices, exchange(): return lax.ppermute(block, axis, pairs)  66.4 us
    pallas_call x3, Pallas kernels, on_device(): pl.pallas_call(functools.partial(step_kernel, classes, last), grid=grid,...  13.3 us
    ppermute x18, waiting for transfers between devices, exchange(): return lax.ppermute(block, axis, pairs)  4.06 us
    pallas_call x1, Pallas kernels, on_device(): pl.pallas_call(functools.partial(prepare_kernel, classes), grid=grid, in_...  3.18 us
    unnamed x8, local copies, waits for them, and re-layouts  2.95 us
  transfers between devices with their start and end apart: 18, of which 3 were waited for; matrix products, arithmetic and copies ran while one was open for 0% of the time, Pallas kernels for 1%

profile of v1, /device:TPU:155, one launch (start us, length us, event | category | flops | bytes accessed | tf_op | source)
XLA Modules:
  0.0 103.2 jit_solution(4853582073674030687)
XLA Ops:
  0.0 0.7 broadcast_in_dim.6.seeds_ref
  0.7 0.7 broadcast_in_dim.7.degree_ref
  1.4 1.6 %fusion = (s32[1,1]{1,0:T(1,128)}, s32[1,1]{1,0:T(1,128)}, s32[1,1]{1,0:T(1,128)}, s32[1,1]{1,0:T(1,128)}, s32[1,1]{1,0:T(1,128)}, /*index=5*/s32[1,1]{1,0:T(1,128)}) fusion(s32[1,6]{1,0:T(1,128)} %param.13), kind=kLoop, calls=%fused_computation | loop fusion | bytes 48 | tf_op jit(solution)/shard_map/slice | solution.py:111
  10.8 0.1 stack.48.which_ref
  10.9 1.1 %copy-done = bf16[384,1000]{0,1:T(8,128)(2,1)S(1)} copy-done((bf16[384,1000]{0,1:T(8,128)(2,1)S(1)}, bf16[384,1000]{0,1:T(8,128)(2,1)}, u32[]{:S(2)}) %copy-start) | copy-done | bytes 768024
  12.1 3.2 %shard_map.74 = (bf16[1000,384]{1,0:T(8,128)(2,1)S(1)}, bf16[1000,128]{1,0:T(8,128)(2,1)S(1)}, bf16[1000,128]{1,0:T(8,128)(2,1)}, bf16[1000,128]{1,0:T(8,128)(2,...) custom-call(s32[6]{0:T(128)S(1)} %stack.48.which_ref, ...), custom_call_target="tpu_custom_call" | custom-call | tf_op jit(solution)/shard_map/pallas_call | solution.py:129
  15.2 3.7 %collective-permute-start = (bf16[1000,128]{1,0:T(8,128)(2,1)S(1)}, bf16[1000,128]{1,0:T(8,128)(2,1)S(1)}, u32[]{:S(2)}, u32[]{:S(2)}) collective-permute-start(bf16[1000,128]{1,0:T(8,128)(2,1)S(1)} %get-tuple-element.27), channel_id=1, source_target_pairs={{0,2},{1,3},{4,6},{5,7},{8,10},{9,11},{12,14},{13,15},{16,18},{17,... | collective-permute-start | bytes 768008 | tf_op jit(solution)/shard_map/ppermute | solution.py:38
  19.0 2.1 %collective-permute-start.1 = (bf16[1000,128]{1,0:T(8,128)(2,1)}, bf16[1000,128]{1,0:T(8,128)(2,1)S(1)}, u32[]{:S(2)}, u32[]{:S(2)}) collective-permute-start(bf16[1000,128]{1,0:T(8,128)(2,1)} %get-tuple-element.28), channel_id=1, source_target_pairs={{2,4},{3,5},{6,8},{7,9},{10,12},{11,13},{14,16},{15,17},{18,20},{1... | collective-permute-start | bytes 768008 | tf_op jit(solution)/shard_map/ppermute | solution.py:38
  21.1 2.9 %collective-permute-start.2 = (bf16[1000,128]{1,0:T(8,128)(2,1)}, bf16[1000,128]{1,0:T(8,128)(2,1)S(1)}, u32[]{:S(2)}, u32[]{:S(2)}) collective-permute-start(bf16[1000,128]{1,0:T(8,128)(2,1)} %get-tuple-element.29), channel_id=1, source_target_pairs={{0,1},{2,3},{4,5},{6,7},{8,9},{10,11},{12,13},{14,15},{16,17},{18,... | collective-permute-start | bytes 768008 | tf_op jit(solution)/shard_map/ppermute | solution.py:38
  24.0 5.8 %collective-permute-start.3 = (bf16[1000,128]{1,0:T(8,128)(2,1)}, bf16[1000,128]{1,0:T(8,128)(2,1)S(1)}, u32[]{:S(2)}, u32[]{:S(2)}) collective-permute-start(bf16[1000,128]{1,0:T(8,128)(2,1)} %get-tuple-element.30), channel_id=1, source_target_pairs={{1,2},{3,4},{5,6},{7,8},{9,10},{11,12},{13,14},{15,16},{17,18},{19... | collective-permute-start | bytes 768008 | tf_op jit(solution)/shard_map/ppermute | solution.py:38
  29.8 6.1 %collective-permute-start.4 = (bf16[1000,128]{1,0:T(8,128)(2,1)}, bf16[1000,128]{1,0:T(8,128)(2,1)S(1)}, u32[]{:S(2)}, u32[]{:S(2)}) collective-permute-start(bf16[1000,128]{1,0:T(8,128)(2,1)} %get-tuple-element.31), channel_id=1, source_target_pairs={{48,96},{144,192},{240,288},{336,384},{432,480},{528,576},{624,672... | collective-permute-start | bytes 768008 | tf_op jit(solution)/shard_map/ppermute | solution.py:38
  35.9 0.0 collective-permute-done.refs_0_
  35.9 1.9 %collective-permute-start.5 = (bf16[1000,128]{1,0:T(8,128)(2,1)S(1)}, bf16[1000,128]{1,0:T(8,128)(2,1)S(1)}, u32[]{:S(2)}, u32[]{:S(2)}) collective-permute-start(bf16[1000,128]{1,0:T(8,128)(2,1)S(1)} %get-tuple-element.32), channel_id=1, source_target_pairs={{0,48},{96,144},{192,240},{288,336},{384,432},{480,528},{576,624},... | collective-permute-start | bytes 768008 | tf_op jit(solution)/shard_map/ppermute | solution.py:38
  38.5 0.1 stack.55.place_ref
  38.6 1.1 %copy-done.2 = bf16[3,8,128,128]{3,2,1,0:T(8,128)(2,1)S(1)} copy-done((bf16[3,8,128,128]{3,2,1,0:T(8,128)(2,1)S(1)}, bf16[3,8,128,128]{3,2,1,0:T(8,128)(2,1)}, u32[]{:S(2)}) %copy-start.2) | copy-done | bytes 786456
  39.7 0.7 copy-done.3
  40.4 1.4 %shard_map.73.weight_ref = bf16[1152,384]{1,0:T(8,128)(2,1)S(1)} custom-call(s32[9]{0:T(128)S(1)} %stack.55.place_ref, s32[3,8]{1,0:T(4,128)S(1)} %copy-done.3, s32[1]{0:T(128)S(6)} %copy.8.count_ref, bf16[3,8,128,128]{3,2,1,0:T(8,128)(2,1)S(1)} %copy-done.2), custom_call_target="tpu_custom_call" | custom-call | bytes 8000000 | tf_op jit(solution)/shard_map/pallas_call | solution.py:137
  41.8 0.0 collective-permute-done.1.refs_1_
  41.8 0.0 collective-permute-done.2.refs_2_
  41.9 0.0 collective-permute-done.3.refs_3_
  41.9 0.0 collective-permute-done.4.refs_4_
  41.9 0.0 collective-permute-done.5.refs_5_
  41.9 4.9 %shard_map.75 = (bf16[1000,384]{1,0:T(8,128)(2,1)S(1)}, bf16[1000,128]{1,0:T(8,128)(2,1)S(1)}, bf16[1000,128]{1,0:T(8,128)(2,1)S(1)}, bf16[1000,128]{1,0:T(8,128...) custom-call(s32[6]{0:T(128)S(1)} %stack.48.which_ref, ...), custom_call_target="tpu_custom_call" | custom-call | tf_op jit(solution)/shard_map/pallas_call | solution.py:149
  46.8 2.1 %collective-permute-start.6 = (bf16[1000,128]{1,0:T(8,128)(2,1)S(1)}, bf16[1000,128]{1,0:T(8,128)(2,1)S(1)}, u32[]{:S(2)}, u32[]{:S(2)}) collective-permute-start(bf16[1000,128]{1,0:T(8,128)(2,1)S(1)} %get-tuple-element.34), channel_id=1, source_target_pairs={{0,2},{1,3},{4,6},{5,7},{8,10},{9,11},{12,14},{13,15},{16,18},{17,... | collective-permute-start | bytes 768008 | tf_op jit(solution)/shard_map/ppermute | solution.py:38
  48.9 3.8 %collective-permute-start.7 = (bf16[1000,128]{1,0:T(8,128)(2,1)S(1)}, bf16[1000,128]{1,0:T(8,128)(2,1)S(1)}, u32[]{:S(2)}, u32[]{:S(2)}) collective-permute-start(bf16[1000,128]{1,0:T(8,128)(2,1)S(1)} %get-tuple-element.35), channel_id=1, source_target_pairs={{2,4},{3,5},{6,8},{7,9},{10,12},{11,13},{14,16},{15,17},{18,20},{1... | collective-permute-start | bytes 768008 | tf_op jit(solution)/shard_map/ppermute | solution.py:38
  52.7 2.1 %collective-permute-start.8 = (bf16[1000,128]{1,0:T(8,128)(2,1)S(1)}, bf16[1000,128]{1,0:T(8,128)(2,1)S(1)}, u32[]{:S(2)}, u32[]{:S(2)}) collective-permute-start(bf16[1000,128]{1,0:T(8,128)(2,1)S(1)} %get-tuple-element.36), channel_id=1, source_target_pairs={{0,1},{2,3},{4,5},{6,7},{8,9},{10,11},{12,13},{14,15},{16,17},{18,... | collective-permute-start | bytes 768008 | tf_op jit(solution)/shard_map/ppermute | solution.py:38
  54.8 6.1 %collective-permute-start.9 = (bf16[1000,128]{1,0:T(8,128)(2,1)S(1)}, bf16[1000,128]{1,0:T(8,128)(2,1)S(1)}, u32[]{:S(2)}, u32[]{:S(2)}) collective-permute-start(bf16[1000,128]{1,0:T(8,128)(2,1)S(1)} %get-tuple-element.37), channel_id=1, source_target_pairs={{1,2},{3,4},{5,6},{7,8},{9,10},{11,12},{13,14},{15,16},{17,18},{19... | collective-permute-start | bytes 768008 | tf_op jit(solution)/shard_map/ppermute | solution.py:38
  61.0 5.5 %collective-permute-start.10 = (bf16[1000,128]{1,0:T(8,128)(2,1)S(1)}, bf16[1000,128]{1,0:T(8,128)(2,1)S(1)}, u32[]{:S(2)}, u32[]{:S(2)}) collective-permute-start(bf16[1000,128]{1,0:T(8,128)(2,1)S(1)} %get-tuple-element.38), channel_id=1, source_target_pairs={{48,96},{144,192},{240,288},{336,384},{432,480},{528,576},{624,672... | collective-permute-start | bytes 768008 | tf_op jit(solution)/shard_map/ppermute | solution.py:38
  66.4 0.0 collective-permute-done.6.refs_0_
  66.5 1.9 %collective-permute-start.11 = (bf16[1000,128]{1,0:T(8,128)(2,1)S(1)}, bf16[1000,128]{1,0:T(8,128)(2,1)S(1)}, u32[]{:S(2)}, u32[]{:S(2)}) collective-permute-start(bf16[1000,128]{1,0:T(8,128)(2,1)S(1)} %get-tuple-element.39), channel_id=1, source_target_pairs={{0,48},{96,144},{192,240},{288,336},{384,432},{480,528},{576,624},... | collective-permute-start | bytes 768008 | tf_op jit(solution)/shard_map/ppermute | solution.py:38
  68.4 0.0 collective-permute-done.7.refs_1_
  68.4 0.0 collective-permute-done.8.refs_2_
  68.4 0.5 collective-permute-done.9.refs_3_
  68.9 1.5 %collective-permute-done.10.refs_4_ = bf16[1000,128]{1,0:T(8,128)(2,1)S(1)} collective-permute-done((bf16[1000,128]{1,0:T(8,128)(2,1)S(1)}, bf16[1000,128]{1,0:T(8,128)(2,1)S(1)}, u32[]{:S(2)}, u32[]{:S(2)}) %collective-permute-start.10) | collective-permute-done | bytes 256032 | tf_op jit(solution)/shard_map/ppermute | solution.py:38
  70.4 0.0 collective-permute-done.11.refs_5_
  70.4 4.8 %shard_map.76 = (bf16[1000,384]{1,0:T(8,128)(2,1)S(1)}, bf16[1000,128]{1,0:T(8,128)(2,1)S(1)}, bf16[1000,128]{1,0:T(8,128)(2,1)S(1)}, bf16[1000,128]{1,0:T(8,128...) custom-call(s32[6]{0:T(128)S(1)} %stack.48.which_ref, ...), custom_call_target="tpu_custom_call" | custom-call | tf_op jit(solution)/shard_map/pallas_call | solution.py:149
  75.3 2.2 %collective-permute-start.12 = (bf16[1000,128]{1,0:T(8,128)(2,1)S(1)}, bf16[1000,128]{1,0:T(8,128)(2,1)S(1)}, u32[]{:S(2)}, u32[]{:S(2)}) collective-permute-start(bf16[1000,128]{1,0:T(8,128)(2,1)S(1)} %get-tuple-element.41), channel_id=1, source_target_pairs={{0,2},{1,3},{4,6},{5,7},{8,10},{9,11},{12,14},{13,15},{16,18},{17,... | collective-permute-start | bytes 768008 | tf_op jit(solution)/shard_map/ppermute | solution.py:38
  77.5 2.5 %collective-permute-start.13 = (bf16[1000,128]{1,0:T(8,128)(2,1)S(1)}, bf16[1000,128]{1,0:T(8,128)(2,1)S(1)}, u32[]{:S(2)}, u32[]{:S(2)}) collective-permute-start(bf16[1000,128]{1,0:T(8,128)(2,1)S(1)} %get-tuple-element.42), channel_id=1, source_target_pairs={{2,4},{3,5},{6,8},{7,9},{10,12},{11,13},{14,16},{15,17},{18,20},{1... | collective-permute-start | bytes 768008 | tf_op jit(solution)/shard_map/ppermute | solution.py:38
  80.0 2.5 %collective-permute-start.14 = (bf16[1000,128]{1,0:T(8,128)(2,1)S(1)}, bf16[1000,128]{1,0:T(8,128)(2,1)S(1)}, u32[]{:S(2)}, u32[]{:S(2)}) collective-permute-start(bf16[1000,128]{1,0:T(8,128)(2,1)S(1)} %get-tuple-element.43), channel_id=1, source_target_pairs={{0,1},{2,3},{4,5},{6,7},{8,9},{10,11},{12,13},{14,15},{16,17},{18,... | collective-permute-start | bytes 768008 | tf_op jit(solution)/shard_map/ppermute | solution.py:38
  82.6 7.8 %collective-permute-start.15 = (bf16[1000,128]{1,0:T(8,128)(2,1)S(1)}, bf16[1000,128]{1,0:T(8,128)(2,1)S(1)}, u32[]{:S(2)}, u32[]{:S(2)}) collective-permute-start(bf16[1000,128]{1,0:T(8,128)(2,1)S(1)} %get-tuple-element.44), channel_id=1, source_target_pairs={{1,2},{3,4},{5,6},{7,8},{9,10},{11,12},{13,14},{15,16},{17,18},{19... | collective-permute-start | bytes 768008 | tf_op jit(solution)/shard_map/ppermute | solution.py:38
  90.4 5.3 %collective-permute-start.16 = (bf16[1000,128]{1,0:T(8,128)(2,1)S(1)}, bf16[1000,128]{1,0:T(8,128)(2,1)S(1)}, u32[]{:S(2)}, u32[]{:S(2)}) collective-permute-start(bf16[1000,128]{1,0:T(8,128)(2,1)S(1)} %get-tuple-element.45), channel_id=1, source_target_pairs={{48,96},{144,192},{240,288},{336,384},{432,480},{528,576},{624,672... | collective-permute-start | bytes 768008 | tf_op jit(solution)/shard_map/ppermute | solution.py:38
  95.7 0.0 collective-permute-done.12.refs_0_
  95.7 1.9 %collective-permute-start.17 = (bf16[1000,128]{1,0:T(8,128)(2,1)S(1)}, bf16[1000,128]{1,0:T(8,128)(2,1)S(1)}, u32[]{:S(2)}, u32[]{:S(2)}) collective-permute-start(bf16[1000,128]{1,0:T(8,128)(2,1)S(1)} %get-tuple-element.46), channel_id=1, source_target_pairs={{0,48},{96,144},{192,240},{288,336},{384,432},{480,528},{576,624},... | collective-permute-start | bytes 768008 | tf_op jit(solution)/shard_map/ppermute | solution.py:38
  97.6 0.0 collective-permute-done.13.refs_1_
  97.6 0.0 collective-permute-done.14.refs_2_
  97.7 2.0 %collective-permute-done.16.refs_4_ = bf16[1000,128]{1,0:T(8,128)(2,1)S(1)} collective-permute-done((bf16[1000,128]{1,0:T(8,128)(2,1)S(1)}, bf16[1000,128]{1,0:T(8,128)(2,1)S(1)}, u32[]{:S(2)}, u32[]{:S(2)}) %collective-permute-start.16) | collective-permute-done | bytes 256032 | tf_op jit(solution)/shard_map/ppermute | solution.py:38
  99.7 0.0 collective-permute-done.17.refs_5_
  99.7 3.5 %shard_map.77 = f32[1000,384]{1,0:T(8,128)} custom-call(s32[6]{0:T(128)S(1)} %stack.48.which_ref, bf16[1000,384]{1,0:T(8,128)(2,1)S(1)} %bitcast.23, s32[1,384]{1,0:T(1,128)S(1)} %broadcast_in_dim.6.seeds_ref, s32[1,384]{1,0:T(1,128)S(1)} %broadcast_in_dim.7.degree_ref, bf16[1152,384]{1,0:T(8,128)(2,1)S(1)} %shard_map.73.weight_ref, ...), custom_call_target="tpu_custom_call" | custom-call | tf_op jit(solution)/shard_map/pallas_call | solution.py:149
  (6 shorter events, 0.0 us)
Async XLA Ops:
  10.9 1.1 %copy-start = (bf16[384,1000]{0,1:T(8,128)(2,1)S(1)}, bf16[384,1000]{0,1:T(8,128)(2,1)}, u32[]{:S(2)}) copy-start(bf16[384,1000]{0,1:T(8,128)(2,1)} %param.7) | copy-start | bytes 2304004
  12.0 29.8 %copy-start.1 = (bf16[384,1000]{0,1:T(8,128)(2,1)S(1)}, bf16[384,1000]{0,1:T(8,128)(2,1)}, u32[]{:S(2)}) copy-start(bf16[384,1000]{0,1:T(8,128)(2,1)} %param.7) | copy-start | bytes 2304004
  15.2 20.7 %collective-permute-start = (bf16[1000,128]{1,0:T(8,128)(2,1)S(1)}, bf16[1000,128]{1,0:T(8,128)(2,1)S(1)}, u32[]{:S(2)}, u32[]{:S(2)}) collective-permute-start(bf16[1000,128]{1,0:T(8,128)(2,1)S(1)} %get-tuple-element.27), channel_id=1, source_target_pairs={{0,2},{1,3},{4,6},{5,7},{8,10},{9,11},{12,14},{13,15},{16,18},{17,... | collective-permute-start | bytes 768008 | tf_op jit(solution)/shard_map/ppermute | solution.py:38
  19.0 22.9 %collective-permute-start.1 = (bf16[1000,128]{1,0:T(8,128)(2,1)}, bf16[1000,128]{1,0:T(8,128)(2,1)S(1)}, u32[]{:S(2)}, u32[]{:S(2)}) collective-permute-start(bf16[1000,128]{1,0:T(8,128)(2,1)} %get-tuple-element.28), channel_id=1, source_target_pairs={{2,4},{3,5},{6,8},{7,9},{10,12},{11,13},{14,16},{15,17},{18,20},{1... | collective-permute-start | bytes 768008 | tf_op jit(solution)/shard_map/ppermute | solution.py:38
  21.1 20.7 %collective-permute-start.2 = (bf16[1000,128]{1,0:T(8,128)(2,1)}, bf16[1000,128]{1,0:T(8,128)(2,1)S(1)}, u32[]{:S(2)}, u32[]{:S(2)}) collective-permute-start(bf16[1000,128]{1,0:T(8,128)(2,1)} %get-tuple-element.29), channel_id=1, source_target_pairs={{0,1},{2,3},{4,5},{6,7},{8,9},{10,11},{12,13},{14,15},{16,17},{18,... | collective-permute-start | bytes 768008 | tf_op jit(solution)/shard_map/ppermute | solution.py:38
  24.0 17.9 %collective-permute-start.3 = (bf16[1000,128]{1,0:T(8,128)(2,1)}, bf16[1000,128]{1,0:T(8,128)(2,1)S(1)}, u32[]{:S(2)}, u32[]{:S(2)}) collective-permute-start(bf16[1000,128]{1,0:T(8,128)(2,1)} %get-tuple-element.30), channel_id=1, source_target_pairs={{1,2},{3,4},{5,6},{7,8},{9,10},{11,12},{13,14},{15,16},{17,18},{19... | collective-permute-start | bytes 768008 | tf_op jit(solution)/shard_map/ppermute | solution.py:38
  29.8 12.1 %collective-permute-start.4 = (bf16[1000,128]{1,0:T(8,128)(2,1)}, bf16[1000,128]{1,0:T(8,128)(2,1)S(1)}, u32[]{:S(2)}, u32[]{:S(2)}) collective-permute-start(bf16[1000,128]{1,0:T(8,128)(2,1)} %get-tuple-element.31), channel_id=1, source_target_pairs={{48,96},{144,192},{240,288},{336,384},{432,480},{528,576},{624,672... | collective-permute-start | bytes 768008 | tf_op jit(solution)/shard_map/ppermute | solution.py:38
  35.9 6.0 %collective-permute-start.5 = (bf16[1000,128]{1,0:T(8,128)(2,1)S(1)}, bf16[1000,128]{1,0:T(8,128)(2,1)S(1)}, u32[]{:S(2)}, u32[]{:S(2)}) collective-permute-start(bf16[1000,128]{1,0:T(8,128)(2,1)S(1)} %get-tuple-element.32), channel_id=1, source_target_pairs={{0,48},{96,144},{192,240},{288,336},{384,432},{480,528},{576,624},... | collective-permute-start | bytes 768008 | tf_op jit(solution)/shard_map/ppermute | solution.py:38
  38.6 1.1 %copy-start.2 = (bf16[3,8,128,128]{3,2,1,0:T(8,128)(2,1)S(1)}, bf16[3,8,128,128]{3,2,1,0:T(8,128)(2,1)}, u32[]{:S(2)}) copy-start(bf16[3,8,128,128]{3,2,1,0:T(8,128)(2,1)} %tiles_ref.1) | copy-start | bytes 2359300
  39.7 0.7 copy-start.3
  46.8 19.6 %collective-permute-start.6 = (bf16[1000,128]{1,0:T(8,128)(2,1)S(1)}, bf16[1000,128]{1,0:T(8,128)(2,1)S(1)}, u32[]{:S(2)}, u32[]{:S(2)}) collective-permute-start(bf16[1000,128]{1,0:T(8,128)(2,1)S(1)} %get-tuple-element.34), channel_id=1, source_target_pairs={{0,2},{1,3},{4,6},{5,7},{8,10},{9,11},{12,14},{13,15},{16,18},{17,... | collective-permute-start | bytes 768008 | tf_op jit(solution)/shard_map/ppermute | solution.py:38
  48.9 19.5 %collective-permute-start.7 = (bf16[1000,128]{1,0:T(8,128)(2,1)S(1)}, bf16[1000,128]{1,0:T(8,128)(2,1)S(1)}, u32[]{:S(2)}, u32[]{:S(2)}) collective-permute-start(bf16[1000,128]{1,0:T(8,128)(2,1)S(1)} %get-tuple-element.35), channel_id=1, source_target_pairs={{2,4},{3,5},{6,8},{7,9},{10,12},{11,13},{14,16},{15,17},{18,20},{1... | collective-permute-start | bytes 768008 | tf_op jit(solution)/shard_map/ppermute | solution.py:38
  52.7 15.7 %collective-permute-start.8 = (bf16[1000,128]{1,0:T(8,128)(2,1)S(1)}, bf16[1000,128]{1,0:T(8,128)(2,1)S(1)}, u32[]{:S(2)}, u32[]{:S(2)}) collective-permute-start(bf16[1000,128]{1,0:T(8,128)(2,1)S(1)} %get-tuple-element.36), channel_id=1, source_target_pairs={{0,1},{2,3},{4,5},{6,7},{8,9},{10,11},{12,13},{14,15},{16,17},{18,... | collective-permute-start | bytes 768008 | tf_op jit(solution)/shard_map/ppermute | solution.py:38
  54.8 14.1 %collective-permute-start.9 = (bf16[1000,128]{1,0:T(8,128)(2,1)S(1)}, bf16[1000,128]{1,0:T(8,128)(2,1)S(1)}, u32[]{:S(2)}, u32[]{:S(2)}) collective-permute-start(bf16[1000,128]{1,0:T(8,128)(2,1)S(1)} %get-tuple-element.37), channel_id=1, source_target_pairs={{1,2},{3,4},{5,6},{7,8},{9,10},{11,12},{13,14},{15,16},{17,18},{19... | collective-permute-start | bytes 768008 | tf_op jit(solution)/shard_map/ppermute | solution.py:38
  61.0 9.5 %collective-permute-start.10 = (bf16[1000,128]{1,0:T(8,128)(2,1)S(1)}, bf16[1000,128]{1,0:T(8,128)(2,1)S(1)}, u32[]{:S(2)}, u32[]{:S(2)}) collective-permute-start(bf16[1000,128]{1,0:T(8,128)(2,1)S(1)} %get-tuple-element.38), channel_id=1, source_target_pairs={{48,96},{144,192},{240,288},{336,384},{432,480},{528,576},{624,672... | collective-permute-start | bytes 768008 | tf_op jit(solution)/shard_map/ppermute | solution.py:38
  66.5 4.0 %collective-permute-start.11 = (bf16[1000,128]{1,0:T(8,128)(2,1)S(1)}, bf16[1000,128]{1,0:T(8,128)(2,1)S(1)}, u32[]{:S(2)}, u32[]{:S(2)}) collective-permute-start(bf16[1000,128]{1,0:T(8,128)(2,1)S(1)} %get-tuple-element.39), channel_id=1, source_target_pairs={{0,48},{96,144},{192,240},{288,336},{384,432},{480,528},{576,624},... | collective-permute-start | bytes 768008 | tf_op jit(solution)/shard_map/ppermute | solution.py:38
  75.3 20.4 %collective-permute-start.12 = (bf16[1000,128]{1,0:T(8,128)(2,1)S(1)}, bf16[1000,128]{1,0:T(8,128)(2,1)S(1)}, u32[]{:S(2)}, u32[]{:S(2)}) collective-permute-start(bf16[1000,128]{1,0:T(8,128)(2,1)S(1)} %get-tuple-element.41), channel_id=1, source_target_pairs={{0,2},{1,3},{4,6},{5,7},{8,10},{9,11},{12,14},{13,15},{16,18},{17,... | collective-permute-start | bytes 768008 | tf_op jit(solution)/shard_map/ppermute | solution.py:38
  77.5 20.1 %collective-permute-start.13 = (bf16[1000,128]{1,0:T(8,128)(2,1)S(1)}, bf16[1000,128]{1,0:T(8,128)(2,1)S(1)}, u32[]{:S(2)}, u32[]{:S(2)}) collective-permute-start(bf16[1000,128]{1,0:T(8,128)(2,1)S(1)} %get-tuple-element.42), channel_id=1, source_target_pairs={{2,4},{3,5},{6,8},{7,9},{10,12},{11,13},{14,16},{15,17},{18,20},{1... | collective-permute-start | bytes 768008 | tf_op jit(solution)/shard_map/ppermute | solution.py:38
  80.0 17.6 %collective-permute-start.14 = (bf16[1000,128]{1,0:T(8,128)(2,1)S(1)}, bf16[1000,128]{1,0:T(8,128)(2,1)S(1)}, u32[]{:S(2)}, u32[]{:S(2)}) collective-permute-start(bf16[1000,128]{1,0:T(8,128)(2,1)S(1)} %get-tuple-element.43), channel_id=1, source_target_pairs={{0,1},{2,3},{4,5},{6,7},{8,9},{10,11},{12,13},{14,15},{16,17},{18,... | collective-permute-start | bytes 768008 | tf_op jit(solution)/shard_map/ppermute | solution.py:38
  82.6 15.1 %collective-permute-start.15 = (bf16[1000,128]{1,0:T(8,128)(2,1)S(1)}, bf16[1000,128]{1,0:T(8,128)(2,1)S(1)}, u32[]{:S(2)}, u32[]{:S(2)}) collective-permute-start(bf16[1000,128]{1,0:T(8,128)(2,1)S(1)} %get-tuple-element.44), channel_id=1, source_target_pairs={{1,2},{3,4},{5,6},{7,8},{9,10},{11,12},{13,14},{15,16},{17,18},{19... | collective-permute-start | bytes 768008 | tf_op jit(solution)/shard_map/ppermute | solution.py:38
  90.4 9.3 %collective-permute-start.16 = (bf16[1000,128]{1,0:T(8,128)(2,1)S(1)}, bf16[1000,128]{1,0:T(8,128)(2,1)S(1)}, u32[]{:S(2)}, u32[]{:S(2)}) collective-permute-start(bf16[1000,128]{1,0:T(8,128)(2,1)S(1)} %get-tuple-element.45), channel_id=1, source_target_pairs={{48,96},{144,192},{240,288},{336,384},{432,480},{528,576},{624,672... | collective-permute-start | bytes 768008 | tf_op jit(solution)/shard_map/ppermute | solution.py:38
  95.7 4.0 %collective-permute-start.17 = (bf16[1000,128]{1,0:T(8,128)(2,1)S(1)}, bf16[1000,128]{1,0:T(8,128)(2,1)S(1)}, u32[]{:S(2)}, u32[]{:S(2)}) collective-permute-start(bf16[1000,128]{1,0:T(8,128)(2,1)S(1)} %get-tuple-element.46), channel_id=1, source_target_pairs={{0,48},{96,144},{192,240},{288,336},{384,432},{480,528},{576,624},... | collective-permute-start | bytes 768008 | tf_op jit(solution)/shard_map/ppermute | solution.py:38

commit v2 on v0

v2 whole, which is shorter than its diff:
```python
import functools

import jax
import jax.numpy as jnp
from jax import lax
from jax.experimental import pallas as pl
from jax.experimental.pallas import tpu as pltpu
from jax.sharding import PartitionSpec as P

ITERS = 3
CORES = 2
ROW = 4
CHUNK = 256
SIDE = 128
SMEM = pl.BlockSpec(memory_space=pltpu.SMEM)
VMEM = pl.BlockSpec(memory_space=pltpu.VMEM)
HBM = pl.BlockSpec(memory_space=pltpu.HBM)
PARAMS = pltpu.CompilerParams(vmem_limit_bytes=40 * 1024 * 1024)

RING, BACK, TWO, CROSS, EDGE, UP, DOWN = range(7)
PERMUTES = 7


def routes(n_group, n_dom):
    def flat(g, d):
        return (g % n_group) * n_dom + d

    places = [(g, d) for g in range(n_group) for d in range(n_dom)]

    def ring(g, d):
        if g % CORES == 0:
            return (g, d + 1) if d % ROW < ROW - 1 else (g + 1, d)
        return (g, d - 1) if d % ROW > 0 else (g - 1, d)

    def pairs(distance, takes):
        both = []
        for g, d in places:
            if takes(d % ROW) and d + distance < n_dom:
                both += [(flat(g, d), flat(g, d + distance)), (flat(g, d + distance), flat(g, d))]
        return both

    forward = [(flat(*p), flat(*ring(*p))) for p in places]
    return {
        RING: forward,
        BACK: [(b, a) for a, b in forward],
        TWO: pairs(2, lambda x: x < 2),
        CROSS: pairs(2, lambda x: x >= 2),
        EDGE: pairs(1, lambda x: x == ROW - 1),
        UP: [(flat(g, d), flat(g + 1, d)) for g, d in places],
        DOWN: [(flat(g, d), flat(g - 1, d)) for g, d in places],
    }


def position():
    group, dom = lax.axis_index("group"), lax.axis_index("dom")
    return group, jnp.bitwise_and(group, CORES - 1), jnp.bitwise_and(dom, ROW - 1)


def columns_to_send():
    _, core, x = position()
    high = x >= 2
    return {
        RING: jnp.where(core == 0, 1, 0),
        BACK: jnp.where(core == 0, 0, 1),
        TWO: jnp.where(high, 2, 3),
        CROSS: jnp.where(high, 3, 2),
        EDGE: jnp.where(x == 0, 0, 1),
        UP: 5,
        DOWN: 4,
    }


def chunks(rows):
    return [(at, min(CHUNK, rows - at)) for at in range(0, rows, CHUNK)]


def put_sends(rows, send_ref, own_ref, send_refs):
    for k, column in columns_to_send().items():
        block = pl.ds(pl.multiple_of(send_ref[0, column] * SIDE, SIDE), SIDE)
        send_refs[k][rows, :] = own_ref[rows, block]


def prepare_kernel(send_ref, seeds_ref, degree_ref, prior_ref, start_ref, own_ref, *refs):
    send_refs, (held, arrived) = refs[:PERMUTES], refs[PERMUTES:]
    classes = prior_ref.shape[0]
    copies = []
    for k, (at, size) in enumerate(chunks(classes)):
        rows = pl.ds(at, size)
        copies.append(pltpu.make_async_copy(prior_ref.at[rows], held.at[rows], arrived.at[k]))
        copies[-1].start()
    inv_root = 1.0 / jnp.sqrt(degree_ref[...].astype(jnp.float32))
    seeds = seeds_ref[...]
    for k, (at, size) in enumerate(chunks(classes)):
        rows = pl.ds(at, size)
        copies[k].wait()
        label = lax.broadcasted_iota(jnp.int32, (size, seeds.shape[1]), 0) + at
        onehot = jnp.where(label == seeds, 1.0, 0.0)
        start = jnp.where(seeds < classes, onehot, held[rows, :].astype(jnp.float32))
        start_ref[rows, :] = start.astype(jnp.bfloat16)
        own_ref[rows, :] = (inv_root * start).astype(jnp.bfloat16)
        put_sends(rows, send_ref, own_ref, send_refs)


def new_labels(rows, degree_ref, start_ref, weight_ref, own_ref, received):
    inv_root = 1.0 / jnp.sqrt(degree_ref[...].astype(jnp.float32))
    sources = jnp.concatenate([own_ref[rows, :]] + [ref[rows, :] for ref in received], axis=1)
    product = jnp.dot(sources, weight_ref[...], preferred_element_type=jnp.float32)
    labels = 0.9 * inv_root * product + 0.1 * start_ref[rows, :].astype(jnp.float32)
    return inv_root, labels


def step_kernel(send_ref, degree_ref, start_ref, weight_ref, own_ref, *refs):
    received, next_ref, send_refs = refs[:PERMUTES], refs[PERMUTES], refs[PERMUTES + 1 :]
    for at, size in chunks(own_ref.shape[0]):
        rows = pl.ds(at, size)
        inv_root, labels = new_labels(rows, degree_ref, start_ref, weight_ref, own_ref, received)
        next_ref[rows, :] = (inv_root * labels).astype(jnp.bfloat16)
        put_sends(rows, send_ref, next_ref, send_refs)


def last_kernel(degree_ref, start_ref, weight_ref, own_ref, *refs):
    received, (out_ref, held, left) = refs[:PERMUTES], refs[PERMUTES:]
    copies = []
    for k, (at, size) in enumerate(chunks(own_ref.shape[0])):
        rows = pl.ds(at, size)
        _, labels = new_labels(rows, degree_ref, start_ref, weight_ref, own_ref, received)
        held[rows, :] = labels
        copies.append(pltpu.make_async_copy(held.at[rows], out_ref.at[rows], left.at[k]))
        copies[-1].start()
    for copy in copies:
        copy.wait()


def weight_kernel(n_group, source_ref, count_ref, tiles_ref, weight_ref, total_ref):
    row_blocks, per_row, side, _ = tiles_ref.shape
    group, core, x = position()
    own = row_blocks
    place = [
        jnp.where(x == 0, own + EDGE, jnp.where(core == 0, own + RING, own + BACK)),
        jnp.where(x == ROW - 1, own + EDGE, jnp.where(core == 0, own + BACK, own + RING)),
        jnp.where(x >= 2, own + TWO, own + CROSS),
        jnp.where(x >= 2, own + CROSS, own + TWO),
        own + UP,
        own + DOWN,
    ]
    for r in range(row_blocks):
        total_ref[...] = jnp.zeros_like(total_ref)
        for t in range(per_row):
            source = source_ref[r, t]
            slot = source
            for k, where in enumerate(place):
                slot = jnp.where(source == own + k, where, slot)
            live = r * per_row + t < count_ref[0]
            live = live & ((source != own + 4) | (group > 0))
            live = live & ((source != own + 5) | (group < n_group - 1))

            @pl.when(live)
            def _():
                total_ref[slot] += tiles_ref[r, t].astype(jnp.float32)

        for s in range(own + PERMUTES):
            weight_ref[pl.ds(s * side, side), pl.ds(r * side, side)] = total_ref[s].T.astype(
                weight_ref.dtype
            )


def on_device(prior, seed_labels, degree, tiles, tile_source, tile_count, send_list):
    row_blocks, _, side, _ = tiles.shape
    nodes, classes = prior.shape
    n_group, n_dom = lax.axis_size("group"), lax.axis_size("dom")
    route = routes(n_group, n_dom)
    slots = row_blocks + PERMUTES
    pieces = len(chunks(classes))
    seeds, degrees = seed_labels[None, :], degree[None, :]
    wide = jax.ShapeDtypeStruct((classes, nodes), jnp.bfloat16)
    narrow = [jax.ShapeDtypeStruct((classes, side), jnp.bfloat16)] * PERMUTES

    start, own, *sends = pl.pallas_call(
        prepare_kernel,
        in_specs=[SMEM, VMEM, VMEM, HBM],
        out_specs=[VMEM] * (2 + PERMUTES),
        out_shape=[wide, wide] + narrow,
        scratch_shapes=[
            pltpu.VMEM((classes, nodes), jnp.bfloat16),
            pltpu.SemaphoreType.DMA((pieces,)),
        ],
        compiler_params=PARAMS,
    )(send_list, seeds, degrees, prior.T)
    weight = pl.pallas_call(
        functools.partial(weight_kernel, n_group),
        in_specs=[SMEM, SMEM, VMEM],
        out_specs=VMEM,
        out_shape=jax.ShapeDtypeStruct((slots * side, nodes), jnp.bfloat16),
        scratch_shapes=[pltpu.VMEM((slots, side, side), jnp.float32)],
        compiler_params=PARAMS,
        cost_estimate=pl.CostEstimate(flops=0, bytes_accessed=8_000_000, transcendentals=0),
    )(tile_source, tile_count, tiles)
    for step in range(ITERS):
        received = [lax.ppermute(sends[k], ("group", "dom"), route[k]) for k in range(PERMUTES)]
        if step < ITERS - 1:
            own, *sends = pl.pallas_call(
                step_kernel,
                in_specs=[SMEM] + [VMEM] * (4 + PERMUTES),
                out_specs=[VMEM] * (1 + PERMUTES),
                out_shape=[wide] + narrow,
                compiler_params=PARAMS,
            )(send_list, degrees, start, weight, own, *received)
    labels = pl.pallas_call(
        last_kernel,
        in_specs=[VMEM] * (4 + PERMUTES),
        out_specs=HBM,
        out_shape=jax.ShapeDtypeStruct((classes, nodes), jnp.float32),
        scratch_shapes=[
            pltpu.VMEM((classes, nodes), jnp.float32),
            pltpu.SemaphoreType.DMA((pieces,)),
        ],
        compiler_params=PARAMS,
    )(degrees, start, weight, own, *received)
    return labels.T


def solution(mesh):
    return jax.shard_map(
        on_device,
        mesh=mesh,
        in_specs=(
            P(("group", "dom"), None),
            P(("group", "dom")),
            P(("group", "dom")),
            P(("group", "dom"), None, None, None),
            P(("group", "dom"), None),
            P(("group", "dom")),
            P(("group", "dom"), None),
        ),
        out_specs=P(("group", "dom"), None),
        check_vma=False,
    )
```

time: 158 us -> 89.6 us (0.57)
  the two profiles are of different devices: /device:TPU:512 before, /device:TPU:281 now
where the time goes in v2:
time: 89.6 us; the launch traced here: 89.1 us
  starting transfers between devices  55.6 us (62%)
  waiting for transfers between devices  16.8 us (19%)
  Pallas kernels  10.9 us (12%)
  local copies, waits for them, and re-layouts  4.97 us (6%)
    ppermute x21, starting transfers between devices, on_device(): lax.ppermute(sends[k], ('group', 'dom'), route[k])  55.6 us
    ppermute x21, waiting for transfers between devices, on_device(): lax.ppermute(sends[k], ('group', 'dom'), route[k])  16.8 us
    pallas_call x2, Pallas kernels, on_device(): pl.pallas_call(step_kernel, in_specs=[SMEM] + [VMEM] * (4 + PERMUTES), ou...  4.6 us
    unnamed x10, local copies, waits for them, and re-layouts  3.59 us
    pallas_call x1, Pallas kernels, on_device(): pl.pallas_call(prepare_kernel, in_specs=[SMEM, VMEM, VMEM, HBM], out_spec...  2.43 us
    pallas_call x1, Pallas kernels, on_device(): pl.pallas_call(last_kernel, in_specs=[VMEM] * (4 + PERMUTES), out_specs=H...  2.3 us
  transfers between devices with their start and end apart: 21, of which 9 were waited for; matrix products, arithmetic and copies ran while one was open for 0% of the time, Pallas kernels for 2%

profile of v2, /device:TPU:281, one launch (start us, length us, event | category | flops | bytes accessed | tf_op | source)
XLA Modules:
  0.0 89.1 jit_solution(14507459660648233188)
XLA Ops:
  0.0 0.7 broadcast_in_dim.6.degree_ref
  0.7 0.7 broadcast_in_dim.7.seeds_ref
  1.4 1.1 %copy-done.1 = bf16[384,1000]{0,1:T(8,128)(2,1)S(1)} copy-done((bf16[384,1000]{0,1:T(8,128)(2,1)S(1)}, bf16[384,1000]{0,1:T(8,128)(2,1)}, u32[]{:S(2)}) %copy-start.1) | copy-done | bytes 768024
  2.5 0.7 copy-done.2
  3.2 2.4 %shard_map.73 = (bf16[1000,384]{1,0:T(8,128)(2,1)S(1)}, bf16[1000,384]{1,0:T(8,128)(2,1)S(1)}, bf16[1000,128]{1,0:T(8,128)(2,1)S(1)}, bf16[1000,128]{1,0:T(8,128...) custom-call(s32[1,6]{1,0:T(1,128)S(1)} %copy-done.2, ...), custom_call_target="tpu_custom_call" | custom-call | tf_op jit(solution)/shard_map/pallas_call | solution.py:178
  5.6 0.7 collective-permute-start
  6.3 0.8 collective-permute-start.1
  7.1 4.6 %collective-permute-start.2 = (bf16[1000,128]{1,0:T(8,128)(2,1)S(1)}, bf16[1000,128]{1,0:T(8,128)(2,1)S(1)}, u32[]{:S(2)}, u32[]{:S(2)}) collective-permute-start(bf16[1000,128]{1,0:T(8,128)(2,1)S(1)} %get-tuple-element.34), channel_id=1, source_target_pairs={{0,2},{2,0},{1,3},{3,1},{4,6},{6,4},{5,7},{7,5},{8,10},{10,8},{9,1... | collective-permute-start | bytes 768008 | tf_op jit(solution)/shard_map/ppermute | solution.py:199
  11.7 1.9 %collective-permute-start.3 = (bf16[1000,128]{1,0:T(8,128)(2,1)S(1)}, bf16[1000,128]{1,0:T(8,128)(2,1)S(1)}, u32[]{:S(2)}, u32[]{:S(2)}) collective-permute-start(bf16[1000,128]{1,0:T(8,128)(2,1)S(1)} %get-tuple-element.35), channel_id=1, source_target_pairs={{2,4},{4,2},{3,5},{5,3},{6,8},{8,6},{7,9},{9,7},{10,12},{12,10},{1... | collective-permute-start | bytes 768008 | tf_op jit(solution)/shard_map/ppermute | solution.py:199
  13.7 5.9 %collective-permute-start.4 = (bf16[1000,128]{1,0:T(8,128)(2,1)S(1)}, bf16[1000,128]{1,0:T(8,128)(2,1)S(1)}, u32[]{:S(2)}, u32[]{:S(2)}) collective-permute-start(bf16[1000,128]{1,0:T(8,128)(2,1)S(1)} %get-tuple-element.36), channel_id=1, source_target_pairs={{3,4},{4,3},{7,8},{8,7},{11,12},{12,11},{15,16},{16,15},{19,20},{2... | collective-permute-start | bytes 768008 | tf_op jit(solution)/shard_map/ppermute | solution.py:199
  19.6 0.0 collective-permute-done.refs_0_
  19.6 5.3 %collective-permute-start.5 = (bf16[1000,128]{1,0:T(8,128)(2,1)S(1)}, bf16[1000,128]{1,0:T(8,128)(2,1)S(1)}, u32[]{:S(2)}, u32[]{:S(2)}) collective-permute-start(bf16[1000,128]{1,0:T(8,128)(2,1)S(1)} %get-tuple-element.37), channel_id=1, source_target_pairs={{0,48},{1,49},{2,50},{3,51},{4,52},{5,53},{6,54},{7,55},{8,56},{9,... | collective-permute-start | bytes 768008 | tf_op jit(solution)/shard_map/ppermute | solution.py:199
  24.9 0.0 collective-permute-done.1.refs_1_
  24.9 0.0 collective-permute-start.6
  25.5 0.0 copy-start
  25.6 1.1 %copy-done = bf16[3,8,128,128]{3,2,1,0:T(8,128)(2,1)S(1)} copy-done((bf16[3,8,128,128]{3,2,1,0:T(8,128)(2,1)S(1)}, bf16[3,8,128,128]{3,2,1,0:T(8,128)(2,1)}, u32[]{:S(2)}) %copy-start) | copy-done | bytes 786456
  26.7 0.7 copy-done.4
  27.4 1.5 %shard_map.74.weight_ref = bf16[1280,384]{1,0:T(8,128)(2,1)S(1)} custom-call(s32[3,8]{1,0:T(4,128)S(1)} %copy-done.4, s32[1]{0:T(128)S(6)} %copy.8.count_ref, bf16[3,8,128,128]{3,2,1,0:T(8,128)(2,1)S(1)} %copy-done), custom_call_target="tpu_custom_call" | custom-call | bytes 8000000 | tf_op jit(solution)/shard_map/pallas_call | solution.py:189
  28.9 2.7 %collective-permute-done.2.refs_2_ = bf16[1000,128]{1,0:T(8,128)(2,1)S(1)} collective-permute-done((bf16[1000,128]{1,0:T(8,128)(2,1)S(1)}, bf16[1000,128]{1,0:T(8,128)(2,1)S(1)}, u32[]{:S(2)}, u32[]{:S(2)}) %collective-permute-start.2) | collective-permute-done | bytes 256032 | tf_op jit(solution)/shard_map/ppermute | solution.py:199
  31.6 0.0 collective-permute-done.3.refs_3_
  31.6 0.0 collective-permute-done.4.refs_4_
  31.6 0.0 collective-permute-done.5.refs_5_
  31.6 0.2 collective-permute-done.6.refs_6_
  31.8 2.3 %shard_map.75 = (bf16[1000,384]{1,0:T(8,128)(2,1)S(1)}, bf16[1000,128]{1,0:T(8,128)(2,1)S(1)}, bf16[1000,128]{1,0:T(8,128)(2,1)S(1)}, bf16[1000,128]{1,0:T(8,128...) custom-call(s32[1,6]{1,0:T(1,128)S(1)} %copy-done.3, ...), custom_call_target="tpu_custom_call" | custom-call | tf_op jit(solution)/shard_map/pallas_call | solution.py:201
  34.2 1.6 %collective-permute-start.7 = (bf16[1000,128]{1,0:T(8,128)(2,1)S(1)}, bf16[1000,128]{1,0:T(8,128)(2,1)S(1)}, u32[]{:S(2)}, u32[]{:S(2)}) collective-permute-start(bf16[1000,128]{1,0:T(8,128)(2,1)S(1)} %get-tuple-element.40), channel_id=1, source_target_pairs={{0,1},{1,2},{2,3},{3,51},{4,5},{5,6},{6,7},{7,55},{8,9},{9,10},{10... | collective-permute-start | bytes 768008 | tf_op jit(solution)/shard_map/ppermute | solution.py:199
  35.8 0.0 collective-permute-start.8
  35.8 1.9 %collective-permute-start.9 = (bf16[1000,128]{1,0:T(8,128)(2,1)S(1)}, bf16[1000,128]{1,0:T(8,128)(2,1)S(1)}, u32[]{:S(2)}, u32[]{:S(2)}) collective-permute-start(bf16[1000,128]{1,0:T(8,128)(2,1)S(1)} %get-tuple-element.42), channel_id=1, source_target_pairs={{0,2},{2,0},{1,3},{3,1},{4,6},{6,4},{5,7},{7,5},{8,10},{10,8},{9,1... | collective-permute-start | bytes 768008 | tf_op jit(solution)/shard_map/ppermute | solution.py:199
  37.7 4.0 %collective-permute-start.10 = (bf16[1000,128]{1,0:T(8,128)(2,1)S(1)}, bf16[1000,128]{1,0:T(8,128)(2,1)S(1)}, u32[]{:S(2)}, u32[]{:S(2)}) collective-permute-start(bf16[1000,128]{1,0:T(8,128)(2,1)S(1)} %get-tuple-element.43), channel_id=1, source_target_pairs={{2,4},{4,2},{3,5},{5,3},{6,8},{8,6},{7,9},{9,7},{10,12},{12,10},{1... | collective-permute-start | bytes 768008 | tf_op jit(solution)/shard_map/ppermute | solution.py:199
  41.7 4.6 %collective-permute-start.11 = (bf16[1000,128]{1,0:T(8,128)(2,1)S(1)}, bf16[1000,128]{1,0:T(8,128)(2,1)S(1)}, u32[]{:S(2)}, u32[]{:S(2)}) collective-permute-start(bf16[1000,128]{1,0:T(8,128)(2,1)S(1)} %get-tuple-element.44), channel_id=1, source_target_pairs={{3,4},{4,3},{7,8},{8,7},{11,12},{12,11},{15,16},{16,15},{19,20},{2... | collective-permute-start | bytes 768008 | tf_op jit(solution)/shard_map/ppermute | solution.py:199
  46.3 5.2 %collective-permute-start.12 = (bf16[1000,128]{1,0:T(8,128)(2,1)S(1)}, bf16[1000,128]{1,0:T(8,128)(2,1)S(1)}, u32[]{:S(2)}, u32[]{:S(2)}) collective-permute-start(bf16[1000,128]{1,0:T(8,128)(2,1)S(1)} %get-tuple-element.45), channel_id=1, source_target_pairs={{0,48},{1,49},{2,50},{3,51},{4,52},{5,53},{6,54},{7,55},{8,56},{9,... | collective-permute-start | bytes 768008 | tf_op jit(solution)/shard_map/ppermute | solution.py:199
  51.5 0.0 collective-permute-done.8.refs_1_
  51.5 0.0 collective-permute-start.13
  51.5 1.5 %collective-permute-done.9.refs_2_ = bf16[1000,128]{1,0:T(8,128)(2,1)S(1)} collective-permute-done((bf16[1000,128]{1,0:T(8,128)(2,1)S(1)}, bf16[1000,128]{1,0:T(8,128)(2,1)S(1)}, u32[]{:S(2)}, u32[]{:S(2)}) %collective-permute-start.9) | collective-permute-done | bytes 256032 | tf_op jit(solution)/shard_map/ppermute | solution.py:199
  53.0 0.0 collective-permute-done.10.refs_3_
  53.0 3.6 %collective-permute-done.11.refs_4_ = bf16[1000,128]{1,0:T(8,128)(2,1)S(1)} collective-permute-done((bf16[1000,128]{1,0:T(8,128)(2,1)S(1)}, bf16[1000,128]{1,0:T(8,128)(2,1)S(1)}, u32[]{:S(2)}, u32[]{:S(2)}) %collective-permute-start.11) | collective-permute-done | bytes 256032 | tf_op jit(solution)/shard_map/ppermute | solution.py:199
  56.6 1.9 %collective-permute-done.13.refs_6_ = bf16[1000,128]{1,0:T(8,128)(2,1)S(1)} collective-permute-done((bf16[1000,128]{1,0:T(8,128)(2,1)S(1)}, bf16[1000,128]{1,0:T(8,128)(2,1)S(1)}, u32[]{:S(2)}, u32[]{:S(2)}) %collective-permute-start.13) | collective-permute-done | bytes 256032 | tf_op jit(solution)/shard_map/ppermute | solution.py:199
  58.5 2.3 %shard_map.76 = (bf16[1000,384]{1,0:T(8,128)(2,1)S(1)}, bf16[1000,128]{1,0:T(8,128)(2,1)S(1)}, bf16[1000,128]{1,0:T(8,128)(2,1)S(1)}, bf16[1000,128]{1,0:T(8,128...) custom-call(s32[1,6]{1,0:T(1,128)S(1)} %copy-done.3, ...), custom_call_target="tpu_custom_call" | custom-call | tf_op jit(solution)/shard_map/pallas_call | solution.py:201
  60.8 0.3 collective-permute-start.14
  61.1 1.2 %collective-permute-start.15 = (bf16[1000,128]{1,0:T(8,128)(2,1)S(1)}, bf16[1000,128]{1,0:T(8,128)(2,1)S(1)}, u32[]{:S(2)}, u32[]{:S(2)}) collective-permute-start(bf16[1000,128]{1,0:T(8,128)(2,1)S(1)} %get-tuple-element.49), channel_id=1, source_target_pairs={{1,0},{2,1},{3,2},{51,3},{5,4},{6,5},{7,6},{55,7},{9,8},{10,9},{11... | collective-permute-start | bytes 768008 | tf_op jit(solution)/shard_map/ppermute | solution.py:199
  62.2 3.1 %collective-permute-start.16 = (bf16[1000,128]{1,0:T(8,128)(2,1)S(1)}, bf16[1000,128]{1,0:T(8,128)(2,1)S(1)}, u32[]{:S(2)}, u32[]{:S(2)}) collective-permute-start(bf16[1000,128]{1,0:T(8,128)(2,1)S(1)} %get-tuple-element.50), channel_id=1, source_target_pairs={{0,2},{2,0},{1,3},{3,1},{4,6},{6,4},{5,7},{7,5},{8,10},{10,8},{9,1... | collective-permute-start | bytes 768008 | tf_op jit(solution)/shard_map/ppermute | solution.py:199
  65.3 2.6 %collective-permute-start.17 = (bf16[1000,128]{1,0:T(8,128)(2,1)S(1)}, bf16[1000,128]{1,0:T(8,128)(2,1)S(1)}, u32[]{:S(2)}, u32[]{:S(2)}) collective-permute-start(bf16[1000,128]{1,0:T(8,128)(2,1)S(1)} %get-tuple-element.51), channel_id=1, source_target_pairs={{2,4},{4,2},{3,5},{5,3},{6,8},{8,6},{7,9},{9,7},{10,12},{12,10},{1... | collective-permute-start | bytes 768008 | tf_op jit(solution)/shard_map/ppermute | solution.py:199
  67.9 6.8 %collective-permute-start.18 = (bf16[1000,128]{1,0:T(8,128)(2,1)S(1)}, bf16[1000,128]{1,0:T(8,128)(2,1)S(1)}, u32[]{:S(2)}, u32[]{:S(2)}) collective-permute-start(bf16[1000,128]{1,0:T(8,128)(2,1)S(1)} %get-tuple-element.52), channel_id=1, source_target_pairs={{3,4},{4,3},{7,8},{8,7},{11,12},{12,11},{15,16},{16,15},{19,20},{2... | collective-permute-start | bytes 768008 | tf_op jit(solution)/shard_map/ppermute | solution.py:199
  74.8 5.0 %collective-permute-start.19 = (bf16[1000,128]{1,0:T(8,128)(2,1)S(1)}, bf16[1000,128]{1,0:T(8,128)(2,1)S(1)}, u32[]{:S(2)}, u32[]{:S(2)}) collective-permute-start(bf16[1000,128]{1,0:T(8,128)(2,1)S(1)} %get-tuple-element.53), channel_id=1, source_target_pairs={{0,48},{1,49},{2,50},{3,51},{4,52},{5,53},{6,54},{7,55},{8,56},{9,... | collective-permute-start | bytes 768008 | tf_op jit(solution)/shard_map/ppermute | solution.py:199
  79.8 0.9 collective-permute-done.16.refs_2_
  80.7 2.3 %collective-permute-done.18.refs_4_ = bf16[1000,128]{1,0:T(8,128)(2,1)S(1)} collective-permute-done((bf16[1000,128]{1,0:T(8,128)(2,1)S(1)}, bf16[1000,128]{1,0:T(8,128)(2,1)S(1)}, u32[]{:S(2)}, u32[]{:S(2)}) %collective-permute-start.18) | collective-permute-done | bytes 256032 | tf_op jit(solution)/shard_map/ppermute | solution.py:199
  83.0 0.1 collective-permute-done.19.refs_5_
  83.1 3.7 %collective-permute-done.20.refs_6_ = bf16[1000,128]{1,0:T(8,128)(2,1)S(1)} collective-permute-done((bf16[1000,128]{1,0:T(8,128)(2,1)S(1)}, bf16[1000,128]{1,0:T(8,128)(2,1)S(1)}, u32[]{:S(2)}, u32[]{:S(2)}) %collective-permute-start.20) | collective-permute-done | bytes 256032 | tf_op jit(solution)/shard_map/ppermute | solution.py:199
  86.8 2.3 %shard_map.77 = f32[1000,384]{1,0:T(8,128)} custom-call(s32[1,384]{1,0:T(1,128)S(1)} %broadcast_in_dim.6.degree_ref, bf16[1000,384]{1,0:T(8,128)(2,1)S(1)} %get-tuple-element.30.start_ref, bf16[1280,384]{1,0:T(8,128)(2,1)S(1)} %shard_map.74.weight_ref, bf16[1000,384]{1,0:T(8,128)(2,1)S(1)} %get-tuple-element.47.own_ref, ...), custom_call_target="tpu_custom_call" | custom-call | tf_op jit(solution)/shard_map/pallas_call | solution.py:208
  (11 shorter events, 0.0 us)
Async XLA Ops:
  0.0 31.8 %copy-start.3 = (s32[1,6]{1,0:T(1,128)S(1)}, s32[1,6]{1,0:T(1,128)}, u32[]{:S(2)}) copy-start(s32[1,6]{1,0:T(1,128)} %send_ref.5) | copy-start | bytes 76
  1.4 1.1 %copy-start.1 = (bf16[384,1000]{0,1:T(8,128)(2,1)S(1)}, bf16[384,1000]{0,1:T(8,128)(2,1)}, u32[]{:S(2)}) copy-start(bf16[384,1000]{0,1:T(8,128)(2,1)} %param.7) | copy-start | bytes 2304004
  2.5 0.7 copy-start.2
  5.6 14.0 %collective-permute-start = (bf16[1000,128]{1,0:T(8,128)(2,1)S(1)}, bf16[1000,128]{1,0:T(8,128)(2,1)S(1)}, u32[]{:S(2)}, u32[]{:S(2)}) collective-permute-start(bf16[1000,128]{1,0:T(8,128)(2,1)S(1)} %get-tuple-element.32), channel_id=1, source_target_pairs={{0,1},{1,2},{2,3},{3,51},{4,5},{5,6},{6,7},{7,55},{8,9},{9,10},{10... | collective-permute-start | bytes 768008 | tf_op jit(solution)/shard_map/ppermute | solution.py:199
  6.3 18.6 %collective-permute-start.1 = (bf16[1000,128]{1,0:T(8,128)(2,1)S(1)}, bf16[1000,128]{1,0:T(8,128)(2,1)S(1)}, u32[]{:S(2)}, u32[]{:S(2)}) collective-permute-start(bf16[1000,128]{1,0:T(8,128)(2,1)S(1)} %get-tuple-element.33), channel_id=1, source_target_pairs={{1,0},{2,1},{3,2},{51,3},{5,4},{6,5},{7,6},{55,7},{9,8},{10,9},{11... | collective-permute-start | bytes 768008 | tf_op jit(solution)/shard_map/ppermute | solution.py:199
  7.1 24.5 %collective-permute-start.2 = (bf16[1000,128]{1,0:T(8,128)(2,1)S(1)}, bf16[1000,128]{1,0:T(8,128)(2,1)S(1)}, u32[]{:S(2)}, u32[]{:S(2)}) collective-permute-start(bf16[1000,128]{1,0:T(8,128)(2,1)S(1)} %get-tuple-element.34), channel_id=1, source_target_pairs={{0,2},{2,0},{1,3},{3,1},{4,6},{6,4},{5,7},{7,5},{8,10},{10,8},{9,1... | collective-permute-start | bytes 768008 | tf_op jit(solution)/shard_map/ppermute | solution.py:199
  11.7 19.9 %collective-permute-start.3 = (bf16[1000,128]{1,0:T(8,128)(2,1)S(1)}, bf16[1000,128]{1,0:T(8,128)(2,1)S(1)}, u32[]{:S(2)}, u32[]{:S(2)}) collective-permute-start(bf16[1000,128]{1,0:T(8,128)(2,1)S(1)} %get-tuple-element.35), channel_id=1, source_target_pairs={{2,4},{4,2},{3,5},{5,3},{6,8},{8,6},{7,9},{9,7},{10,12},{12,10},{1... | collective-permute-start | bytes 768008 | tf_op jit(solution)/shard_map/ppermute | solution.py:199
  13.7 18.0 %collective-permute-start.4 = (bf16[1000,128]{1,0:T(8,128)(2,1)S(1)}, bf16[1000,128]{1,0:T(8,128)(2,1)S(1)}, u32[]{:S(2)}, u32[]{:S(2)}) collective-permute-start(bf16[1000,128]{1,0:T(8,128)(2,1)S(1)} %get-tuple-element.36), channel_id=1, source_target_pairs={{3,4},{4,3},{7,8},{8,7},{11,12},{12,11},{15,16},{16,15},{19,20},{2... | collective-permute-start | bytes 768008 | tf_op jit(solution)/shard_map/ppermute | solution.py:199
  19.6 12.0 %collective-permute-start.5 = (bf16[1000,128]{1,0:T(8,128)(2,1)S(1)}, bf16[1000,128]{1,0:T(8,128)(2,1)S(1)}, u32[]{:S(2)}, u32[]{:S(2)}) collective-permute-start(bf16[1000,128]{1,0:T(8,128)(2,1)S(1)} %get-tuple-element.37), channel_id=1, source_target_pairs={{0,48},{1,49},{2,50},{3,51},{4,52},{5,53},{6,54},{7,55},{8,56},{9,... | collective-permute-start | bytes 768008 | tf_op jit(solution)/shard_map/ppermute | solution.py:199
  24.9 6.9 %collective-permute-start.6 = (bf16[1000,128]{1,0:T(8,128)(2,1)S(1)}, bf16[1000,128]{1,0:T(8,128)(2,1)S(1)}, u32[]{:S(2)}, u32[]{:S(2)}) collective-permute-start(bf16[1000,128]{1,0:T(8,128)(2,1)S(1)} %get-tuple-element.38), channel_id=1, source_target_pairs={{0,720},{1,721},{2,722},{3,723},{4,724},{5,725},{6,726},{7,727},{8... | collective-permute-start | bytes 768008 | tf_op jit(solution)/shard_map/ppermute | solution.py:199
  25.5 1.1 %copy-start = (bf16[3,8,128,128]{3,2,1,0:T(8,128)(2,1)S(1)}, bf16[3,8,128,128]{3,2,1,0:T(8,128)(2,1)}, u32[]{:S(2)}) copy-start(bf16[3,8,128,128]{3,2,1,0:T(8,128)(2,1)} %tiles_ref.1) | copy-start | bytes 2359300
  26.7 0.7 copy-start.4
  34.2 12.1 %collective-permute-start.7 = (bf16[1000,128]{1,0:T(8,128)(2,1)S(1)}, bf16[1000,128]{1,0:T(8,128)(2,1)S(1)}, u32[]{:S(2)}, u32[]{:S(2)}) collective-permute-start(bf16[1000,128]{1,0:T(8,128)(2,1)S(1)} %get-tuple-element.40), channel_id=1, source_target_pairs={{0,1},{1,2},{2,3},{3,51},{4,5},{5,6},{6,7},{7,55},{8,9},{9,10},{10... | collective-permute-start | bytes 768008 | tf_op jit(solution)/shard_map/ppermute | solution.py:199
  35.8 15.7 %collective-permute-start.8 = (bf16[1000,128]{1,0:T(8,128)(2,1)S(1)}, bf16[1000,128]{1,0:T(8,128)(2,1)S(1)}, u32[]{:S(2)}, u32[]{:S(2)}) collective-permute-start(bf16[1000,128]{1,0:T(8,128)(2,1)S(1)} %get-tuple-element.41), channel_id=1, source_target_pairs={{1,0},{2,1},{3,2},{51,3},{5,4},{6,5},{7,6},{55,7},{9,8},{10,9},{11... | collective-permute-start | bytes 768008 | tf_op jit(solution)/shard_map/ppermute | solution.py:199
  35.8 17.2 %collective-permute-start.9 = (bf16[1000,128]{1,0:T(8,128)(2,1)S(1)}, bf16[1000,128]{1,0:T(8,128)(2,1)S(1)}, u32[]{:S(2)}, u32[]{:S(2)}) collective-permute-start(bf16[1000,128]{1,0:T(8,128)(2,1)S(1)} %get-tuple-element.42), channel_id=1, source_target_pairs={{0,2},{2,0},{1,3},{3,1},{4,6},{6,4},{5,7},{7,5},{8,10},{10,8},{9,1... | collective-permute-start | bytes 768008 | tf_op jit(solution)/shard_map/ppermute | solution.py:199
  37.7 15.3 %collective-permute-start.10 = (bf16[1000,128]{1,0:T(8,128)(2,1)S(1)}, bf16[1000,128]{1,0:T(8,128)(2,1)S(1)}, u32[]{:S(2)}, u32[]{:S(2)}) collective-permute-start(bf16[1000,128]{1,0:T(8,128)(2,1)S(1)} %get-tuple-element.43), channel_id=1, source_target_pairs={{2,4},{4,2},{3,5},{5,3},{6,8},{8,6},{7,9},{9,7},{10,12},{12,10},{1... | collective-permute-start | bytes 768008 | tf_op jit(solution)/shard_map/ppermute | solution.py:199
  41.7 14.9 %collective-permute-start.11 = (bf16[1000,128]{1,0:T(8,128)(2,1)S(1)}, bf16[1000,128]{1,0:T(8,128)(2,1)S(1)}, u32[]{:S(2)}, u32[]{:S(2)}) collective-permute-start(bf16[1000,128]{1,0:T(8,128)(2,1)S(1)} %get-tuple-element.44), channel_id=1, source_target_pairs={{3,4},{4,3},{7,8},{8,7},{11,12},{12,11},{15,16},{16,15},{19,20},{2... | collective-permute-start | bytes 768008 | tf_op jit(solution)/shard_map/ppermute | solution.py:199
  46.3 10.3 %collective-permute-start.12 = (bf16[1000,128]{1,0:T(8,128)(2,1)S(1)}, bf16[1000,128]{1,0:T(8,128)(2,1)S(1)}, u32[]{:S(2)}, u32[]{:S(2)}) collective-permute-start(bf16[1000,128]{1,0:T(8,128)(2,1)S(1)} %get-tuple-element.45), channel_id=1, source_target_pairs={{0,48},{1,49},{2,50},{3,51},{4,52},{5,53},{6,54},{7,55},{8,56},{9,... | collective-permute-start | bytes 768008 | tf_op jit(solution)/shard_map/ppermute | solution.py:199
  51.5 6.9 %collective-permute-start.13 = (bf16[1000,128]{1,0:T(8,128)(2,1)S(1)}, bf16[1000,128]{1,0:T(8,128)(2,1)S(1)}, u32[]{:S(2)}, u32[]{:S(2)}) collective-permute-start(bf16[1000,128]{1,0:T(8,128)(2,1)S(1)} %get-tuple-element.46), channel_id=1, source_target_pairs={{0,720},{1,721},{2,722},{3,723},{4,724},{5,725},{6,726},{7,727},{8... | collective-permute-start | bytes 768008 | tf_op jit(solution)/shard_map/ppermute | solution.py:199
  60.8 14.0 %collective-permute-start.14 = (bf16[1000,128]{1,0:T(8,128)(2,1)S(1)}, bf16[1000,128]{1,0:T(8,128)(2,1)S(1)}, u32[]{:S(2)}, u32[]{:S(2)}) collective-permute-start(bf16[1000,128]{1,0:T(8,128)(2,1)S(1)} %get-tuple-element.48), channel_id=1, source_target_pairs={{0,1},{1,2},{2,3},{3,51},{4,5},{5,6},{6,7},{7,55},{8,9},{9,10},{10... | collective-permute-start | bytes 768008 | tf_op jit(solution)/shard_map/ppermute | solution.py:199
  61.1 18.8 %collective-permute-start.15 = (bf16[1000,128]{1,0:T(8,128)(2,1)S(1)}, bf16[1000,128]{1,0:T(8,128)(2,1)S(1)}, u32[]{:S(2)}, u32[]{:S(2)}) collective-permute-start(bf16[1000,128]{1,0:T(8,128)(2,1)S(1)} %get-tuple-element.49), channel_id=1, source_target_pairs={{1,0},{2,1},{3,2},{51,3},{5,4},{6,5},{7,6},{55,7},{9,8},{10,9},{11... | collective-permute-start | bytes 768008 | tf_op jit(solution)/shard_map/ppermute | solution.py:199
  62.2 18.5 %collective-permute-start.16 = (bf16[1000,128]{1,0:T(8,128)(2,1)S(1)}, bf16[1000,128]{1,0:T(8,128)(2,1)S(1)}, u32[]{:S(2)}, u32[]{:S(2)}) collective-permute-start(bf16[1000,128]{1,0:T(8,128)(2,1)S(1)} %get-tuple-element.50), channel_id=1, source_target_pairs={{0,2},{2,0},{1,3},{3,1},{4,6},{6,4},{5,7},{7,5},{8,10},{10,8},{9,1... | collective-permute-start | bytes 768008 | tf_op jit(solution)/shard_map/ppermute | solution.py:199
  65.3 15.4 %collective-permute-start.17 = (bf16[1000,128]{1,0:T(8,128)(2,1)S(1)}, bf16[1000,128]{1,0:T(8,128)(2,1)S(1)}, u32[]{:S(2)}, u32[]{:S(2)}) collective-permute-start(bf16[1000,128]{1,0:T(8,128)(2,1)S(1)} %get-tuple-element.51), channel_id=1, source_target_pairs={{2,4},{4,2},{3,5},{5,3},{6,8},{8,6},{7,9},{9,7},{10,12},{12,10},{1... | collective-permute-start | bytes 768008 | tf_op jit(solution)/shard_map/ppermute | solution.py:199
  67.9 15.1 %collective-permute-start.18 = (bf16[1000,128]{1,0:T(8,128)(2,1)S(1)}, bf16[1000,128]{1,0:T(8,128)(2,1)S(1)}, u32[]{:S(2)}, u32[]{:S(2)}) collective-permute-start(bf16[1000,128]{1,0:T(8,128)(2,1)S(1)} %get-tuple-element.52), channel_id=1, source_target_pairs={{3,4},{4,3},{7,8},{8,7},{11,12},{12,11},{15,16},{16,15},{19,20},{2... | collective-permute-start | bytes 768008 | tf_op jit(solution)/shard_map/ppermute | solution.py:199
  74.8 8.3 %collective-permute-start.19 = (bf16[1000,128]{1,0:T(8,128)(2,1)S(1)}, bf16[1000,128]{1,0:T(8,128)(2,1)S(1)}, u32[]{:S(2)}, u32[]{:S(2)}) collective-permute-start(bf16[1000,128]{1,0:T(8,128)(2,1)S(1)} %get-tuple-element.53), channel_id=1, source_target_pairs={{0,48},{1,49},{2,50},{3,51},{4,52},{5,53},{6,54},{7,55},{8,56},{9,... | collective-permute-start | bytes 768008 | tf_op jit(solution)/shard_map/ppermute | solution.py:199
  79.8 6.9 %collective-permute-start.20 = (bf16[1000,128]{1,0:T(8,128)(2,1)S(1)}, bf16[1000,128]{1,0:T(8,128)(2,1)S(1)}, u32[]{:S(2)}, u32[]{:S(2)}) collective-permute-start(bf16[1000,128]{1,0:T(8,128)(2,1)S(1)} %get-tuple-element.54), channel_id=1, source_target_pairs={{0,720},{1,721},{2,722},{3,723},{4,724},{5,725},{6,726},{7,727},{8... | collective-permute-start | bytes 768008 | tf_op jit(solution)/shard_map/ppermute | solution.py:199

commit v3 on v2

--- a/solution.py
+++ b/solution.py
@@ -17,8 +17,9 @@
 HBM = pl.BlockSpec(memory_space=pltpu.HBM)
 PARAMS = pltpu.CompilerParams(vmem_limit_bytes=40 * 1024 * 1024)
 
-RING, BACK, TWO, CROSS, EDGE, UP, DOWN = range(7)
+EDGE, RING, BACK, UP, DOWN, TWO, CROSS = range(7)
 PERMUTES = 7
+EARLY = 5
 
 
 def routes(n_group, n_dom):
@@ -70,6 +71,10 @@
     }
 
 
+def in_hbm(x):
+    return pltpu.with_memory_space_constraint(x, pltpu.HBM)
+
+
 def chunks(rows):
     return [(at, min(CHUNK, rows - at)) for at in range(0, rows, CHUNK)]
 
@@ -80,16 +85,25 @@
         send_refs[k][rows, :] = own_ref[rows, block]
 
 
-def prepare_kernel(send_ref, seeds_ref, degree_ref, prior_ref, start_ref, own_ref, *refs):
-    send_refs, (held, arrived) = refs[:PERMUTES], refs[PERMUTES:]
-    classes = prior_ref.shape[0]
+def prepare_kernel(send_any, seeds_any, degree_any, prior_any, root_ref, start_ref, own_ref, *refs):
+    send_refs, (sends, seeds_held, degree_held, held, small, arrived) = refs[:PERMUTES], refs[PERMUTES:]
+    classes = prior_any.shape[0]
+    firsts = [
+        pltpu.make_async_copy(seeds_any, seeds_held, small.at[0]),
+        pltpu.make_async_copy(degree_any, degree_held, small.at[1]),
+        pltpu.make_async_copy(send_any, sends, small.at[2]),
+    ]
     copies = []
     for k, (at, size) in enumerate(chunks(classes)):
         rows = pl.ds(at, size)
-        copies.append(pltpu.make_async_copy(prior_ref.at[rows], held.at[rows], arrived.at[k]))
-        copies[-1].start()
-    inv_root = 1.0 / jnp.sqrt(degree_ref[...].astype(jnp.float32))
-    seeds = seeds_ref[...]
+        copies.append(pltpu.make_async_copy(prior_any.at[rows], held.at[rows], arrived.at[k]))
+    for copy in firsts + copies:
+        copy.start()
+    for copy in firsts:
+        copy.wait()
+    inv_root = 1.0 / jnp.sqrt(degree_held[...].astype(jnp.float32)[None, :])
+    seeds = seeds_held[...][None, :]
+    root_ref[...] = inv_root
     for k, (at, size) in enumerate(chunks(classes)):
         rows = pl.ds(at, size)
         copies[k].wait()
@@ -98,32 +112,50 @@
         start = jnp.where(seeds < classes, onehot, held[rows, :].astype(jnp.float32))
         start_ref[rows, :] = start.astype(jnp.bfloat16)
         own_ref[rows, :] = (inv_root * start).astype(jnp.bfloat16)
-        put_sends(rows, send_ref, own_ref, send_refs)
-
-
-def new_labels(rows, degree_ref, start_ref, weight_ref, own_ref, received):
-    inv_root = 1.0 / jnp.sqrt(degree_ref[...].astype(jnp.float32))
-    sources = jnp.concatenate([own_ref[rows, :]] + [ref[rows, :] for ref in received], axis=1)
-    product = jnp.dot(sources, weight_ref[...], preferred_element_type=jnp.float32)
+        put_sends(rows, sends, own_ref, send_refs)
+
+
+def early_kernel(weight_ref, own_ref, *refs):
+    received, sum_ref = refs[:EARLY], refs[EARLY]
+    depth = own_ref.shape[1] + EARLY * SIDE
+    for at, size in chunks(own_ref.shape[0]):
+        rows = pl.ds(at, size)
+        sources = jnp.concatenate([own_ref[rows, :]] + [ref[rows, :] for ref in received], axis=1)
+        sum_ref[rows, :] = jnp.dot(
+            sources, weight_ref[pl.ds(0, depth), :], preferred_element_type=jnp.float32
+        )
+
+
+def new_labels(rows, root_ref, start_ref, weight_ref, sum_ref, received):
+    inv_root = root_ref[...]
+    depth = len(received) * SIDE
+    sources = jnp.concatenate([ref[rows, :] for ref in received], axis=1)
+    product = sum_ref[rows, :] + jnp.dot(
+        sources,
+        weight_ref[pl.ds(weight_ref.shape[0] - depth, depth), :],
+        preferred_element_type=jnp.float32,
+    )
     labels = 0.9 * inv_root * product + 0.1 * start_ref[rows, :].astype(jnp.float32)
     return inv_root, labels
 
 
-def step_kernel(send_ref, degree_ref, start_ref, weight_ref, own_ref, *refs):
-    received, next_ref, send_refs = refs[:PERMUTES], refs[PERMUTES], refs[PERMUTES + 1 :]
-    for at, size in chunks(own_ref.shape[0]):
-        rows = pl.ds(at, size)
-        inv_root, labels = new_labels(rows, degree_ref, start_ref, weight_ref, own_ref, received)
+def step_kernel(send_ref, root_ref, start_ref, weight_ref, sum_ref, *refs):
+    late = PERMUTES - EARLY
+    received, next_ref, send_refs = refs[:late], refs[late], refs[late + 1 :]
+    for at, size in chunks(next_ref.shape[0]):
+        rows = pl.ds(at, size)
+        inv_root, labels = new_labels(rows, root_ref, start_ref, weight_ref, sum_ref, received)
         next_ref[rows, :] = (inv_root * labels).astype(jnp.bfloat16)
         put_sends(rows, send_ref, next_ref, send_refs)
 
 
-def last_kernel(degree_ref, start_ref, weight_ref, own_ref, *refs):
-    received, (out_ref, held, left) = refs[:PERMUTES], refs[PERMUTES:]
+def last_kernel(root_ref, start_ref, weight_ref, sum_ref, *refs):
+    late = PERMUTES - EARLY
+    received, (out_ref, held, left) = refs[:late], refs[late:]
     copies = []
-    for k, (at, size) in enumerate(chunks(own_ref.shape[0])):
-        rows = pl.ds(at, size)
-        _, labels = new_labels(rows, degree_ref, start_ref, weight_ref, own_ref, received)
+    for k, (at, size) in enumerate(chunks(held.shape[0])):
+        rows = pl.ds(at, size)
+        _, labels = new_labels(rows, root_ref, start_ref, weight_ref, sum_ref, received)
         held[rows, :] = labels
         copies.append(pltpu.make_async_copy(held.at[rows], out_ref.at[rows], left.at[k]))
         copies[-1].start()
@@ -171,21 +203,24 @@
     route = routes(n_group, n_dom)
     slots = row_blocks + PERMUTES
     pieces = len(chunks(classes))
-    seeds, degrees = seed_labels[None, :], degree[None, :]
     wide = jax.ShapeDtypeStruct((classes, nodes), jnp.bfloat16)
     narrow = [jax.ShapeDtypeStruct((classes, side), jnp.bfloat16)] * PERMUTES
 
-    start, own, *sends = pl.pallas_call(
+    inv_root, start, own, *sends = pl.pallas_call(
         prepare_kernel,
-        in_specs=[SMEM, VMEM, VMEM, HBM],
-        out_specs=[VMEM] * (2 + PERMUTES),
-        out_shape=[wide, wide] + narrow,
+        in_specs=[HBM] * 4,
+        out_specs=[VMEM] * (3 + PERMUTES),
+        out_shape=[jax.ShapeDtypeStruct((1, nodes), jnp.float32), wide, wide] + narrow,
         scratch_shapes=[
+            pltpu.SMEM(send_list.shape, jnp.int32),
+            pltpu.VMEM((nodes,), jnp.int32),
+            pltpu.VMEM((nodes,), jnp.int32),
             pltpu.VMEM((classes, nodes), jnp.bfloat16),
+            pltpu.SemaphoreType.DMA((3,)),
             pltpu.SemaphoreType.DMA((pieces,)),
         ],
         compiler_params=PARAMS,
-    )(send_list, seeds, degrees, prior.T)
+    )(*[in_hbm(x) for x in (send_list, seed_labels, degree, prior.T)])
     weight = pl.pallas_call(
         functools.partial(weight_kernel, n_group),
         in_specs=[SMEM, SMEM, VMEM],
@@ -197,17 +232,30 @@
     )(tile_source, tile_count, tiles)
     for step in range(ITERS):
         received = [lax.ppermute(sends[k], ("group", "dom"), route[k]) for k in range(PERMUTES)]
+        total = pl.pallas_call(
+            early_kernel,
+            in_specs=[VMEM] * (2 + EARLY),
+            out_specs=VMEM,
+            out_shape=jax.ShapeDtypeStruct((classes, nodes), jnp.float32),
+            compiler_params=PARAMS,
+            cost_estimate=pl.CostEstimate(
+                flops=2 * classes * nodes * (row_blocks + EARLY) * side,
+                bytes_accessed=4_000_000,
+                transcendentals=0,
+            ),
+        )(weight, own, *received[:EARLY])
+        late = received[EARLY:]
         if step < ITERS - 1:
             own, *sends = pl.pallas_call(
                 step_kernel,
-                in_specs=[SMEM] + [VMEM] * (4 + PERMUTES),
+                in_specs=[SMEM] + [VMEM] * (4 + len(late)),
                 out_specs=[VMEM] * (1 + PERMUTES),
                 out_shape=[wide] + narrow,
                 compiler_params=PARAMS,
-            )(send_list, degrees, start, weight, own, *received)
+            )(send_list, inv_root, start, weight, total, *late)
     labels = pl.pallas_call(
         last_kernel,
-        in_specs=[VMEM] * (4 + PERMUTES),
+        in_specs=[VMEM] * (4 + len(late)),
         out_specs=HBM,
         out_shape=jax.ShapeDtypeStruct((classes, nodes), jnp.float32),
         scratch_shapes=[
@@ -215,7 +263,7 @@
             pltpu.SemaphoreType.DMA((pieces,)),
         ],
         compiler_params=PARAMS,
-    )(degrees, start, weight, own, *received)
+    )(inv_root, start, weight, total, *late)
     return labels.T
 
 

time: 89.6 us -> 90.4 us (level)
  the two profiles are of different devices: /device:TPU:281 before, /device:TPU:216 now
where the time goes in v3:
time: 90.4 us; the launch traced here: 89.9 us
  waiting for transfers between devices  42.2 us (47%)
  starting transfers between devices  33.7 us (37%)
  Pallas kernels  11.3 us (12%)
  local copies, waits for them, and re-layouts  1.82 us (2%)
  between operations  0.91 us (1%)
    ppermute x21, waiting for transfers between devices, on_device(): lax.ppermute(sends[k], ('group', 'dom'), route[k])  42.2 us
    ppermute x21, starting transfers between devices, on_device(): lax.ppermute(sends[k], ('group', 'dom'), route[k])  33.7 us
    pallas_call x3, Pallas kernels, on_device(): pl.pallas_call(early_kernel, in_specs=[VMEM] * (2 + EARLY), out_specs=VME...  3.75 us
    pallas_call x2, Pallas kernels, on_device(): pl.pallas_call(step_kernel, in_specs=[SMEM] + [VMEM] * (4 + len(late)), o...  2.78 us
    pallas_call x1, Pallas kernels, on_device(): pl.pallas_call(prepare_kernel, in_specs=[HBM] * 4, out_specs=[VMEM] * (3...  1.84 us
    unnamed x6, local copies, waits for them, and re-layouts  1.82 us
  transfers between devices with their start and end apart: 21, of which 7 were waited for; matrix products, arithmetic and copies ran while one was open for 0% of the time, Pallas kernels for 6%

profile of v3, /device:TPU:216, one launch (start us, length us, event | category | flops | bytes accessed | tf_op | source)
XLA Modules:
  0.0 89.9 jit_solution(636198454354903848)
XLA Ops:
  0.0 1.8 %shard_map.73 = (f32[1,384]{1,0:T(1,128)S(1)}, bf16[1000,384]{1,0:T(8,128)(2,1)S(1)}, bf16[1000,384]{1,0:T(8,128)(2,1)S(1)}, bf16[1000,128]{1,0:T(8,128)(2,1)S(1...) custom-call(s32[1,6]{1,0:T(1,128)} %send_ref.3, ...), custom_call_target="tpu_custom_call" | custom-call | tf_op jit(solution)/shard_map/pallas_call | solution.py:209
  1.8 3.8 %collective-permute-start = (bf16[1000,128]{1,0:T(8,128)(2,1)S(1)}, bf16[1000,128]{1,0:T(8,128)(2,1)S(1)}, u32[]{:S(2)}, u32[]{:S(2)}) collective-permute-start(bf16[1000,128]{1,0:T(8,128)(2,1)S(1)} %get-tuple-element.34), channel_id=1, source_target_pairs={{3,4},{4,3},{7,8},{8,7},{11,12},{12,11},{15,16},{16,15},{19,20},{2... | collective-permute-start | bytes 768008 | tf_op jit(solution)/shard_map/ppermute | solution.py:234
  5.6 0.0 collective-permute-start.1
  5.6 0.5 collective-permute-start.2
  6.1 0.5 collective-permute-start.3
  6.6 1.2 %collective-permute-start.4 = (bf16[1000,128]{1,0:T(8,128)(2,1)S(1)}, bf16[1000,128]{1,0:T(8,128)(2,1)S(1)}, u32[]{:S(2)}, u32[]{:S(2)}) collective-permute-start(bf16[1000,128]{1,0:T(8,128)(2,1)S(1)} %get-tuple-element.38), channel_id=1, source_target_pairs={{0,720},{1,721},{2,722},{3,723},{4,724},{5,725},{6,726},{7,727},{8... | collective-permute-start | bytes 768008 | tf_op jit(solution)/shard_map/ppermute | solution.py:234
  7.9 5.9 %collective-permute-done.refs_0_ = bf16[1000,128]{1,0:T(8,128)(2,1)S(1)} collective-permute-done((bf16[1000,128]{1,0:T(8,128)(2,1)S(1)}, bf16[1000,128]{1,0:T(8,128)(2,1)S(1)}, u32[]{:S(2)}, u32[]{:S(2)}) %collective-permute-start) | collective-permute-done | bytes 256032 | tf_op jit(solution)/shard_map/ppermute | solution.py:234
  13.8 1.9 %collective-permute-start.5 = (bf16[1000,128]{1,0:T(8,128)(2,1)S(1)}, bf16[1000,128]{1,0:T(8,128)(2,1)S(1)}, u32[]{:S(2)}, u32[]{:S(2)}) collective-permute-start(bf16[1000,128]{1,0:T(8,128)(2,1)S(1)} %get-tuple-element.39), channel_id=1, source_target_pairs={{0,2},{2,0},{1,3},{3,1},{4,6},{6,4},{5,7},{7,5},{8,10},{10,8},{9,1... | collective-permute-start | bytes 768008 | tf_op jit(solution)/shard_map/ppermute | solution.py:234
  15.7 0.0 collective-permute-done.1.refs_1_
  15.7 4.5 %collective-permute-start.6 = (bf16[1000,128]{1,0:T(8,128)(2,1)S(1)}, bf16[1000,128]{1,0:T(8,128)(2,1)S(1)}, u32[]{:S(2)}, u32[]{:S(2)}) collective-permute-start(bf16[1000,128]{1,0:T(8,128)(2,1)S(1)} %get-tuple-element.40), channel_id=1, source_target_pairs={{2,4},{4,2},{3,5},{5,3},{6,8},{8,6},{7,9},{9,7},{10,12},{12,10},{1... | collective-permute-start | bytes 768008 | tf_op jit(solution)/shard_map/ppermute | solution.py:234
  20.9 0.0 copy-start
  20.9 1.1 %copy-done = bf16[3,8,128,128]{3,2,1,0:T(8,128)(2,1)S(1)} copy-done((bf16[3,8,128,128]{3,2,1,0:T(8,128)(2,1)S(1)}, bf16[3,8,128,128]{3,2,1,0:T(8,128)(2,1)}, u32[]{:S(2)}) %copy-start) | copy-done | bytes 786456
  22.0 0.7 copy-done.2
  22.7 1.5 %shard_map.74.weight_ref = bf16[1280,384]{1,0:T(8,128)(2,1)S(1)} custom-call(s32[3,8]{1,0:T(4,128)S(1)} %copy-done.2, s32[1]{0:T(128)S(6)} %copy.8.count_ref, bf16[3,8,128,128]{3,2,1,0:T(8,128)(2,1)S(1)} %copy-done), custom_call_target="tpu_custom_call" | custom-call | bytes 8000000 | tf_op jit(solution)/shard_map/pallas_call | solution.py:224
  24.2 0.0 collective-permute-done.2.refs_2_
  24.2 0.0 collective-permute-done.4.refs_4_
  24.2 0.0 copy-start.1
  24.3 1.2 %shard_map.75.sum_ref = f32[1000,384]{1,0:T(8,128)S(1)} custom-call(bf16[1280,384]{1,0:T(8,128)(2,1)S(1)} %shard_map.74.weight_ref, bf16[1000,384]{1,0:T(8,128)(2,1)S(1)} %get-tuple-element.33.own_ref, bf16[1000,128]{1,0:T(8,128)(2,1)S(1)} %collective-permute-done.refs_0_, bf16[1000,128]{1,0:T(8,128)(2,1)S(1)} %collective-permute-done.1.refs_1_, ...), custom_call_target="tpu_custom_call" | custom-call | flops 786432000 | bytes 4000000 | tf_op jit(solution)/shard_map/pallas_call | solution.py:235
  25.5 4.2 %collective-permute-done.5.refs_0_ = bf16[1000,128]{1,0:T(8,128)(2,1)S(1)} collective-permute-done((bf16[1000,128]{1,0:T(8,128)(2,1)S(1)}, bf16[1000,128]{1,0:T(8,128)(2,1)S(1)}, u32[]{:S(2)}, u32[]{:S(2)}) %collective-permute-start.5) | collective-permute-done | bytes 256032 | tf_op jit(solution)/shard_map/ppermute | solution.py:234
  29.7 0.0 collective-permute-done.6.refs_1_
  29.7 1.4 %shard_map.76 = (bf16[1000,384]{1,0:T(8,128)(2,1)S(1)}, bf16[1000,128]{1,0:T(8,128)(2,1)S(1)}, bf16[1000,128]{1,0:T(8,128)(2,1)S(1)}, bf16[1000,128]{1,0:T(8,128...) custom-call(s32[1,6]{1,0:T(1,128)S(1)} %copy-done.1, ...), custom_call_target="tpu_custom_call" | custom-call | tf_op jit(solution)/shard_map/pallas_call | solution.py:249
  31.1 3.8 %collective-permute-start.7 = (bf16[1000,128]{1,0:T(8,128)(2,1)S(1)}, bf16[1000,128]{1,0:T(8,128)(2,1)S(1)}, u32[]{:S(2)}, u32[]{:S(2)}) collective-permute-start(bf16[1000,128]{1,0:T(8,128)(2,1)S(1)} %get-tuple-element.42), channel_id=1, source_target_pairs={{3,4},{4,3},{7,8},{8,7},{11,12},{12,11},{15,16},{16,15},{19,20},{2... | collective-permute-start | bytes 768008 | tf_op jit(solution)/shard_map/ppermute | solution.py:234
  34.8 0.0 collective-permute-start.8
  34.9 0.5 collective-permute-start.9
  35.4 0.0 collective-permute-start.10
  35.4 1.7 %collective-permute-start.11 = (bf16[1000,128]{1,0:T(8,128)(2,1)S(1)}, bf16[1000,128]{1,0:T(8,128)(2,1)S(1)}, u32[]{:S(2)}, u32[]{:S(2)}) collective-permute-start(bf16[1000,128]{1,0:T(8,128)(2,1)S(1)} %get-tuple-element.46), channel_id=1, source_target_pairs={{0,720},{1,721},{2,722},{3,723},{4,724},{5,725},{6,726},{7,727},{8... | collective-permute-start | bytes 768008 | tf_op jit(solution)/shard_map/ppermute | solution.py:234
  37.1 4.4 %collective-permute-done.7.refs_0_ = bf16[1000,128]{1,0:T(8,128)(2,1)S(1)} collective-permute-done((bf16[1000,128]{1,0:T(8,128)(2,1)S(1)}, bf16[1000,128]{1,0:T(8,128)(2,1)S(1)}, u32[]{:S(2)}, u32[]{:S(2)}) %collective-permute-start.7) | collective-permute-done | bytes 256032 | tf_op jit(solution)/shard_map/ppermute | solution.py:234
  41.5 4.1 %collective-permute-start.12 = (bf16[1000,128]{1,0:T(8,128)(2,1)S(1)}, bf16[1000,128]{1,0:T(8,128)(2,1)S(1)}, u32[]{:S(2)}, u32[]{:S(2)}) collective-permute-start(bf16[1000,128]{1,0:T(8,128)(2,1)S(1)} %get-tuple-element.47), channel_id=1, source_target_pairs={{0,2},{2,0},{1,3},{3,1},{4,6},{6,4},{5,7},{7,5},{8,10},{10,8},{9,1... | collective-permute-start | bytes 768008 | tf_op jit(solution)/shard_map/ppermute | solution.py:234
  45.6 0.0 collective-permute-done.8.refs_1_
  45.6 2.2 %collective-permute-start.13 = (bf16[1000,128]{1,0:T(8,128)(2,1)S(1)}, bf16[1000,128]{1,0:T(8,128)(2,1)S(1)}, u32[]{:S(2)}, u32[]{:S(2)}) collective-permute-start(bf16[1000,128]{1,0:T(8,128)(2,1)S(1)} %get-tuple-element.48), channel_id=1, source_target_pairs={{2,4},{4,2},{3,5},{5,3},{6,8},{8,6},{7,9},{9,7},{10,12},{12,10},{1... | collective-permute-start | bytes 768008 | tf_op jit(solution)/shard_map/ppermute | solution.py:234
  47.8 0.0 collective-permute-done.9.refs_2_
  47.9 0.0 collective-permute-done.10.refs_3_
  47.9 1.2 %shard_map.77.sum_ref = f32[1000,384]{1,0:T(8,128)S(1)} custom-call(bf16[1280,384]{1,0:T(8,128)(2,1)S(1)} %shard_map.74.weight_ref, bf16[1000,384]{1,0:T(8,128)(2,1)S(1)} %get-tuple-element.41.own_ref, bf16[1000,128]{1,0:T(8,128)(2,1)S(1)} %collective-permute-done.7.refs_0_, bf16[1000,128]{1,0:T(8,128)(2,1)S(1)} %collective-permute-done.8.refs_1_, ...), custom_call_target="tpu_custom_call" | custom-call | flops 786432000 | bytes 4000000 | tf_op jit(solution)/shard_map/pallas_call | solution.py:235
  49.1 8.3 %collective-permute-done.12.refs_0_ = bf16[1000,128]{1,0:T(8,128)(2,1)S(1)} collective-permute-done((bf16[1000,128]{1,0:T(8,128)(2,1)S(1)}, bf16[1000,128]{1,0:T(8,128)(2,1)S(1)}, u32[]{:S(2)}, u32[]{:S(2)}) %collective-permute-start.12) | collective-permute-done | bytes 256032 | tf_op jit(solution)/shard_map/ppermute | solution.py:234
  57.4 1.5 %collective-permute-done.13.refs_1_ = bf16[1000,128]{1,0:T(8,128)(2,1)S(1)} collective-permute-done((bf16[1000,128]{1,0:T(8,128)(2,1)S(1)}, bf16[1000,128]{1,0:T(8,128)(2,1)S(1)}, u32[]{:S(2)}, u32[]{:S(2)}) %collective-permute-start.13) | collective-permute-done | bytes 256032 | tf_op jit(solution)/shard_map/ppermute | solution.py:234
  58.9 1.4 %shard_map.78 = (bf16[1000,384]{1,0:T(8,128)(2,1)S(1)}, bf16[1000,128]{1,0:T(8,128)(2,1)S(1)}, bf16[1000,128]{1,0:T(8,128)(2,1)S(1)}, bf16[1000,128]{1,0:T(8,128...) custom-call(s32[1,6]{1,0:T(1,128)S(1)} %copy-done.1, ...), custom_call_target="tpu_custom_call" | custom-call | tf_op jit(solution)/shard_map/pallas_call | solution.py:249
  60.3 2.8 %collective-permute-start.14 = (bf16[1000,128]{1,0:T(8,128)(2,1)S(1)}, bf16[1000,128]{1,0:T(8,128)(2,1)S(1)}, u32[]{:S(2)}, u32[]{:S(2)}) collective-permute-start(bf16[1000,128]{1,0:T(8,128)(2,1)S(1)} %get-tuple-element.50), channel_id=1, source_target_pairs={{3,4},{4,3},{7,8},{8,7},{11,12},{12,11},{15,16},{16,15},{19,20},{2... | collective-permute-start | bytes 768008 | tf_op jit(solution)/shard_map/ppermute | solution.py:234
  63.0 0.0 collective-permute-start.15
  63.1 0.5 collective-permute-start.16
  63.6 0.2 collective-permute-start.17
  63.7 1.6 %collective-permute-start.18 = (bf16[1000,128]{1,0:T(8,128)(2,1)S(1)}, bf16[1000,128]{1,0:T(8,128)(2,1)S(1)}, u32[]{:S(2)}, u32[]{:S(2)}) collective-permute-start(bf16[1000,128]{1,0:T(8,128)(2,1)S(1)} %get-tuple-element.54), channel_id=1, source_target_pairs={{0,720},{1,721},{2,722},{3,723},{4,724},{5,725},{6,726},{7,727},{8... | collective-permute-start | bytes 768008 | tf_op jit(solution)/shard_map/ppermute | solution.py:234
  65.3 7.1 %collective-permute-done.14.refs_0_ = bf16[1000,128]{1,0:T(8,128)(2,1)S(1)} collective-permute-done((bf16[1000,128]{1,0:T(8,128)(2,1)S(1)}, bf16[1000,128]{1,0:T(8,128)(2,1)S(1)}, u32[]{:S(2)}, u32[]{:S(2)}) %collective-permute-start.14) | collective-permute-done | bytes 256032 | tf_op jit(solution)/shard_map/ppermute | solution.py:234
  72.4 1.9 %collective-permute-start.19 = (bf16[1000,128]{1,0:T(8,128)(2,1)S(1)}, bf16[1000,128]{1,0:T(8,128)(2,1)S(1)}, u32[]{:S(2)}, u32[]{:S(2)}) collective-permute-start(bf16[1000,128]{1,0:T(8,128)(2,1)S(1)} %get-tuple-element.55), channel_id=1, source_target_pairs={{0,2},{2,0},{1,3},{3,1},{4,6},{6,4},{5,7},{7,5},{8,10},{10,8},{9,1... | collective-permute-start | bytes 768008 | tf_op jit(solution)/shard_map/ppermute | solution.py:234
  74.3 0.0 collective-permute-done.15.refs_1_
  74.3 2.0 %collective-permute-start.20 = (bf16[1000,128]{1,0:T(8,128)(2,1)S(1)}, bf16[1000,128]{1,0:T(8,128)(2,1)S(1)}, u32[]{:S(2)}, u32[]{:S(2)}) collective-permute-start(bf16[1000,128]{1,0:T(8,128)(2,1)S(1)} %get-tuple-element.56), channel_id=1, source_target_pairs={{2,4},{4,2},{3,5},{5,3},{6,8},{8,6},{7,9},{9,7},{10,12},{12,10},{1... | collective-permute-start | bytes 768008 | tf_op jit(solution)/shard_map/ppermute | solution.py:234
  76.3 1.3 %shard_map.79.sum_ref = f32[1000,384]{1,0:T(8,128)S(1)} custom-call(bf16[1280,384]{1,0:T(8,128)(2,1)S(1)} %shard_map.74.weight_ref, bf16[1000,384]{1,0:T(8,128)(2,1)S(1)} %get-tuple-element.49.own_ref, bf16[1000,128]{1,0:T(8,128)(2,1)S(1)} %collective-permute-done.14.refs_0_, bf16[1000,128]{1,0:T(8,128)(2,1)S(1)} %collective-permute-done.15.refs_1_, ...), custom_call_target="tpu_custom_call" | custom-call | flops 786432000 | bytes 4000000 | tf_op jit(solution)/shard_map/pallas_call | solution.py:235
  77.6 10.9 %collective-permute-done.19.refs_0_ = bf16[1000,128]{1,0:T(8,128)(2,1)S(1)} collective-permute-done((bf16[1000,128]{1,0:T(8,128)(2,1)S(1)}, bf16[1000,128]{1,0:T(8,128)(2,1)S(1)}, u32[]{:S(2)}, u32[]{:S(2)}) %collective-permute-start.19) | collective-permute-done | bytes 256032 | tf_op jit(solution)/shard_map/ppermute | solution.py:234
  88.5 1.4 %shard_map.80 = f32[1000,384]{1,0:T(8,128)} custom-call(f32[1,384]{1,0:T(1,128)S(1)} %get-tuple-element.31.root_ref, bf16[1000,384]{1,0:T(8,128)(2,1)S(1)} %get-tuple-element.32.start_ref, bf16[1280,384]{1,0:T(8,128)(2,1)S(1)} %shard_map.74.weight_ref, f32[1000,384]{1,0:T(8,128)S(1)} %shard_map.79.sum_ref, ...), custom_call_target="tpu_custom_call" | custom-call | tf_op jit(solution)/shard_map/pallas_call | solution.py:256
  (8 shorter events, 0.0 us)
Async XLA Ops:
  1.8 11.9 %collective-permute-start = (bf16[1000,128]{1,0:T(8,128)(2,1)S(1)}, bf16[1000,128]{1,0:T(8,128)(2,1)S(1)}, u32[]{:S(2)}, u32[]{:S(2)}) collective-permute-start(bf16[1000,128]{1,0:T(8,128)(2,1)S(1)} %get-tuple-element.34), channel_id=1, source_target_pairs={{3,4},{4,3},{7,8},{8,7},{11,12},{12,11},{15,16},{16,15},{19,20},{2... | collective-permute-start | bytes 768008 | tf_op jit(solution)/shard_map/ppermute | solution.py:234
  5.6 10.1 %collective-permute-start.1 = (bf16[1000,128]{1,0:T(8,128)(2,1)S(1)}, bf16[1000,128]{1,0:T(8,128)(2,1)S(1)}, u32[]{:S(2)}, u32[]{:S(2)}) collective-permute-start(bf16[1000,128]{1,0:T(8,128)(2,1)S(1)} %get-tuple-element.35), channel_id=1, source_target_pairs={{0,1},{1,2},{2,3},{3,51},{4,5},{5,6},{6,7},{7,55},{8,9},{9,10},{10... | collective-permute-start | bytes 768008 | tf_op jit(solution)/shard_map/ppermute | solution.py:234
  5.6 18.6 %collective-permute-start.2 = (bf16[1000,128]{1,0:T(8,128)(2,1)S(1)}, bf16[1000,128]{1,0:T(8,128)(2,1)S(1)}, u32[]{:S(2)}, u32[]{:S(2)}) collective-permute-start(bf16[1000,128]{1,0:T(8,128)(2,1)S(1)} %get-tuple-element.36), channel_id=1, source_target_pairs={{1,0},{2,1},{3,2},{51,3},{5,4},{6,5},{7,6},{55,7},{9,8},{10,9},{11... | collective-permute-start | bytes 768008 | tf_op jit(solution)/shard_map/ppermute | solution.py:234
  6.1 18.1 %collective-permute-start.3 = (bf16[1000,128]{1,0:T(8,128)(2,1)S(1)}, bf16[1000,128]{1,0:T(8,128)(2,1)S(1)}, u32[]{:S(2)}, u32[]{:S(2)}) collective-permute-start(bf16[1000,128]{1,0:T(8,128)(2,1)S(1)} %get-tuple-element.37), channel_id=1, source_target_pairs={{0,48},{1,49},{2,50},{3,51},{4,52},{5,53},{6,54},{7,55},{8,56},{9,... | collective-permute-start | bytes 768008 | tf_op jit(solution)/shard_map/ppermute | solution.py:234
  6.6 17.6 %collective-permute-start.4 = (bf16[1000,128]{1,0:T(8,128)(2,1)S(1)}, bf16[1000,128]{1,0:T(8,128)(2,1)S(1)}, u32[]{:S(2)}, u32[]{:S(2)}) collective-permute-start(bf16[1000,128]{1,0:T(8,128)(2,1)S(1)} %get-tuple-element.38), channel_id=1, source_target_pairs={{0,720},{1,721},{2,722},{3,723},{4,724},{5,725},{6,726},{7,727},{8... | collective-permute-start | bytes 768008 | tf_op jit(solution)/shard_map/ppermute | solution.py:234
  13.8 15.9 %collective-permute-start.5 = (bf16[1000,128]{1,0:T(8,128)(2,1)S(1)}, bf16[1000,128]{1,0:T(8,128)(2,1)S(1)}, u32[]{:S(2)}, u32[]{:S(2)}) collective-permute-start(bf16[1000,128]{1,0:T(8,128)(2,1)S(1)} %get-tuple-element.39), channel_id=1, source_target_pairs={{0,2},{2,0},{1,3},{3,1},{4,6},{6,4},{5,7},{7,5},{8,10},{10,8},{9,1... | collective-permute-start | bytes 768008 | tf_op jit(solution)/shard_map/ppermute | solution.py:234
  15.7 14.0 %collective-permute-start.6 = (bf16[1000,128]{1,0:T(8,128)(2,1)S(1)}, bf16[1000,128]{1,0:T(8,128)(2,1)S(1)}, u32[]{:S(2)}, u32[]{:S(2)}) collective-permute-start(bf16[1000,128]{1,0:T(8,128)(2,1)S(1)} %get-tuple-element.40), channel_id=1, source_target_pairs={{2,4},{4,2},{3,5},{5,3},{6,8},{8,6},{7,9},{9,7},{10,12},{12,10},{1... | collective-permute-start | bytes 768008 | tf_op jit(solution)/shard_map/ppermute | solution.py:234
  20.9 1.1 %copy-start = (bf16[3,8,128,128]{3,2,1,0:T(8,128)(2,1)S(1)}, bf16[3,8,128,128]{3,2,1,0:T(8,128)(2,1)}, u32[]{:S(2)}) copy-start(bf16[3,8,128,128]{3,2,1,0:T(8,128)(2,1)} %tiles_ref.1) | copy-start | bytes 2359300
  22.0 0.7 copy-start.2
  24.2 5.4 %copy-start.1 = (s32[1,6]{1,0:T(1,128)S(1)}, s32[1,6]{1,0:T(1,128)}, u32[]{:S(2)}) copy-start(s32[1,6]{1,0:T(1,128)} %send_ref.3) | copy-start | bytes 76
  31.1 10.4 %collective-permute-start.7 = (bf16[1000,128]{1,0:T(8,128)(2,1)S(1)}, bf16[1000,128]{1,0:T(8,128)(2,1)S(1)}, u32[]{:S(2)}, u32[]{:S(2)}) collective-permute-start(bf16[1000,128]{1,0:T(8,128)(2,1)S(1)} %get-tuple-element.42), channel_id=1, source_target_pairs={{3,4},{4,3},{7,8},{8,7},{11,12},{12,11},{15,16},{16,15},{19,20},{2... | collective-permute-start | bytes 768008 | tf_op jit(solution)/shard_map/ppermute | solution.py:234
  34.8 10.7 %collective-permute-start.8 = (bf16[1000,128]{1,0:T(8,128)(2,1)S(1)}, bf16[1000,128]{1,0:T(8,128)(2,1)S(1)}, u32[]{:S(2)}, u32[]{:S(2)}) collective-permute-start(bf16[1000,128]{1,0:T(8,128)(2,1)S(1)} %get-tuple-element.43), channel_id=1, source_target_pairs={{0,1},{1,2},{2,3},{3,51},{4,5},{5,6},{6,7},{7,55},{8,9},{9,10},{10... | collective-permute-start | bytes 768008 | tf_op jit(solution)/shard_map/ppermute | solution.py:234
  34.9 13.0 %collective-permute-start.9 = (bf16[1000,128]{1,0:T(8,128)(2,1)S(1)}, bf16[1000,128]{1,0:T(8,128)(2,1)S(1)}, u32[]{:S(2)}, u32[]{:S(2)}) collective-permute-start(bf16[1000,128]{1,0:T(8,128)(2,1)S(1)} %get-tuple-element.44), channel_id=1, source_target_pairs={{1,0},{2,1},{3,2},{51,3},{5,4},{6,5},{7,6},{55,7},{9,8},{10,9},{11... | collective-permute-start | bytes 768008 | tf_op jit(solution)/shard_map/ppermute | solution.py:234
  35.4 12.5 %collective-permute-start.10 = (bf16[1000,128]{1,0:T(8,128)(2,1)S(1)}, bf16[1000,128]{1,0:T(8,128)(2,1)S(1)}, u32[]{:S(2)}, u32[]{:S(2)}) collective-permute-start(bf16[1000,128]{1,0:T(8,128)(2,1)S(1)} %get-tuple-element.45), channel_id=1, source_target_pairs={{0,48},{1,49},{2,50},{3,51},{4,52},{5,53},{6,54},{7,55},{8,56},{9,... | collective-permute-start | bytes 768008 | tf_op jit(solution)/shard_map/ppermute | solution.py:234
  35.4 12.5 %collective-permute-start.11 = (bf16[1000,128]{1,0:T(8,128)(2,1)S(1)}, bf16[1000,128]{1,0:T(8,128)(2,1)S(1)}, u32[]{:S(2)}, u32[]{:S(2)}) collective-permute-start(bf16[1000,128]{1,0:T(8,128)(2,1)S(1)} %get-tuple-element.46), channel_id=1, source_target_pairs={{0,720},{1,721},{2,722},{3,723},{4,724},{5,725},{6,726},{7,727},{8... | collective-permute-start | bytes 768008 | tf_op jit(solution)/shard_map/ppermute | solution.py:234
  41.5 15.9 %collective-permute-start.12 = (bf16[1000,128]{1,0:T(8,128)(2,1)S(1)}, bf16[1000,128]{1,0:T(8,128)(2,1)S(1)}, u32[]{:S(2)}, u32[]{:S(2)}) collective-permute-start(bf16[1000,128]{1,0:T(8,128)(2,1)S(1)} %get-tuple-element.47), channel_id=1, source_target_pairs={{0,2},{2,0},{1,3},{3,1},{4,6},{6,4},{5,7},{7,5},{8,10},{10,8},{9,1... | collective-permute-start | bytes 768008 | tf_op jit(solution)/shard_map/ppermute | solution.py:234
  45.6 13.3 %collective-permute-start.13 = (bf16[1000,128]{1,0:T(8,128)(2,1)S(1)}, bf16[1000,128]{1,0:T(8,128)(2,1)S(1)}, u32[]{:S(2)}, u32[]{:S(2)}) collective-permute-start(bf16[1000,128]{1,0:T(8,128)(2,1)S(1)} %get-tuple-element.48), channel_id=1, source_target_pairs={{2,4},{4,2},{3,5},{5,3},{6,8},{8,6},{7,9},{9,7},{10,12},{12,10},{1... | collective-permute-start | bytes 768008 | tf_op jit(solution)/shard_map/ppermute | solution.py:234
  60.3 12.1 %collective-permute-start.14 = (bf16[1000,128]{1,0:T(8,128)(2,1)S(1)}, bf16[1000,128]{1,0:T(8,128)(2,1)S(1)}, u32[]{:S(2)}, u32[]{:S(2)}) collective-permute-start(bf16[1000,128]{1,0:T(8,128)(2,1)S(1)} %get-tuple-element.50), channel_id=1, source_target_pairs={{3,4},{4,3},{7,8},{8,7},{11,12},{12,11},{15,16},{16,15},{19,20},{2... | collective-permute-start | bytes 768008 | tf_op jit(solution)/shard_map/ppermute | solution.py:234
  63.0 11.3 %collective-permute-start.15 = (bf16[1000,128]{1,0:T(8,128)(2,1)S(1)}, bf16[1000,128]{1,0:T(8,128)(2,1)S(1)}, u32[]{:S(2)}, u32[]{:S(2)}) collective-permute-start(bf16[1000,128]{1,0:T(8,128)(2,1)S(1)} %get-tuple-element.51), channel_id=1, source_target_pairs={{0,1},{1,2},{2,3},{3,51},{4,5},{5,6},{6,7},{7,55},{8,9},{9,10},{10... | collective-permute-start | bytes 768008 | tf_op jit(solution)/shard_map/ppermute | solution.py:234
  63.1 13.2 %collective-permute-start.16 = (bf16[1000,128]{1,0:T(8,128)(2,1)S(1)}, bf16[1000,128]{1,0:T(8,128)(2,1)S(1)}, u32[]{:S(2)}, u32[]{:S(2)}) collective-permute-start(bf16[1000,128]{1,0:T(8,128)(2,1)S(1)} %get-tuple-element.52), channel_id=1, source_target_pairs={{1,0},{2,1},{3,2},{51,3},{5,4},{6,5},{7,6},{55,7},{9,8},{10,9},{11... | collective-permute-start | bytes 768008 | tf_op jit(solution)/shard_map/ppermute | solution.py:234
  63.6 12.8 %collective-permute-start.17 = (bf16[1000,128]{1,0:T(8,128)(2,1)S(1)}, bf16[1000,128]{1,0:T(8,128)(2,1)S(1)}, u32[]{:S(2)}, u32[]{:S(2)}) collective-permute-start(bf16[1000,128]{1,0:T(8,128)(2,1)S(1)} %get-tuple-element.53), channel_id=1, source_target_pairs={{0,48},{1,49},{2,50},{3,51},{4,52},{5,53},{6,54},{7,55},{8,56},{9,... | collective-permute-start | bytes 768008 | tf_op jit(solution)/shard_map/ppermute | solution.py:234
  63.7 12.6 %collective-permute-start.18 = (bf16[1000,128]{1,0:T(8,128)(2,1)S(1)}, bf16[1000,128]{1,0:T(8,128)(2,1)S(1)}, u32[]{:S(2)}, u32[]{:S(2)}) collective-permute-start(bf16[1000,128]{1,0:T(8,128)(2,1)S(1)} %get-tuple-element.54), channel_id=1, source_target_pairs={{0,720},{1,721},{2,722},{3,723},{4,724},{5,725},{6,726},{7,727},{8... | collective-permute-start | bytes 768008 | tf_op jit(solution)/shard_map/ppermute | solution.py:234
  72.4 16.1 %collective-permute-start.19 = (bf16[1000,128]{1,0:T(8,128)(2,1)S(1)}, bf16[1000,128]{1,0:T(8,128)(2,1)S(1)}, u32[]{:S(2)}, u32[]{:S(2)}) collective-permute-start(bf16[1000,128]{1,0:T(8,128)(2,1)S(1)} %get-tuple-element.55), channel_id=1, source_target_pairs={{0,2},{2,0},{1,3},{3,1},{4,6},{6,4},{5,7},{7,5},{8,10},{10,8},{9,1... | collective-permute-start | bytes 768008 | tf_op jit(solution)/shard_map/ppermute | solution.py:234
  74.3 14.2 %collective-permute-start.20 = (bf16[1000,128]{1,0:T(8,128)(2,1)S(1)}, bf16[1000,128]{1,0:T(8,128)(2,1)S(1)}, u32[]{:S(2)}, u32[]{:S(2)}) collective-permute-start(bf16[1000,128]{1,0:T(8,128)(2,1)S(1)} %get-tuple-element.56), channel_id=1, source_target_pairs={{2,4},{4,2},{3,5},{5,3},{6,8},{8,6},{7,9},{9,7},{10,12},{12,10},{1... | collective-permute-start | bytes 768008 | tf_op jit(solution)/shard_map/ppermute | solution.py:234

commit v4 on v3

--- a/solution.py
+++ b/solution.py
@@ -17,9 +17,9 @@
 HBM = pl.BlockSpec(memory_space=pltpu.HBM)
 PARAMS = pltpu.CompilerParams(vmem_limit_bytes=40 * 1024 * 1024)
 
-EDGE, RING, BACK, UP, DOWN, TWO, CROSS = range(7)
+RING, BACK, TWO, CROSS, EDGE, UP, DOWN = range(7)
 PERMUTES = 7
-EARLY = 5
+EARLY = 2
 
 
 def routes(n_group, n_dom):

time: 90.4 us -> 84.1 us (0.930)
  the two profiles are of different devices: /device:TPU:216 before, /device:TPU:281 now
where the time goes in v4:
time: 84.1 us; the launch traced here: 83.7 us
  starting transfers between devices  55.6 us (66%)
  waiting for transfers between devices  14.1 us (17%)
  Pallas kernels  11.3 us (13%)
  local copies, waits for them, and re-layouts  1.82 us (2%)
    ppermute x21, starting transfers between devices, on_device(): lax.ppermute(sends[k], ('group', 'dom'), route[k])  55.6 us
    ppermute x21, waiting for transfers between devices, on_device(): lax.ppermute(sends[k], ('group', 'dom'), route[k])  14.1 us
    pallas_call x2, Pallas kernels, on_device(): pl.pallas_call(step_kernel, in_specs=[SMEM] + [VMEM] * (4 + len(late)), o...  3.51 us
    pallas_call x3, Pallas kernels, on_device(): pl.pallas_call(early_kernel, in_specs=[VMEM] * (2 + EARLY), out_specs=VME...  2.75 us
    pallas_call x1, Pallas kernels, on_device(): pl.pallas_call(prepare_kernel, in_specs=[HBM] * 4, out_specs=[VMEM] * (3...  1.84 us
    unnamed x6, local copies, waits for them, and re-layouts  1.82 us
    pallas_call x1, Pallas kernels, on_device(): pl.pallas_call(last_kernel, in_specs=[VMEM] * (4 + len(late)), out_specs=...  1.75 us
  transfers between devices with their start and end apart: 21, of which 8 were waited for; matrix products, arithmetic and copies ran while one was open for 0% of the time, Pallas kernels for 5%

profile of v4, /device:TPU:281, one launch (start us, length us, event | category | flops | bytes accessed | tf_op | source)
XLA Modules:
  0.0 83.7 jit_solution(3803960551097724784)
XLA Ops:
  0.0 1.8 %shard_map.73 = (f32[1,384]{1,0:T(1,128)S(1)}, bf16[1000,384]{1,0:T(8,128)(2,1)S(1)}, bf16[1000,384]{1,0:T(8,128)(2,1)S(1)}, bf16[1000,128]{1,0:T(8,128)(2,1)S(1...) custom-call(s32[1,6]{1,0:T(1,128)} %send_ref.3, ...), custom_call_target="tpu_custom_call" | custom-call | tf_op jit(solution)/shard_map/pallas_call | solution.py:209
  1.8 0.7 collective-permute-start
  2.5 0.8 collective-permute-start.1
  3.3 4.6 %collective-permute-start.2 = (bf16[1000,128]{1,0:T(8,128)(2,1)S(1)}, bf16[1000,128]{1,0:T(8,128)(2,1)S(1)}, u32[]{:S(2)}, u32[]{:S(2)}) collective-permute-start(bf16[1000,128]{1,0:T(8,128)(2,1)S(1)} %get-tuple-element.36), channel_id=1, source_target_pairs={{0,2},{2,0},{1,3},{3,1},{4,6},{6,4},{5,7},{7,5},{8,10},{10,8},{9,1... | collective-permute-start | bytes 768008 | tf_op jit(solution)/shard_map/ppermute | solution.py:234
  8.0 1.9 %collective-permute-start.3 = (bf16[1000,128]{1,0:T(8,128)(2,1)S(1)}, bf16[1000,128]{1,0:T(8,128)(2,1)S(1)}, u32[]{:S(2)}, u32[]{:S(2)}) collective-permute-start(bf16[1000,128]{1,0:T(8,128)(2,1)S(1)} %get-tuple-element.37), channel_id=1, source_target_pairs={{2,4},{4,2},{3,5},{5,3},{6,8},{8,6},{7,9},{9,7},{10,12},{12,10},{1... | collective-permute-start | bytes 768008 | tf_op jit(solution)/shard_map/ppermute | solution.py:234
  9.9 5.9 %collective-permute-start.4 = (bf16[1000,128]{1,0:T(8,128)(2,1)S(1)}, bf16[1000,128]{1,0:T(8,128)(2,1)S(1)}, u32[]{:S(2)}, u32[]{:S(2)}) collective-permute-start(bf16[1000,128]{1,0:T(8,128)(2,1)S(1)} %get-tuple-element.38), channel_id=1, source_target_pairs={{3,4},{4,3},{7,8},{8,7},{11,12},{12,11},{15,16},{16,15},{19,20},{2... | collective-permute-start | bytes 768008 | tf_op jit(solution)/shard_map/ppermute | solution.py:234
  15.9 0.0 collective-permute-done.refs_0_
  15.9 5.3 %collective-permute-start.5 = (bf16[1000,128]{1,0:T(8,128)(2,1)S(1)}, bf16[1000,128]{1,0:T(8,128)(2,1)S(1)}, u32[]{:S(2)}, u32[]{:S(2)}) collective-permute-start(bf16[1000,128]{1,0:T(8,128)(2,1)S(1)} %get-tuple-element.39), channel_id=1, source_target_pairs={{0,48},{1,49},{2,50},{3,51},{4,52},{5,53},{6,54},{7,55},{8,56},{9,... | collective-permute-start | bytes 768008 | tf_op jit(solution)/shard_map/ppermute | solution.py:234
  21.1 0.0 collective-permute-done.1.refs_1_
  21.8 0.0 copy-start
  21.8 1.1 %copy-done = bf16[3,8,128,128]{3,2,1,0:T(8,128)(2,1)S(1)} copy-done((bf16[3,8,128,128]{3,2,1,0:T(8,128)(2,1)S(1)}, bf16[3,8,128,128]{3,2,1,0:T(8,128)(2,1)}, u32[]{:S(2)}) %copy-start) | copy-done | bytes 786456
  22.9 0.7 copy-done.2
  23.6 1.5 %shard_map.74.weight_ref = bf16[1280,384]{1,0:T(8,128)(2,1)S(1)} custom-call(s32[3,8]{1,0:T(4,128)S(1)} %copy-done.2, s32[1]{0:T(128)S(6)} %copy.8.count_ref, bf16[3,8,128,128]{3,2,1,0:T(8,128)(2,1)S(1)} %copy-done), custom_call_target="tpu_custom_call" | custom-call | bytes 8000000 | tf_op jit(solution)/shard_map/pallas_call | solution.py:224
  25.1 0.0 copy-start.1
  25.1 0.9 %shard_map.75.sum_ref = f32[1000,384]{1,0:T(8,128)S(1)} custom-call(bf16[1280,384]{1,0:T(8,128)(2,1)S(1)} %shard_map.74.weight_ref, bf16[1000,384]{1,0:T(8,128)(2,1)S(1)} %get-tuple-element.33.own_ref, bf16[1000,128]{1,0:T(8,128)(2,1)S(1)} %collective-permute-done.refs_0_, bf16[1000,128]{1,0:T(8,128)(2,1)S(1)} %collective-permute-done.1.refs_1_), custom_call_target="tpu_custom_call" | custom-call | flops 491520000 | bytes 4000000 | tf_op jit(solution)/shard_map/pallas_call | solution.py:235
  26.1 1.8 %collective-permute-done.2.refs_0_ = bf16[1000,128]{1,0:T(8,128)(2,1)S(1)} collective-permute-done((bf16[1000,128]{1,0:T(8,128)(2,1)S(1)}, bf16[1000,128]{1,0:T(8,128)(2,1)S(1)}, u32[]{:S(2)}, u32[]{:S(2)}) %collective-permute-start.2) | collective-permute-done | bytes 256032 | tf_op jit(solution)/shard_map/ppermute | solution.py:234
  27.9 0.0 collective-permute-done.3.refs_1_
  27.9 0.0 collective-permute-done.4.refs_2_
  27.9 0.2 collective-permute-done.6.refs_4_
  28.1 1.8 %shard_map.76 = (bf16[1000,384]{1,0:T(8,128)(2,1)S(1)}, bf16[1000,128]{1,0:T(8,128)(2,1)S(1)}, bf16[1000,128]{1,0:T(8,128)(2,1)S(1)}, bf16[1000,128]{1,0:T(8,128...) custom-call(s32[1,6]{1,0:T(1,128)S(1)} %copy-done.1, ...), custom_call_target="tpu_custom_call" | custom-call | tf_op jit(solution)/shard_map/pallas_call | solution.py:249
  29.8 1.6 %collective-permute-start.7 = (bf16[1000,128]{1,0:T(8,128)(2,1)S(1)}, bf16[1000,128]{1,0:T(8,128)(2,1)S(1)}, u32[]{:S(2)}, u32[]{:S(2)}) collective-permute-start(bf16[1000,128]{1,0:T(8,128)(2,1)S(1)} %get-tuple-element.42), channel_id=1, source_target_pairs={{0,1},{1,2},{2,3},{3,51},{4,5},{5,6},{6,7},{7,55},{8,9},{9,10},{10... | collective-permute-start | bytes 768008 | tf_op jit(solution)/shard_map/ppermute | solution.py:234
  31.5 0.0 collective-permute-start.8
  31.5 1.9 %collective-permute-start.9 = (bf16[1000,128]{1,0:T(8,128)(2,1)S(1)}, bf16[1000,128]{1,0:T(8,128)(2,1)S(1)}, u32[]{:S(2)}, u32[]{:S(2)}) collective-permute-start(bf16[1000,128]{1,0:T(8,128)(2,1)S(1)} %get-tuple-element.44), channel_id=1, source_target_pairs={{0,2},{2,0},{1,3},{3,1},{4,6},{6,4},{5,7},{7,5},{8,10},{10,8},{9,1... | collective-permute-start | bytes 768008 | tf_op jit(solution)/shard_map/ppermute | solution.py:234
  33.4 4.0 %collective-permute-start.10 = (bf16[1000,128]{1,0:T(8,128)(2,1)S(1)}, bf16[1000,128]{1,0:T(8,128)(2,1)S(1)}, u32[]{:S(2)}, u32[]{:S(2)}) collective-permute-start(bf16[1000,128]{1,0:T(8,128)(2,1)S(1)} %get-tuple-element.45), channel_id=1, source_target_pairs={{2,4},{4,2},{3,5},{5,3},{6,8},{8,6},{7,9},{9,7},{10,12},{12,10},{1... | collective-permute-start | bytes 768008 | tf_op jit(solution)/shard_map/ppermute | solution.py:234
  37.4 4.6 %collective-permute-start.11 = (bf16[1000,128]{1,0:T(8,128)(2,1)S(1)}, bf16[1000,128]{1,0:T(8,128)(2,1)S(1)}, u32[]{:S(2)}, u32[]{:S(2)}) collective-permute-start(bf16[1000,128]{1,0:T(8,128)(2,1)S(1)} %get-tuple-element.46), channel_id=1, source_target_pairs={{3,4},{4,3},{7,8},{8,7},{11,12},{12,11},{15,16},{16,15},{19,20},{2... | collective-permute-start | bytes 768008 | tf_op jit(solution)/shard_map/ppermute | solution.py:234
  42.0 0.0 collective-permute-done.7.refs_0_
  42.0 5.2 %collective-permute-start.12 = (bf16[1000,128]{1,0:T(8,128)(2,1)S(1)}, bf16[1000,128]{1,0:T(8,128)(2,1)S(1)}, u32[]{:S(2)}, u32[]{:S(2)}) collective-permute-start(bf16[1000,128]{1,0:T(8,128)(2,1)S(1)} %get-tuple-element.47), channel_id=1, source_target_pairs={{0,48},{1,49},{2,50},{3,51},{4,52},{5,53},{6,54},{7,55},{8,56},{9,... | collective-permute-start | bytes 768008 | tf_op jit(solution)/shard_map/ppermute | solution.py:234
  47.2 0.0 collective-permute-start.13
  47.2 0.9 %shard_map.77.sum_ref = f32[1000,384]{1,0:T(8,128)S(1)} custom-call(bf16[1280,384]{1,0:T(8,128)(2,1)S(1)} %shard_map.74.weight_ref, bf16[1000,384]{1,0:T(8,128)(2,1)S(1)} %get-tuple-element.41.own_ref, bf16[1000,128]{1,0:T(8,128)(2,1)S(1)} %collective-permute-done.7.refs_0_, bf16[1000,128]{1,0:T(8,128)(2,1)S(1)} %collective-permute-done.8.refs_1_), custom_call_target="tpu_custom_call" | custom-call | flops 491520000 | bytes 4000000 | tf_op jit(solution)/shard_map/pallas_call | solution.py:235
  48.1 0.6 collective-permute-done.9.refs_0_
  48.7 0.0 collective-permute-done.10.refs_1_
  48.7 3.6 %collective-permute-done.11.refs_2_ = bf16[1000,128]{1,0:T(8,128)(2,1)S(1)} collective-permute-done((bf16[1000,128]{1,0:T(8,128)(2,1)S(1)}, bf16[1000,128]{1,0:T(8,128)(2,1)S(1)}, u32[]{:S(2)}, u32[]{:S(2)}) %collective-permute-start.11) | collective-permute-done | bytes 256032 | tf_op jit(solution)/shard_map/ppermute | solution.py:234
  52.3 0.0 collective-permute-done.12.refs_3_
  52.3 1.9 %collective-permute-done.13.refs_4_ = bf16[1000,128]{1,0:T(8,128)(2,1)S(1)} collective-permute-done((bf16[1000,128]{1,0:T(8,128)(2,1)S(1)}, bf16[1000,128]{1,0:T(8,128)(2,1)S(1)}, u32[]{:S(2)}, u32[]{:S(2)}) %collective-permute-start.13) | collective-permute-done | bytes 256032 | tf_op jit(solution)/shard_map/ppermute | solution.py:234
  54.2 1.8 %shard_map.78 = (bf16[1000,384]{1,0:T(8,128)(2,1)S(1)}, bf16[1000,128]{1,0:T(8,128)(2,1)S(1)}, bf16[1000,128]{1,0:T(8,128)(2,1)S(1)}, bf16[1000,128]{1,0:T(8,128...) custom-call(s32[1,6]{1,0:T(1,128)S(1)} %copy-done.1, ...), custom_call_target="tpu_custom_call" | custom-call | tf_op jit(solution)/shard_map/pallas_call | solution.py:249
  55.9 0.3 collective-permute-start.14
  56.2 1.2 %collective-permute-start.15 = (bf16[1000,128]{1,0:T(8,128)(2,1)S(1)}, bf16[1000,128]{1,0:T(8,128)(2,1)S(1)}, u32[]{:S(2)}, u32[]{:S(2)}) collective-permute-start(bf16[1000,128]{1,0:T(8,128)(2,1)S(1)} %get-tuple-element.51), channel_id=1, source_target_pairs={{1,0},{2,1},{3,2},{51,3},{5,4},{6,5},{7,6},{55,7},{9,8},{10,9},{11... | collective-permute-start | bytes 768008 | tf_op jit(solution)/shard_map/ppermute | solution.py:234
  57.4 3.1 %collective-permute-start.16 = (bf16[1000,128]{1,0:T(8,128)(2,1)S(1)}, bf16[1000,128]{1,0:T(8,128)(2,1)S(1)}, u32[]{:S(2)}, u32[]{:S(2)}) collective-permute-start(bf16[1000,128]{1,0:T(8,128)(2,1)S(1)} %get-tuple-element.52), channel_id=1, source_target_pairs={{0,2},{2,0},{1,3},{3,1},{4,6},{6,4},{5,7},{7,5},{8,10},{10,8},{9,1... | collective-permute-start | bytes 768008 | tf_op jit(solution)/shard_map/ppermute | solution.py:234
  60.5 2.6 %collective-permute-start.17 = (bf16[1000,128]{1,0:T(8,128)(2,1)S(1)}, bf16[1000,128]{1,0:T(8,128)(2,1)S(1)}, u32[]{:S(2)}, u32[]{:S(2)}) collective-permute-start(bf16[1000,128]{1,0:T(8,128)(2,1)S(1)} %get-tuple-element.53), channel_id=1, source_target_pairs={{2,4},{4,2},{3,5},{5,3},{6,8},{8,6},{7,9},{9,7},{10,12},{12,10},{1... | collective-permute-start | bytes 768008 | tf_op jit(solution)/shard_map/ppermute | solution.py:234
  63.1 6.8 %collective-permute-start.18 = (bf16[1000,128]{1,0:T(8,128)(2,1)S(1)}, bf16[1000,128]{1,0:T(8,128)(2,1)S(1)}, u32[]{:S(2)}, u32[]{:S(2)}) collective-permute-start(bf16[1000,128]{1,0:T(8,128)(2,1)S(1)} %get-tuple-element.54), channel_id=1, source_target_pairs={{3,4},{4,3},{7,8},{8,7},{11,12},{12,11},{15,16},{16,15},{19,20},{2... | collective-permute-start | bytes 768008 | tf_op jit(solution)/shard_map/ppermute | solution.py:234
  69.9 5.1 %collective-permute-start.19 = (bf16[1000,128]{1,0:T(8,128)(2,1)S(1)}, bf16[1000,128]{1,0:T(8,128)(2,1)S(1)}, u32[]{:S(2)}, u32[]{:S(2)}) collective-permute-start(bf16[1000,128]{1,0:T(8,128)(2,1)S(1)} %get-tuple-element.55), channel_id=1, source_target_pairs={{0,48},{1,49},{2,50},{3,51},{4,52},{5,53},{6,54},{7,55},{8,56},{9,... | collective-permute-start | bytes 768008 | tf_op jit(solution)/shard_map/ppermute | solution.py:234
  75.0 0.9 %shard_map.79.sum_ref = f32[1000,384]{1,0:T(8,128)S(1)} custom-call(bf16[1280,384]{1,0:T(8,128)(2,1)S(1)} %shard_map.74.weight_ref, bf16[1000,384]{1,0:T(8,128)(2,1)S(1)} %get-tuple-element.49.own_ref, bf16[1000,128]{1,0:T(8,128)(2,1)S(1)} %collective-permute-done.14.refs_0_, bf16[1000,128]{1,0:T(8,128)(2,1)S(1)} %collective-permute-done.15.refs_1_), custom_call_target="tpu_custom_call" | custom-call | flops 491520000 | bytes 4000000 | tf_op jit(solution)/shard_map/pallas_call | solution.py:235
  75.9 0.0 collective-permute-done.16.refs_0_
  75.9 0.0 collective-permute-done.17.refs_1_
  76.0 2.2 %collective-permute-done.18.refs_2_ = bf16[1000,128]{1,0:T(8,128)(2,1)S(1)} collective-permute-done((bf16[1000,128]{1,0:T(8,128)(2,1)S(1)}, bf16[1000,128]{1,0:T(8,128)(2,1)S(1)}, u32[]{:S(2)}, u32[]{:S(2)}) %collective-permute-start.18) | collective-permute-done | bytes 256032 | tf_op jit(solution)/shard_map/ppermute | solution.py:234
  78.2 0.1 collective-permute-done.19.refs_3_
  78.3 3.7 %collective-permute-done.20.refs_4_ = bf16[1000,128]{1,0:T(8,128)(2,1)S(1)} collective-permute-done((bf16[1000,128]{1,0:T(8,128)(2,1)S(1)}, bf16[1000,128]{1,0:T(8,128)(2,1)S(1)}, u32[]{:S(2)}, u32[]{:S(2)}) %collective-permute-start.20) | collective-permute-done | bytes 256032 | tf_op jit(solution)/shard_map/ppermute | solution.py:234
  82.0 1.7 %shard_map.80 = f32[1000,384]{1,0:T(8,128)} custom-call(f32[1,384]{1,0:T(1,128)S(1)} %get-tuple-element.31.root_ref, bf16[1000,384]{1,0:T(8,128)(2,1)S(1)} %get-tuple-element.32.start_ref, bf16[1280,384]{1,0:T(8,128)(2,1)S(1)} %shard_map.74.weight_ref, f32[1000,384]{1,0:T(8,128)S(1)} %shard_map.79.sum_ref, ...), custom_call_target="tpu_custom_call" | custom-call | tf_op jit(solution)/shard_map/pallas_call | solution.py:256
  (8 shorter events, 0.0 us)
Async XLA Ops:
  1.8 14.0 %collective-permute-start = (bf16[1000,128]{1,0:T(8,128)(2,1)S(1)}, bf16[1000,128]{1,0:T(8,128)(2,1)S(1)}, u32[]{:S(2)}, u32[]{:S(2)}) collective-permute-start(bf16[1000,128]{1,0:T(8,128)(2,1)S(1)} %get-tuple-element.34), channel_id=1, source_target_pairs={{0,1},{1,2},{2,3},{3,51},{4,5},{5,6},{6,7},{7,55},{8,9},{9,10},{10... | collective-permute-start | bytes 768008 | tf_op jit(solution)/shard_map/ppermute | solution.py:234
  2.5 18.6 %collective-permute-start.1 = (bf16[1000,128]{1,0:T(8,128)(2,1)S(1)}, bf16[1000,128]{1,0:T(8,128)(2,1)S(1)}, u32[]{:S(2)}, u32[]{:S(2)}) collective-permute-start(bf16[1000,128]{1,0:T(8,128)(2,1)S(1)} %get-tuple-element.35), channel_id=1, source_target_pairs={{1,0},{2,1},{3,2},{51,3},{5,4},{6,5},{7,6},{55,7},{9,8},{10,9},{11... | collective-permute-start | bytes 768008 | tf_op jit(solution)/shard_map/ppermute | solution.py:234
  3.3 24.5 %collective-permute-start.2 = (bf16[1000,128]{1,0:T(8,128)(2,1)S(1)}, bf16[1000,128]{1,0:T(8,128)(2,1)S(1)}, u32[]{:S(2)}, u32[]{:S(2)}) collective-permute-start(bf16[1000,128]{1,0:T(8,128)(2,1)S(1)} %get-tuple-element.36), channel_id=1, source_target_pairs={{0,2},{2,0},{1,3},{3,1},{4,6},{6,4},{5,7},{7,5},{8,10},{10,8},{9,1... | collective-permute-start | bytes 768008 | tf_op jit(solution)/shard_map/ppermute | solution.py:234
  8.0 19.9 %collective-permute-start.3 = (bf16[1000,128]{1,0:T(8,128)(2,1)S(1)}, bf16[1000,128]{1,0:T(8,128)(2,1)S(1)}, u32[]{:S(2)}, u32[]{:S(2)}) collective-permute-start(bf16[1000,128]{1,0:T(8,128)(2,1)S(1)} %get-tuple-element.37), channel_id=1, source_target_pairs={{2,4},{4,2},{3,5},{5,3},{6,8},{8,6},{7,9},{9,7},{10,12},{12,10},{1... | collective-permute-start | bytes 768008 | tf_op jit(solution)/shard_map/ppermute | solution.py:234
  9.9 18.0 %collective-permute-start.4 = (bf16[1000,128]{1,0:T(8,128)(2,1)S(1)}, bf16[1000,128]{1,0:T(8,128)(2,1)S(1)}, u32[]{:S(2)}, u32[]{:S(2)}) collective-permute-start(bf16[1000,128]{1,0:T(8,128)(2,1)S(1)} %get-tuple-element.38), channel_id=1, source_target_pairs={{3,4},{4,3},{7,8},{8,7},{11,12},{12,11},{15,16},{16,15},{19,20},{2... | collective-permute-start | bytes 768008 | tf_op jit(solution)/shard_map/ppermute | solution.py:234
  15.9 12.0 %collective-permute-start.5 = (bf16[1000,128]{1,0:T(8,128)(2,1)S(1)}, bf16[1000,128]{1,0:T(8,128)(2,1)S(1)}, u32[]{:S(2)}, u32[]{:S(2)}) collective-permute-start(bf16[1000,128]{1,0:T(8,128)(2,1)S(1)} %get-tuple-element.39), channel_id=1, source_target_pairs={{0,48},{1,49},{2,50},{3,51},{4,52},{5,53},{6,54},{7,55},{8,56},{9,... | collective-permute-start | bytes 768008 | tf_op jit(solution)/shard_map/ppermute | solution.py:234
  21.1 6.9 %collective-permute-start.6 = (bf16[1000,128]{1,0:T(8,128)(2,1)S(1)}, bf16[1000,128]{1,0:T(8,128)(2,1)S(1)}, u32[]{:S(2)}, u32[]{:S(2)}) collective-permute-start(bf16[1000,128]{1,0:T(8,128)(2,1)S(1)} %get-tuple-element.40), channel_id=1, source_target_pairs={{0,720},{1,721},{2,722},{3,723},{4,724},{5,725},{6,726},{7,727},{8... | collective-permute-start | bytes 768008 | tf_op jit(solution)/shard_map/ppermute | solution.py:234
  21.8 1.1 %copy-start = (bf16[3,8,128,128]{3,2,1,0:T(8,128)(2,1)S(1)}, bf16[3,8,128,128]{3,2,1,0:T(8,128)(2,1)}, u32[]{:S(2)}) copy-start(bf16[3,8,128,128]{3,2,1,0:T(8,128)(2,1)} %tiles_ref.1) | copy-start | bytes 2359300
  22.9 0.7 copy-start.2
  25.1 3.0 %copy-start.1 = (s32[1,6]{1,0:T(1,128)S(1)}, s32[1,6]{1,0:T(1,128)}, u32[]{:S(2)}) copy-start(s32[1,6]{1,0:T(1,128)} %send_ref.3) | copy-start | bytes 76
  29.8 12.1 %collective-permute-start.7 = (bf16[1000,128]{1,0:T(8,128)(2,1)S(1)}, bf16[1000,128]{1,0:T(8,128)(2,1)S(1)}, u32[]{:S(2)}, u32[]{:S(2)}) collective-permute-start(bf16[1000,128]{1,0:T(8,128)(2,1)S(1)} %get-tuple-element.42), channel_id=1, source_target_pairs={{0,1},{1,2},{2,3},{3,51},{4,5},{5,6},{6,7},{7,55},{8,9},{9,10},{10... | collective-permute-start | bytes 768008 | tf_op jit(solution)/shard_map/ppermute | solution.py:234
  31.5 15.7 %collective-permute-start.8 = (bf16[1000,128]{1,0:T(8,128)(2,1)S(1)}, bf16[1000,128]{1,0:T(8,128)(2,1)S(1)}, u32[]{:S(2)}, u32[]{:S(2)}) collective-permute-start(bf16[1000,128]{1,0:T(8,128)(2,1)S(1)} %get-tuple-element.43), channel_id=1, source_target_pairs={{1,0},{2,1},{3,2},{51,3},{5,4},{6,5},{7,6},{55,7},{9,8},{10,9},{11... | collective-permute-start | bytes 768008 | tf_op jit(solution)/shard_map/ppermute | solution.py:234
  31.5 17.2 %collective-permute-start.9 = (bf16[1000,128]{1,0:T(8,128)(2,1)S(1)}, bf16[1000,128]{1,0:T(8,128)(2,1)S(1)}, u32[]{:S(2)}, u32[]{:S(2)}) collective-permute-start(bf16[1000,128]{1,0:T(8,128)(2,1)S(1)} %get-tuple-element.44), channel_id=1, source_target_pairs={{0,2},{2,0},{1,3},{3,1},{4,6},{6,4},{5,7},{7,5},{8,10},{10,8},{9,1... | collective-permute-start | bytes 768008 | tf_op jit(solution)/shard_map/ppermute | solution.py:234
  33.4 15.3 %collective-permute-start.10 = (bf16[1000,128]{1,0:T(8,128)(2,1)S(1)}, bf16[1000,128]{1,0:T(8,128)(2,1)S(1)}, u32[]{:S(2)}, u32[]{:S(2)}) collective-permute-start(bf16[1000,128]{1,0:T(8,128)(2,1)S(1)} %get-tuple-element.45), channel_id=1, source_target_pairs={{2,4},{4,2},{3,5},{5,3},{6,8},{8,6},{7,9},{9,7},{10,12},{12,10},{1... | collective-permute-start | bytes 768008 | tf_op jit(solution)/shard_map/ppermute | solution.py:234
  37.4 14.9 %collective-permute-start.11 = (bf16[1000,128]{1,0:T(8,128)(2,1)S(1)}, bf16[1000,128]{1,0:T(8,128)(2,1)S(1)}, u32[]{:S(2)}, u32[]{:S(2)}) collective-permute-start(bf16[1000,128]{1,0:T(8,128)(2,1)S(1)} %get-tuple-element.46), channel_id=1, source_target_pairs={{3,4},{4,3},{7,8},{8,7},{11,12},{12,11},{15,16},{16,15},{19,20},{2... | collective-permute-start | bytes 768008 | tf_op jit(solution)/shard_map/ppermute | solution.py:234
  42.0 10.3 %collective-permute-start.12 = (bf16[1000,128]{1,0:T(8,128)(2,1)S(1)}, bf16[1000,128]{1,0:T(8,128)(2,1)S(1)}, u32[]{:S(2)}, u32[]{:S(2)}) collective-permute-start(bf16[1000,128]{1,0:T(8,128)(2,1)S(1)} %get-tuple-element.47), channel_id=1, source_target_pairs={{0,48},{1,49},{2,50},{3,51},{4,52},{5,53},{6,54},{7,55},{8,56},{9,... | collective-permute-start | bytes 768008 | tf_op jit(solution)/shard_map/ppermute | solution.py:234
  47.2 6.9 %collective-permute-start.13 = (bf16[1000,128]{1,0:T(8,128)(2,1)S(1)}, bf16[1000,128]{1,0:T(8,128)(2,1)S(1)}, u32[]{:S(2)}, u32[]{:S(2)}) collective-permute-start(bf16[1000,128]{1,0:T(8,128)(2,1)S(1)} %get-tuple-element.48), channel_id=1, source_target_pairs={{0,720},{1,721},{2,722},{3,723},{4,724},{5,725},{6,726},{7,727},{8... | collective-permute-start | bytes 768008 | tf_op jit(solution)/shard_map/ppermute | solution.py:234
  55.9 14.0 %collective-permute-start.14 = (bf16[1000,128]{1,0:T(8,128)(2,1)S(1)}, bf16[1000,128]{1,0:T(8,128)(2,1)S(1)}, u32[]{:S(2)}, u32[]{:S(2)}) collective-permute-start(bf16[1000,128]{1,0:T(8,128)(2,1)S(1)} %get-tuple-element.50), channel_id=1, source_target_pairs={{0,1},{1,2},{2,3},{3,51},{4,5},{5,6},{6,7},{7,55},{8,9},{9,10},{10... | collective-permute-start | bytes 768008 | tf_op jit(solution)/shard_map/ppermute | solution.py:234
  56.2 18.8 %collective-permute-start.15 = (bf16[1000,128]{1,0:T(8,128)(2,1)S(1)}, bf16[1000,128]{1,0:T(8,128)(2,1)S(1)}, u32[]{:S(2)}, u32[]{:S(2)}) collective-permute-start(bf16[1000,128]{1,0:T(8,128)(2,1)S(1)} %get-tuple-element.51), channel_id=1, source_target_pairs={{1,0},{2,1},{3,2},{51,3},{5,4},{6,5},{7,6},{55,7},{9,8},{10,9},{11... | collective-permute-start | bytes 768008 | tf_op jit(solution)/shard_map/ppermute | solution.py:234
  57.4 18.5 %collective-permute-start.16 = (bf16[1000,128]{1,0:T(8,128)(2,1)S(1)}, bf16[1000,128]{1,0:T(8,128)(2,1)S(1)}, u32[]{:S(2)}, u32[]{:S(2)}) collective-permute-start(bf16[1000,128]{1,0:T(8,128)(2,1)S(1)} %get-tuple-element.52), channel_id=1, source_target_pairs={{0,2},{2,0},{1,3},{3,1},{4,6},{6,4},{5,7},{7,5},{8,10},{10,8},{9,1... | collective-permute-start | bytes 768008 | tf_op jit(solution)/shard_map/ppermute | solution.py:234
  60.5 15.5 %collective-permute-start.17 = (bf16[1000,128]{1,0:T(8,128)(2,1)S(1)}, bf16[1000,128]{1,0:T(8,128)(2,1)S(1)}, u32[]{:S(2)}, u32[]{:S(2)}) collective-permute-start(bf16[1000,128]{1,0:T(8,128)(2,1)S(1)} %get-tuple-element.53), channel_id=1, source_target_pairs={{2,4},{4,2},{3,5},{5,3},{6,8},{8,6},{7,9},{9,7},{10,12},{12,10},{1... | collective-permute-start | bytes 768008 | tf_op jit(solution)/shard_map/ppermute | solution.py:234
  63.1 15.1 %collective-permute-start.18 = (bf16[1000,128]{1,0:T(8,128)(2,1)S(1)}, bf16[1000,128]{1,0:T(8,128)(2,1)S(1)}, u32[]{:S(2)}, u32[]{:S(2)}) collective-permute-start(bf16[1000,128]{1,0:T(8,128)(2,1)S(1)} %get-tuple-element.54), channel_id=1, source_target_pairs={{3,4},{4,3},{7,8},{8,7},{11,12},{12,11},{15,16},{16,15},{19,20},{2... | collective-permute-start | bytes 768008 | tf_op jit(solution)/shard_map/ppermute | solution.py:234
  69.9 8.3 %collective-permute-start.19 = (bf16[1000,128]{1,0:T(8,128)(2,1)S(1)}, bf16[1000,128]{1,0:T(8,128)(2,1)S(1)}, u32[]{:S(2)}, u32[]{:S(2)}) collective-permute-start(bf16[1000,128]{1,0:T(8,128)(2,1)S(1)} %get-tuple-element.55), channel_id=1, source_target_pairs={{0,48},{1,49},{2,50},{3,51},{4,52},{5,53},{6,54},{7,55},{8,56},{9,... | collective-permute-start | bytes 768008 | tf_op jit(solution)/shard_map/ppermute | solution.py:234
  75.0 6.9 %collective-permute-start.20 = (bf16[1000,128]{1,0:T(8,128)(2,1)S(1)}, bf16[1000,128]{1,0:T(8,128)(2,1)S(1)}, u32[]{:S(2)}, u32[]{:S(2)}) collective-permute-start(bf16[1000,128]{1,0:T(8,128)(2,1)S(1)} %get-tuple-element.56), channel_id=1, source_target_pairs={{0,720},{1,721},{2,722},{3,723},{4,724},{5,725},{6,726},{7,727},{8... | collective-permute-start | bytes 768008 | tf_op jit(solution)/shard_map/ppermute | solution.py:234

commit v5 on v4

--- a/solution.py
+++ b/solution.py
@@ -17,9 +17,9 @@
 HBM = pl.BlockSpec(memory_space=pltpu.HBM)
 PARAMS = pltpu.CompilerParams(vmem_limit_bytes=40 * 1024 * 1024)
 
-RING, BACK, TWO, CROSS, EDGE, UP, DOWN = range(7)
+EDGE, RING, BACK, TWO, CROSS, UP, DOWN = range(7)
 PERMUTES = 7
-EARLY = 2
+EARLY = 3
 
 
 def routes(n_group, n_dom):

time: 84.1 us -> 82.5 us (0.981)
  the two profiles are of different devices: /device:TPU:281 before, /device:TPU:95 now
where the time goes in v5:
time: 82.5 us; the launch traced here: 82.1 us
  starting transfers between devices  54.7 us (66%)
  waiting for transfers between devices  13.8 us (17%)
  Pallas kernels  10.9 us (13%)
  local copies, waits for them, and re-layouts  1.82 us (2%)
  between operations  0.92 us (1%)
    ppermute x21, starting transfers between devices, on_device(): lax.ppermute(sends[k], ('group', 'dom'), route[k])  54.7 us
    ppermute x21, waiting for transfers between devices, on_device(): lax.ppermute(sends[k], ('group', 'dom'), route[k])  13.8 us
    pallas_call x2, Pallas kernels, on_device(): pl.pallas_call(step_kernel, in_specs=[SMEM] + [VMEM] * (4 + len(late)), o...  3.07 us
    pallas_call x3, Pallas kernels, on_device(): pl.pallas_call(early_kernel, in_specs=[VMEM] * (2 + EARLY), out_specs=VME...  2.91 us
    pallas_call x1, Pallas kernels, on_device(): pl.pallas_call(prepare_kernel, in_specs=[HBM] * 4, out_specs=[VMEM] * (3...  1.84 us
    unnamed x6, local copies, waits for them, and re-layouts  1.82 us
  transfers between devices with their start and end apart: 21, of which 5 were waited for; matrix products, arithmetic and copies ran while one was open for 0% of the time, Pallas kernels for 5%

profile of v5, /device:TPU:95, one launch (start us, length us, event | category | flops | bytes accessed | tf_op | source)
XLA Modules:
  0.0 82.1 jit_solution(15756354979138089772)
XLA Ops:
  0.0 1.8 %shard_map.73 = (f32[1,384]{1,0:T(1,128)S(1)}, bf16[1000,384]{1,0:T(8,128)(2,1)S(1)}, bf16[1000,384]{1,0:T(8,128)(2,1)S(1)}, bf16[1000,128]{1,0:T(8,128)(2,1)S(1...) custom-call(s32[1,6]{1,0:T(1,128)} %send_ref.3, ...), custom_call_target="tpu_custom_call" | custom-call | tf_op jit(solution)/shard_map/pallas_call | solution.py:209
  1.8 3.9 %collective-permute-start = (bf16[1000,128]{1,0:T(8,128)(2,1)S(1)}, bf16[1000,128]{1,0:T(8,128)(2,1)S(1)}, u32[]{:S(2)}, u32[]{:S(2)}) collective-permute-start(bf16[1000,128]{1,0:T(8,128)(2,1)S(1)} %get-tuple-element.34), channel_id=1, source_target_pairs={{3,4},{4,3},{7,8},{8,7},{11,12},{12,11},{15,16},{16,15},{19,20},{2... | collective-permute-start | bytes 768008 | tf_op jit(solution)/shard_map/ppermute | solution.py:234
  5.8 0.0 collective-permute-start.1
  5.8 1.0 %collective-permute-start.2 = (bf16[1000,128]{1,0:T(8,128)(2,1)S(1)}, bf16[1000,128]{1,0:T(8,128)(2,1)S(1)}, u32[]{:S(2)}, u32[]{:S(2)}) collective-permute-start(bf16[1000,128]{1,0:T(8,128)(2,1)S(1)} %get-tuple-element.36), channel_id=1, source_target_pairs={{1,0},{2,1},{3,2},{51,3},{5,4},{6,5},{7,6},{55,7},{9,8},{10,9},{11... | collective-permute-start | bytes 768008 | tf_op jit(solution)/shard_map/ppermute | solution.py:234
  6.8 1.9 %collective-permute-start.3 = (bf16[1000,128]{1,0:T(8,128)(2,1)S(1)}, bf16[1000,128]{1,0:T(8,128)(2,1)S(1)}, u32[]{:S(2)}, u32[]{:S(2)}) collective-permute-start(bf16[1000,128]{1,0:T(8,128)(2,1)S(1)} %get-tuple-element.37), channel_id=1, source_target_pairs={{0,2},{2,0},{1,3},{3,1},{4,6},{6,4},{5,7},{7,5},{8,10},{10,8},{9,1... | collective-permute-start | bytes 768008 | tf_op jit(solution)/shard_map/ppermute | solution.py:234
  8.7 6.7 %collective-permute-start.4 = (bf16[1000,128]{1,0:T(8,128)(2,1)S(1)}, bf16[1000,128]{1,0:T(8,128)(2,1)S(1)}, u32[]{:S(2)}, u32[]{:S(2)}) collective-permute-start(bf16[1000,128]{1,0:T(8,128)(2,1)S(1)} %get-tuple-element.38), channel_id=1, source_target_pairs={{2,4},{4,2},{3,5},{5,3},{6,8},{8,6},{7,9},{9,7},{10,12},{12,10},{1... | collective-permute-start | bytes 768008 | tf_op jit(solution)/shard_map/ppermute | solution.py:234
  15.4 0.0 collective-permute-done.refs_0_
  15.4 5.0 %collective-permute-start.5 = (bf16[1000,128]{1,0:T(8,128)(2,1)S(1)}, bf16[1000,128]{1,0:T(8,128)(2,1)S(1)}, u32[]{:S(2)}, u32[]{:S(2)}) collective-permute-start(bf16[1000,128]{1,0:T(8,128)(2,1)S(1)} %get-tuple-element.39), channel_id=1, source_target_pairs={{0,48},{1,49},{2,50},{3,51},{4,52},{5,53},{6,54},{7,55},{8,56},{9,... | collective-permute-start | bytes 768008 | tf_op jit(solution)/shard_map/ppermute | solution.py:234
  20.3 0.0 collective-permute-done.1.refs_1_
  20.3 0.0 collective-permute-start.6
  21.0 0.0 copy-start
  21.0 1.1 %copy-done = bf16[3,8,128,128]{3,2,1,0:T(8,128)(2,1)S(1)} copy-done((bf16[3,8,128,128]{3,2,1,0:T(8,128)(2,1)S(1)}, bf16[3,8,128,128]{3,2,1,0:T(8,128)(2,1)}, u32[]{:S(2)}) %copy-start) | copy-done | bytes 786456
  22.1 0.7 copy-done.2
  22.8 1.5 %shard_map.74.weight_ref = bf16[1280,384]{1,0:T(8,128)(2,1)S(1)} custom-call(s32[3,8]{1,0:T(4,128)S(1)} %copy-done.2, s32[1]{0:T(128)S(6)} %copy.8.count_ref, bf16[3,8,128,128]{3,2,1,0:T(8,128)(2,1)S(1)} %copy-done), custom_call_target="tpu_custom_call" | custom-call | bytes 8000000 | tf_op jit(solution)/shard_map/pallas_call | solution.py:224
  24.3 0.0 collective-permute-done.2.refs_2_
  24.4 0.0 copy-start.1
  24.4 1.0 %shard_map.75.sum_ref = f32[1000,384]{1,0:T(8,128)S(1)} custom-call(bf16[1280,384]{1,0:T(8,128)(2,1)S(1)} %shard_map.74.weight_ref, bf16[1000,384]{1,0:T(8,128)(2,1)S(1)} %get-tuple-element.33.own_ref, bf16[1000,128]{1,0:T(8,128)(2,1)S(1)} %collective-permute-done.refs_0_, bf16[1000,128]{1,0:T(8,128)(2,1)S(1)} %collective-permute-done.1.refs_1_, ...), custom_call_target="tpu_custom_call" | custom-call | flops 589824000 | bytes 4000000 | tf_op jit(solution)/shard_map/pallas_call | solution.py:235
  25.3 0.0 collective-permute-done.3.refs_0_
  25.4 0.0 collective-permute-done.5.refs_2_
  25.4 1.9 %collective-permute-done.6.refs_3_ = bf16[1000,128]{1,0:T(8,128)(2,1)S(1)} collective-permute-done((bf16[1000,128]{1,0:T(8,128)(2,1)S(1)}, bf16[1000,128]{1,0:T(8,128)(2,1)S(1)}, u32[]{:S(2)}, u32[]{:S(2)}) %collective-permute-start.6) | collective-permute-done | bytes 256032 | tf_op jit(solution)/shard_map/ppermute | solution.py:234
  27.3 1.5 %shard_map.76 = (bf16[1000,384]{1,0:T(8,128)(2,1)S(1)}, bf16[1000,128]{1,0:T(8,128)(2,1)S(1)}, bf16[1000,128]{1,0:T(8,128)(2,1)S(1)}, bf16[1000,128]{1,0:T(8,128...) custom-call(s32[1,6]{1,0:T(1,128)S(1)} %copy-done.1, ...), custom_call_target="tpu_custom_call" | custom-call | tf_op jit(solution)/shard_map/pallas_call | solution.py:249
  28.8 2.4 %collective-permute-start.7 = (bf16[1000,128]{1,0:T(8,128)(2,1)S(1)}, bf16[1000,128]{1,0:T(8,128)(2,1)S(1)}, u32[]{:S(2)}, u32[]{:S(2)}) collective-permute-start(bf16[1000,128]{1,0:T(8,128)(2,1)S(1)} %get-tuple-element.42), channel_id=1, source_target_pairs={{3,4},{4,3},{7,8},{8,7},{11,12},{12,11},{15,16},{16,15},{19,20},{2... | collective-permute-start | bytes 768008 | tf_op jit(solution)/shard_map/ppermute | solution.py:234
  31.2 0.0 collective-permute-start.8
  31.3 2.1 %collective-permute-start.9 = (bf16[1000,128]{1,0:T(8,128)(2,1)S(1)}, bf16[1000,128]{1,0:T(8,128)(2,1)S(1)}, u32[]{:S(2)}, u32[]{:S(2)}) collective-permute-start(bf16[1000,128]{1,0:T(8,128)(2,1)S(1)} %get-tuple-element.44), channel_id=1, source_target_pairs={{1,0},{2,1},{3,2},{51,3},{5,4},{6,5},{7,6},{55,7},{9,8},{10,9},{11... | collective-permute-start | bytes 768008 | tf_op jit(solution)/shard_map/ppermute | solution.py:234
  33.4 2.2 %collective-permute-start.10 = (bf16[1000,128]{1,0:T(8,128)(2,1)S(1)}, bf16[1000,128]{1,0:T(8,128)(2,1)S(1)}, u32[]{:S(2)}, u32[]{:S(2)}) collective-permute-start(bf16[1000,128]{1,0:T(8,128)(2,1)S(1)} %get-tuple-element.45), channel_id=1, source_target_pairs={{0,2},{2,0},{1,3},{3,1},{4,6},{6,4},{5,7},{7,5},{8,10},{10,8},{9,1... | collective-permute-start | bytes 768008 | tf_op jit(solution)/shard_map/ppermute | solution.py:234
  35.6 7.6 %collective-permute-start.11 = (bf16[1000,128]{1,0:T(8,128)(2,1)S(1)}, bf16[1000,128]{1,0:T(8,128)(2,1)S(1)}, u32[]{:S(2)}, u32[]{:S(2)}) collective-permute-start(bf16[1000,128]{1,0:T(8,128)(2,1)S(1)} %get-tuple-element.46), channel_id=1, source_target_pairs={{2,4},{4,2},{3,5},{5,3},{6,8},{8,6},{7,9},{9,7},{10,12},{12,10},{1... | collective-permute-start | bytes 768008 | tf_op jit(solution)/shard_map/ppermute | solution.py:234
  43.2 5.0 %collective-permute-start.12 = (bf16[1000,128]{1,0:T(8,128)(2,1)S(1)}, bf16[1000,128]{1,0:T(8,128)(2,1)S(1)}, u32[]{:S(2)}, u32[]{:S(2)}) collective-permute-start(bf16[1000,128]{1,0:T(8,128)(2,1)S(1)} %get-tuple-element.47), channel_id=1, source_target_pairs={{0,48},{1,49},{2,50},{3,51},{4,52},{5,53},{6,54},{7,55},{8,56},{9,... | collective-permute-start | bytes 768008 | tf_op jit(solution)/shard_map/ppermute | solution.py:234
  48.2 0.0 collective-permute-done.9.refs_2_
  48.2 1.0 %shard_map.77.sum_ref = f32[1000,384]{1,0:T(8,128)S(1)} custom-call(bf16[1280,384]{1,0:T(8,128)(2,1)S(1)} %shard_map.74.weight_ref, bf16[1000,384]{1,0:T(8,128)(2,1)S(1)} %get-tuple-element.41.own_ref, bf16[1000,128]{1,0:T(8,128)(2,1)S(1)} %collective-permute-done.7.refs_0_, bf16[1000,128]{1,0:T(8,128)(2,1)S(1)} %collective-permute-done.8.refs_1_, ...), custom_call_target="tpu_custom_call" | custom-call | flops 589824000 | bytes 4000000 | tf_op jit(solution)/shard_map/pallas_call | solution.py:235
  49.2 0.0 collective-permute-done.10.refs_0_
  49.2 0.0 collective-permute-done.11.refs_1_
  49.2 2.2 %collective-permute-done.12.refs_2_ = bf16[1000,128]{1,0:T(8,128)(2,1)S(1)} collective-permute-done((bf16[1000,128]{1,0:T(8,128)(2,1)S(1)}, bf16[1000,128]{1,0:T(8,128)(2,1)S(1)}, u32[]{:S(2)}, u32[]{:S(2)}) %collective-permute-start.12) | collective-permute-done | bytes 256032 | tf_op jit(solution)/shard_map/ppermute | solution.py:234
  51.4 3.7 %collective-permute-done.13.refs_3_ = bf16[1000,128]{1,0:T(8,128)(2,1)S(1)} collective-permute-done((bf16[1000,128]{1,0:T(8,128)(2,1)S(1)}, bf16[1000,128]{1,0:T(8,128)(2,1)S(1)}, u32[]{:S(2)}, u32[]{:S(2)}) %collective-permute-start.13) | collective-permute-done | bytes 256032 | tf_op jit(solution)/shard_map/ppermute | solution.py:234
  55.1 1.5 %shard_map.78 = (bf16[1000,384]{1,0:T(8,128)(2,1)S(1)}, bf16[1000,128]{1,0:T(8,128)(2,1)S(1)}, bf16[1000,128]{1,0:T(8,128)(2,1)S(1)}, bf16[1000,128]{1,0:T(8,128...) custom-call(s32[1,6]{1,0:T(1,128)S(1)} %copy-done.1, ...), custom_call_target="tpu_custom_call" | custom-call | tf_op jit(solution)/shard_map/pallas_call | solution.py:249
  56.7 1.9 %collective-permute-start.14 = (bf16[1000,128]{1,0:T(8,128)(2,1)S(1)}, bf16[1000,128]{1,0:T(8,128)(2,1)S(1)}, u32[]{:S(2)}, u32[]{:S(2)}) collective-permute-start(bf16[1000,128]{1,0:T(8,128)(2,1)S(1)} %get-tuple-element.50), channel_id=1, source_target_pairs={{3,4},{4,3},{7,8},{8,7},{11,12},{12,11},{15,16},{16,15},{19,20},{2... | collective-permute-start | bytes 768008 | tf_op jit(solution)/shard_map/ppermute | solution.py:234
  58.6 0.0 collective-permute-start.15
  58.6 1.4 %collective-permute-start.16 = (bf16[1000,128]{1,0:T(8,128)(2,1)S(1)}, bf16[1000,128]{1,0:T(8,128)(2,1)S(1)}, u32[]{:S(2)}, u32[]{:S(2)}) collective-permute-start(bf16[1000,128]{1,0:T(8,128)(2,1)S(1)} %get-tuple-element.52), channel_id=1, source_target_pairs={{1,0},{2,1},{3,2},{51,3},{5,4},{6,5},{7,6},{55,7},{9,8},{10,9},{11... | collective-permute-start | bytes 768008 | tf_op jit(solution)/shard_map/ppermute | solution.py:234
  60.1 2.2 %collective-permute-start.17 = (bf16[1000,128]{1,0:T(8,128)(2,1)S(1)}, bf16[1000,128]{1,0:T(8,128)(2,1)S(1)}, u32[]{:S(2)}, u32[]{:S(2)}) collective-permute-start(bf16[1000,128]{1,0:T(8,128)(2,1)S(1)} %get-tuple-element.53), channel_id=1, source_target_pairs={{0,2},{2,0},{1,3},{3,1},{4,6},{6,4},{5,7},{7,5},{8,10},{10,8},{9,1... | collective-permute-start | bytes 768008 | tf_op jit(solution)/shard_map/ppermute | solution.py:234
  62.3 6.4 %collective-permute-start.18 = (bf16[1000,128]{1,0:T(8,128)(2,1)S(1)}, bf16[1000,128]{1,0:T(8,128)(2,1)S(1)}, u32[]{:S(2)}, u32[]{:S(2)}) collective-permute-start(bf16[1000,128]{1,0:T(8,128)(2,1)S(1)} %get-tuple-element.54), channel_id=1, source_target_pairs={{2,4},{4,2},{3,5},{5,3},{6,8},{8,6},{7,9},{9,7},{10,12},{12,10},{1... | collective-permute-start | bytes 768008 | tf_op jit(solution)/shard_map/ppermute | solution.py:234
  68.7 0.0 collective-permute-done.14.refs_0_
  68.7 5.0 %collective-permute-start.19 = (bf16[1000,128]{1,0:T(8,128)(2,1)S(1)}, bf16[1000,128]{1,0:T(8,128)(2,1)S(1)}, u32[]{:S(2)}, u32[]{:S(2)}) collective-permute-start(bf16[1000,128]{1,0:T(8,128)(2,1)S(1)} %get-tuple-element.55), channel_id=1, source_target_pairs={{0,48},{1,49},{2,50},{3,51},{4,52},{5,53},{6,54},{7,55},{8,56},{9,... | collective-permute-start | bytes 768008 | tf_op jit(solution)/shard_map/ppermute | solution.py:234
  73.6 0.0 collective-permute-done.15.refs_1_
  73.6 0.0 collective-permute-start.20
  73.7 1.0 %shard_map.79.sum_ref = f32[1000,384]{1,0:T(8,128)S(1)} custom-call(bf16[1280,384]{1,0:T(8,128)(2,1)S(1)} %shard_map.74.weight_ref, bf16[1000,384]{1,0:T(8,128)(2,1)S(1)} %get-tuple-element.49.own_ref, bf16[1000,128]{1,0:T(8,128)(2,1)S(1)} %collective-permute-done.14.refs_0_, bf16[1000,128]{1,0:T(8,128)(2,1)S(1)} %collective-permute-done.15.refs_1_, ...), custom_call_target="tpu_custom_call" | custom-call | flops 589824000 | bytes 4000000 | tf_op jit(solution)/shard_map/pallas_call | solution.py:235
  74.6 0.0 collective-permute-done.17.refs_0_
  74.7 2.2 %collective-permute-done.19.refs_2_ = bf16[1000,128]{1,0:T(8,128)(2,1)S(1)} collective-permute-done((bf16[1000,128]{1,0:T(8,128)(2,1)S(1)}, bf16[1000,128]{1,0:T(8,128)(2,1)S(1)}, u32[]{:S(2)}, u32[]{:S(2)}) %collective-permute-start.19) | collective-permute-done | bytes 256032 | tf_op jit(solution)/shard_map/ppermute | solution.py:234
  76.9 3.7 %collective-permute-done.20.refs_3_ = bf16[1000,128]{1,0:T(8,128)(2,1)S(1)} collective-permute-done((bf16[1000,128]{1,0:T(8,128)(2,1)S(1)}, bf16[1000,128]{1,0:T(8,128)(2,1)S(1)}, u32[]{:S(2)}, u32[]{:S(2)}) %collective-permute-start.20) | collective-permute-done | bytes 256032 | tf_op jit(solution)/shard_map/ppermute | solution.py:234
  80.6 1.5 %shard_map.80 = f32[1000,384]{1,0:T(8,128)} custom-call(f32[1,384]{1,0:T(1,128)S(1)} %get-tuple-element.31.root_ref, bf16[1000,384]{1,0:T(8,128)(2,1)S(1)} %get-tuple-element.32.start_ref, bf16[1280,384]{1,0:T(8,128)(2,1)S(1)} %shard_map.74.weight_ref, f32[1000,384]{1,0:T(8,128)S(1)} %shard_map.79.sum_ref, ...), custom_call_target="tpu_custom_call" | custom-call | tf_op jit(solution)/shard_map/pallas_call | solution.py:256
  (8 shorter events, 0.0 us)
Async XLA Ops:
  1.8 13.5 %collective-permute-start = (bf16[1000,128]{1,0:T(8,128)(2,1)S(1)}, bf16[1000,128]{1,0:T(8,128)(2,1)S(1)}, u32[]{:S(2)}, u32[]{:S(2)}) collective-permute-start(bf16[1000,128]{1,0:T(8,128)(2,1)S(1)} %get-tuple-element.34), channel_id=1, source_target_pairs={{3,4},{4,3},{7,8},{8,7},{11,12},{12,11},{15,16},{16,15},{19,20},{2... | collective-permute-start | bytes 768008 | tf_op jit(solution)/shard_map/ppermute | solution.py:234
  5.8 14.6 %collective-permute-start.1 = (bf16[1000,128]{1,0:T(8,128)(2,1)S(1)}, bf16[1000,128]{1,0:T(8,128)(2,1)S(1)}, u32[]{:S(2)}, u32[]{:S(2)}) collective-permute-start(bf16[1000,128]{1,0:T(8,128)(2,1)S(1)} %get-tuple-element.35), channel_id=1, source_target_pairs={{0,1},{1,2},{2,3},{3,51},{4,5},{5,6},{6,7},{7,55},{8,9},{9,10},{10... | collective-permute-start | bytes 768008 | tf_op jit(solution)/shard_map/ppermute | solution.py:234
  5.8 18.5 %collective-permute-start.2 = (bf16[1000,128]{1,0:T(8,128)(2,1)S(1)}, bf16[1000,128]{1,0:T(8,128)(2,1)S(1)}, u32[]{:S(2)}, u32[]{:S(2)}) collective-permute-start(bf16[1000,128]{1,0:T(8,128)(2,1)S(1)} %get-tuple-element.36), channel_id=1, source_target_pairs={{1,0},{2,1},{3,2},{51,3},{5,4},{6,5},{7,6},{55,7},{9,8},{10,9},{11... | collective-permute-start | bytes 768008 | tf_op jit(solution)/shard_map/ppermute | solution.py:234
  6.8 18.6 %collective-permute-start.3 = (bf16[1000,128]{1,0:T(8,128)(2,1)S(1)}, bf16[1000,128]{1,0:T(8,128)(2,1)S(1)}, u32[]{:S(2)}, u32[]{:S(2)}) collective-permute-start(bf16[1000,128]{1,0:T(8,128)(2,1)S(1)} %get-tuple-element.37), channel_id=1, source_target_pairs={{0,2},{2,0},{1,3},{3,1},{4,6},{6,4},{5,7},{7,5},{8,10},{10,8},{9,1... | collective-permute-start | bytes 768008 | tf_op jit(solution)/shard_map/ppermute | solution.py:234
  8.7 16.7 %collective-permute-start.4 = (bf16[1000,128]{1,0:T(8,128)(2,1)S(1)}, bf16[1000,128]{1,0:T(8,128)(2,1)S(1)}, u32[]{:S(2)}, u32[]{:S(2)}) collective-permute-start(bf16[1000,128]{1,0:T(8,128)(2,1)S(1)} %get-tuple-element.38), channel_id=1, source_target_pairs={{2,4},{4,2},{3,5},{5,3},{6,8},{8,6},{7,9},{9,7},{10,12},{12,10},{1... | collective-permute-start | bytes 768008 | tf_op jit(solution)/shard_map/ppermute | solution.py:234
  15.4 10.0 %collective-permute-start.5 = (bf16[1000,128]{1,0:T(8,128)(2,1)S(1)}, bf16[1000,128]{1,0:T(8,128)(2,1)S(1)}, u32[]{:S(2)}, u32[]{:S(2)}) collective-permute-start(bf16[1000,128]{1,0:T(8,128)(2,1)S(1)} %get-tuple-element.39), channel_id=1, source_target_pairs={{0,48},{1,49},{2,50},{3,51},{4,52},{5,53},{6,54},{7,55},{8,56},{9,... | collective-permute-start | bytes 768008 | tf_op jit(solution)/shard_map/ppermute | solution.py:234
  20.3 6.9 %collective-permute-start.6 = (bf16[1000,128]{1,0:T(8,128)(2,1)S(1)}, bf16[1000,128]{1,0:T(8,128)(2,1)S(1)}, u32[]{:S(2)}, u32[]{:S(2)}) collective-permute-start(bf16[1000,128]{1,0:T(8,128)(2,1)S(1)} %get-tuple-element.40), channel_id=1, source_target_pairs={{0,720},{1,721},{2,722},{3,723},{4,724},{5,725},{6,726},{7,727},{8... | collective-permute-start | bytes 768008 | tf_op jit(solution)/shard_map/ppermute | solution.py:234
  21.0 1.1 %copy-start = (bf16[3,8,128,128]{3,2,1,0:T(8,128)(2,1)S(1)}, bf16[3,8,128,128]{3,2,1,0:T(8,128)(2,1)}, u32[]{:S(2)}) copy-start(bf16[3,8,128,128]{3,2,1,0:T(8,128)(2,1)} %tiles_ref.1) | copy-start | bytes 2359300
  22.1 0.7 copy-start.2
  24.4 2.9 %copy-start.1 = (s32[1,6]{1,0:T(1,128)S(1)}, s32[1,6]{1,0:T(1,128)}, u32[]{:S(2)}) copy-start(s32[1,6]{1,0:T(1,128)} %send_ref.3) | copy-start | bytes 76
  28.8 14.4 %collective-permute-start.7 = (bf16[1000,128]{1,0:T(8,128)(2,1)S(1)}, bf16[1000,128]{1,0:T(8,128)(2,1)S(1)}, u32[]{:S(2)}, u32[]{:S(2)}) collective-permute-start(bf16[1000,128]{1,0:T(8,128)(2,1)S(1)} %get-tuple-element.42), channel_id=1, source_target_pairs={{3,4},{4,3},{7,8},{8,7},{11,12},{12,11},{15,16},{16,15},{19,20},{2... | collective-permute-start | bytes 768008 | tf_op jit(solution)/shard_map/ppermute | solution.py:234
  31.2 16.9 %collective-permute-start.8 = (bf16[1000,128]{1,0:T(8,128)(2,1)S(1)}, bf16[1000,128]{1,0:T(8,128)(2,1)S(1)}, u32[]{:S(2)}, u32[]{:S(2)}) collective-permute-start(bf16[1000,128]{1,0:T(8,128)(2,1)S(1)} %get-tuple-element.43), channel_id=1, source_target_pairs={{0,1},{1,2},{2,3},{3,51},{4,5},{5,6},{6,7},{7,55},{8,9},{9,10},{10... | collective-permute-start | bytes 768008 | tf_op jit(solution)/shard_map/ppermute | solution.py:234
  31.3 16.9 %collective-permute-start.9 = (bf16[1000,128]{1,0:T(8,128)(2,1)S(1)}, bf16[1000,128]{1,0:T(8,128)(2,1)S(1)}, u32[]{:S(2)}, u32[]{:S(2)}) collective-permute-start(bf16[1000,128]{1,0:T(8,128)(2,1)S(1)} %get-tuple-element.44), channel_id=1, source_target_pairs={{1,0},{2,1},{3,2},{51,3},{5,4},{6,5},{7,6},{55,7},{9,8},{10,9},{11... | collective-permute-start | bytes 768008 | tf_op jit(solution)/shard_map/ppermute | solution.py:234
  33.4 15.8 %collective-permute-start.10 = (bf16[1000,128]{1,0:T(8,128)(2,1)S(1)}, bf16[1000,128]{1,0:T(8,128)(2,1)S(1)}, u32[]{:S(2)}, u32[]{:S(2)}) collective-permute-start(bf16[1000,128]{1,0:T(8,128)(2,1)S(1)} %get-tuple-element.45), channel_id=1, source_target_pairs={{0,2},{2,0},{1,3},{3,1},{4,6},{6,4},{5,7},{7,5},{8,10},{10,8},{9,1... | collective-permute-start | bytes 768008 | tf_op jit(solution)/shard_map/ppermute | solution.py:234
  35.6 13.6 %collective-permute-start.11 = (bf16[1000,128]{1,0:T(8,128)(2,1)S(1)}, bf16[1000,128]{1,0:T(8,128)(2,1)S(1)}, u32[]{:S(2)}, u32[]{:S(2)}) collective-permute-start(bf16[1000,128]{1,0:T(8,128)(2,1)S(1)} %get-tuple-element.46), channel_id=1, source_target_pairs={{2,4},{4,2},{3,5},{5,3},{6,8},{8,6},{7,9},{9,7},{10,12},{12,10},{1... | collective-permute-start | bytes 768008 | tf_op jit(solution)/shard_map/ppermute | solution.py:234
  43.2 8.2 %collective-permute-start.12 = (bf16[1000,128]{1,0:T(8,128)(2,1)S(1)}, bf16[1000,128]{1,0:T(8,128)(2,1)S(1)}, u32[]{:S(2)}, u32[]{:S(2)}) collective-permute-start(bf16[1000,128]{1,0:T(8,128)(2,1)S(1)} %get-tuple-element.47), channel_id=1, source_target_pairs={{0,48},{1,49},{2,50},{3,51},{4,52},{5,53},{6,54},{7,55},{8,56},{9,... | collective-permute-start | bytes 768008 | tf_op jit(solution)/shard_map/ppermute | solution.py:234
  48.2 6.9 %collective-permute-start.13 = (bf16[1000,128]{1,0:T(8,128)(2,1)S(1)}, bf16[1000,128]{1,0:T(8,128)(2,1)S(1)}, u32[]{:S(2)}, u32[]{:S(2)}) collective-permute-start(bf16[1000,128]{1,0:T(8,128)(2,1)S(1)} %get-tuple-element.48), channel_id=1, source_target_pairs={{0,720},{1,721},{2,722},{3,723},{4,724},{5,725},{6,726},{7,727},{8... | collective-permute-start | bytes 768008 | tf_op jit(solution)/shard_map/ppermute | solution.py:234
  56.7 12.0 %collective-permute-start.14 = (bf16[1000,128]{1,0:T(8,128)(2,1)S(1)}, bf16[1000,128]{1,0:T(8,128)(2,1)S(1)}, u32[]{:S(2)}, u32[]{:S(2)}) collective-permute-start(bf16[1000,128]{1,0:T(8,128)(2,1)S(1)} %get-tuple-element.50), channel_id=1, source_target_pairs={{3,4},{4,3},{7,8},{8,7},{11,12},{12,11},{15,16},{16,15},{19,20},{2... | collective-permute-start | bytes 768008 | tf_op jit(solution)/shard_map/ppermute | solution.py:234
  58.6 15.0 %collective-permute-start.15 = (bf16[1000,128]{1,0:T(8,128)(2,1)S(1)}, bf16[1000,128]{1,0:T(8,128)(2,1)S(1)}, u32[]{:S(2)}, u32[]{:S(2)}) collective-permute-start(bf16[1000,128]{1,0:T(8,128)(2,1)S(1)} %get-tuple-element.51), channel_id=1, source_target_pairs={{0,1},{1,2},{2,3},{3,51},{4,5},{5,6},{6,7},{7,55},{8,9},{9,10},{10... | collective-permute-start | bytes 768008 | tf_op jit(solution)/shard_map/ppermute | solution.py:234
  58.6 15.0 %collective-permute-start.16 = (bf16[1000,128]{1,0:T(8,128)(2,1)S(1)}, bf16[1000,128]{1,0:T(8,128)(2,1)S(1)}, u32[]{:S(2)}, u32[]{:S(2)}) collective-permute-start(bf16[1000,128]{1,0:T(8,128)(2,1)S(1)} %get-tuple-element.52), channel_id=1, source_target_pairs={{1,0},{2,1},{3,2},{51,3},{5,4},{6,5},{7,6},{55,7},{9,8},{10,9},{11... | collective-permute-start | bytes 768008 | tf_op jit(solution)/shard_map/ppermute | solution.py:234
  60.1 14.6 %collective-permute-start.17 = (bf16[1000,128]{1,0:T(8,128)(2,1)S(1)}, bf16[1000,128]{1,0:T(8,128)(2,1)S(1)}, u32[]{:S(2)}, u32[]{:S(2)}) collective-permute-start(bf16[1000,128]{1,0:T(8,128)(2,1)S(1)} %get-tuple-element.53), channel_id=1, source_target_pairs={{0,2},{2,0},{1,3},{3,1},{4,6},{6,4},{5,7},{7,5},{8,10},{10,8},{9,1... | collective-permute-start | bytes 768008 | tf_op jit(solution)/shard_map/ppermute | solution.py:234
  62.3 12.4 %collective-permute-start.18 = (bf16[1000,128]{1,0:T(8,128)(2,1)S(1)}, bf16[1000,128]{1,0:T(8,128)(2,1)S(1)}, u32[]{:S(2)}, u32[]{:S(2)}) collective-permute-start(bf16[1000,128]{1,0:T(8,128)(2,1)S(1)} %get-tuple-element.54), channel_id=1, source_target_pairs={{2,4},{4,2},{3,5},{5,3},{6,8},{8,6},{7,9},{9,7},{10,12},{12,10},{1... | collective-permute-start | bytes 768008 | tf_op jit(solution)/shard_map/ppermute | solution.py:234
  68.7 8.2 %collective-permute-start.19 = (bf16[1000,128]{1,0:T(8,128)(2,1)S(1)}, bf16[1000,128]{1,0:T(8,128)(2,1)S(1)}, u32[]{:S(2)}, u32[]{:S(2)}) collective-permute-start(bf16[1000,128]{1,0:T(8,128)(2,1)S(1)} %get-tuple-element.55), channel_id=1, source_target_pairs={{0,48},{1,49},{2,50},{3,51},{4,52},{5,53},{6,54},{7,55},{8,56},{9,... | collective-permute-start | bytes 768008 | tf_op jit(solution)/shard_map/ppermute | solution.py:234
  73.6 6.9 %collective-permute-start.20 = (bf16[1000,128]{1,0:T(8,128)(2,1)S(1)}, bf16[1000,128]{1,0:T(8,128)(2,1)S(1)}, u32[]{:S(2)}, u32[]{:S(2)}) collective-permute-start(bf16[1000,128]{1,0:T(8,128)(2,1)S(1)} %get-tuple-element.56), channel_id=1, source_target_pairs={{0,720},{1,721},{2,722},{3,723},{4,724},{5,725},{6,726},{7,727},{8... | collective-permute-start | bytes 768008 | tf_op jit(solution)/shard_map/ppermute | solution.py:234

commit v6 on v5

--- a/solution.py
+++ b/solution.py
@@ -115,48 +115,54 @@
         put_sends(rows, sends, own_ref, send_refs)
 
 
-def early_kernel(weight_ref, own_ref, *refs):
+def gains(root_ref, last):
+    inv_root = root_ref[...]
+    if last:
+        return 0.9 * inv_root, 0.1
+    return inv_root * (0.9 * inv_root), 0.1 * inv_root
+
+
+def early_kernel(last, root_ref, start_ref, weight_ref, own_ref, *refs):
     received, sum_ref = refs[:EARLY], refs[EARLY]
     depth = own_ref.shape[1] + EARLY * SIDE
+    of_product, of_start = gains(root_ref, last)
     for at, size in chunks(own_ref.shape[0]):
         rows = pl.ds(at, size)
         sources = jnp.concatenate([own_ref[rows, :]] + [ref[rows, :] for ref in received], axis=1)
-        sum_ref[rows, :] = jnp.dot(
+        product = jnp.dot(
             sources, weight_ref[pl.ds(0, depth), :], preferred_element_type=jnp.float32
         )
-
-
-def new_labels(rows, root_ref, start_ref, weight_ref, sum_ref, received):
-    inv_root = root_ref[...]
+        start = start_ref[rows, :].astype(jnp.float32)
+        sum_ref[rows, :] = of_product * product + of_start * start
+
+
+def finished(last, rows, root_ref, weight_ref, sum_ref, received):
     depth = len(received) * SIDE
-    sources = jnp.concatenate([ref[rows, :] for ref in received], axis=1)
-    product = sum_ref[rows, :] + jnp.dot(
-        sources,
+    product = jnp.dot(
+        jnp.concatenate([ref[rows, :] for ref in received], axis=1),
         weight_ref[pl.ds(weight_ref.shape[0] - depth, depth), :],
         preferred_element_type=jnp.float32,
     )
-    labels = 0.9 * inv_root * product + 0.1 * start_ref[rows, :].astype(jnp.float32)
-    return inv_root, labels
-
-
-def step_kernel(send_ref, root_ref, start_ref, weight_ref, sum_ref, *refs):
+    return sum_ref[rows, :] + gains(root_ref, last)[0] * product
+
+
+def step_kernel(send_ref, root_ref, weight_ref, sum_ref, *refs):
     late = PERMUTES - EARLY
     received, next_ref, send_refs = refs[:late], refs[late], refs[late + 1 :]
     for at, size in chunks(next_ref.shape[0]):
         rows = pl.ds(at, size)
-        inv_root, labels = new_labels(rows, root_ref, start_ref, weight_ref, sum_ref, received)
-        next_ref[rows, :] = (inv_root * labels).astype(jnp.bfloat16)
+        scaled = finished(False, rows, root_ref, weight_ref, sum_ref, received)
+        next_ref[rows, :] = scaled.astype(jnp.bfloat16)
         put_sends(rows, send_ref, next_ref, send_refs)
 
 
-def last_kernel(root_ref, start_ref, weight_ref, sum_ref, *refs):
+def last_kernel(root_ref, weight_ref, sum_ref, *refs):
     late = PERMUTES - EARLY
     received, (out_ref, held, left) = refs[:late], refs[late:]
     copies = []
     for k, (at, size) in enumerate(chunks(held.shape[0])):
         rows = pl.ds(at, size)
-        _, labels = new_labels(rows, root_ref, start_ref, weight_ref, sum_ref, received)
-        held[rows, :] = labels
+        held[rows, :] = finished(True, rows, root_ref, weight_ref, sum_ref, received)
         copies.append(pltpu.make_async_copy(held.at[rows], out_ref.at[rows], left.at[k]))
         copies[-1].start()
     for copy in copies:
@@ -233,8 +239,8 @@
     for step in range(ITERS):
         received = [lax.ppermute(sends[k], ("group", "dom"), route[k]) for k in range(PERMUTES)]
         total = pl.pallas_call(
-            early_kernel,
-            in_specs=[VMEM] * (2 + EARLY),
+            functools.partial(early_kernel, step == ITERS - 1),
+            in_specs=[VMEM] * (4 + EARLY),
             out_specs=VMEM,
             out_shape=jax.ShapeDtypeStruct((classes, nodes), jnp.float32),
             compiler_params=PARAMS,
@@ -243,19 +249,19 @@
                 bytes_accessed=4_000_000,
                 transcendentals=0,
             ),
-        )(weight, own, *received[:EARLY])
+        )(inv_root, start, weight, own, *received[:EARLY])
         late = received[EARLY:]
         if step < ITERS - 1:
             own, *sends = pl.pallas_call(
                 step_kernel,
-                in_specs=[SMEM] + [VMEM] * (4 + len(late)),
+                in_specs=[SMEM] + [VMEM] * (3 + len(late)),
                 out_specs=[VMEM] * (1 + PERMUTES),
                 out_shape=[wide] + narrow,
                 compiler_params=PARAMS,
-            )(send_list, inv_root, start, weight, total, *late)
+            )(send_list, inv_root, weight, total, *late)
     labels = pl.pallas_call(
         last_kernel,
-        in_specs=[VMEM] * (4 + len(late)),
+        in_specs=[VMEM] * (3 + len(late)),
         out_specs=HBM,
         out_shape=jax.ShapeDtypeStruct((classes, nodes), jnp.float32),
         scratch_shapes=[
@@ -263,7 +269,7 @@
             pltpu.SemaphoreType.DMA((pieces,)),
         ],
         compiler_params=PARAMS,
-    )(inv_root, start, weight, total, *late)
+    )(inv_root, weight, total, *late)
     return labels.T
 
 

time: 82.5 us -> 82.3 us (level)
  the two profiles are of different devices: /device:TPU:95 before, /device:TPU:159 now
where the time goes in v6:
time: 82.3 us; the launch traced here: 81.9 us
  starting transfers between devices  55.2 us (67%)
  waiting for transfers between devices  13.2 us (16%)
  Pallas kernels  10.7 us (13%)
  local copies, waits for them, and re-layouts  1.82 us (2%)
  between operations  0.89 us (1%)
    ppermute x21, starting transfers between devices, on_device(): lax.ppermute(sends[k], ('group', 'dom'), route[k])  55.2 us
    ppermute x21, waiting for transfers between devices, on_device(): lax.ppermute(sends[k], ('group', 'dom'), route[k])  13.2 us
    pallas_call x3, Pallas kernels, on_device(): pl.pallas_call(functools.partial(early_kernel, step == ITERS - 1), in_spe...  2.95 us
    pallas_call x2, Pallas kernels, on_device(): pl.pallas_call(step_kernel, in_specs=[SMEM] + [VMEM] * (3 + len(late)), o...  2.9 us
    pallas_call x1, Pallas kernels, on_device(): pl.pallas_call(prepare_kernel, in_specs=[HBM] * 4, out_specs=[VMEM] * (3...  1.84 us
    unnamed x6, local copies, waits for them, and re-layouts  1.82 us
  transfers between devices with their start and end apart: 21, of which 6 were waited for; matrix products, arithmetic and copies ran while one was open for 0% of the time, Pallas kernels for 5%

profile of v6, /device:TPU:159, one launch (start us, length us, event | category | flops | bytes accessed | tf_op | source)
XLA Modules:
  0.0 81.9 jit_solution(806043813860691027)
XLA Ops:
  0.0 1.8 %shard_map.73 = (f32[1,384]{1,0:T(1,128)S(1)}, bf16[1000,384]{1,0:T(8,128)(2,1)S(1)}, bf16[1000,384]{1,0:T(8,128)(2,1)S(1)}, bf16[1000,128]{1,0:T(8,128)(2,1)S(1...) custom-call(s32[1,6]{1,0:T(1,128)} %send_ref.3, ...), custom_call_target="tpu_custom_call" | custom-call | tf_op jit(solution)/shard_map/pallas_call | solution.py:215
  1.8 3.9 %collective-permute-start = (bf16[1000,128]{1,0:T(8,128)(2,1)S(1)}, bf16[1000,128]{1,0:T(8,128)(2,1)S(1)}, u32[]{:S(2)}, u32[]{:S(2)}) collective-permute-start(bf16[1000,128]{1,0:T(8,128)(2,1)S(1)} %get-tuple-element.34), channel_id=1, source_target_pairs={{3,4},{4,3},{7,8},{8,7},{11,12},{12,11},{15,16},{16,15},{19,20},{2... | collective-permute-start | bytes 768008 | tf_op jit(solution)/shard_map/ppermute | solution.py:240
  5.8 0.0 collective-permute-start.1
  5.8 1.0 %collective-permute-start.2 = (bf16[1000,128]{1,0:T(8,128)(2,1)S(1)}, bf16[1000,128]{1,0:T(8,128)(2,1)S(1)}, u32[]{:S(2)}, u32[]{:S(2)}) collective-permute-start(bf16[1000,128]{1,0:T(8,128)(2,1)S(1)} %get-tuple-element.36), channel_id=1, source_target_pairs={{1,0},{2,1},{3,2},{51,3},{5,4},{6,5},{7,6},{55,7},{9,8},{10,9},{11... | collective-permute-start | bytes 768008 | tf_op jit(solution)/shard_map/ppermute | solution.py:240
  6.8 1.9 %collective-permute-start.3 = (bf16[1000,128]{1,0:T(8,128)(2,1)S(1)}, bf16[1000,128]{1,0:T(8,128)(2,1)S(1)}, u32[]{:S(2)}, u32[]{:S(2)}) collective-permute-start(bf16[1000,128]{1,0:T(8,128)(2,1)S(1)} %get-tuple-element.37), channel_id=1, source_target_pairs={{0,2},{2,0},{1,3},{3,1},{4,6},{6,4},{5,7},{7,5},{8,10},{10,8},{9,1... | collective-permute-start | bytes 768008 | tf_op jit(solution)/shard_map/ppermute | solution.py:240
  8.7 7.9 %collective-permute-start.4 = (bf16[1000,128]{1,0:T(8,128)(2,1)S(1)}, bf16[1000,128]{1,0:T(8,128)(2,1)S(1)}, u32[]{:S(2)}, u32[]{:S(2)}) collective-permute-start(bf16[1000,128]{1,0:T(8,128)(2,1)S(1)} %get-tuple-element.38), channel_id=1, source_target_pairs={{2,4},{4,2},{3,5},{5,3},{6,8},{8,6},{7,9},{9,7},{10,12},{12,10},{1... | collective-permute-start | bytes 768008 | tf_op jit(solution)/shard_map/ppermute | solution.py:240
  16.6 0.0 collective-permute-done.refs_0_
  16.6 5.0 %collective-permute-start.5 = (bf16[1000,128]{1,0:T(8,128)(2,1)S(1)}, bf16[1000,128]{1,0:T(8,128)(2,1)S(1)}, u32[]{:S(2)}, u32[]{:S(2)}) collective-permute-start(bf16[1000,128]{1,0:T(8,128)(2,1)S(1)} %get-tuple-element.39), channel_id=1, source_target_pairs={{0,48},{1,49},{2,50},{3,51},{4,52},{5,53},{6,54},{7,55},{8,56},{9,... | collective-permute-start | bytes 768008 | tf_op jit(solution)/shard_map/ppermute | solution.py:240
  21.6 0.0 collective-permute-done.1.refs_1_
  21.6 0.0 collective-permute-start.6
  22.2 0.0 copy-start
  22.2 1.1 %copy-done = bf16[3,8,128,128]{3,2,1,0:T(8,128)(2,1)S(1)} copy-done((bf16[3,8,128,128]{3,2,1,0:T(8,128)(2,1)S(1)}, bf16[3,8,128,128]{3,2,1,0:T(8,128)(2,1)}, u32[]{:S(2)}) %copy-start) | copy-done | bytes 786456
  23.3 0.7 copy-done.2
  24.0 1.5 %shard_map.74.weight_ref = bf16[1280,384]{1,0:T(8,128)(2,1)S(1)} custom-call(s32[3,8]{1,0:T(4,128)S(1)} %copy-done.2, s32[1]{0:T(128)S(6)} %copy.8.count_ref, bf16[3,8,128,128]{3,2,1,0:T(8,128)(2,1)S(1)} %copy-done), custom_call_target="tpu_custom_call" | custom-call | bytes 8000000 | tf_op jit(solution)/shard_map/pallas_call | solution.py:230
  25.6 0.0 collective-permute-done.2.refs_2_
  25.6 0.0 copy-start.1
  25.6 1.0 %shard_map.75.sum_ref = f32[1000,384]{1,0:T(8,128)S(1)} custom-call(f32[1,384]{1,0:T(1,128)S(1)} %get-tuple-element.31.root_ref, bf16[1000,384]{1,0:T(8,128)(2,1)S(1)} %get-tuple-element.32.start_ref, bf16[1280,384]{1,0:T(8,128)(2,1)S(1)} %shard_map.74.weight_ref, bf16[1000,384]{1,0:T(8,128)(2,1)S(1)} %get-tuple-element.33.own_ref, ...), custom_call_target="tpu_custom_call" | custom-call | flops 589824000 | bytes 4000000 | tf_op jit(solution)/shard_map/pallas_call | solution.py:241
  26.6 0.0 collective-permute-done.4.refs_1_
  26.6 0.0 collective-permute-done.5.refs_2_
  26.6 1.9 %collective-permute-done.6.refs_3_ = bf16[1000,128]{1,0:T(8,128)(2,1)S(1)} collective-permute-done((bf16[1000,128]{1,0:T(8,128)(2,1)S(1)}, bf16[1000,128]{1,0:T(8,128)(2,1)S(1)}, u32[]{:S(2)}, u32[]{:S(2)}) %collective-permute-start.6) | collective-permute-done | bytes 256032 | tf_op jit(solution)/shard_map/ppermute | solution.py:240
  28.5 1.5 %shard_map.76 = (bf16[1000,384]{1,0:T(8,128)(2,1)S(1)}, bf16[1000,128]{1,0:T(8,128)(2,1)S(1)}, bf16[1000,128]{1,0:T(8,128)(2,1)S(1)}, bf16[1000,128]{1,0:T(8,128...) custom-call(s32[1,6]{1,0:T(1,128)S(1)} %copy-done.1, ...), custom_call_target="tpu_custom_call" | custom-call | tf_op jit(solution)/shard_map/pallas_call | solution.py:255
  30.0 2.4 %collective-permute-start.7 = (bf16[1000,128]{1,0:T(8,128)(2,1)S(1)}, bf16[1000,128]{1,0:T(8,128)(2,1)S(1)}, u32[]{:S(2)}, u32[]{:S(2)}) collective-permute-start(bf16[1000,128]{1,0:T(8,128)(2,1)S(1)} %get-tuple-element.42), channel_id=1, source_target_pairs={{3,4},{4,3},{7,8},{8,7},{11,12},{12,11},{15,16},{16,15},{19,20},{2... | collective-permute-start | bytes 768008 | tf_op jit(solution)/shard_map/ppermute | solution.py:240
  32.4 0.0 collective-permute-start.8
  32.4 2.1 %collective-permute-start.9 = (bf16[1000,128]{1,0:T(8,128)(2,1)S(1)}, bf16[1000,128]{1,0:T(8,128)(2,1)S(1)}, u32[]{:S(2)}, u32[]{:S(2)}) collective-permute-start(bf16[1000,128]{1,0:T(8,128)(2,1)S(1)} %get-tuple-element.44), channel_id=1, source_target_pairs={{1,0},{2,1},{3,2},{51,3},{5,4},{6,5},{7,6},{55,7},{9,8},{10,9},{11... | collective-permute-start | bytes 768008 | tf_op jit(solution)/shard_map/ppermute | solution.py:240
  34.5 1.9 %collective-permute-start.10 = (bf16[1000,128]{1,0:T(8,128)(2,1)S(1)}, bf16[1000,128]{1,0:T(8,128)(2,1)S(1)}, u32[]{:S(2)}, u32[]{:S(2)}) collective-permute-start(bf16[1000,128]{1,0:T(8,128)(2,1)S(1)} %get-tuple-element.45), channel_id=1, source_target_pairs={{0,2},{2,0},{1,3},{3,1},{4,6},{6,4},{5,7},{7,5},{8,10},{10,8},{9,1... | collective-permute-start | bytes 768008 | tf_op jit(solution)/shard_map/ppermute | solution.py:240
  36.4 6.7 %collective-permute-start.11 = (bf16[1000,128]{1,0:T(8,128)(2,1)S(1)}, bf16[1000,128]{1,0:T(8,128)(2,1)S(1)}, u32[]{:S(2)}, u32[]{:S(2)}) collective-permute-start(bf16[1000,128]{1,0:T(8,128)(2,1)S(1)} %get-tuple-element.46), channel_id=1, source_target_pairs={{2,4},{4,2},{3,5},{5,3},{6,8},{8,6},{7,9},{9,7},{10,12},{12,10},{1... | collective-permute-start | bytes 768008 | tf_op jit(solution)/shard_map/ppermute | solution.py:240
  43.1 5.0 %collective-permute-start.12 = (bf16[1000,128]{1,0:T(8,128)(2,1)S(1)}, bf16[1000,128]{1,0:T(8,128)(2,1)S(1)}, u32[]{:S(2)}, u32[]{:S(2)}) collective-permute-start(bf16[1000,128]{1,0:T(8,128)(2,1)S(1)} %get-tuple-element.47), channel_id=1, source_target_pairs={{0,48},{1,49},{2,50},{3,51},{4,52},{5,53},{6,54},{7,55},{8,56},{9,... | collective-permute-start | bytes 768008 | tf_op jit(solution)/shard_map/ppermute | solution.py:240
  48.1 1.0 %collective-permute-start.13 = (bf16[1000,128]{1,0:T(8,128)(2,1)S(1)}, bf16[1000,128]{1,0:T(8,128)(2,1)S(1)}, u32[]{:S(2)}, u32[]{:S(2)}) collective-permute-start(bf16[1000,128]{1,0:T(8,128)(2,1)S(1)} %get-tuple-element.48), channel_id=1, source_target_pairs={{0,720},{1,721},{2,722},{3,723},{4,724},{5,725},{6,726},{7,727},{8... | collective-permute-start | bytes 768008 | tf_op jit(solution)/shard_map/ppermute | solution.py:240
  49.1 1.0 %shard_map.77.sum_ref = f32[1000,384]{1,0:T(8,128)S(1)} custom-call(f32[1,384]{1,0:T(1,128)S(1)} %get-tuple-element.31.root_ref, bf16[1000,384]{1,0:T(8,128)(2,1)S(1)} %get-tuple-element.32.start_ref, bf16[1280,384]{1,0:T(8,128)(2,1)S(1)} %shard_map.74.weight_ref, bf16[1000,384]{1,0:T(8,128)(2,1)S(1)} %get-tuple-element.41.own_ref, ...), custom_call_target="tpu_custom_call" | custom-call | flops 589824000 | bytes 4000000 | tf_op jit(solution)/shard_map/pallas_call | solution.py:241
  50.1 0.0 collective-permute-done.11.refs_1_
  50.1 1.2 %collective-permute-done.12.refs_2_ = bf16[1000,128]{1,0:T(8,128)(2,1)S(1)} collective-permute-done((bf16[1000,128]{1,0:T(8,128)(2,1)S(1)}, bf16[1000,128]{1,0:T(8,128)(2,1)S(1)}, u32[]{:S(2)}, u32[]{:S(2)}) %collective-permute-start.12) | collective-permute-done | bytes 256032 | tf_op jit(solution)/shard_map/ppermute | solution.py:240
  51.3 4.1 %collective-permute-done.13.refs_3_ = bf16[1000,128]{1,0:T(8,128)(2,1)S(1)} collective-permute-done((bf16[1000,128]{1,0:T(8,128)(2,1)S(1)}, bf16[1000,128]{1,0:T(8,128)(2,1)S(1)}, u32[]{:S(2)}, u32[]{:S(2)}) %collective-permute-start.13) | collective-permute-done | bytes 256032 | tf_op jit(solution)/shard_map/ppermute | solution.py:240
  55.5 1.5 %shard_map.78 = (bf16[1000,384]{1,0:T(8,128)(2,1)S(1)}, bf16[1000,128]{1,0:T(8,128)(2,1)S(1)}, bf16[1000,128]{1,0:T(8,128)(2,1)S(1)}, bf16[1000,128]{1,0:T(8,128...) custom-call(s32[1,6]{1,0:T(1,128)S(1)} %copy-done.1, ...), custom_call_target="tpu_custom_call" | custom-call | tf_op jit(solution)/shard_map/pallas_call | solution.py:255
  56.9 1.9 %collective-permute-start.14 = (bf16[1000,128]{1,0:T(8,128)(2,1)S(1)}, bf16[1000,128]{1,0:T(8,128)(2,1)S(1)}, u32[]{:S(2)}, u32[]{:S(2)}) collective-permute-start(bf16[1000,128]{1,0:T(8,128)(2,1)S(1)} %get-tuple-element.50), channel_id=1, source_target_pairs={{3,4},{4,3},{7,8},{8,7},{11,12},{12,11},{15,16},{16,15},{19,20},{2... | collective-permute-start | bytes 768008 | tf_op jit(solution)/shard_map/ppermute | solution.py:240
  58.8 0.0 collective-permute-start.15
  58.9 1.0 %collective-permute-start.16 = (bf16[1000,128]{1,0:T(8,128)(2,1)S(1)}, bf16[1000,128]{1,0:T(8,128)(2,1)S(1)}, u32[]{:S(2)}, u32[]{:S(2)}) collective-permute-start(bf16[1000,128]{1,0:T(8,128)(2,1)S(1)} %get-tuple-element.52), channel_id=1, source_target_pairs={{1,0},{2,1},{3,2},{51,3},{5,4},{6,5},{7,6},{55,7},{9,8},{10,9},{11... | collective-permute-start | bytes 768008 | tf_op jit(solution)/shard_map/ppermute | solution.py:240
  59.9 3.4 %collective-permute-start.17 = (bf16[1000,128]{1,0:T(8,128)(2,1)S(1)}, bf16[1000,128]{1,0:T(8,128)(2,1)S(1)}, u32[]{:S(2)}, u32[]{:S(2)}) collective-permute-start(bf16[1000,128]{1,0:T(8,128)(2,1)S(1)} %get-tuple-element.53), channel_id=1, source_target_pairs={{0,2},{2,0},{1,3},{3,1},{4,6},{6,4},{5,7},{7,5},{8,10},{10,8},{9,1... | collective-permute-start | bytes 768008 | tf_op jit(solution)/shard_map/ppermute | solution.py:240
  63.3 5.2 %collective-permute-start.18 = (bf16[1000,128]{1,0:T(8,128)(2,1)S(1)}, bf16[1000,128]{1,0:T(8,128)(2,1)S(1)}, u32[]{:S(2)}, u32[]{:S(2)}) collective-permute-start(bf16[1000,128]{1,0:T(8,128)(2,1)S(1)} %get-tuple-element.54), channel_id=1, source_target_pairs={{2,4},{4,2},{3,5},{5,3},{6,8},{8,6},{7,9},{9,7},{10,12},{12,10},{1... | collective-permute-start | bytes 768008 | tf_op jit(solution)/shard_map/ppermute | solution.py:240
  68.5 0.0 collective-permute-done.14.refs_0_
  68.5 5.0 %collective-permute-start.19 = (bf16[1000,128]{1,0:T(8,128)(2,1)S(1)}, bf16[1000,128]{1,0:T(8,128)(2,1)S(1)}, u32[]{:S(2)}, u32[]{:S(2)}) collective-permute-start(bf16[1000,128]{1,0:T(8,128)(2,1)S(1)} %get-tuple-element.55), channel_id=1, source_target_pairs={{0,48},{1,49},{2,50},{3,51},{4,52},{5,53},{6,54},{7,55},{8,56},{9,... | collective-permute-start | bytes 768008 | tf_op jit(solution)/shard_map/ppermute | solution.py:240
  73.5 0.0 collective-permute-done.15.refs_1_
  73.5 0.0 collective-permute-start.20
  73.5 1.0 %shard_map.79.sum_ref = f32[1000,384]{1,0:T(8,128)S(1)} custom-call(f32[1,384]{1,0:T(1,128)S(1)} %get-tuple-element.31.root_ref, bf16[1000,384]{1,0:T(8,128)(2,1)S(1)} %get-tuple-element.32.start_ref, bf16[1280,384]{1,0:T(8,128)(2,1)S(1)} %shard_map.74.weight_ref, bf16[1000,384]{1,0:T(8,128)(2,1)S(1)} %get-tuple-element.49.own_ref, ...), custom_call_target="tpu_custom_call" | custom-call | flops 589824000 | bytes 4000000 | tf_op jit(solution)/shard_map/pallas_call | solution.py:241
  74.5 1.8 %collective-permute-done.17.refs_0_ = bf16[1000,128]{1,0:T(8,128)(2,1)S(1)} collective-permute-done((bf16[1000,128]{1,0:T(8,128)(2,1)S(1)}, bf16[1000,128]{1,0:T(8,128)(2,1)S(1)}, u32[]{:S(2)}, u32[]{:S(2)}) %collective-permute-start.17) | collective-permute-done | bytes 256032 | tf_op jit(solution)/shard_map/ppermute | solution.py:240
  76.2 0.0 collective-permute-done.18.refs_1_
  76.2 0.5 collective-permute-done.19.refs_2_
  76.7 3.7 %collective-permute-done.20.refs_3_ = bf16[1000,128]{1,0:T(8,128)(2,1)S(1)} collective-permute-done((bf16[1000,128]{1,0:T(8,128)(2,1)S(1)}, bf16[1000,128]{1,0:T(8,128)(2,1)S(1)}, u32[]{:S(2)}, u32[]{:S(2)}) %collective-permute-start.20) | collective-permute-done | bytes 256032 | tf_op jit(solution)/shard_map/ppermute | solution.py:240
  80.4 1.5 %shard_map.80 = f32[1000,384]{1,0:T(8,128)} custom-call(f32[1,384]{1,0:T(1,128)S(1)} %get-tuple-element.31.root_ref, bf16[1280,384]{1,0:T(8,128)(2,1)S(1)} %shard_map.74.weight_ref, f32[1000,384]{1,0:T(8,128)S(1)} %shard_map.79.sum_ref, bf16[1000,128]{1,0:T(8,128)(2,1)S(1)} %collective-permute-done.17.refs_0_, ...), custom_call_target="tpu_custom_call" | custom-call | tf_op jit(solution)/shard_map/pallas_call | solution.py:262
  (8 shorter events, 0.0 us)
Async XLA Ops:
  1.8 14.7 %collective-permute-start = (bf16[1000,128]{1,0:T(8,128)(2,1)S(1)}, bf16[1000,128]{1,0:T(8,128)(2,1)S(1)}, u32[]{:S(2)}, u32[]{:S(2)}) collective-permute-start(bf16[1000,128]{1,0:T(8,128)(2,1)S(1)} %get-tuple-element.34), channel_id=1, source_target_pairs={{3,4},{4,3},{7,8},{8,7},{11,12},{12,11},{15,16},{16,15},{19,20},{2... | collective-permute-start | bytes 768008 | tf_op jit(solution)/shard_map/ppermute | solution.py:240
  5.8 15.8 %collective-permute-start.1 = (bf16[1000,128]{1,0:T(8,128)(2,1)S(1)}, bf16[1000,128]{1,0:T(8,128)(2,1)S(1)}, u32[]{:S(2)}, u32[]{:S(2)}) collective-permute-start(bf16[1000,128]{1,0:T(8,128)(2,1)S(1)} %get-tuple-element.35), channel_id=1, source_target_pairs={{0,1},{1,2},{2,3},{3,51},{4,5},{5,6},{6,7},{7,55},{8,9},{9,10},{10... | collective-permute-start | bytes 768008 | tf_op jit(solution)/shard_map/ppermute | solution.py:240
  5.8 19.8 %collective-permute-start.2 = (bf16[1000,128]{1,0:T(8,128)(2,1)S(1)}, bf16[1000,128]{1,0:T(8,128)(2,1)S(1)}, u32[]{:S(2)}, u32[]{:S(2)}) collective-permute-start(bf16[1000,128]{1,0:T(8,128)(2,1)S(1)} %get-tuple-element.36), channel_id=1, source_target_pairs={{1,0},{2,1},{3,2},{51,3},{5,4},{6,5},{7,6},{55,7},{9,8},{10,9},{11... | collective-permute-start | bytes 768008 | tf_op jit(solution)/shard_map/ppermute | solution.py:240
  6.8 19.8 %collective-permute-start.3 = (bf16[1000,128]{1,0:T(8,128)(2,1)S(1)}, bf16[1000,128]{1,0:T(8,128)(2,1)S(1)}, u32[]{:S(2)}, u32[]{:S(2)}) collective-permute-start(bf16[1000,128]{1,0:T(8,128)(2,1)S(1)} %get-tuple-element.37), channel_id=1, source_target_pairs={{0,2},{2,0},{1,3},{3,1},{4,6},{6,4},{5,7},{7,5},{8,10},{10,8},{9,1... | collective-permute-start | bytes 768008 | tf_op jit(solution)/shard_map/ppermute | solution.py:240
  8.7 17.9 %collective-permute-start.4 = (bf16[1000,128]{1,0:T(8,128)(2,1)S(1)}, bf16[1000,128]{1,0:T(8,128)(2,1)S(1)}, u32[]{:S(2)}, u32[]{:S(2)}) collective-permute-start(bf16[1000,128]{1,0:T(8,128)(2,1)S(1)} %get-tuple-element.38), channel_id=1, source_target_pairs={{2,4},{4,2},{3,5},{5,3},{6,8},{8,6},{7,9},{9,7},{10,12},{12,10},{1... | collective-permute-start | bytes 768008 | tf_op jit(solution)/shard_map/ppermute | solution.py:240
  16.6 10.0 %collective-permute-start.5 = (bf16[1000,128]{1,0:T(8,128)(2,1)S(1)}, bf16[1000,128]{1,0:T(8,128)(2,1)S(1)}, u32[]{:S(2)}, u32[]{:S(2)}) collective-permute-start(bf16[1000,128]{1,0:T(8,128)(2,1)S(1)} %get-tuple-element.39), channel_id=1, source_target_pairs={{0,48},{1,49},{2,50},{3,51},{4,52},{5,53},{6,54},{7,55},{8,56},{9,... | collective-permute-start | bytes 768008 | tf_op jit(solution)/shard_map/ppermute | solution.py:240
  21.6 6.9 %collective-permute-start.6 = (bf16[1000,128]{1,0:T(8,128)(2,1)S(1)}, bf16[1000,128]{1,0:T(8,128)(2,1)S(1)}, u32[]{:S(2)}, u32[]{:S(2)}) collective-permute-start(bf16[1000,128]{1,0:T(8,128)(2,1)S(1)} %get-tuple-element.40), channel_id=1, source_target_pairs={{0,720},{1,721},{2,722},{3,723},{4,724},{5,725},{6,726},{7,727},{8... | collective-permute-start | bytes 768008 | tf_op jit(solution)/shard_map/ppermute | solution.py:240
  22.2 1.1 %copy-start = (bf16[3,8,128,128]{3,2,1,0:T(8,128)(2,1)S(1)}, bf16[3,8,128,128]{3,2,1,0:T(8,128)(2,1)}, u32[]{:S(2)}) copy-start(bf16[3,8,128,128]{3,2,1,0:T(8,128)(2,1)} %tiles_ref.1) | copy-start | bytes 2359300
  23.3 0.7 copy-start.2
  25.6 2.9 %copy-start.1 = (s32[1,6]{1,0:T(1,128)S(1)}, s32[1,6]{1,0:T(1,128)}, u32[]{:S(2)}) copy-start(s32[1,6]{1,0:T(1,128)} %send_ref.3) | copy-start | bytes 76
  30.0 13.1 %collective-permute-start.7 = (bf16[1000,128]{1,0:T(8,128)(2,1)S(1)}, bf16[1000,128]{1,0:T(8,128)(2,1)S(1)}, u32[]{:S(2)}, u32[]{:S(2)}) collective-permute-start(bf16[1000,128]{1,0:T(8,128)(2,1)S(1)} %get-tuple-element.42), channel_id=1, source_target_pairs={{3,4},{4,3},{7,8},{8,7},{11,12},{12,11},{15,16},{16,15},{19,20},{2... | collective-permute-start | bytes 768008 | tf_op jit(solution)/shard_map/ppermute | solution.py:240
  32.4 15.7 %collective-permute-start.8 = (bf16[1000,128]{1,0:T(8,128)(2,1)S(1)}, bf16[1000,128]{1,0:T(8,128)(2,1)S(1)}, u32[]{:S(2)}, u32[]{:S(2)}) collective-permute-start(bf16[1000,128]{1,0:T(8,128)(2,1)S(1)} %get-tuple-element.43), channel_id=1, source_target_pairs={{0,1},{1,2},{2,3},{3,51},{4,5},{5,6},{6,7},{7,55},{8,9},{9,10},{10... | collective-permute-start | bytes 768008 | tf_op jit(solution)/shard_map/ppermute | solution.py:240
  32.4 16.7 %collective-permute-start.9 = (bf16[1000,128]{1,0:T(8,128)(2,1)S(1)}, bf16[1000,128]{1,0:T(8,128)(2,1)S(1)}, u32[]{:S(2)}, u32[]{:S(2)}) collective-permute-start(bf16[1000,128]{1,0:T(8,128)(2,1)S(1)} %get-tuple-element.44), channel_id=1, source_target_pairs={{1,0},{2,1},{3,2},{51,3},{5,4},{6,5},{7,6},{55,7},{9,8},{10,9},{11... | collective-permute-start | bytes 768008 | tf_op jit(solution)/shard_map/ppermute | solution.py:240
  34.5 15.6 %collective-permute-start.10 = (bf16[1000,128]{1,0:T(8,128)(2,1)S(1)}, bf16[1000,128]{1,0:T(8,128)(2,1)S(1)}, u32[]{:S(2)}, u32[]{:S(2)}) collective-permute-start(bf16[1000,128]{1,0:T(8,128)(2,1)S(1)} %get-tuple-element.45), channel_id=1, source_target_pairs={{0,2},{2,0},{1,3},{3,1},{4,6},{6,4},{5,7},{7,5},{8,10},{10,8},{9,1... | collective-permute-start | bytes 768008 | tf_op jit(solution)/shard_map/ppermute | solution.py:240
  36.4 13.7 %collective-permute-start.11 = (bf16[1000,128]{1,0:T(8,128)(2,1)S(1)}, bf16[1000,128]{1,0:T(8,128)(2,1)S(1)}, u32[]{:S(2)}, u32[]{:S(2)}) collective-permute-start(bf16[1000,128]{1,0:T(8,128)(2,1)S(1)} %get-tuple-element.46), channel_id=1, source_target_pairs={{2,4},{4,2},{3,5},{5,3},{6,8},{8,6},{7,9},{9,7},{10,12},{12,10},{1... | collective-permute-start | bytes 768008 | tf_op jit(solution)/shard_map/ppermute | solution.py:240
  43.1 8.2 %collective-permute-start.12 = (bf16[1000,128]{1,0:T(8,128)(2,1)S(1)}, bf16[1000,128]{1,0:T(8,128)(2,1)S(1)}, u32[]{:S(2)}, u32[]{:S(2)}) collective-permute-start(bf16[1000,128]{1,0:T(8,128)(2,1)S(1)} %get-tuple-element.47), channel_id=1, source_target_pairs={{0,48},{1,49},{2,50},{3,51},{4,52},{5,53},{6,54},{7,55},{8,56},{9,... | collective-permute-start | bytes 768008 | tf_op jit(solution)/shard_map/ppermute | solution.py:240
  48.1 7.4 %collective-permute-start.13 = (bf16[1000,128]{1,0:T(8,128)(2,1)S(1)}, bf16[1000,128]{1,0:T(8,128)(2,1)S(1)}, u32[]{:S(2)}, u32[]{:S(2)}) collective-permute-start(bf16[1000,128]{1,0:T(8,128)(2,1)S(1)} %get-tuple-element.48), channel_id=1, source_target_pairs={{0,720},{1,721},{2,722},{3,723},{4,724},{5,725},{6,726},{7,727},{8... | collective-permute-start | bytes 768008 | tf_op jit(solution)/shard_map/ppermute | solution.py:240
  56.9 11.6 %collective-permute-start.14 = (bf16[1000,128]{1,0:T(8,128)(2,1)S(1)}, bf16[1000,128]{1,0:T(8,128)(2,1)S(1)}, u32[]{:S(2)}, u32[]{:S(2)}) collective-permute-start(bf16[1000,128]{1,0:T(8,128)(2,1)S(1)} %get-tuple-element.50), channel_id=1, source_target_pairs={{3,4},{4,3},{7,8},{8,7},{11,12},{12,11},{15,16},{16,15},{19,20},{2... | collective-permute-start | bytes 768008 | tf_op jit(solution)/shard_map/ppermute | solution.py:240
  58.8 14.6 %collective-permute-start.15 = (bf16[1000,128]{1,0:T(8,128)(2,1)S(1)}, bf16[1000,128]{1,0:T(8,128)(2,1)S(1)}, u32[]{:S(2)}, u32[]{:S(2)}) collective-permute-start(bf16[1000,128]{1,0:T(8,128)(2,1)S(1)} %get-tuple-element.51), channel_id=1, source_target_pairs={{0,1},{1,2},{2,3},{3,51},{4,5},{5,6},{6,7},{7,55},{8,9},{9,10},{10... | collective-permute-start | bytes 768008 | tf_op jit(solution)/shard_map/ppermute | solution.py:240
  58.9 14.6 %collective-permute-start.16 = (bf16[1000,128]{1,0:T(8,128)(2,1)S(1)}, bf16[1000,128]{1,0:T(8,128)(2,1)S(1)}, u32[]{:S(2)}, u32[]{:S(2)}) collective-permute-start(bf16[1000,128]{1,0:T(8,128)(2,1)S(1)} %get-tuple-element.52), channel_id=1, source_target_pairs={{1,0},{2,1},{3,2},{51,3},{5,4},{6,5},{7,6},{55,7},{9,8},{10,9},{11... | collective-permute-start | bytes 768008 | tf_op jit(solution)/shard_map/ppermute | solution.py:240
  59.9 16.4 %collective-permute-start.17 = (bf16[1000,128]{1,0:T(8,128)(2,1)S(1)}, bf16[1000,128]{1,0:T(8,128)(2,1)S(1)}, u32[]{:S(2)}, u32[]{:S(2)}) collective-permute-start(bf16[1000,128]{1,0:T(8,128)(2,1)S(1)} %get-tuple-element.53), channel_id=1, source_target_pairs={{0,2},{2,0},{1,3},{3,1},{4,6},{6,4},{5,7},{7,5},{8,10},{10,8},{9,1... | collective-permute-start | bytes 768008 | tf_op jit(solution)/shard_map/ppermute | solution.py:240
  63.3 13.0 %collective-permute-start.18 = (bf16[1000,128]{1,0:T(8,128)(2,1)S(1)}, bf16[1000,128]{1,0:T(8,128)(2,1)S(1)}, u32[]{:S(2)}, u32[]{:S(2)}) collective-permute-start(bf16[1000,128]{1,0:T(8,128)(2,1)S(1)} %get-tuple-element.54), channel_id=1, source_target_pairs={{2,4},{4,2},{3,5},{5,3},{6,8},{8,6},{7,9},{9,7},{10,12},{12,10},{1... | collective-permute-start | bytes 768008 | tf_op jit(solution)/shard_map/ppermute | solution.py:240
  68.5 8.2 %collective-permute-start.19 = (bf16[1000,128]{1,0:T(8,128)(2,1)S(1)}, bf16[1000,128]{1,0:T(8,128)(2,1)S(1)}, u32[]{:S(2)}, u32[]{:S(2)}) collective-permute-start(bf16[1000,128]{1,0:T(8,128)(2,1)S(1)} %get-tuple-element.55), channel_id=1, source_target_pairs={{0,48},{1,49},{2,50},{3,51},{4,52},{5,53},{6,54},{7,55},{8,56},{9,... | collective-permute-start | bytes 768008 | tf_op jit(solution)/shard_map/ppermute | solution.py:240
  73.5 6.9 %collective-permute-start.20 = (bf16[1000,128]{1,0:T(8,128)(2,1)S(1)}, bf16[1000,128]{1,0:T(8,128)(2,1)S(1)}, u32[]{:S(2)}, u32[]{:S(2)}) collective-permute-start(bf16[1000,128]{1,0:T(8,128)(2,1)S(1)} %get-tuple-element.56), channel_id=1, source_target_pairs={{0,720},{1,721},{2,722},{3,723},{4,724},{5,725},{6,726},{7,727},{8... | collective-permute-start | bytes 768008 | tf_op jit(solution)/shard_map/ppermute | solution.py:240

commit v7 on v6

--- a/solution.py
+++ b/solution.py
@@ -17,7 +17,7 @@
 HBM = pl.BlockSpec(memory_space=pltpu.HBM)
 PARAMS = pltpu.CompilerParams(vmem_limit_bytes=40 * 1024 * 1024)
 
-EDGE, RING, BACK, TWO, CROSS, UP, DOWN = range(7)
+RING, EDGE, BACK, TWO, CROSS, UP, DOWN = range(7)
 PERMUTES = 7
 EARLY = 3
 
@@ -85,32 +85,34 @@
         send_refs[k][rows, :] = own_ref[rows, block]
 
 
-def prepare_kernel(send_any, seeds_any, degree_any, prior_any, root_ref, start_ref, own_ref, *refs):
-    send_refs, (sends, seeds_held, degree_held, held, small, arrived) = refs[:PERMUTES], refs[PERMUTES:]
+def start_of(rows, at, classes, seeds, prior_ref):
+    soft = prior_ref[rows, :].astype(jnp.float32)
+    label = lax.broadcasted_iota(jnp.int32, soft.shape, 0) + at
+    return jnp.where(seeds < classes, jnp.where(label == seeds, 1.0, 0.0), soft)
+
+
+def prepare_kernel(
+    send_any, seeds_any, degree_any, prior_any, root_ref, seeds_ref, prior_ref, own_ref, *refs
+):
+    send_refs, (sends, seeds_held, degree_held, arrived) = refs[:PERMUTES], refs[PERMUTES:]
     classes = prior_any.shape[0]
-    firsts = [
-        pltpu.make_async_copy(seeds_any, seeds_held, small.at[0]),
-        pltpu.make_async_copy(degree_any, degree_held, small.at[1]),
-        pltpu.make_async_copy(send_any, sends, small.at[2]),
+    copies = [
+        pltpu.make_async_copy(prior_any, prior_ref, arrived.at[0]),
+        pltpu.make_async_copy(seeds_any, seeds_held, arrived.at[1]),
+        pltpu.make_async_copy(degree_any, degree_held, arrived.at[2]),
+        pltpu.make_async_copy(send_any, sends, arrived.at[3]),
     ]
-    copies = []
-    for k, (at, size) in enumerate(chunks(classes)):
-        rows = pl.ds(at, size)
-        copies.append(pltpu.make_async_copy(prior_any.at[rows], held.at[rows], arrived.at[k]))
-    for copy in firsts + copies:
+    for copy in copies:
         copy.start()
-    for copy in firsts:
+    for copy in copies:
         copy.wait()
     inv_root = 1.0 / jnp.sqrt(degree_held[...].astype(jnp.float32)[None, :])
     seeds = seeds_held[...][None, :]
     root_ref[...] = inv_root
-    for k, (at, size) in enumerate(chunks(classes)):
-        rows = pl.ds(at, size)
-        copies[k].wait()
-        label = lax.broadcasted_iota(jnp.int32, (size, seeds.shape[1]), 0) + at
-        onehot = jnp.where(label == seeds, 1.0, 0.0)
-        start = jnp.where(seeds < classes, onehot, held[rows, :].astype(jnp.float32))
-        start_ref[rows, :] = start.astype(jnp.bfloat16)
+    seeds_ref[...] = seeds
+    for at, size in chunks(classes):
+        rows = pl.ds(at, size)
+        start = start_of(rows, at, classes, seeds, prior_ref)
         own_ref[rows, :] = (inv_root * start).astype(jnp.bfloat16)
         put_sends(rows, sends, own_ref, send_refs)
 
@@ -122,7 +124,7 @@
     return inv_root * (0.9 * inv_root), 0.1 * inv_root
 
 
-def early_kernel(last, root_ref, start_ref, weight_ref, own_ref, *refs):
+def early_kernel(last, root_ref, seeds_ref, prior_ref, weight_ref, own_ref, *refs):
     received, sum_ref = refs[:EARLY], refs[EARLY]
     depth = own_ref.shape[1] + EARLY * SIDE
     of_product, of_start = gains(root_ref, last)
@@ -132,7 +134,7 @@
         product = jnp.dot(
             sources, weight_ref[pl.ds(0, depth), :], preferred_element_type=jnp.float32
         )
-        start = start_ref[rows, :].astype(jnp.float32)
+        start = start_of(rows, at, prior_ref.shape[0], seeds_ref[...], prior_ref)
         sum_ref[rows, :] = of_product * product + of_start * start
 
 
@@ -212,18 +214,22 @@
     wide = jax.ShapeDtypeStruct((classes, nodes), jnp.bfloat16)
     narrow = [jax.ShapeDtypeStruct((classes, side), jnp.bfloat16)] * PERMUTES
 
-    inv_root, start, own, *sends = pl.pallas_call(
+    inv_root, seeds, soft, own, *sends = pl.pallas_call(
         prepare_kernel,
         in_specs=[HBM] * 4,
-        out_specs=[VMEM] * (3 + PERMUTES),
-        out_shape=[jax.ShapeDtypeStruct((1, nodes), jnp.float32), wide, wide] + narrow,
+        out_specs=[VMEM] * (4 + PERMUTES),
+        out_shape=[
+            jax.ShapeDtypeStruct((1, nodes), jnp.float32),
+            jax.ShapeDtypeStruct((1, nodes), jnp.int32),
+            wide,
+            wide,
+        ]
+        + narrow,
         scratch_shapes=[
             pltpu.SMEM(send_list.shape, jnp.int32),
             pltpu.VMEM((nodes,), jnp.int32),
             pltpu.VMEM((nodes,), jnp.int32),
-            pltpu.VMEM((classes, nodes), jnp.bfloat16),
-            pltpu.SemaphoreType.DMA((3,)),
-            pltpu.SemaphoreType.DMA((pieces,)),
+            pltpu.SemaphoreType.DMA((4,)),
         ],
         compiler_params=PARAMS,
     )(*[in_hbm(x) for x in (send_list, seed_labels, degree, prior.T)])
@@ -240,7 +246,7 @@
         received = [lax.ppermute(sends[k], ("group", "dom"), route[k]) for k in range(PERMUTES)]
         total = pl.pallas_call(
             functools.partial(early_kernel, step == ITERS - 1),
-            in_specs=[VMEM] * (4 + EARLY),
+            in_specs=[VMEM] * (5 + EARLY),
             out_specs=VMEM,
             out_shape=jax.ShapeDtypeStruct((classes, nodes), jnp.float32),
             compiler_params=PARAMS,
@@ -249,7 +255,7 @@
                 bytes_accessed=4_000_000,
                 transcendentals=0,
             ),
-        )(inv_root, start, weight, own, *received[:EARLY])
+        )(inv_root, seeds, soft, weight, own, *received[:EARLY])
         late = received[EARLY:]
         if step < ITERS - 1:
             own, *sends = pl.pallas_call(

time: 82.3 us -> 81.3 us (0.988)
  the two profiles are of different devices: /device:TPU:159 before, /device:TPU:512 now
where the time goes in v7:
time: 81.3 us; the launch traced here: 80.9 us
  starting transfers between devices  41.9 us (52%)
  waiting for transfers between devices  25.2 us (31%)
  Pallas kernels  11.1 us (14%)
  local copies, waits for them, and re-layouts  1.82 us (2%)
  between operations  0.89 us (1%)
    ppermute x21, starting transfers between devices, on_device(): lax.ppermute(sends[k], ('group', 'dom'), route[k])  41.9 us
    ppermute x21, waiting for transfers between devices, on_device(): lax.ppermute(sends[k], ('group', 'dom'), route[k])  25.2 us
    pallas_call x3, Pallas kernels, on_device(): pl.pallas_call(functools.partial(early_kernel, step == ITERS - 1), in_spe...  3.11 us
    pallas_call x2, Pallas kernels, on_device(): pl.pallas_call(step_kernel, in_specs=[SMEM] + [VMEM] * (3 + len(late)), o...  2.91 us
    pallas_call x1, Pallas kernels, on_device(): pl.pallas_call(prepare_kernel, in_specs=[HBM] * 4, out_specs=[VMEM] * (4...  2.06 us
    unnamed x6, local copies, waits for them, and re-layouts  1.82 us
  transfers between devices with their start and end apart: 21, of which 6 were waited for; matrix products, arithmetic and copies ran while one was open for 0% of the time, Pallas kernels for 6%

profile of v7, /device:TPU:512, one launch (start us, length us, event | category | flops | bytes accessed | tf_op | source)
XLA Modules:
  0.0 80.9 jit_solution(9733650486163125256)
XLA Ops:
  0.0 2.1 %shard_map.73 = (f32[1,384]{1,0:T(1,128)S(1)}, s32[1,384]{1,0:T(1,128)S(1)}, bf16[1000,384]{1,0:T(8,128)(2,1)S(1)}, bf16[1000,384]{1,0:T(8,128)(2,1)S(1)}, bf16[...) custom-call(s32[1,6]{1,0:T(1,128)} %send_ref.3, ...), custom_call_target="tpu_custom_call" | custom-call | tf_op jit(solution)/shard_map/pallas_call | solution.py:217
  2.1 1.5 %collective-permute-start = (bf16[1000,128]{1,0:T(8,128)(2,1)S(1)}, bf16[1000,128]{1,0:T(8,128)(2,1)S(1)}, u32[]{:S(2)}, u32[]{:S(2)}) collective-permute-start(bf16[1000,128]{1,0:T(8,128)(2,1)S(1)} %get-tuple-element.36), channel_id=1, source_target_pairs={{0,1},{1,2},{2,3},{3,51},{4,5},{5,6},{6,7},{7,55},{8,9},{9,10},{10... | collective-permute-start | bytes 768008 | tf_op jit(solution)/shard_map/ppermute | solution.py:246
  3.6 4.4 %collective-permute-start.1 = (bf16[1000,128]{1,0:T(8,128)(2,1)S(1)}, bf16[1000,128]{1,0:T(8,128)(2,1)S(1)}, u32[]{:S(2)}, u32[]{:S(2)}) collective-permute-start(bf16[1000,128]{1,0:T(8,128)(2,1)S(1)} %get-tuple-element.37), channel_id=1, source_target_pairs={{3,4},{4,3},{7,8},{8,7},{11,12},{12,11},{15,16},{16,15},{19,20},{2... | collective-permute-start | bytes 768008 | tf_op jit(solution)/shard_map/ppermute | solution.py:246
  8.0 0.1 collective-permute-start.2
  8.1 1.9 %collective-permute-start.3 = (bf16[1000,128]{1,0:T(8,128)(2,1)S(1)}, bf16[1000,128]{1,0:T(8,128)(2,1)S(1)}, u32[]{:S(2)}, u32[]{:S(2)}) collective-permute-start(bf16[1000,128]{1,0:T(8,128)(2,1)S(1)} %get-tuple-element.39), channel_id=1, source_target_pairs={{0,2},{2,0},{1,3},{3,1},{4,6},{6,4},{5,7},{7,5},{8,10},{10,8},{9,1... | collective-permute-start | bytes 768008 | tf_op jit(solution)/shard_map/ppermute | solution.py:246
  10.0 4.8 %collective-permute-start.4 = (bf16[1000,128]{1,0:T(8,128)(2,1)S(1)}, bf16[1000,128]{1,0:T(8,128)(2,1)S(1)}, u32[]{:S(2)}, u32[]{:S(2)}) collective-permute-start(bf16[1000,128]{1,0:T(8,128)(2,1)S(1)} %get-tuple-element.40), channel_id=1, source_target_pairs={{2,4},{4,2},{3,5},{5,3},{6,8},{8,6},{7,9},{9,7},{10,12},{12,10},{1... | collective-permute-start | bytes 768008 | tf_op jit(solution)/shard_map/ppermute | solution.py:246
  14.8 0.0 collective-permute-done.refs_0_
  14.8 0.0 collective-permute-start.5
  14.8 2.5 %collective-permute-done.1.refs_1_ = bf16[1000,128]{1,0:T(8,128)(2,1)S(1)} collective-permute-done((bf16[1000,128]{1,0:T(8,128)(2,1)S(1)}, bf16[1000,128]{1,0:T(8,128)(2,1)S(1)}, u32[]{:S(2)}, u32[]{:S(2)}) %collective-permute-start.1) | collective-permute-done | bytes 256032 | tf_op jit(solution)/shard_map/ppermute | solution.py:246
  17.3 0.5 collective-permute-start.6
  18.4 0.0 copy-start
  18.4 1.1 %copy-done = bf16[3,8,128,128]{3,2,1,0:T(8,128)(2,1)S(1)} copy-done((bf16[3,8,128,128]{3,2,1,0:T(8,128)(2,1)S(1)}, bf16[3,8,128,128]{3,2,1,0:T(8,128)(2,1)}, u32[]{:S(2)}) %copy-start) | copy-done | bytes 786456
  19.6 0.7 copy-done.2
  20.2 1.5 %shard_map.74.weight_ref = bf16[1280,384]{1,0:T(8,128)(2,1)S(1)} custom-call(s32[3,8]{1,0:T(4,128)S(1)} %copy-done.2, s32[1]{0:T(128)S(6)} %copy.8.count_ref, bf16[3,8,128,128]{3,2,1,0:T(8,128)(2,1)S(1)} %copy-done), custom_call_target="tpu_custom_call" | custom-call | bytes 8000000 | tf_op jit(solution)/shard_map/pallas_call | solution.py:236
  21.8 0.0 collective-permute-done.2.refs_2_
  21.8 0.0 copy-start.1
  21.8 1.0 %shard_map.75.sum_ref = f32[1000,384]{1,0:T(8,128)S(1)} custom-call(f32[1,384]{1,0:T(1,128)S(1)} %get-tuple-element.32.root_ref, s32[1,384]{1,0:T(1,128)S(1)} %get-tuple-element.33.seeds_ref, bf16[1000,384]{1,0:T(8,128)(2,1)S(1)} %get-tuple-element.34.prior_ref, bf16[1280,384]{1,0:T(8,128)(2,1)S(1)} %shard_map.74.weight_ref, ...), custom_call_target="tpu_custom_call" | custom-call | flops 589824000 | bytes 4000000 | tf_op jit(solution)/shard_map/pallas_call | solution.py:247
  22.8 4.0 %collective-permute-done.3.refs_0_ = bf16[1000,128]{1,0:T(8,128)(2,1)S(1)} collective-permute-done((bf16[1000,128]{1,0:T(8,128)(2,1)S(1)}, bf16[1000,128]{1,0:T(8,128)(2,1)S(1)}, u32[]{:S(2)}, u32[]{:S(2)}) %collective-permute-start.3) | collective-permute-done | bytes 256032 | tf_op jit(solution)/shard_map/ppermute | solution.py:246
  26.8 0.0 collective-permute-done.4.refs_1_
  26.9 1.5 %shard_map.76 = (bf16[1000,384]{1,0:T(8,128)(2,1)S(1)}, bf16[1000,128]{1,0:T(8,128)(2,1)S(1)}, bf16[1000,128]{1,0:T(8,128)(2,1)S(1)}, bf16[1000,128]{1,0:T(8,128...) custom-call(s32[1,6]{1,0:T(1,128)S(1)} %copy-done.1, ...), custom_call_target="tpu_custom_call" | custom-call | tf_op jit(solution)/shard_map/pallas_call | solution.py:261
  28.3 0.0 collective-permute-start.7
  28.4 5.7 %collective-permute-start.8 = (bf16[1000,128]{1,0:T(8,128)(2,1)S(1)}, bf16[1000,128]{1,0:T(8,128)(2,1)S(1)}, u32[]{:S(2)}, u32[]{:S(2)}) collective-permute-start(bf16[1000,128]{1,0:T(8,128)(2,1)S(1)} %get-tuple-element.45), channel_id=1, source_target_pairs={{3,4},{4,3},{7,8},{8,7},{11,12},{12,11},{15,16},{16,15},{19,20},{2... | collective-permute-start | bytes 768008 | tf_op jit(solution)/shard_map/ppermute | solution.py:246
  34.1 0.0 collective-permute-start.9
  34.1 1.9 %collective-permute-start.10 = (bf16[1000,128]{1,0:T(8,128)(2,1)S(1)}, bf16[1000,128]{1,0:T(8,128)(2,1)S(1)}, u32[]{:S(2)}, u32[]{:S(2)}) collective-permute-start(bf16[1000,128]{1,0:T(8,128)(2,1)S(1)} %get-tuple-element.47), channel_id=1, source_target_pairs={{0,2},{2,0},{1,3},{3,1},{4,6},{6,4},{5,7},{7,5},{8,10},{10,8},{9,1... | collective-permute-start | bytes 768008 | tf_op jit(solution)/shard_map/ppermute | solution.py:246
  36.1 3.6 %collective-permute-start.11 = (bf16[1000,128]{1,0:T(8,128)(2,1)S(1)}, bf16[1000,128]{1,0:T(8,128)(2,1)S(1)}, u32[]{:S(2)}, u32[]{:S(2)}) collective-permute-start(bf16[1000,128]{1,0:T(8,128)(2,1)S(1)} %get-tuple-element.48), channel_id=1, source_target_pairs={{2,4},{4,2},{3,5},{5,3},{6,8},{8,6},{7,9},{9,7},{10,12},{12,10},{1... | collective-permute-start | bytes 768008 | tf_op jit(solution)/shard_map/ppermute | solution.py:246
  39.7 0.0 collective-permute-done.7.refs_0_
  39.7 0.9 %collective-permute-start.12 = (bf16[1000,128]{1,0:T(8,128)(2,1)S(1)}, bf16[1000,128]{1,0:T(8,128)(2,1)S(1)}, u32[]{:S(2)}, u32[]{:S(2)}) collective-permute-start(bf16[1000,128]{1,0:T(8,128)(2,1)S(1)} %get-tuple-element.49), channel_id=1, source_target_pairs={{0,48},{1,49},{2,50},{3,51},{4,52},{5,53},{6,54},{7,55},{8,56},{9,... | collective-permute-start | bytes 768008 | tf_op jit(solution)/shard_map/ppermute | solution.py:246
  40.6 3.6 %collective-permute-done.8.refs_1_ = bf16[1000,128]{1,0:T(8,128)(2,1)S(1)} collective-permute-done((bf16[1000,128]{1,0:T(8,128)(2,1)S(1)}, bf16[1000,128]{1,0:T(8,128)(2,1)S(1)}, u32[]{:S(2)}, u32[]{:S(2)}) %collective-permute-start.8) | collective-permute-done | bytes 256032 | tf_op jit(solution)/shard_map/ppermute | solution.py:246
  44.2 2.1 %collective-permute-start.13 = (bf16[1000,128]{1,0:T(8,128)(2,1)S(1)}, bf16[1000,128]{1,0:T(8,128)(2,1)S(1)}, u32[]{:S(2)}, u32[]{:S(2)}) collective-permute-start(bf16[1000,128]{1,0:T(8,128)(2,1)S(1)} %get-tuple-element.50), channel_id=1, source_target_pairs={{0,720},{1,721},{2,722},{3,723},{4,724},{5,725},{6,726},{7,727},{8... | collective-permute-start | bytes 768008 | tf_op jit(solution)/shard_map/ppermute | solution.py:246
  46.2 1.0 %shard_map.77.sum_ref = f32[1000,384]{1,0:T(8,128)S(1)} custom-call(f32[1,384]{1,0:T(1,128)S(1)} %get-tuple-element.32.root_ref, s32[1,384]{1,0:T(1,128)S(1)} %get-tuple-element.33.seeds_ref, bf16[1000,384]{1,0:T(8,128)(2,1)S(1)} %get-tuple-element.34.prior_ref, bf16[1280,384]{1,0:T(8,128)(2,1)S(1)} %shard_map.74.weight_ref, ...), custom_call_target="tpu_custom_call" | custom-call | flops 589824000 | bytes 4000000 | tf_op jit(solution)/shard_map/pallas_call | solution.py:247
  47.3 5.8 %collective-permute-done.10.refs_0_ = bf16[1000,128]{1,0:T(8,128)(2,1)S(1)} collective-permute-done((bf16[1000,128]{1,0:T(8,128)(2,1)S(1)}, bf16[1000,128]{1,0:T(8,128)(2,1)S(1)}, u32[]{:S(2)}, u32[]{:S(2)}) %collective-permute-start.10) | collective-permute-done | bytes 256032 | tf_op jit(solution)/shard_map/ppermute | solution.py:246
  53.1 0.0 collective-permute-done.11.refs_1_
  53.1 0.0 collective-permute-done.12.refs_2_
  53.1 1.4 %shard_map.78 = (bf16[1000,384]{1,0:T(8,128)(2,1)S(1)}, bf16[1000,128]{1,0:T(8,128)(2,1)S(1)}, bf16[1000,128]{1,0:T(8,128)(2,1)S(1)}, bf16[1000,128]{1,0:T(8,128...) custom-call(s32[1,6]{1,0:T(1,128)S(1)} %copy-done.1, ...), custom_call_target="tpu_custom_call" | custom-call | tf_op jit(solution)/shard_map/pallas_call | solution.py:261
  54.6 0.0 collective-permute-start.14
  54.6 4.9 %collective-permute-start.15 = (bf16[1000,128]{1,0:T(8,128)(2,1)S(1)}, bf16[1000,128]{1,0:T(8,128)(2,1)S(1)}, u32[]{:S(2)}, u32[]{:S(2)}) collective-permute-start(bf16[1000,128]{1,0:T(8,128)(2,1)S(1)} %get-tuple-element.53), channel_id=1, source_target_pairs={{3,4},{4,3},{7,8},{8,7},{11,12},{12,11},{15,16},{16,15},{19,20},{2... | collective-permute-start | bytes 768008 | tf_op jit(solution)/shard_map/ppermute | solution.py:246
  59.5 0.0 collective-permute-start.16
  59.5 1.9 %collective-permute-start.17 = (bf16[1000,128]{1,0:T(8,128)(2,1)S(1)}, bf16[1000,128]{1,0:T(8,128)(2,1)S(1)}, u32[]{:S(2)}, u32[]{:S(2)}) collective-permute-start(bf16[1000,128]{1,0:T(8,128)(2,1)S(1)} %get-tuple-element.55), channel_id=1, source_target_pairs={{0,2},{2,0},{1,3},{3,1},{4,6},{6,4},{5,7},{7,5},{8,10},{10,8},{9,1... | collective-permute-start | bytes 768008 | tf_op jit(solution)/shard_map/ppermute | solution.py:246
  61.5 2.4 %collective-permute-start.18 = (bf16[1000,128]{1,0:T(8,128)(2,1)S(1)}, bf16[1000,128]{1,0:T(8,128)(2,1)S(1)}, u32[]{:S(2)}, u32[]{:S(2)}) collective-permute-start(bf16[1000,128]{1,0:T(8,128)(2,1)S(1)} %get-tuple-element.56), channel_id=1, source_target_pairs={{2,4},{4,2},{3,5},{5,3},{6,8},{8,6},{7,9},{9,7},{10,12},{12,10},{1... | collective-permute-start | bytes 768008 | tf_op jit(solution)/shard_map/ppermute | solution.py:246
  63.9 3.0 %collective-permute-start.19 = (bf16[1000,128]{1,0:T(8,128)(2,1)S(1)}, bf16[1000,128]{1,0:T(8,128)(2,1)S(1)}, u32[]{:S(2)}, u32[]{:S(2)}) collective-permute-start(bf16[1000,128]{1,0:T(8,128)(2,1)S(1)} %get-tuple-element.57), channel_id=1, source_target_pairs={{0,48},{1,49},{2,50},{3,51},{4,52},{5,53},{6,54},{7,55},{8,56},{9,... | collective-permute-start | bytes 768008 | tf_op jit(solution)/shard_map/ppermute | solution.py:246
  66.9 4.1 %collective-permute-done.15.refs_1_ = bf16[1000,128]{1,0:T(8,128)(2,1)S(1)} collective-permute-done((bf16[1000,128]{1,0:T(8,128)(2,1)S(1)}, bf16[1000,128]{1,0:T(8,128)(2,1)S(1)}, u32[]{:S(2)}, u32[]{:S(2)}) %collective-permute-start.15) | collective-permute-done | bytes 256032 | tf_op jit(solution)/shard_map/ppermute | solution.py:246
  71.0 2.2 %collective-permute-start.20 = (bf16[1000,128]{1,0:T(8,128)(2,1)S(1)}, bf16[1000,128]{1,0:T(8,128)(2,1)S(1)}, u32[]{:S(2)}, u32[]{:S(2)}) collective-permute-start(bf16[1000,128]{1,0:T(8,128)(2,1)S(1)} %get-tuple-element.58), channel_id=1, source_target_pairs={{0,720},{1,721},{2,722},{3,723},{4,724},{5,725},{6,726},{7,727},{8... | collective-permute-start | bytes 768008 | tf_op jit(solution)/shard_map/ppermute | solution.py:246
  73.2 0.0 collective-permute-done.16.refs_2_
  73.2 1.0 %shard_map.79.sum_ref = f32[1000,384]{1,0:T(8,128)S(1)} custom-call(f32[1,384]{1,0:T(1,128)S(1)} %get-tuple-element.32.root_ref, s32[1,384]{1,0:T(1,128)S(1)} %get-tuple-element.33.seeds_ref, bf16[1000,384]{1,0:T(8,128)(2,1)S(1)} %get-tuple-element.34.prior_ref, bf16[1280,384]{1,0:T(8,128)(2,1)S(1)} %shard_map.74.weight_ref, ...), custom_call_target="tpu_custom_call" | custom-call | flops 589824000 | bytes 4000000 | tf_op jit(solution)/shard_map/pallas_call | solution.py:247
  74.2 5.2 %collective-permute-done.17.refs_0_ = bf16[1000,128]{1,0:T(8,128)(2,1)S(1)} collective-permute-done((bf16[1000,128]{1,0:T(8,128)(2,1)S(1)}, bf16[1000,128]{1,0:T(8,128)(2,1)S(1)}, u32[]{:S(2)}, u32[]{:S(2)}) %collective-permute-start.17) | collective-permute-done | bytes 256032 | tf_op jit(solution)/shard_map/ppermute | solution.py:246
  79.4 0.0 collective-permute-done.18.refs_1_
  79.4 0.0 collective-permute-done.19.refs_2_
  79.4 1.5 %shard_map.80 = f32[1000,384]{1,0:T(8,128)} custom-call(f32[1,384]{1,0:T(1,128)S(1)} %get-tuple-element.32.root_ref, bf16[1280,384]{1,0:T(8,128)(2,1)S(1)} %shard_map.74.weight_ref, f32[1000,384]{1,0:T(8,128)S(1)} %shard_map.79.sum_ref, bf16[1000,128]{1,0:T(8,128)(2,1)S(1)} %collective-permute-done.17.refs_0_, ...), custom_call_target="tpu_custom_call" | custom-call | tf_op jit(solution)/shard_map/pallas_call | solution.py:268
  (8 shorter events, 0.0 us)
Async XLA Ops:
  2.1 12.7 %collective-permute-start = (bf16[1000,128]{1,0:T(8,128)(2,1)S(1)}, bf16[1000,128]{1,0:T(8,128)(2,1)S(1)}, u32[]{:S(2)}, u32[]{:S(2)}) collective-permute-start(bf16[1000,128]{1,0:T(8,128)(2,1)S(1)} %get-tuple-element.36), channel_id=1, source_target_pairs={{0,1},{1,2},{2,3},{3,51},{4,5},{5,6},{6,7},{7,55},{8,9},{9,10},{10... | collective-permute-start | bytes 768008 | tf_op jit(solution)/shard_map/ppermute | solution.py:246
  3.6 13.7 %collective-permute-start.1 = (bf16[1000,128]{1,0:T(8,128)(2,1)S(1)}, bf16[1000,128]{1,0:T(8,128)(2,1)S(1)}, u32[]{:S(2)}, u32[]{:S(2)}) collective-permute-start(bf16[1000,128]{1,0:T(8,128)(2,1)S(1)} %get-tuple-element.37), channel_id=1, source_target_pairs={{3,4},{4,3},{7,8},{8,7},{11,12},{12,11},{15,16},{16,15},{19,20},{2... | collective-permute-start | bytes 768008 | tf_op jit(solution)/shard_map/ppermute | solution.py:246
  8.0 13.8 %collective-permute-start.2 = (bf16[1000,128]{1,0:T(8,128)(2,1)S(1)}, bf16[1000,128]{1,0:T(8,128)(2,1)S(1)}, u32[]{:S(2)}, u32[]{:S(2)}) collective-permute-start(bf16[1000,128]{1,0:T(8,128)(2,1)S(1)} %get-tuple-element.38), channel_id=1, source_target_pairs={{1,0},{2,1},{3,2},{51,3},{5,4},{6,5},{7,6},{55,7},{9,8},{10,9},{11... | collective-permute-start | bytes 768008 | tf_op jit(solution)/shard_map/ppermute | solution.py:246
  8.1 18.8 %collective-permute-start.3 = (bf16[1000,128]{1,0:T(8,128)(2,1)S(1)}, bf16[1000,128]{1,0:T(8,128)(2,1)S(1)}, u32[]{:S(2)}, u32[]{:S(2)}) collective-permute-start(bf16[1000,128]{1,0:T(8,128)(2,1)S(1)} %get-tuple-element.39), channel_id=1, source_target_pairs={{0,2},{2,0},{1,3},{3,1},{4,6},{6,4},{5,7},{7,5},{8,10},{10,8},{9,1... | collective-permute-start | bytes 768008 | tf_op jit(solution)/shard_map/ppermute | solution.py:246
  10.0 16.9 %collective-permute-start.4 = (bf16[1000,128]{1,0:T(8,128)(2,1)S(1)}, bf16[1000,128]{1,0:T(8,128)(2,1)S(1)}, u32[]{:S(2)}, u32[]{:S(2)}) collective-permute-start(bf16[1000,128]{1,0:T(8,128)(2,1)S(1)} %get-tuple-element.40), channel_id=1, source_target_pairs={{2,4},{4,2},{3,5},{5,3},{6,8},{8,6},{7,9},{9,7},{10,12},{12,10},{1... | collective-permute-start | bytes 768008 | tf_op jit(solution)/shard_map/ppermute | solution.py:246
  14.8 12.0 %collective-permute-start.5 = (bf16[1000,128]{1,0:T(8,128)(2,1)S(1)}, bf16[1000,128]{1,0:T(8,128)(2,1)S(1)}, u32[]{:S(2)}, u32[]{:S(2)}) collective-permute-start(bf16[1000,128]{1,0:T(8,128)(2,1)S(1)} %get-tuple-element.41), channel_id=1, source_target_pairs={{0,48},{1,49},{2,50},{3,51},{4,52},{5,53},{6,54},{7,55},{8,56},{9,... | collective-permute-start | bytes 768008 | tf_op jit(solution)/shard_map/ppermute | solution.py:246
  17.3 9.6 %collective-permute-start.6 = (bf16[1000,128]{1,0:T(8,128)(2,1)S(1)}, bf16[1000,128]{1,0:T(8,128)(2,1)S(1)}, u32[]{:S(2)}, u32[]{:S(2)}) collective-permute-start(bf16[1000,128]{1,0:T(8,128)(2,1)S(1)} %get-tuple-element.42), channel_id=1, source_target_pairs={{0,720},{1,721},{2,722},{3,723},{4,724},{5,725},{6,726},{7,727},{8... | collective-permute-start | bytes 768008 | tf_op jit(solution)/shard_map/ppermute | solution.py:246
  18.4 1.1 %copy-start = (bf16[3,8,128,128]{3,2,1,0:T(8,128)(2,1)S(1)}, bf16[3,8,128,128]{3,2,1,0:T(8,128)(2,1)}, u32[]{:S(2)}) copy-start(bf16[3,8,128,128]{3,2,1,0:T(8,128)(2,1)} %tiles_ref.1) | copy-start | bytes 2359300
  19.6 0.7 copy-start.2
  21.8 5.1 %copy-start.1 = (s32[1,6]{1,0:T(1,128)S(1)}, s32[1,6]{1,0:T(1,128)}, u32[]{:S(2)}) copy-start(s32[1,6]{1,0:T(1,128)} %send_ref.3) | copy-start | bytes 76
  28.3 11.3 %collective-permute-start.7 = (bf16[1000,128]{1,0:T(8,128)(2,1)S(1)}, bf16[1000,128]{1,0:T(8,128)(2,1)S(1)}, u32[]{:S(2)}, u32[]{:S(2)}) collective-permute-start(bf16[1000,128]{1,0:T(8,128)(2,1)S(1)} %get-tuple-element.44), channel_id=1, source_target_pairs={{0,1},{1,2},{2,3},{3,51},{4,5},{5,6},{6,7},{7,55},{8,9},{9,10},{10... | collective-permute-start | bytes 768008 | tf_op jit(solution)/shard_map/ppermute | solution.py:246
  28.4 15.8 %collective-permute-start.8 = (bf16[1000,128]{1,0:T(8,128)(2,1)S(1)}, bf16[1000,128]{1,0:T(8,128)(2,1)S(1)}, u32[]{:S(2)}, u32[]{:S(2)}) collective-permute-start(bf16[1000,128]{1,0:T(8,128)(2,1)S(1)} %get-tuple-element.45), channel_id=1, source_target_pairs={{3,4},{4,3},{7,8},{8,7},{11,12},{12,11},{15,16},{16,15},{19,20},{2... | collective-permute-start | bytes 768008 | tf_op jit(solution)/shard_map/ppermute | solution.py:246
  34.1 12.1 %collective-permute-start.9 = (bf16[1000,128]{1,0:T(8,128)(2,1)S(1)}, bf16[1000,128]{1,0:T(8,128)(2,1)S(1)}, u32[]{:S(2)}, u32[]{:S(2)}) collective-permute-start(bf16[1000,128]{1,0:T(8,128)(2,1)S(1)} %get-tuple-element.46), channel_id=1, source_target_pairs={{1,0},{2,1},{3,2},{51,3},{5,4},{6,5},{7,6},{55,7},{9,8},{10,9},{11... | collective-permute-start | bytes 768008 | tf_op jit(solution)/shard_map/ppermute | solution.py:246
  34.1 19.0 %collective-permute-start.10 = (bf16[1000,128]{1,0:T(8,128)(2,1)S(1)}, bf16[1000,128]{1,0:T(8,128)(2,1)S(1)}, u32[]{:S(2)}, u32[]{:S(2)}) collective-permute-start(bf16[1000,128]{1,0:T(8,128)(2,1)S(1)} %get-tuple-element.47), channel_id=1, source_target_pairs={{0,2},{2,0},{1,3},{3,1},{4,6},{6,4},{5,7},{7,5},{8,10},{10,8},{9,1... | collective-permute-start | bytes 768008 | tf_op jit(solution)/shard_map/ppermute | solution.py:246
  36.1 17.1 %collective-permute-start.11 = (bf16[1000,128]{1,0:T(8,128)(2,1)S(1)}, bf16[1000,128]{1,0:T(8,128)(2,1)S(1)}, u32[]{:S(2)}, u32[]{:S(2)}) collective-permute-start(bf16[1000,128]{1,0:T(8,128)(2,1)S(1)} %get-tuple-element.48), channel_id=1, source_target_pairs={{2,4},{4,2},{3,5},{5,3},{6,8},{8,6},{7,9},{9,7},{10,12},{12,10},{1... | collective-permute-start | bytes 768008 | tf_op jit(solution)/shard_map/ppermute | solution.py:246
  39.7 13.4 %collective-permute-start.12 = (bf16[1000,128]{1,0:T(8,128)(2,1)S(1)}, bf16[1000,128]{1,0:T(8,128)(2,1)S(1)}, u32[]{:S(2)}, u32[]{:S(2)}) collective-permute-start(bf16[1000,128]{1,0:T(8,128)(2,1)S(1)} %get-tuple-element.49), channel_id=1, source_target_pairs={{0,48},{1,49},{2,50},{3,51},{4,52},{5,53},{6,54},{7,55},{8,56},{9,... | collective-permute-start | bytes 768008 | tf_op jit(solution)/shard_map/ppermute | solution.py:246
  44.2 9.0 %collective-permute-start.13 = (bf16[1000,128]{1,0:T(8,128)(2,1)S(1)}, bf16[1000,128]{1,0:T(8,128)(2,1)S(1)}, u32[]{:S(2)}, u32[]{:S(2)}) collective-permute-start(bf16[1000,128]{1,0:T(8,128)(2,1)S(1)} %get-tuple-element.50), channel_id=1, source_target_pairs={{0,720},{1,721},{2,722},{3,723},{4,724},{5,725},{6,726},{7,727},{8... | collective-permute-start | bytes 768008 | tf_op jit(solution)/shard_map/ppermute | solution.py:246
  54.6 9.3 %collective-permute-start.14 = (bf16[1000,128]{1,0:T(8,128)(2,1)S(1)}, bf16[1000,128]{1,0:T(8,128)(2,1)S(1)}, u32[]{:S(2)}, u32[]{:S(2)}) collective-permute-start(bf16[1000,128]{1,0:T(8,128)(2,1)S(1)} %get-tuple-element.52), channel_id=1, source_target_pairs={{0,1},{1,2},{2,3},{3,51},{4,5},{5,6},{6,7},{7,55},{8,9},{9,10},{10... | collective-permute-start | bytes 768008 | tf_op jit(solution)/shard_map/ppermute | solution.py:246
  54.6 16.4 %collective-permute-start.15 = (bf16[1000,128]{1,0:T(8,128)(2,1)S(1)}, bf16[1000,128]{1,0:T(8,128)(2,1)S(1)}, u32[]{:S(2)}, u32[]{:S(2)}) collective-permute-start(bf16[1000,128]{1,0:T(8,128)(2,1)S(1)} %get-tuple-element.53), channel_id=1, source_target_pairs={{3,4},{4,3},{7,8},{8,7},{11,12},{12,11},{15,16},{16,15},{19,20},{2... | collective-permute-start | bytes 768008 | tf_op jit(solution)/shard_map/ppermute | solution.py:246
  59.5 13.6 %collective-permute-start.16 = (bf16[1000,128]{1,0:T(8,128)(2,1)S(1)}, bf16[1000,128]{1,0:T(8,128)(2,1)S(1)}, u32[]{:S(2)}, u32[]{:S(2)}) collective-permute-start(bf16[1000,128]{1,0:T(8,128)(2,1)S(1)} %get-tuple-element.54), channel_id=1, source_target_pairs={{1,0},{2,1},{3,2},{51,3},{5,4},{6,5},{7,6},{55,7},{9,8},{10,9},{11... | collective-permute-start | bytes 768008 | tf_op jit(solution)/shard_map/ppermute | solution.py:246
  59.5 19.8 %collective-permute-start.17 = (bf16[1000,128]{1,0:T(8,128)(2,1)S(1)}, bf16[1000,128]{1,0:T(8,128)(2,1)S(1)}, u32[]{:S(2)}, u32[]{:S(2)}) collective-permute-start(bf16[1000,128]{1,0:T(8,128)(2,1)S(1)} %get-tuple-element.55), channel_id=1, source_target_pairs={{0,2},{2,0},{1,3},{3,1},{4,6},{6,4},{5,7},{7,5},{8,10},{10,8},{9,1... | collective-permute-start | bytes 768008 | tf_op jit(solution)/shard_map/ppermute | solution.py:246
  61.5 17.9 %collective-permute-start.18 = (bf16[1000,128]{1,0:T(8,128)(2,1)S(1)}, bf16[1000,128]{1,0:T(8,128)(2,1)S(1)}, u32[]{:S(2)}, u32[]{:S(2)}) collective-permute-start(bf16[1000,128]{1,0:T(8,128)(2,1)S(1)} %get-tuple-element.56), channel_id=1, source_target_pairs={{2,4},{4,2},{3,5},{5,3},{6,8},{8,6},{7,9},{9,7},{10,12},{12,10},{1... | collective-permute-start | bytes 768008 | tf_op jit(solution)/shard_map/ppermute | solution.py:246
  63.9 15.5 %collective-permute-start.19 = (bf16[1000,128]{1,0:T(8,128)(2,1)S(1)}, bf16[1000,128]{1,0:T(8,128)(2,1)S(1)}, u32[]{:S(2)}, u32[]{:S(2)}) collective-permute-start(bf16[1000,128]{1,0:T(8,128)(2,1)S(1)} %get-tuple-element.57), channel_id=1, source_target_pairs={{0,48},{1,49},{2,50},{3,51},{4,52},{5,53},{6,54},{7,55},{8,56},{9,... | collective-permute-start | bytes 768008 | tf_op jit(solution)/shard_map/ppermute | solution.py:246
  71.0 8.4 %collective-permute-start.20 = (bf16[1000,128]{1,0:T(8,128)(2,1)S(1)}, bf16[1000,128]{1,0:T(8,128)(2,1)S(1)}, u32[]{:S(2)}, u32[]{:S(2)}) collective-permute-start(bf16[1000,128]{1,0:T(8,128)(2,1)S(1)} %get-tuple-element.58), channel_id=1, source_target_pairs={{0,720},{1,721},{2,722},{3,723},{4,724},{5,725},{6,726},{7,727},{8... | collective-permute-start | bytes 768008 | tf_op jit(solution)/shard_map/ppermute | solution.py:246

commit v8 on v7

--- a/solution.py
+++ b/solution.py
@@ -85,8 +85,8 @@
         send_refs[k][rows, :] = own_ref[rows, block]
 
 
-def start_of(rows, at, classes, seeds, prior_ref):
-    soft = prior_ref[rows, :].astype(jnp.float32)
+def start_of(rows, at, classes, seeds, prior_ref, columns=slice(None)):
+    soft = prior_ref[rows, columns].astype(jnp.float32)
     label = lax.broadcasted_iota(jnp.int32, soft.shape, 0) + at
     return jnp.where(seeds < classes, jnp.where(label == seeds, 1.0, 0.0), soft)
 
@@ -94,27 +94,33 @@
 def prepare_kernel(
     send_any, seeds_any, degree_any, prior_any, root_ref, seeds_ref, prior_ref, own_ref, *refs
 ):
-    send_refs, (sends, seeds_held, degree_held, arrived) = refs[:PERMUTES], refs[PERMUTES:]
-    classes = prior_any.shape[0]
+    send_refs, (sends, seeds_held, degree_held, small, arrived) = refs[:PERMUTES], refs[PERMUTES:]
+    classes, nodes = prior_any.shape
+    firsts = [
+        pltpu.make_async_copy(seeds_any, seeds_held, small.at[0]),
+        pltpu.make_async_copy(degree_any, degree_held, small.at[1]),
+        pltpu.make_async_copy(send_any, sends, small.at[2]),
+    ]
+    blocks = [pl.ds(at, SIDE) for at in range(0, nodes, SIDE)]
     copies = [
-        pltpu.make_async_copy(prior_any, prior_ref, arrived.at[0]),
-        pltpu.make_async_copy(seeds_any, seeds_held, arrived.at[1]),
-        pltpu.make_async_copy(degree_any, degree_held, arrived.at[2]),
-        pltpu.make_async_copy(send_any, sends, arrived.at[3]),
+        pltpu.make_async_copy(prior_any.at[:, block], prior_ref.at[:, block], arrived.at[k])
+        for k, block in enumerate(blocks)
     ]
-    for copy in copies:
+    for copy in firsts + copies:
         copy.start()
-    for copy in copies:
+    for copy in firsts:
         copy.wait()
-    inv_root = 1.0 / jnp.sqrt(degree_held[...].astype(jnp.float32)[None, :])
-    seeds = seeds_held[...][None, :]
-    root_ref[...] = inv_root
-    seeds_ref[...] = seeds
+    root_ref[...] = 1.0 / jnp.sqrt(degree_held[...].astype(jnp.float32)[None, :])
+    seeds_ref[...] = seeds_held[...][None, :]
+    for block, copy in zip(blocks, copies):
+        copy.wait()
+        seeds, inv_root = seeds_ref[:, block], root_ref[:, block]
+        for at, size in chunks(classes):
+            rows = pl.ds(at, size)
+            start = start_of(rows, at, classes, seeds, prior_ref, block)
+            own_ref[rows, block] = (inv_root * start).astype(jnp.bfloat16)
     for at, size in chunks(classes):
-        rows = pl.ds(at, size)
-        start = start_of(rows, at, classes, seeds, prior_ref)
-        own_ref[rows, :] = (inv_root * start).astype(jnp.bfloat16)
-        put_sends(rows, sends, own_ref, send_refs)
+        put_sends(pl.ds(at, size), sends, own_ref, send_refs)
 
 
 def gains(root_ref, last):
@@ -229,7 +235,8 @@
             pltpu.SMEM(send_list.shape, jnp.int32),
             pltpu.VMEM((nodes,), jnp.int32),
             pltpu.VMEM((nodes,), jnp.int32),
-            pltpu.SemaphoreType.DMA((4,)),
+            pltpu.SemaphoreType.DMA((3,)),
+            pltpu.SemaphoreType.DMA((row_blocks,)),
         ],
         compiler_params=PARAMS,
     )(*[in_hbm(x) for x in (send_list, seed_labels, degree, prior.T)])

time: 81.3 us -> 81 us (level)
  no operation moved by 1% of the time
where the time goes in v8:
time: 81 us; the launch traced here: 80.5 us
  starting transfers between devices  42 us (52%)
  waiting for transfers between devices  25.1 us (31%)
  Pallas kernels  10.7 us (13%)
  local copies, waits for them, and re-layouts  1.82 us (2%)
  between operations  0.89 us (1%)
    ppermute x21, starting transfers between devices, on_device(): lax.ppermute(sends[k], ('group', 'dom'), route[k])  42 us
    ppermute x21, waiting for transfers between devices, on_device(): lax.ppermute(sends[k], ('group', 'dom'), route[k])  25.1 us
    pallas_call x3, Pallas kernels, on_device(): pl.pallas_call(functools.partial(early_kernel, step == ITERS - 1), in_spe...  3.11 us
    pallas_call x2, Pallas kernels, on_device(): pl.pallas_call(step_kernel, in_specs=[SMEM] + [VMEM] * (3 + len(late)), o...  2.9 us
    unnamed x6, local copies, waits for them, and re-layouts  1.82 us
    pallas_call x1, Pallas kernels, on_device(): pl.pallas_call(prepare_kernel, in_specs=[HBM] * 4, out_specs=[VMEM] * (4...  1.71 us
  transfers between devices with their start and end apart: 21, of which 6 were waited for; matrix products, arithmetic and copies ran while one was open for 0% of the time, Pallas kernels for 6%

profile of v8, /device:TPU:512, one launch (start us, length us, event | category | flops | bytes accessed | tf_op | source)
XLA Modules:
  0.0 80.5 jit_solution(2893620844586131047)
XLA Ops:
  0.0 1.7 %shard_map.73 = (f32[1,384]{1,0:T(1,128)S(1)}, s32[1,384]{1,0:T(1,128)S(1)}, bf16[1000,384]{1,0:T(8,128)(2,1)S(1)}, bf16[1000,384]{1,0:T(8,128)(2,1)S(1)}, bf16[...) custom-call(s32[1,6]{1,0:T(1,128)} %send_ref.3, ...), custom_call_target="tpu_custom_call" | custom-call | tf_op jit(solution)/shard_map/pallas_call | solution.py:223
  1.7 1.5 %collective-permute-start = (bf16[1000,128]{1,0:T(8,128)(2,1)S(1)}, bf16[1000,128]{1,0:T(8,128)(2,1)S(1)}, u32[]{:S(2)}, u32[]{:S(2)}) collective-permute-start(bf16[1000,128]{1,0:T(8,128)(2,1)S(1)} %get-tuple-element.36), channel_id=1, source_target_pairs={{0,1},{1,2},{2,3},{3,51},{4,5},{5,6},{6,7},{7,55},{8,9},{9,10},{10... | collective-permute-start | bytes 768008 | tf_op jit(solution)/shard_map/ppermute | solution.py:253
  3.2 4.4 %collective-permute-start.1 = (bf16[1000,128]{1,0:T(8,128)(2,1)S(1)}, bf16[1000,128]{1,0:T(8,128)(2,1)S(1)}, u32[]{:S(2)}, u32[]{:S(2)}) collective-permute-start(bf16[1000,128]{1,0:T(8,128)(2,1)S(1)} %get-tuple-element.37), channel_id=1, source_target_pairs={{3,4},{4,3},{7,8},{8,7},{11,12},{12,11},{15,16},{16,15},{19,20},{2... | collective-permute-start | bytes 768008 | tf_op jit(solution)/shard_map/ppermute | solution.py:253
  7.6 0.1 collective-permute-start.2
  7.7 1.9 %collective-permute-start.3 = (bf16[1000,128]{1,0:T(8,128)(2,1)S(1)}, bf16[1000,128]{1,0:T(8,128)(2,1)S(1)}, u32[]{:S(2)}, u32[]{:S(2)}) collective-permute-start(bf16[1000,128]{1,0:T(8,128)(2,1)S(1)} %get-tuple-element.39), channel_id=1, source_target_pairs={{0,2},{2,0},{1,3},{3,1},{4,6},{6,4},{5,7},{7,5},{8,10},{10,8},{9,1... | collective-permute-start | bytes 768008 | tf_op jit(solution)/shard_map/ppermute | solution.py:253
  9.6 4.8 %collective-permute-start.4 = (bf16[1000,128]{1,0:T(8,128)(2,1)S(1)}, bf16[1000,128]{1,0:T(8,128)(2,1)S(1)}, u32[]{:S(2)}, u32[]{:S(2)}) collective-permute-start(bf16[1000,128]{1,0:T(8,128)(2,1)S(1)} %get-tuple-element.40), channel_id=1, source_target_pairs={{2,4},{4,2},{3,5},{5,3},{6,8},{8,6},{7,9},{9,7},{10,12},{12,10},{1... | collective-permute-start | bytes 768008 | tf_op jit(solution)/shard_map/ppermute | solution.py:253
  14.5 0.0 collective-permute-done.refs_0_
  14.5 0.0 collective-permute-start.5
  14.5 2.5 %collective-permute-done.1.refs_1_ = bf16[1000,128]{1,0:T(8,128)(2,1)S(1)} collective-permute-done((bf16[1000,128]{1,0:T(8,128)(2,1)S(1)}, bf16[1000,128]{1,0:T(8,128)(2,1)S(1)}, u32[]{:S(2)}, u32[]{:S(2)}) %collective-permute-start.1) | collective-permute-done | bytes 256032 | tf_op jit(solution)/shard_map/ppermute | solution.py:253
  16.9 0.5 collective-permute-start.6
  18.1 0.0 copy-start
  18.1 1.1 %copy-done = bf16[3,8,128,128]{3,2,1,0:T(8,128)(2,1)S(1)} copy-done((bf16[3,8,128,128]{3,2,1,0:T(8,128)(2,1)S(1)}, bf16[3,8,128,128]{3,2,1,0:T(8,128)(2,1)}, u32[]{:S(2)}) %copy-start) | copy-done | bytes 786456
  19.2 0.7 copy-done.2
  19.9 1.5 %shard_map.74.weight_ref = bf16[1280,384]{1,0:T(8,128)(2,1)S(1)} custom-call(s32[3,8]{1,0:T(4,128)S(1)} %copy-done.2, s32[1]{0:T(128)S(6)} %copy.8.count_ref, bf16[3,8,128,128]{3,2,1,0:T(8,128)(2,1)S(1)} %copy-done), custom_call_target="tpu_custom_call" | custom-call | bytes 8000000 | tf_op jit(solution)/shard_map/pallas_call | solution.py:243
  21.4 0.0 collective-permute-done.2.refs_2_
  21.4 0.0 copy-start.1
  21.4 1.0 %shard_map.75.sum_ref = f32[1000,384]{1,0:T(8,128)S(1)} custom-call(f32[1,384]{1,0:T(1,128)S(1)} %get-tuple-element.32.root_ref, s32[1,384]{1,0:T(1,128)S(1)} %get-tuple-element.33.seeds_ref, bf16[1000,384]{1,0:T(8,128)(2,1)S(1)} %get-tuple-element.34.prior_ref, bf16[1280,384]{1,0:T(8,128)(2,1)S(1)} %shard_map.74.weight_ref, ...), custom_call_target="tpu_custom_call" | custom-call | flops 589824000 | bytes 4000000 | tf_op jit(solution)/shard_map/pallas_call | solution.py:254
  22.5 4.0 %collective-permute-done.3.refs_0_ = bf16[1000,128]{1,0:T(8,128)(2,1)S(1)} collective-permute-done((bf16[1000,128]{1,0:T(8,128)(2,1)S(1)}, bf16[1000,128]{1,0:T(8,128)(2,1)S(1)}, u32[]{:S(2)}, u32[]{:S(2)}) %collective-permute-start.3) | collective-permute-done | bytes 256032 | tf_op jit(solution)/shard_map/ppermute | solution.py:253
  26.5 0.0 collective-permute-done.4.refs_1_
  26.5 0.0 collective-permute-done.5.refs_2_
  26.5 0.0 collective-permute-done.6.refs_3_
  26.5 1.5 %shard_map.76 = (bf16[1000,384]{1,0:T(8,128)(2,1)S(1)}, bf16[1000,128]{1,0:T(8,128)(2,1)S(1)}, bf16[1000,128]{1,0:T(8,128)(2,1)S(1)}, bf16[1000,128]{1,0:T(8,128...) custom-call(s32[1,6]{1,0:T(1,128)S(1)} %copy-done.1, ...), custom_call_target="tpu_custom_call" | custom-call | tf_op jit(solution)/shard_map/pallas_call | solution.py:268
  28.0 0.0 collective-permute-start.7
  28.0 5.7 %collective-permute-start.8 = (bf16[1000,128]{1,0:T(8,128)(2,1)S(1)}, bf16[1000,128]{1,0:T(8,128)(2,1)S(1)}, u32[]{:S(2)}, u32[]{:S(2)}) collective-permute-start(bf16[1000,128]{1,0:T(8,128)(2,1)S(1)} %get-tuple-element.45), channel_id=1, source_target_pairs={{3,4},{4,3},{7,8},{8,7},{11,12},{12,11},{15,16},{16,15},{19,20},{2... | collective-permute-start | bytes 768008 | tf_op jit(solution)/shard_map/ppermute | solution.py:253
  33.8 0.0 collective-permute-start.9
  33.8 1.9 %collective-permute-start.10 = (bf16[1000,128]{1,0:T(8,128)(2,1)S(1)}, bf16[1000,128]{1,0:T(8,128)(2,1)S(1)}, u32[]{:S(2)}, u32[]{:S(2)}) collective-permute-start(bf16[1000,128]{1,0:T(8,128)(2,1)S(1)} %get-tuple-element.47), channel_id=1, source_target_pairs={{0,2},{2,0},{1,3},{3,1},{4,6},{6,4},{5,7},{7,5},{8,10},{10,8},{9,1... | collective-permute-start | bytes 768008 | tf_op jit(solution)/shard_map/ppermute | solution.py:253
  35.7 3.6 %collective-permute-start.11 = (bf16[1000,128]{1,0:T(8,128)(2,1)S(1)}, bf16[1000,128]{1,0:T(8,128)(2,1)S(1)}, u32[]{:S(2)}, u32[]{:S(2)}) collective-permute-start(bf16[1000,128]{1,0:T(8,128)(2,1)S(1)} %get-tuple-element.48), channel_id=1, source_target_pairs={{2,4},{4,2},{3,5},{5,3},{6,8},{8,6},{7,9},{9,7},{10,12},{12,10},{1... | collective-permute-start | bytes 768008 | tf_op jit(solution)/shard_map/ppermute | solution.py:253
  39.3 0.0 collective-permute-done.7.refs_0_
  39.3 0.9 %collective-permute-start.12 = (bf16[1000,128]{1,0:T(8,128)(2,1)S(1)}, bf16[1000,128]{1,0:T(8,128)(2,1)S(1)}, u32[]{:S(2)}, u32[]{:S(2)}) collective-permute-start(bf16[1000,128]{1,0:T(8,128)(2,1)S(1)} %get-tuple-element.49), channel_id=1, source_target_pairs={{0,48},{1,49},{2,50},{3,51},{4,52},{5,53},{6,54},{7,55},{8,56},{9,... | collective-permute-start | bytes 768008 | tf_op jit(solution)/shard_map/ppermute | solution.py:253
  40.3 3.5 %collective-permute-done.8.refs_1_ = bf16[1000,128]{1,0:T(8,128)(2,1)S(1)} collective-permute-done((bf16[1000,128]{1,0:T(8,128)(2,1)S(1)}, bf16[1000,128]{1,0:T(8,128)(2,1)S(1)}, u32[]{:S(2)}, u32[]{:S(2)}) %collective-permute-start.8) | collective-permute-done | bytes 256032 | tf_op jit(solution)/shard_map/ppermute | solution.py:253
  43.8 2.1 %collective-permute-start.13 = (bf16[1000,128]{1,0:T(8,128)(2,1)S(1)}, bf16[1000,128]{1,0:T(8,128)(2,1)S(1)}, u32[]{:S(2)}, u32[]{:S(2)}) collective-permute-start(bf16[1000,128]{1,0:T(8,128)(2,1)S(1)} %get-tuple-element.50), channel_id=1, source_target_pairs={{0,720},{1,721},{2,722},{3,723},{4,724},{5,725},{6,726},{7,727},{8... | collective-permute-start | bytes 768008 | tf_op jit(solution)/shard_map/ppermute | solution.py:253
  45.9 1.0 %shard_map.77.sum_ref = f32[1000,384]{1,0:T(8,128)S(1)} custom-call(f32[1,384]{1,0:T(1,128)S(1)} %get-tuple-element.32.root_ref, s32[1,384]{1,0:T(1,128)S(1)} %get-tuple-element.33.seeds_ref, bf16[1000,384]{1,0:T(8,128)(2,1)S(1)} %get-tuple-element.34.prior_ref, bf16[1280,384]{1,0:T(8,128)(2,1)S(1)} %shard_map.74.weight_ref, ...), custom_call_target="tpu_custom_call" | custom-call | flops 589824000 | bytes 4000000 | tf_op jit(solution)/shard_map/pallas_call | solution.py:254
  46.9 5.8 %collective-permute-done.10.refs_0_ = bf16[1000,128]{1,0:T(8,128)(2,1)S(1)} collective-permute-done((bf16[1000,128]{1,0:T(8,128)(2,1)S(1)}, bf16[1000,128]{1,0:T(8,128)(2,1)S(1)}, u32[]{:S(2)}, u32[]{:S(2)}) %collective-permute-start.10) | collective-permute-done | bytes 256032 | tf_op jit(solution)/shard_map/ppermute | solution.py:253
  52.8 0.0 collective-permute-done.11.refs_1_
  52.8 1.4 %shard_map.78 = (bf16[1000,384]{1,0:T(8,128)(2,1)S(1)}, bf16[1000,128]{1,0:T(8,128)(2,1)S(1)}, bf16[1000,128]{1,0:T(8,128)(2,1)S(1)}, bf16[1000,128]{1,0:T(8,128...) custom-call(s32[1,6]{1,0:T(1,128)S(1)} %copy-done.1, ...), custom_call_target="tpu_custom_call" | custom-call | tf_op jit(solution)/shard_map/pallas_call | solution.py:268
  54.2 0.0 collective-permute-start.14
  54.3 4.9 %collective-permute-start.15 = (bf16[1000,128]{1,0:T(8,128)(2,1)S(1)}, bf16[1000,128]{1,0:T(8,128)(2,1)S(1)}, u32[]{:S(2)}, u32[]{:S(2)}) collective-permute-start(bf16[1000,128]{1,0:T(8,128)(2,1)S(1)} %get-tuple-element.53), channel_id=1, source_target_pairs={{3,4},{4,3},{7,8},{8,7},{11,12},{12,11},{15,16},{16,15},{19,20},{2... | collective-permute-start | bytes 768008 | tf_op jit(solution)/shard_map/ppermute | solution.py:253
  59.2 0.0 collective-permute-start.16
  59.2 1.9 %collective-permute-start.17 = (bf16[1000,128]{1,0:T(8,128)(2,1)S(1)}, bf16[1000,128]{1,0:T(8,128)(2,1)S(1)}, u32[]{:S(2)}, u32[]{:S(2)}) collective-permute-start(bf16[1000,128]{1,0:T(8,128)(2,1)S(1)} %get-tuple-element.55), channel_id=1, source_target_pairs={{0,2},{2,0},{1,3},{3,1},{4,6},{6,4},{5,7},{7,5},{8,10},{10,8},{9,1... | collective-permute-start | bytes 768008 | tf_op jit(solution)/shard_map/ppermute | solution.py:253
  61.1 2.4 %collective-permute-start.18 = (bf16[1000,128]{1,0:T(8,128)(2,1)S(1)}, bf16[1000,128]{1,0:T(8,128)(2,1)S(1)}, u32[]{:S(2)}, u32[]{:S(2)}) collective-permute-start(bf16[1000,128]{1,0:T(8,128)(2,1)S(1)} %get-tuple-element.56), channel_id=1, source_target_pairs={{2,4},{4,2},{3,5},{5,3},{6,8},{8,6},{7,9},{9,7},{10,12},{12,10},{1... | collective-permute-start | bytes 768008 | tf_op jit(solution)/shard_map/ppermute | solution.py:253
  63.5 0.0 collective-permute-done.14.refs_0_
  63.5 3.0 %collective-permute-start.19 = (bf16[1000,128]{1,0:T(8,128)(2,1)S(1)}, bf16[1000,128]{1,0:T(8,128)(2,1)S(1)}, u32[]{:S(2)}, u32[]{:S(2)}) collective-permute-start(bf16[1000,128]{1,0:T(8,128)(2,1)S(1)} %get-tuple-element.57), channel_id=1, source_target_pairs={{0,48},{1,49},{2,50},{3,51},{4,52},{5,53},{6,54},{7,55},{8,56},{9,... | collective-permute-start | bytes 768008 | tf_op jit(solution)/shard_map/ppermute | solution.py:253
  66.5 4.1 %collective-permute-done.15.refs_1_ = bf16[1000,128]{1,0:T(8,128)(2,1)S(1)} collective-permute-done((bf16[1000,128]{1,0:T(8,128)(2,1)S(1)}, bf16[1000,128]{1,0:T(8,128)(2,1)S(1)}, u32[]{:S(2)}, u32[]{:S(2)}) %collective-permute-start.15) | collective-permute-done | bytes 256032 | tf_op jit(solution)/shard_map/ppermute | solution.py:253
  70.6 2.2 %collective-permute-start.20 = (bf16[1000,128]{1,0:T(8,128)(2,1)S(1)}, bf16[1000,128]{1,0:T(8,128)(2,1)S(1)}, u32[]{:S(2)}, u32[]{:S(2)}) collective-permute-start(bf16[1000,128]{1,0:T(8,128)(2,1)S(1)} %get-tuple-element.58), channel_id=1, source_target_pairs={{0,720},{1,721},{2,722},{3,723},{4,724},{5,725},{6,726},{7,727},{8... | collective-permute-start | bytes 768008 | tf_op jit(solution)/shard_map/ppermute | solution.py:253
  72.8 0.0 collective-permute-done.16.refs_2_
  72.8 1.0 %shard_map.79.sum_ref = f32[1000,384]{1,0:T(8,128)S(1)} custom-call(f32[1,384]{1,0:T(1,128)S(1)} %get-tuple-element.32.root_ref, s32[1,384]{1,0:T(1,128)S(1)} %get-tuple-element.33.seeds_ref, bf16[1000,384]{1,0:T(8,128)(2,1)S(1)} %get-tuple-element.34.prior_ref, bf16[1280,384]{1,0:T(8,128)(2,1)S(1)} %shard_map.74.weight_ref, ...), custom_call_target="tpu_custom_call" | custom-call | flops 589824000 | bytes 4000000 | tf_op jit(solution)/shard_map/pallas_call | solution.py:254
  73.9 5.1 %collective-permute-done.17.refs_0_ = bf16[1000,128]{1,0:T(8,128)(2,1)S(1)} collective-permute-done((bf16[1000,128]{1,0:T(8,128)(2,1)S(1)}, bf16[1000,128]{1,0:T(8,128)(2,1)S(1)}, u32[]{:S(2)}, u32[]{:S(2)}) %collective-permute-start.17) | collective-permute-done | bytes 256032 | tf_op jit(solution)/shard_map/ppermute | solution.py:253
  79.0 1.5 %shard_map.80 = f32[1000,384]{1,0:T(8,128)} custom-call(f32[1,384]{1,0:T(1,128)S(1)} %get-tuple-element.32.root_ref, bf16[1280,384]{1,0:T(8,128)(2,1)S(1)} %shard_map.74.weight_ref, f32[1000,384]{1,0:T(8,128)S(1)} %shard_map.79.sum_ref, bf16[1000,128]{1,0:T(8,128)(2,1)S(1)} %collective-permute-done.17.refs_0_, ...), custom_call_target="tpu_custom_call" | custom-call | tf_op jit(solution)/shard_map/pallas_call | solution.py:275
  (8 shorter events, 0.0 us)
Async XLA Ops:
  1.7 12.7 %collective-permute-start = (bf16[1000,128]{1,0:T(8,128)(2,1)S(1)}, bf16[1000,128]{1,0:T(8,128)(2,1)S(1)}, u32[]{:S(2)}, u32[]{:S(2)}) collective-permute-start(bf16[1000,128]{1,0:T(8,128)(2,1)S(1)} %get-tuple-element.36), channel_id=1, source_target_pairs={{0,1},{1,2},{2,3},{3,51},{4,5},{5,6},{6,7},{7,55},{8,9},{9,10},{10... | collective-permute-start | bytes 768008 | tf_op jit(solution)/shard_map/ppermute | solution.py:253
  3.2 13.7 %collective-permute-start.1 = (bf16[1000,128]{1,0:T(8,128)(2,1)S(1)}, bf16[1000,128]{1,0:T(8,128)(2,1)S(1)}, u32[]{:S(2)}, u32[]{:S(2)}) collective-permute-start(bf16[1000,128]{1,0:T(8,128)(2,1)S(1)} %get-tuple-element.37), channel_id=1, source_target_pairs={{3,4},{4,3},{7,8},{8,7},{11,12},{12,11},{15,16},{16,15},{19,20},{2... | collective-permute-start | bytes 768008 | tf_op jit(solution)/shard_map/ppermute | solution.py:253
  7.6 13.8 %collective-permute-start.2 = (bf16[1000,128]{1,0:T(8,128)(2,1)S(1)}, bf16[1000,128]{1,0:T(8,128)(2,1)S(1)}, u32[]{:S(2)}, u32[]{:S(2)}) collective-permute-start(bf16[1000,128]{1,0:T(8,128)(2,1)S(1)} %get-tuple-element.38), channel_id=1, source_target_pairs={{1,0},{2,1},{3,2},{51,3},{5,4},{6,5},{7,6},{55,7},{9,8},{10,9},{11... | collective-permute-start | bytes 768008 | tf_op jit(solution)/shard_map/ppermute | solution.py:253
  7.7 18.8 %collective-permute-start.3 = (bf16[1000,128]{1,0:T(8,128)(2,1)S(1)}, bf16[1000,128]{1,0:T(8,128)(2,1)S(1)}, u32[]{:S(2)}, u32[]{:S(2)}) collective-permute-start(bf16[1000,128]{1,0:T(8,128)(2,1)S(1)} %get-tuple-element.39), channel_id=1, source_target_pairs={{0,2},{2,0},{1,3},{3,1},{4,6},{6,4},{5,7},{7,5},{8,10},{10,8},{9,1... | collective-permute-start | bytes 768008 | tf_op jit(solution)/shard_map/ppermute | solution.py:253
  9.6 16.9 %collective-permute-start.4 = (bf16[1000,128]{1,0:T(8,128)(2,1)S(1)}, bf16[1000,128]{1,0:T(8,128)(2,1)S(1)}, u32[]{:S(2)}, u32[]{:S(2)}) collective-permute-start(bf16[1000,128]{1,0:T(8,128)(2,1)S(1)} %get-tuple-element.40), channel_id=1, source_target_pairs={{2,4},{4,2},{3,5},{5,3},{6,8},{8,6},{7,9},{9,7},{10,12},{12,10},{1... | collective-permute-start | bytes 768008 | tf_op jit(solution)/shard_map/ppermute | solution.py:253
  14.5 12.0 %collective-permute-start.5 = (bf16[1000,128]{1,0:T(8,128)(2,1)S(1)}, bf16[1000,128]{1,0:T(8,128)(2,1)S(1)}, u32[]{:S(2)}, u32[]{:S(2)}) collective-permute-start(bf16[1000,128]{1,0:T(8,128)(2,1)S(1)} %get-tuple-element.41), channel_id=1, source_target_pairs={{0,48},{1,49},{2,50},{3,51},{4,52},{5,53},{6,54},{7,55},{8,56},{9,... | collective-permute-start | bytes 768008 | tf_op jit(solution)/shard_map/ppermute | solution.py:253
  16.9 9.6 %collective-permute-start.6 = (bf16[1000,128]{1,0:T(8,128)(2,1)S(1)}, bf16[1000,128]{1,0:T(8,128)(2,1)S(1)}, u32[]{:S(2)}, u32[]{:S(2)}) collective-permute-start(bf16[1000,128]{1,0:T(8,128)(2,1)S(1)} %get-tuple-element.42), channel_id=1, source_target_pairs={{0,720},{1,721},{2,722},{3,723},{4,724},{5,725},{6,726},{7,727},{8... | collective-permute-start | bytes 768008 | tf_op jit(solution)/shard_map/ppermute | solution.py:253
  18.1 1.1 %copy-start = (bf16[3,8,128,128]{3,2,1,0:T(8,128)(2,1)S(1)}, bf16[3,8,128,128]{3,2,1,0:T(8,128)(2,1)}, u32[]{:S(2)}) copy-start(bf16[3,8,128,128]{3,2,1,0:T(8,128)(2,1)} %tiles_ref.1) | copy-start | bytes 2359300
  19.2 0.7 copy-start.2
  21.4 5.1 %copy-start.1 = (s32[1,6]{1,0:T(1,128)S(1)}, s32[1,6]{1,0:T(1,128)}, u32[]{:S(2)}) copy-start(s32[1,6]{1,0:T(1,128)} %send_ref.3) | copy-start | bytes 76
  28.0 11.3 %collective-permute-start.7 = (bf16[1000,128]{1,0:T(8,128)(2,1)S(1)}, bf16[1000,128]{1,0:T(8,128)(2,1)S(1)}, u32[]{:S(2)}, u32[]{:S(2)}) collective-permute-start(bf16[1000,128]{1,0:T(8,128)(2,1)S(1)} %get-tuple-element.44), channel_id=1, source_target_pairs={{0,1},{1,2},{2,3},{3,51},{4,5},{5,6},{6,7},{7,55},{8,9},{9,10},{10... | collective-permute-start | bytes 768008 | tf_op jit(solution)/shard_map/ppermute | solution.py:253
  28.0 15.8 %collective-permute-start.8 = (bf16[1000,128]{1,0:T(8,128)(2,1)S(1)}, bf16[1000,128]{1,0:T(8,128)(2,1)S(1)}, u32[]{:S(2)}, u32[]{:S(2)}) collective-permute-start(bf16[1000,128]{1,0:T(8,128)(2,1)S(1)} %get-tuple-element.45), channel_id=1, source_target_pairs={{3,4},{4,3},{7,8},{8,7},{11,12},{12,11},{15,16},{16,15},{19,20},{2... | collective-permute-start | bytes 768008 | tf_op jit(solution)/shard_map/ppermute | solution.py:253
  33.8 12.1 %collective-permute-start.9 = (bf16[1000,128]{1,0:T(8,128)(2,1)S(1)}, bf16[1000,128]{1,0:T(8,128)(2,1)S(1)}, u32[]{:S(2)}, u32[]{:S(2)}) collective-permute-start(bf16[1000,128]{1,0:T(8,128)(2,1)S(1)} %get-tuple-element.46), channel_id=1, source_target_pairs={{1,0},{2,1},{3,2},{51,3},{5,4},{6,5},{7,6},{55,7},{9,8},{10,9},{11... | collective-permute-start | bytes 768008 | tf_op jit(solution)/shard_map/ppermute | solution.py:253
  33.8 19.0 %collective-permute-start.10 = (bf16[1000,128]{1,0:T(8,128)(2,1)S(1)}, bf16[1000,128]{1,0:T(8,128)(2,1)S(1)}, u32[]{:S(2)}, u32[]{:S(2)}) collective-permute-start(bf16[1000,128]{1,0:T(8,128)(2,1)S(1)} %get-tuple-element.47), channel_id=1, source_target_pairs={{0,2},{2,0},{1,3},{3,1},{4,6},{6,4},{5,7},{7,5},{8,10},{10,8},{9,1... | collective-permute-start | bytes 768008 | tf_op jit(solution)/shard_map/ppermute | solution.py:253
  35.7 17.1 %collective-permute-start.11 = (bf16[1000,128]{1,0:T(8,128)(2,1)S(1)}, bf16[1000,128]{1,0:T(8,128)(2,1)S(1)}, u32[]{:S(2)}, u32[]{:S(2)}) collective-permute-start(bf16[1000,128]{1,0:T(8,128)(2,1)S(1)} %get-tuple-element.48), channel_id=1, source_target_pairs={{2,4},{4,2},{3,5},{5,3},{6,8},{8,6},{7,9},{9,7},{10,12},{12,10},{1... | collective-permute-start | bytes 768008 | tf_op jit(solution)/shard_map/ppermute | solution.py:253
  39.3 13.4 %collective-permute-start.12 = (bf16[1000,128]{1,0:T(8,128)(2,1)S(1)}, bf16[1000,128]{1,0:T(8,128)(2,1)S(1)}, u32[]{:S(2)}, u32[]{:S(2)}) collective-permute-start(bf16[1000,128]{1,0:T(8,128)(2,1)S(1)} %get-tuple-element.49), channel_id=1, source_target_pairs={{0,48},{1,49},{2,50},{3,51},{4,52},{5,53},{6,54},{7,55},{8,56},{9,... | collective-permute-start | bytes 768008 | tf_op jit(solution)/shard_map/ppermute | solution.py:253
  43.8 9.0 %collective-permute-start.13 = (bf16[1000,128]{1,0:T(8,128)(2,1)S(1)}, bf16[1000,128]{1,0:T(8,128)(2,1)S(1)}, u32[]{:S(2)}, u32[]{:S(2)}) collective-permute-start(bf16[1000,128]{1,0:T(8,128)(2,1)S(1)} %get-tuple-element.50), channel_id=1, source_target_pairs={{0,720},{1,721},{2,722},{3,723},{4,724},{5,725},{6,726},{7,727},{8... | collective-permute-start | bytes 768008 | tf_op jit(solution)/shard_map/ppermute | solution.py:253
  54.2 9.3 %collective-permute-start.14 = (bf16[1000,128]{1,0:T(8,128)(2,1)S(1)}, bf16[1000,128]{1,0:T(8,128)(2,1)S(1)}, u32[]{:S(2)}, u32[]{:S(2)}) collective-permute-start(bf16[1000,128]{1,0:T(8,128)(2,1)S(1)} %get-tuple-element.52), channel_id=1, source_target_pairs={{0,1},{1,2},{2,3},{3,51},{4,5},{5,6},{6,7},{7,55},{8,9},{9,10},{10... | collective-permute-start | bytes 768008 | tf_op jit(solution)/shard_map/ppermute | solution.py:253
  54.3 16.3 %collective-permute-start.15 = (bf16[1000,128]{1,0:T(8,128)(2,1)S(1)}, bf16[1000,128]{1,0:T(8,128)(2,1)S(1)}, u32[]{:S(2)}, u32[]{:S(2)}) collective-permute-start(bf16[1000,128]{1,0:T(8,128)(2,1)S(1)} %get-tuple-element.53), channel_id=1, source_target_pairs={{3,4},{4,3},{7,8},{8,7},{11,12},{12,11},{15,16},{16,15},{19,20},{2... | collective-permute-start | bytes 768008 | tf_op jit(solution)/shard_map/ppermute | solution.py:253
  59.2 13.7 %collective-permute-start.16 = (bf16[1000,128]{1,0:T(8,128)(2,1)S(1)}, bf16[1000,128]{1,0:T(8,128)(2,1)S(1)}, u32[]{:S(2)}, u32[]{:S(2)}) collective-permute-start(bf16[1000,128]{1,0:T(8,128)(2,1)S(1)} %get-tuple-element.54), channel_id=1, source_target_pairs={{1,0},{2,1},{3,2},{51,3},{5,4},{6,5},{7,6},{55,7},{9,8},{10,9},{11... | collective-permute-start | bytes 768008 | tf_op jit(solution)/shard_map/ppermute | solution.py:253
  59.2 19.8 %collective-permute-start.17 = (bf16[1000,128]{1,0:T(8,128)(2,1)S(1)}, bf16[1000,128]{1,0:T(8,128)(2,1)S(1)}, u32[]{:S(2)}, u32[]{:S(2)}) collective-permute-start(bf16[1000,128]{1,0:T(8,128)(2,1)S(1)} %get-tuple-element.55), channel_id=1, source_target_pairs={{0,2},{2,0},{1,3},{3,1},{4,6},{6,4},{5,7},{7,5},{8,10},{10,8},{9,1... | collective-permute-start | bytes 768008 | tf_op jit(solution)/shard_map/ppermute | solution.py:253
  61.1 17.9 %collective-permute-start.18 = (bf16[1000,128]{1,0:T(8,128)(2,1)S(1)}, bf16[1000,128]{1,0:T(8,128)(2,1)S(1)}, u32[]{:S(2)}, u32[]{:S(2)}) collective-permute-start(bf16[1000,128]{1,0:T(8,128)(2,1)S(1)} %get-tuple-element.56), channel_id=1, source_target_pairs={{2,4},{4,2},{3,5},{5,3},{6,8},{8,6},{7,9},{9,7},{10,12},{12,10},{1... | collective-permute-start | bytes 768008 | tf_op jit(solution)/shard_map/ppermute | solution.py:253
  63.5 15.5 %collective-permute-start.19 = (bf16[1000,128]{1,0:T(8,128)(2,1)S(1)}, bf16[1000,128]{1,0:T(8,128)(2,1)S(1)}, u32[]{:S(2)}, u32[]{:S(2)}) collective-permute-start(bf16[1000,128]{1,0:T(8,128)(2,1)S(1)} %get-tuple-element.57), channel_id=1, source_target_pairs={{0,48},{1,49},{2,50},{3,51},{4,52},{5,53},{6,54},{7,55},{8,56},{9,... | collective-permute-start | bytes 768008 | tf_op jit(solution)/shard_map/ppermute | solution.py:253
  70.6 8.4 %collective-permute-start.20 = (bf16[1000,128]{1,0:T(8,128)(2,1)S(1)}, bf16[1000,128]{1,0:T(8,128)(2,1)S(1)}, u32[]{:S(2)}, u32[]{:S(2)}) collective-permute-start(bf16[1000,128]{1,0:T(8,128)(2,1)S(1)} %get-tuple-element.58), channel_id=1, source_target_pairs={{0,720},{1,721},{2,722},{3,723},{4,724},{5,725},{6,726},{7,727},{8... | collective-permute-start | bytes 768008 | tf_op jit(solution)/shard_map/ppermute | solution.py:253

commit v9 on v8

--- a/solution.py
+++ b/solution.py
@@ -17,7 +17,7 @@
 HBM = pl.BlockSpec(memory_space=pltpu.HBM)
 PARAMS = pltpu.CompilerParams(vmem_limit_bytes=40 * 1024 * 1024)
 
-RING, EDGE, BACK, TWO, CROSS, UP, DOWN = range(7)
+EDGE, RING, BACK, TWO, CROSS, UP, DOWN = range(7)
 PERMUTES = 7
 EARLY = 3
 

time: 81 us -> 82.2 us (1.015)
  the two profiles are of different devices: /device:TPU:512 before, /device:TPU:95 now
where the time goes in v9:
time: 82.2 us; the launch traced here: 81.8 us
  starting transfers between devices  54.7 us (67%)
  waiting for transfers between devices  13.6 us (17%)
  Pallas kernels  10.7 us (13%)
  local copies, waits for them, and re-layouts  1.82 us (2%)
  between operations  0.92 us (1%)
    ppermute x21, starting transfers between devices, on_device(): lax.ppermute(sends[k], ('group', 'dom'), route[k])  54.7 us
    ppermute x21, waiting for transfers between devices, on_device(): lax.ppermute(sends[k], ('group', 'dom'), route[k])  13.6 us
    pallas_call x3, Pallas kernels, on_device(): pl.pallas_call(functools.partial(early_kernel, step == ITERS - 1), in_spe...  3.11 us
    pallas_call x2, Pallas kernels, on_device(): pl.pallas_call(step_kernel, in_specs=[SMEM] + [VMEM] * (3 + len(late)), o...  2.88 us
    unnamed x6, local copies, waits for them, and re-layouts  1.82 us
    pallas_call x1, Pallas kernels, on_device(): pl.pallas_call(prepare_kernel, in_specs=[HBM] * 4, out_specs=[VMEM] * (4...  1.71 us
  transfers between devices with their start and end apart: 21, of which 5 were waited for; matrix products, arithmetic and copies ran while one was open for 0% of the time, Pallas kernels for 6%

profile of v9, /device:TPU:95, one launch (start us, length us, event | category | flops | bytes accessed | tf_op | source)
XLA Modules:
  0.0 81.8 jit_solution(14887949435429464933)
XLA Ops:
  0.0 1.7 %shard_map.73 = (f32[1,384]{1,0:T(1,128)S(1)}, s32[1,384]{1,0:T(1,128)S(1)}, bf16[1000,384]{1,0:T(8,128)(2,1)S(1)}, bf16[1000,384]{1,0:T(8,128)(2,1)S(1)}, bf16[...) custom-call(s32[1,6]{1,0:T(1,128)} %send_ref.3, ...), custom_call_target="tpu_custom_call" | custom-call | tf_op jit(solution)/shard_map/pallas_call | solution.py:223
  1.7 3.9 %collective-permute-start = (bf16[1000,128]{1,0:T(8,128)(2,1)S(1)}, bf16[1000,128]{1,0:T(8,128)(2,1)S(1)}, u32[]{:S(2)}, u32[]{:S(2)}) collective-permute-start(bf16[1000,128]{1,0:T(8,128)(2,1)S(1)} %get-tuple-element.36), channel_id=1, source_target_pairs={{3,4},{4,3},{7,8},{8,7},{11,12},{12,11},{15,16},{16,15},{19,20},{2... | collective-permute-start | bytes 768008 | tf_op jit(solution)/shard_map/ppermute | solution.py:253
  5.6 0.0 collective-permute-start.1
  5.7 1.0 %collective-permute-start.2 = (bf16[1000,128]{1,0:T(8,128)(2,1)S(1)}, bf16[1000,128]{1,0:T(8,128)(2,1)S(1)}, u32[]{:S(2)}, u32[]{:S(2)}) collective-permute-start(bf16[1000,128]{1,0:T(8,128)(2,1)S(1)} %get-tuple-element.38), channel_id=1, source_target_pairs={{1,0},{2,1},{3,2},{51,3},{5,4},{6,5},{7,6},{55,7},{9,8},{10,9},{11... | collective-permute-start | bytes 768008 | tf_op jit(solution)/shard_map/ppermute | solution.py:253
  6.6 1.9 %collective-permute-start.3 = (bf16[1000,128]{1,0:T(8,128)(2,1)S(1)}, bf16[1000,128]{1,0:T(8,128)(2,1)S(1)}, u32[]{:S(2)}, u32[]{:S(2)}) collective-permute-start(bf16[1000,128]{1,0:T(8,128)(2,1)S(1)} %get-tuple-element.39), channel_id=1, source_target_pairs={{0,2},{2,0},{1,3},{3,1},{4,6},{6,4},{5,7},{7,5},{8,10},{10,8},{9,1... | collective-permute-start | bytes 768008 | tf_op jit(solution)/shard_map/ppermute | solution.py:253
  8.6 6.7 %collective-permute-start.4 = (bf16[1000,128]{1,0:T(8,128)(2,1)S(1)}, bf16[1000,128]{1,0:T(8,128)(2,1)S(1)}, u32[]{:S(2)}, u32[]{:S(2)}) collective-permute-start(bf16[1000,128]{1,0:T(8,128)(2,1)S(1)} %get-tuple-element.40), channel_id=1, source_target_pairs={{2,4},{4,2},{3,5},{5,3},{6,8},{8,6},{7,9},{9,7},{10,12},{12,10},{1... | collective-permute-start | bytes 768008 | tf_op jit(solution)/shard_map/ppermute | solution.py:253
  15.2 0.0 collective-permute-done.refs_0_
  15.3 5.0 %collective-permute-start.5 = (bf16[1000,128]{1,0:T(8,128)(2,1)S(1)}, bf16[1000,128]{1,0:T(8,128)(2,1)S(1)}, u32[]{:S(2)}, u32[]{:S(2)}) collective-permute-start(bf16[1000,128]{1,0:T(8,128)(2,1)S(1)} %get-tuple-element.41), channel_id=1, source_target_pairs={{0,48},{1,49},{2,50},{3,51},{4,52},{5,53},{6,54},{7,55},{8,56},{9,... | collective-permute-start | bytes 768008 | tf_op jit(solution)/shard_map/ppermute | solution.py:253
  20.2 0.0 collective-permute-start.6
  20.9 0.0 copy-start
  20.9 1.1 %copy-done = bf16[3,8,128,128]{3,2,1,0:T(8,128)(2,1)S(1)} copy-done((bf16[3,8,128,128]{3,2,1,0:T(8,128)(2,1)S(1)}, bf16[3,8,128,128]{3,2,1,0:T(8,128)(2,1)}, u32[]{:S(2)}) %copy-start) | copy-done | bytes 786456
  22.0 0.7 copy-done.2
  22.7 1.5 %shard_map.74.weight_ref = bf16[1280,384]{1,0:T(8,128)(2,1)S(1)} custom-call(s32[3,8]{1,0:T(4,128)S(1)} %copy-done.2, s32[1]{0:T(128)S(6)} %copy.8.count_ref, bf16[3,8,128,128]{3,2,1,0:T(8,128)(2,1)S(1)} %copy-done), custom_call_target="tpu_custom_call" | custom-call | bytes 8000000 | tf_op jit(solution)/shard_map/pallas_call | solution.py:243
  24.2 0.0 collective-permute-done.2.refs_2_
  24.2 0.0 copy-start.1
  24.2 1.0 %shard_map.75.sum_ref = f32[1000,384]{1,0:T(8,128)S(1)} custom-call(f32[1,384]{1,0:T(1,128)S(1)} %get-tuple-element.32.root_ref, s32[1,384]{1,0:T(1,128)S(1)} %get-tuple-element.33.seeds_ref, bf16[1000,384]{1,0:T(8,128)(2,1)S(1)} %get-tuple-element.34.prior_ref, bf16[1280,384]{1,0:T(8,128)(2,1)S(1)} %shard_map.74.weight_ref, ...), custom_call_target="tpu_custom_call" | custom-call | flops 589824000 | bytes 4000000 | tf_op jit(solution)/shard_map/pallas_call | solution.py:254
  25.3 0.0 collective-permute-done.3.refs_0_
  25.3 0.0 collective-permute-done.4.refs_1_
  25.3 1.8 %collective-permute-done.6.refs_3_ = bf16[1000,128]{1,0:T(8,128)(2,1)S(1)} collective-permute-done((bf16[1000,128]{1,0:T(8,128)(2,1)S(1)}, bf16[1000,128]{1,0:T(8,128)(2,1)S(1)}, u32[]{:S(2)}, u32[]{:S(2)}) %collective-permute-start.6) | collective-permute-done | bytes 256032 | tf_op jit(solution)/shard_map/ppermute | solution.py:253
  27.2 1.4 %shard_map.76 = (bf16[1000,384]{1,0:T(8,128)(2,1)S(1)}, bf16[1000,128]{1,0:T(8,128)(2,1)S(1)}, bf16[1000,128]{1,0:T(8,128)(2,1)S(1)}, bf16[1000,128]{1,0:T(8,128...) custom-call(s32[1,6]{1,0:T(1,128)S(1)} %copy-done.1, ...), custom_call_target="tpu_custom_call" | custom-call | tf_op jit(solution)/shard_map/pallas_call | solution.py:268
  28.6 2.4 %collective-permute-start.7 = (bf16[1000,128]{1,0:T(8,128)(2,1)S(1)}, bf16[1000,128]{1,0:T(8,128)(2,1)S(1)}, u32[]{:S(2)}, u32[]{:S(2)}) collective-permute-start(bf16[1000,128]{1,0:T(8,128)(2,1)S(1)} %get-tuple-element.44), channel_id=1, source_target_pairs={{3,4},{4,3},{7,8},{8,7},{11,12},{12,11},{15,16},{16,15},{19,20},{2... | collective-permute-start | bytes 768008 | tf_op jit(solution)/shard_map/ppermute | solution.py:253
  31.0 0.0 collective-permute-start.8
  31.0 2.1 %collective-permute-start.9 = (bf16[1000,128]{1,0:T(8,128)(2,1)S(1)}, bf16[1000,128]{1,0:T(8,128)(2,1)S(1)}, u32[]{:S(2)}, u32[]{:S(2)}) collective-permute-start(bf16[1000,128]{1,0:T(8,128)(2,1)S(1)} %get-tuple-element.46), channel_id=1, source_target_pairs={{1,0},{2,1},{3,2},{51,3},{5,4},{6,5},{7,6},{55,7},{9,8},{10,9},{11... | collective-permute-start | bytes 768008 | tf_op jit(solution)/shard_map/ppermute | solution.py:253
  33.2 2.2 %collective-permute-start.10 = (bf16[1000,128]{1,0:T(8,128)(2,1)S(1)}, bf16[1000,128]{1,0:T(8,128)(2,1)S(1)}, u32[]{:S(2)}, u32[]{:S(2)}) collective-permute-start(bf16[1000,128]{1,0:T(8,128)(2,1)S(1)} %get-tuple-element.47), channel_id=1, source_target_pairs={{0,2},{2,0},{1,3},{3,1},{4,6},{6,4},{5,7},{7,5},{8,10},{10,8},{9,1... | collective-permute-start | bytes 768008 | tf_op jit(solution)/shard_map/ppermute | solution.py:253
  35.4 7.6 %collective-permute-start.11 = (bf16[1000,128]{1,0:T(8,128)(2,1)S(1)}, bf16[1000,128]{1,0:T(8,128)(2,1)S(1)}, u32[]{:S(2)}, u32[]{:S(2)}) collective-permute-start(bf16[1000,128]{1,0:T(8,128)(2,1)S(1)} %get-tuple-element.48), channel_id=1, source_target_pairs={{2,4},{4,2},{3,5},{5,3},{6,8},{8,6},{7,9},{9,7},{10,12},{12,10},{1... | collective-permute-start | bytes 768008 | tf_op jit(solution)/shard_map/ppermute | solution.py:253
  43.0 5.0 %collective-permute-start.12 = (bf16[1000,128]{1,0:T(8,128)(2,1)S(1)}, bf16[1000,128]{1,0:T(8,128)(2,1)S(1)}, u32[]{:S(2)}, u32[]{:S(2)}) collective-permute-start(bf16[1000,128]{1,0:T(8,128)(2,1)S(1)} %get-tuple-element.49), channel_id=1, source_target_pairs={{0,48},{1,49},{2,50},{3,51},{4,52},{5,53},{6,54},{7,55},{8,56},{9,... | collective-permute-start | bytes 768008 | tf_op jit(solution)/shard_map/ppermute | solution.py:253
  48.0 0.0 collective-permute-done.8.refs_1_
  48.0 0.0 collective-permute-start.13
  48.0 1.0 %shard_map.77.sum_ref = f32[1000,384]{1,0:T(8,128)S(1)} custom-call(f32[1,384]{1,0:T(1,128)S(1)} %get-tuple-element.32.root_ref, s32[1,384]{1,0:T(1,128)S(1)} %get-tuple-element.33.seeds_ref, bf16[1000,384]{1,0:T(8,128)(2,1)S(1)} %get-tuple-element.34.prior_ref, bf16[1280,384]{1,0:T(8,128)(2,1)S(1)} %shard_map.74.weight_ref, ...), custom_call_target="tpu_custom_call" | custom-call | flops 589824000 | bytes 4000000 | tf_op jit(solution)/shard_map/pallas_call | solution.py:254
  49.0 0.0 collective-permute-done.10.refs_0_
  49.0 0.0 collective-permute-done.11.refs_1_
  49.0 2.2 %collective-permute-done.12.refs_2_ = bf16[1000,128]{1,0:T(8,128)(2,1)S(1)} collective-permute-done((bf16[1000,128]{1,0:T(8,128)(2,1)S(1)}, bf16[1000,128]{1,0:T(8,128)(2,1)S(1)}, u32[]{:S(2)}, u32[]{:S(2)}) %collective-permute-start.12) | collective-permute-done | bytes 256032 | tf_op jit(solution)/shard_map/ppermute | solution.py:253
  51.2 3.7 %collective-permute-done.13.refs_3_ = bf16[1000,128]{1,0:T(8,128)(2,1)S(1)} collective-permute-done((bf16[1000,128]{1,0:T(8,128)(2,1)S(1)}, bf16[1000,128]{1,0:T(8,128)(2,1)S(1)}, u32[]{:S(2)}, u32[]{:S(2)}) %collective-permute-start.13) | collective-permute-done | bytes 256032 | tf_op jit(solution)/shard_map/ppermute | solution.py:253
  54.9 1.4 %shard_map.78 = (bf16[1000,384]{1,0:T(8,128)(2,1)S(1)}, bf16[1000,128]{1,0:T(8,128)(2,1)S(1)}, bf16[1000,128]{1,0:T(8,128)(2,1)S(1)}, bf16[1000,128]{1,0:T(8,128...) custom-call(s32[1,6]{1,0:T(1,128)S(1)} %copy-done.1, ...), custom_call_target="tpu_custom_call" | custom-call | tf_op jit(solution)/shard_map/pallas_call | solution.py:268
  56.3 1.9 %collective-permute-start.14 = (bf16[1000,128]{1,0:T(8,128)(2,1)S(1)}, bf16[1000,128]{1,0:T(8,128)(2,1)S(1)}, u32[]{:S(2)}, u32[]{:S(2)}) collective-permute-start(bf16[1000,128]{1,0:T(8,128)(2,1)S(1)} %get-tuple-element.52), channel_id=1, source_target_pairs={{3,4},{4,3},{7,8},{8,7},{11,12},{12,11},{15,16},{16,15},{19,20},{2... | collective-permute-start | bytes 768008 | tf_op jit(solution)/shard_map/ppermute | solution.py:253
  58.3 0.0 collective-permute-start.15
  58.3 1.4 %collective-permute-start.16 = (bf16[1000,128]{1,0:T(8,128)(2,1)S(1)}, bf16[1000,128]{1,0:T(8,128)(2,1)S(1)}, u32[]{:S(2)}, u32[]{:S(2)}) collective-permute-start(bf16[1000,128]{1,0:T(8,128)(2,1)S(1)} %get-tuple-element.54), channel_id=1, source_target_pairs={{1,0},{2,1},{3,2},{51,3},{5,4},{6,5},{7,6},{55,7},{9,8},{10,9},{11... | collective-permute-start | bytes 768008 | tf_op jit(solution)/shard_map/ppermute | solution.py:253
  59.7 2.2 %collective-permute-start.17 = (bf16[1000,128]{1,0:T(8,128)(2,1)S(1)}, bf16[1000,128]{1,0:T(8,128)(2,1)S(1)}, u32[]{:S(2)}, u32[]{:S(2)}) collective-permute-start(bf16[1000,128]{1,0:T(8,128)(2,1)S(1)} %get-tuple-element.55), channel_id=1, source_target_pairs={{0,2},{2,0},{1,3},{3,1},{4,6},{6,4},{5,7},{7,5},{8,10},{10,8},{9,1... | collective-permute-start | bytes 768008 | tf_op jit(solution)/shard_map/ppermute | solution.py:253
  61.9 6.4 %collective-permute-start.18 = (bf16[1000,128]{1,0:T(8,128)(2,1)S(1)}, bf16[1000,128]{1,0:T(8,128)(2,1)S(1)}, u32[]{:S(2)}, u32[]{:S(2)}) collective-permute-start(bf16[1000,128]{1,0:T(8,128)(2,1)S(1)} %get-tuple-element.56), channel_id=1, source_target_pairs={{2,4},{4,2},{3,5},{5,3},{6,8},{8,6},{7,9},{9,7},{10,12},{12,10},{1... | collective-permute-start | bytes 768008 | tf_op jit(solution)/shard_map/ppermute | solution.py:253
  68.4 5.0 %collective-permute-start.19 = (bf16[1000,128]{1,0:T(8,128)(2,1)S(1)}, bf16[1000,128]{1,0:T(8,128)(2,1)S(1)}, u32[]{:S(2)}, u32[]{:S(2)}) collective-permute-start(bf16[1000,128]{1,0:T(8,128)(2,1)S(1)} %get-tuple-element.57), channel_id=1, source_target_pairs={{0,48},{1,49},{2,50},{3,51},{4,52},{5,53},{6,54},{7,55},{8,56},{9,... | collective-permute-start | bytes 768008 | tf_op jit(solution)/shard_map/ppermute | solution.py:253
  73.3 0.0 collective-permute-done.15.refs_1_
  73.3 0.0 collective-permute-start.20
  73.3 0.0 collective-permute-done.16.refs_2_
  73.3 1.0 %shard_map.79.sum_ref = f32[1000,384]{1,0:T(8,128)S(1)} custom-call(f32[1,384]{1,0:T(1,128)S(1)} %get-tuple-element.32.root_ref, s32[1,384]{1,0:T(1,128)S(1)} %get-tuple-element.33.seeds_ref, bf16[1000,384]{1,0:T(8,128)(2,1)S(1)} %get-tuple-element.34.prior_ref, bf16[1280,384]{1,0:T(8,128)(2,1)S(1)} %shard_map.74.weight_ref, ...), custom_call_target="tpu_custom_call" | custom-call | flops 589824000 | bytes 4000000 | tf_op jit(solution)/shard_map/pallas_call | solution.py:254
  74.4 0.0 collective-permute-done.18.refs_1_
  74.4 2.2 %collective-permute-done.19.refs_2_ = bf16[1000,128]{1,0:T(8,128)(2,1)S(1)} collective-permute-done((bf16[1000,128]{1,0:T(8,128)(2,1)S(1)}, bf16[1000,128]{1,0:T(8,128)(2,1)S(1)}, u32[]{:S(2)}, u32[]{:S(2)}) %collective-permute-start.19) | collective-permute-done | bytes 256032 | tf_op jit(solution)/shard_map/ppermute | solution.py:253
  76.6 3.7 %collective-permute-done.20.refs_3_ = bf16[1000,128]{1,0:T(8,128)(2,1)S(1)} collective-permute-done((bf16[1000,128]{1,0:T(8,128)(2,1)S(1)}, bf16[1000,128]{1,0:T(8,128)(2,1)S(1)}, u32[]{:S(2)}, u32[]{:S(2)}) %collective-permute-start.20) | collective-permute-done | bytes 256032 | tf_op jit(solution)/shard_map/ppermute | solution.py:253
  80.3 1.5 %shard_map.80 = f32[1000,384]{1,0:T(8,128)} custom-call(f32[1,384]{1,0:T(1,128)S(1)} %get-tuple-element.32.root_ref, bf16[1280,384]{1,0:T(8,128)(2,1)S(1)} %shard_map.74.weight_ref, f32[1000,384]{1,0:T(8,128)S(1)} %shard_map.79.sum_ref, bf16[1000,128]{1,0:T(8,128)(2,1)S(1)} %collective-permute-done.17.refs_0_, ...), custom_call_target="tpu_custom_call" | custom-call | tf_op jit(solution)/shard_map/pallas_call | solution.py:275
  (8 shorter events, 0.0 us)
Async XLA Ops:
  1.7 13.5 %collective-permute-start = (bf16[1000,128]{1,0:T(8,128)(2,1)S(1)}, bf16[1000,128]{1,0:T(8,128)(2,1)S(1)}, u32[]{:S(2)}, u32[]{:S(2)}) collective-permute-start(bf16[1000,128]{1,0:T(8,128)(2,1)S(1)} %get-tuple-element.36), channel_id=1, source_target_pairs={{3,4},{4,3},{7,8},{8,7},{11,12},{12,11},{15,16},{16,15},{19,20},{2... | collective-permute-start | bytes 768008 | tf_op jit(solution)/shard_map/ppermute | solution.py:253
  5.6 14.6 %collective-permute-start.1 = (bf16[1000,128]{1,0:T(8,128)(2,1)S(1)}, bf16[1000,128]{1,0:T(8,128)(2,1)S(1)}, u32[]{:S(2)}, u32[]{:S(2)}) collective-permute-start(bf16[1000,128]{1,0:T(8,128)(2,1)S(1)} %get-tuple-element.37), channel_id=1, source_target_pairs={{0,1},{1,2},{2,3},{3,51},{4,5},{5,6},{6,7},{7,55},{8,9},{9,10},{10... | collective-permute-start | bytes 768008 | tf_op jit(solution)/shard_map/ppermute | solution.py:253
  5.7 18.6 %collective-permute-start.2 = (bf16[1000,128]{1,0:T(8,128)(2,1)S(1)}, bf16[1000,128]{1,0:T(8,128)(2,1)S(1)}, u32[]{:S(2)}, u32[]{:S(2)}) collective-permute-start(bf16[1000,128]{1,0:T(8,128)(2,1)S(1)} %get-tuple-element.38), channel_id=1, source_target_pairs={{1,0},{2,1},{3,2},{51,3},{5,4},{6,5},{7,6},{55,7},{9,8},{10,9},{11... | collective-permute-start | bytes 768008 | tf_op jit(solution)/shard_map/ppermute | solution.py:253
  6.6 18.6 %collective-permute-start.3 = (bf16[1000,128]{1,0:T(8,128)(2,1)S(1)}, bf16[1000,128]{1,0:T(8,128)(2,1)S(1)}, u32[]{:S(2)}, u32[]{:S(2)}) collective-permute-start(bf16[1000,128]{1,0:T(8,128)(2,1)S(1)} %get-tuple-element.39), channel_id=1, source_target_pairs={{0,2},{2,0},{1,3},{3,1},{4,6},{6,4},{5,7},{7,5},{8,10},{10,8},{9,1... | collective-permute-start | bytes 768008 | tf_op jit(solution)/shard_map/ppermute | solution.py:253
  8.6 16.7 %collective-permute-start.4 = (bf16[1000,128]{1,0:T(8,128)(2,1)S(1)}, bf16[1000,128]{1,0:T(8,128)(2,1)S(1)}, u32[]{:S(2)}, u32[]{:S(2)}) collective-permute-start(bf16[1000,128]{1,0:T(8,128)(2,1)S(1)} %get-tuple-element.40), channel_id=1, source_target_pairs={{2,4},{4,2},{3,5},{5,3},{6,8},{8,6},{7,9},{9,7},{10,12},{12,10},{1... | collective-permute-start | bytes 768008 | tf_op jit(solution)/shard_map/ppermute | solution.py:253
  15.3 10.1 %collective-permute-start.5 = (bf16[1000,128]{1,0:T(8,128)(2,1)S(1)}, bf16[1000,128]{1,0:T(8,128)(2,1)S(1)}, u32[]{:S(2)}, u32[]{:S(2)}) collective-permute-start(bf16[1000,128]{1,0:T(8,128)(2,1)S(1)} %get-tuple-element.41), channel_id=1, source_target_pairs={{0,48},{1,49},{2,50},{3,51},{4,52},{5,53},{6,54},{7,55},{8,56},{9,... | collective-permute-start | bytes 768008 | tf_op jit(solution)/shard_map/ppermute | solution.py:253
  20.2 6.9 %collective-permute-start.6 = (bf16[1000,128]{1,0:T(8,128)(2,1)S(1)}, bf16[1000,128]{1,0:T(8,128)(2,1)S(1)}, u32[]{:S(2)}, u32[]{:S(2)}) collective-permute-start(bf16[1000,128]{1,0:T(8,128)(2,1)S(1)} %get-tuple-element.42), channel_id=1, source_target_pairs={{0,720},{1,721},{2,722},{3,723},{4,724},{5,725},{6,726},{7,727},{8... | collective-permute-start | bytes 768008 | tf_op jit(solution)/shard_map/ppermute | solution.py:253
  20.9 1.1 %copy-start = (bf16[3,8,128,128]{3,2,1,0:T(8,128)(2,1)S(1)}, bf16[3,8,128,128]{3,2,1,0:T(8,128)(2,1)}, u32[]{:S(2)}) copy-start(bf16[3,8,128,128]{3,2,1,0:T(8,128)(2,1)} %tiles_ref.1) | copy-start | bytes 2359300
  22.0 0.7 copy-start.2
  24.2 2.9 %copy-start.1 = (s32[1,6]{1,0:T(1,128)S(1)}, s32[1,6]{1,0:T(1,128)}, u32[]{:S(2)}) copy-start(s32[1,6]{1,0:T(1,128)} %send_ref.3) | copy-start | bytes 76
  28.6 14.4 %collective-permute-start.7 = (bf16[1000,128]{1,0:T(8,128)(2,1)S(1)}, bf16[1000,128]{1,0:T(8,128)(2,1)S(1)}, u32[]{:S(2)}, u32[]{:S(2)}) collective-permute-start(bf16[1000,128]{1,0:T(8,128)(2,1)S(1)} %get-tuple-element.44), channel_id=1, source_target_pairs={{3,4},{4,3},{7,8},{8,7},{11,12},{12,11},{15,16},{16,15},{19,20},{2... | collective-permute-start | bytes 768008 | tf_op jit(solution)/shard_map/ppermute | solution.py:253
  31.0 16.9 %collective-permute-start.8 = (bf16[1000,128]{1,0:T(8,128)(2,1)S(1)}, bf16[1000,128]{1,0:T(8,128)(2,1)S(1)}, u32[]{:S(2)}, u32[]{:S(2)}) collective-permute-start(bf16[1000,128]{1,0:T(8,128)(2,1)S(1)} %get-tuple-element.45), channel_id=1, source_target_pairs={{0,1},{1,2},{2,3},{3,51},{4,5},{5,6},{6,7},{7,55},{8,9},{9,10},{10... | collective-permute-start | bytes 768008 | tf_op jit(solution)/shard_map/ppermute | solution.py:253
  31.0 16.9 %collective-permute-start.9 = (bf16[1000,128]{1,0:T(8,128)(2,1)S(1)}, bf16[1000,128]{1,0:T(8,128)(2,1)S(1)}, u32[]{:S(2)}, u32[]{:S(2)}) collective-permute-start(bf16[1000,128]{1,0:T(8,128)(2,1)S(1)} %get-tuple-element.46), channel_id=1, source_target_pairs={{1,0},{2,1},{3,2},{51,3},{5,4},{6,5},{7,6},{55,7},{9,8},{10,9},{11... | collective-permute-start | bytes 768008 | tf_op jit(solution)/shard_map/ppermute | solution.py:253
  33.2 15.8 %collective-permute-start.10 = (bf16[1000,128]{1,0:T(8,128)(2,1)S(1)}, bf16[1000,128]{1,0:T(8,128)(2,1)S(1)}, u32[]{:S(2)}, u32[]{:S(2)}) collective-permute-start(bf16[1000,128]{1,0:T(8,128)(2,1)S(1)} %get-tuple-element.47), channel_id=1, source_target_pairs={{0,2},{2,0},{1,3},{3,1},{4,6},{6,4},{5,7},{7,5},{8,10},{10,8},{9,1... | collective-permute-start | bytes 768008 | tf_op jit(solution)/shard_map/ppermute | solution.py:253
  35.4 13.6 %collective-permute-start.11 = (bf16[1000,128]{1,0:T(8,128)(2,1)S(1)}, bf16[1000,128]{1,0:T(8,128)(2,1)S(1)}, u32[]{:S(2)}, u32[]{:S(2)}) collective-permute-start(bf16[1000,128]{1,0:T(8,128)(2,1)S(1)} %get-tuple-element.48), channel_id=1, source_target_pairs={{2,4},{4,2},{3,5},{5,3},{6,8},{8,6},{7,9},{9,7},{10,12},{12,10},{1... | collective-permute-start | bytes 768008 | tf_op jit(solution)/shard_map/ppermute | solution.py:253
  43.0 8.2 %collective-permute-start.12 = (bf16[1000,128]{1,0:T(8,128)(2,1)S(1)}, bf16[1000,128]{1,0:T(8,128)(2,1)S(1)}, u32[]{:S(2)}, u32[]{:S(2)}) collective-permute-start(bf16[1000,128]{1,0:T(8,128)(2,1)S(1)} %get-tuple-element.49), channel_id=1, source_target_pairs={{0,48},{1,49},{2,50},{3,51},{4,52},{5,53},{6,54},{7,55},{8,56},{9,... | collective-permute-start | bytes 768008 | tf_op jit(solution)/shard_map/ppermute | solution.py:253
  48.0 6.9 %collective-permute-start.13 = (bf16[1000,128]{1,0:T(8,128)(2,1)S(1)}, bf16[1000,128]{1,0:T(8,128)(2,1)S(1)}, u32[]{:S(2)}, u32[]{:S(2)}) collective-permute-start(bf16[1000,128]{1,0:T(8,128)(2,1)S(1)} %get-tuple-element.50), channel_id=1, source_target_pairs={{0,720},{1,721},{2,722},{3,723},{4,724},{5,725},{6,726},{7,727},{8... | collective-permute-start | bytes 768008 | tf_op jit(solution)/shard_map/ppermute | solution.py:253
  56.3 12.0 %collective-permute-start.14 = (bf16[1000,128]{1,0:T(8,128)(2,1)S(1)}, bf16[1000,128]{1,0:T(8,128)(2,1)S(1)}, u32[]{:S(2)}, u32[]{:S(2)}) collective-permute-start(bf16[1000,128]{1,0:T(8,128)(2,1)S(1)} %get-tuple-element.52), channel_id=1, source_target_pairs={{3,4},{4,3},{7,8},{8,7},{11,12},{12,11},{15,16},{16,15},{19,20},{2... | collective-permute-start | bytes 768008 | tf_op jit(solution)/shard_map/ppermute | solution.py:253
  58.3 15.1 %collective-permute-start.15 = (bf16[1000,128]{1,0:T(8,128)(2,1)S(1)}, bf16[1000,128]{1,0:T(8,128)(2,1)S(1)}, u32[]{:S(2)}, u32[]{:S(2)}) collective-permute-start(bf16[1000,128]{1,0:T(8,128)(2,1)S(1)} %get-tuple-element.53), channel_id=1, source_target_pairs={{0,1},{1,2},{2,3},{3,51},{4,5},{5,6},{6,7},{7,55},{8,9},{9,10},{10... | collective-permute-start | bytes 768008 | tf_op jit(solution)/shard_map/ppermute | solution.py:253
  58.3 15.0 %collective-permute-start.16 = (bf16[1000,128]{1,0:T(8,128)(2,1)S(1)}, bf16[1000,128]{1,0:T(8,128)(2,1)S(1)}, u32[]{:S(2)}, u32[]{:S(2)}) collective-permute-start(bf16[1000,128]{1,0:T(8,128)(2,1)S(1)} %get-tuple-element.54), channel_id=1, source_target_pairs={{1,0},{2,1},{3,2},{51,3},{5,4},{6,5},{7,6},{55,7},{9,8},{10,9},{11... | collective-permute-start | bytes 768008 | tf_op jit(solution)/shard_map/ppermute | solution.py:253
  59.7 14.6 %collective-permute-start.17 = (bf16[1000,128]{1,0:T(8,128)(2,1)S(1)}, bf16[1000,128]{1,0:T(8,128)(2,1)S(1)}, u32[]{:S(2)}, u32[]{:S(2)}) collective-permute-start(bf16[1000,128]{1,0:T(8,128)(2,1)S(1)} %get-tuple-element.55), channel_id=1, source_target_pairs={{0,2},{2,0},{1,3},{3,1},{4,6},{6,4},{5,7},{7,5},{8,10},{10,8},{9,1... | collective-permute-start | bytes 768008 | tf_op jit(solution)/shard_map/ppermute | solution.py:253
  61.9 12.5 %collective-permute-start.18 = (bf16[1000,128]{1,0:T(8,128)(2,1)S(1)}, bf16[1000,128]{1,0:T(8,128)(2,1)S(1)}, u32[]{:S(2)}, u32[]{:S(2)}) collective-permute-start(bf16[1000,128]{1,0:T(8,128)(2,1)S(1)} %get-tuple-element.56), channel_id=1, source_target_pairs={{2,4},{4,2},{3,5},{5,3},{6,8},{8,6},{7,9},{9,7},{10,12},{12,10},{1... | collective-permute-start | bytes 768008 | tf_op jit(solution)/shard_map/ppermute | solution.py:253
  68.4 8.2 %collective-permute-start.19 = (bf16[1000,128]{1,0:T(8,128)(2,1)S(1)}, bf16[1000,128]{1,0:T(8,128)(2,1)S(1)}, u32[]{:S(2)}, u32[]{:S(2)}) collective-permute-start(bf16[1000,128]{1,0:T(8,128)(2,1)S(1)} %get-tuple-element.57), channel_id=1, source_target_pairs={{0,48},{1,49},{2,50},{3,51},{4,52},{5,53},{6,54},{7,55},{8,56},{9,... | collective-permute-start | bytes 768008 | tf_op jit(solution)/shard_map/ppermute | solution.py:253
  73.3 6.9 %collective-permute-start.20 = (bf16[1000,128]{1,0:T(8,128)(2,1)S(1)}, bf16[1000,128]{1,0:T(8,128)(2,1)S(1)}, u32[]{:S(2)}, u32[]{:S(2)}) collective-permute-start(bf16[1000,128]{1,0:T(8,128)(2,1)S(1)} %get-tuple-element.58), channel_id=1, source_target_pairs={{0,720},{1,721},{2,722},{3,723},{4,724},{5,725},{6,726},{7,727},{8... | collective-permute-start | bytes 768008 | tf_op jit(solution)/shard_map/ppermute | solution.py:253

commit v10 on v9

--- a/solution.py
+++ b/solution.py
@@ -17,7 +17,7 @@
 HBM = pl.BlockSpec(memory_space=pltpu.HBM)
 PARAMS = pltpu.CompilerParams(vmem_limit_bytes=40 * 1024 * 1024)
 
-EDGE, RING, BACK, TWO, CROSS, UP, DOWN = range(7)
+BACK, EDGE, RING, TWO, CROSS, UP, DOWN = range(7)
 PERMUTES = 7
 EARLY = 3
 

time: 82.2 us -> 81.4 us (level)
  the two profiles are of different devices: /device:TPU:95 before, /device:TPU:479 now
where the time goes in v10:
time: 81.4 us; the launch traced here: 81 us
  starting transfers between devices  47.5 us (58%)
  waiting for transfers between devices  20.2 us (25%)
  Pallas kernels  10.7 us (13%)
  local copies, waits for them, and re-layouts  1.82 us (2%)
  between operations  0.87 us (1%)
    ppermute x21, starting transfers between devices, on_device(): lax.ppermute(sends[k], ('group', 'dom'), route[k])  47.5 us
    ppermute x21, waiting for transfers between devices, on_device(): lax.ppermute(sends[k], ('group', 'dom'), route[k])  20.2 us
    pallas_call x3, Pallas kernels, on_device(): pl.pallas_call(functools.partial(early_kernel, step == ITERS - 1), in_spe...  3.11 us
    pallas_call x2, Pallas kernels, on_device(): pl.pallas_call(step_kernel, in_specs=[SMEM] + [VMEM] * (3 + len(late)), o...  2.88 us
    unnamed x6, local copies, waits for them, and re-layouts  1.82 us
    pallas_call x1, Pallas kernels, on_device(): pl.pallas_call(prepare_kernel, in_specs=[HBM] * 4, out_specs=[VMEM] * (4...  1.71 us
  transfers between devices with their start and end apart: 21, of which 7 were waited for; matrix products, arithmetic and copies ran while one was open for 0% of the time, Pallas kernels for 6%

profile of v10, /device:TPU:479, one launch (start us, length us, event | category | flops | bytes accessed | tf_op | source)
XLA Modules:
  0.0 81.0 jit_solution(2943897427265959564)
XLA Ops:
  0.0 1.7 %shard_map.73 = (f32[1,384]{1,0:T(1,128)S(1)}, s32[1,384]{1,0:T(1,128)S(1)}, bf16[1000,384]{1,0:T(8,128)(2,1)S(1)}, bf16[1000,384]{1,0:T(8,128)(2,1)S(1)}, bf16[...) custom-call(s32[1,6]{1,0:T(1,128)} %send_ref.3, ...), custom_call_target="tpu_custom_call" | custom-call | tf_op jit(solution)/shard_map/pallas_call | solution.py:223
  1.7 0.7 collective-permute-start
  2.4 3.5 %collective-permute-start.1 = (bf16[1000,128]{1,0:T(8,128)(2,1)S(1)}, bf16[1000,128]{1,0:T(8,128)(2,1)S(1)}, u32[]{:S(2)}, u32[]{:S(2)}) collective-permute-start(bf16[1000,128]{1,0:T(8,128)(2,1)S(1)} %get-tuple-element.37), channel_id=1, source_target_pairs={{3,4},{4,3},{7,8},{8,7},{11,12},{12,11},{15,16},{16,15},{19,20},{2... | collective-permute-start | bytes 768008 | tf_op jit(solution)/shard_map/ppermute | solution.py:253
  6.0 0.0 collective-permute-start.2
  6.0 3.5 %collective-permute-start.3 = (bf16[1000,128]{1,0:T(8,128)(2,1)S(1)}, bf16[1000,128]{1,0:T(8,128)(2,1)S(1)}, u32[]{:S(2)}, u32[]{:S(2)}) collective-permute-start(bf16[1000,128]{1,0:T(8,128)(2,1)S(1)} %get-tuple-element.39), channel_id=1, source_target_pairs={{0,2},{2,0},{1,3},{3,1},{4,6},{6,4},{5,7},{7,5},{8,10},{10,8},{9,1... | collective-permute-start | bytes 768008 | tf_op jit(solution)/shard_map/ppermute | solution.py:253
  9.5 4.6 %collective-permute-start.4 = (bf16[1000,128]{1,0:T(8,128)(2,1)S(1)}, bf16[1000,128]{1,0:T(8,128)(2,1)S(1)}, u32[]{:S(2)}, u32[]{:S(2)}) collective-permute-start(bf16[1000,128]{1,0:T(8,128)(2,1)S(1)} %get-tuple-element.40), channel_id=1, source_target_pairs={{2,4},{4,2},{3,5},{5,3},{6,8},{8,6},{7,9},{9,7},{10,12},{12,10},{1... | collective-permute-start | bytes 768008 | tf_op jit(solution)/shard_map/ppermute | solution.py:253
  14.1 0.0 collective-permute-done.refs_0_
  14.1 3.0 %collective-permute-start.5 = (bf16[1000,128]{1,0:T(8,128)(2,1)S(1)}, bf16[1000,128]{1,0:T(8,128)(2,1)S(1)}, u32[]{:S(2)}, u32[]{:S(2)}) collective-permute-start(bf16[1000,128]{1,0:T(8,128)(2,1)S(1)} %get-tuple-element.41), channel_id=1, source_target_pairs={{0,48},{1,49},{2,50},{3,51},{4,52},{5,53},{6,54},{7,55},{8,56},{9,... | collective-permute-start | bytes 768008 | tf_op jit(solution)/shard_map/ppermute | solution.py:253
  17.2 0.0 collective-permute-done.1.refs_1_
  17.2 1.7 %collective-permute-start.6 = (bf16[1000,128]{1,0:T(8,128)(2,1)S(1)}, bf16[1000,128]{1,0:T(8,128)(2,1)S(1)}, u32[]{:S(2)}, u32[]{:S(2)}) collective-permute-start(bf16[1000,128]{1,0:T(8,128)(2,1)S(1)} %get-tuple-element.42), channel_id=1, source_target_pairs={{0,720},{1,721},{2,722},{3,723},{4,724},{5,725},{6,726},{7,727},{8... | collective-permute-start | bytes 768008 | tf_op jit(solution)/shard_map/ppermute | solution.py:253
  19.5 0.0 copy-start
  19.5 1.1 %copy-done = bf16[3,8,128,128]{3,2,1,0:T(8,128)(2,1)S(1)} copy-done((bf16[3,8,128,128]{3,2,1,0:T(8,128)(2,1)S(1)}, bf16[3,8,128,128]{3,2,1,0:T(8,128)(2,1)}, u32[]{:S(2)}) %copy-start) | copy-done | bytes 786456
  20.7 0.7 copy-done.2
  21.3 1.5 %shard_map.74.weight_ref = bf16[1280,384]{1,0:T(8,128)(2,1)S(1)} custom-call(s32[3,8]{1,0:T(4,128)S(1)} %copy-done.2, s32[1]{0:T(128)S(6)} %copy.8.count_ref, bf16[3,8,128,128]{3,2,1,0:T(8,128)(2,1)S(1)} %copy-done), custom_call_target="tpu_custom_call" | custom-call | bytes 8000000 | tf_op jit(solution)/shard_map/pallas_call | solution.py:243
  22.9 0.0 collective-permute-done.2.refs_2_
  22.9 0.0 copy-start.1
  22.9 1.0 %shard_map.75.sum_ref = f32[1000,384]{1,0:T(8,128)S(1)} custom-call(f32[1,384]{1,0:T(1,128)S(1)} %get-tuple-element.32.root_ref, s32[1,384]{1,0:T(1,128)S(1)} %get-tuple-element.33.seeds_ref, bf16[1000,384]{1,0:T(8,128)(2,1)S(1)} %get-tuple-element.34.prior_ref, bf16[1280,384]{1,0:T(8,128)(2,1)S(1)} %shard_map.74.weight_ref, ...), custom_call_target="tpu_custom_call" | custom-call | flops 589824000 | bytes 4000000 | tf_op jit(solution)/shard_map/pallas_call | solution.py:254
  23.9 1.9 %collective-permute-done.3.refs_0_ = bf16[1000,128]{1,0:T(8,128)(2,1)S(1)} collective-permute-done((bf16[1000,128]{1,0:T(8,128)(2,1)S(1)}, bf16[1000,128]{1,0:T(8,128)(2,1)S(1)}, u32[]{:S(2)}, u32[]{:S(2)}) %collective-permute-start.3) | collective-permute-done | bytes 256032 | tf_op jit(solution)/shard_map/ppermute | solution.py:253
  25.8 0.0 collective-permute-done.4.refs_1_
  25.8 0.0 collective-permute-done.5.refs_2_
  25.8 0.0 collective-permute-done.6.refs_3_
  25.8 1.4 %shard_map.76 = (bf16[1000,384]{1,0:T(8,128)(2,1)S(1)}, bf16[1000,128]{1,0:T(8,128)(2,1)S(1)}, bf16[1000,128]{1,0:T(8,128)(2,1)S(1)}, bf16[1000,128]{1,0:T(8,128...) custom-call(s32[1,6]{1,0:T(1,128)S(1)} %copy-done.1, ...), custom_call_target="tpu_custom_call" | custom-call | tf_op jit(solution)/shard_map/pallas_call | solution.py:268
  27.3 1.4 %collective-permute-start.7 = (bf16[1000,128]{1,0:T(8,128)(2,1)S(1)}, bf16[1000,128]{1,0:T(8,128)(2,1)S(1)}, u32[]{:S(2)}, u32[]{:S(2)}) collective-permute-start(bf16[1000,128]{1,0:T(8,128)(2,1)S(1)} %get-tuple-element.44), channel_id=1, source_target_pairs={{1,0},{2,1},{3,2},{51,3},{5,4},{6,5},{7,6},{55,7},{9,8},{10,9},{11... | collective-permute-start | bytes 768008 | tf_op jit(solution)/shard_map/ppermute | solution.py:253
  28.7 2.7 %collective-permute-start.8 = (bf16[1000,128]{1,0:T(8,128)(2,1)S(1)}, bf16[1000,128]{1,0:T(8,128)(2,1)S(1)}, u32[]{:S(2)}, u32[]{:S(2)}) collective-permute-start(bf16[1000,128]{1,0:T(8,128)(2,1)S(1)} %get-tuple-element.45), channel_id=1, source_target_pairs={{3,4},{4,3},{7,8},{8,7},{11,12},{12,11},{15,16},{16,15},{19,20},{2... | collective-permute-start | bytes 768008 | tf_op jit(solution)/shard_map/ppermute | solution.py:253
  31.3 0.0 collective-permute-start.9
  31.4 3.2 %collective-permute-start.10 = (bf16[1000,128]{1,0:T(8,128)(2,1)S(1)}, bf16[1000,128]{1,0:T(8,128)(2,1)S(1)}, u32[]{:S(2)}, u32[]{:S(2)}) collective-permute-start(bf16[1000,128]{1,0:T(8,128)(2,1)S(1)} %get-tuple-element.47), channel_id=1, source_target_pairs={{0,2},{2,0},{1,3},{3,1},{4,6},{6,4},{5,7},{7,5},{8,10},{10,8},{9,1... | collective-permute-start | bytes 768008 | tf_op jit(solution)/shard_map/ppermute | solution.py:253
  34.5 5.9 %collective-permute-start.11 = (bf16[1000,128]{1,0:T(8,128)(2,1)S(1)}, bf16[1000,128]{1,0:T(8,128)(2,1)S(1)}, u32[]{:S(2)}, u32[]{:S(2)}) collective-permute-start(bf16[1000,128]{1,0:T(8,128)(2,1)S(1)} %get-tuple-element.48), channel_id=1, source_target_pairs={{2,4},{4,2},{3,5},{5,3},{6,8},{8,6},{7,9},{9,7},{10,12},{12,10},{1... | collective-permute-start | bytes 768008 | tf_op jit(solution)/shard_map/ppermute | solution.py:253
  40.4 0.0 collective-permute-done.7.refs_0_
  40.4 1.6 %collective-permute-start.12 = (bf16[1000,128]{1,0:T(8,128)(2,1)S(1)}, bf16[1000,128]{1,0:T(8,128)(2,1)S(1)}, u32[]{:S(2)}, u32[]{:S(2)}) collective-permute-start(bf16[1000,128]{1,0:T(8,128)(2,1)S(1)} %get-tuple-element.49), channel_id=1, source_target_pairs={{0,48},{1,49},{2,50},{3,51},{4,52},{5,53},{6,54},{7,55},{8,56},{9,... | collective-permute-start | bytes 768008 | tf_op jit(solution)/shard_map/ppermute | solution.py:253
  42.0 2.5 %collective-permute-done.8.refs_1_ = bf16[1000,128]{1,0:T(8,128)(2,1)S(1)} collective-permute-done((bf16[1000,128]{1,0:T(8,128)(2,1)S(1)}, bf16[1000,128]{1,0:T(8,128)(2,1)S(1)}, u32[]{:S(2)}, u32[]{:S(2)}) %collective-permute-start.8) | collective-permute-done | bytes 256032 | tf_op jit(solution)/shard_map/ppermute | solution.py:253
  44.4 1.5 %collective-permute-start.13 = (bf16[1000,128]{1,0:T(8,128)(2,1)S(1)}, bf16[1000,128]{1,0:T(8,128)(2,1)S(1)}, u32[]{:S(2)}, u32[]{:S(2)}) collective-permute-start(bf16[1000,128]{1,0:T(8,128)(2,1)S(1)} %get-tuple-element.50), channel_id=1, source_target_pairs={{0,720},{1,721},{2,722},{3,723},{4,724},{5,725},{6,726},{7,727},{8... | collective-permute-start | bytes 768008 | tf_op jit(solution)/shard_map/ppermute | solution.py:253
  46.0 1.0 %shard_map.77.sum_ref = f32[1000,384]{1,0:T(8,128)S(1)} custom-call(f32[1,384]{1,0:T(1,128)S(1)} %get-tuple-element.32.root_ref, s32[1,384]{1,0:T(1,128)S(1)} %get-tuple-element.33.seeds_ref, bf16[1000,384]{1,0:T(8,128)(2,1)S(1)} %get-tuple-element.34.prior_ref, bf16[1280,384]{1,0:T(8,128)(2,1)S(1)} %shard_map.74.weight_ref, ...), custom_call_target="tpu_custom_call" | custom-call | flops 589824000 | bytes 4000000 | tf_op jit(solution)/shard_map/pallas_call | solution.py:254
  47.0 4.6 %collective-permute-done.10.refs_0_ = bf16[1000,128]{1,0:T(8,128)(2,1)S(1)} collective-permute-done((bf16[1000,128]{1,0:T(8,128)(2,1)S(1)}, bf16[1000,128]{1,0:T(8,128)(2,1)S(1)}, u32[]{:S(2)}, u32[]{:S(2)}) %collective-permute-start.10) | collective-permute-done | bytes 256032 | tf_op jit(solution)/shard_map/ppermute | solution.py:253
  51.6 0.0 collective-permute-done.12.refs_2_
  51.6 1.1 %collective-permute-done.13.refs_3_ = bf16[1000,128]{1,0:T(8,128)(2,1)S(1)} collective-permute-done((bf16[1000,128]{1,0:T(8,128)(2,1)S(1)}, bf16[1000,128]{1,0:T(8,128)(2,1)S(1)}, u32[]{:S(2)}, u32[]{:S(2)}) %collective-permute-start.13) | collective-permute-done | bytes 256032 | tf_op jit(solution)/shard_map/ppermute | solution.py:253
  52.7 1.4 %shard_map.78 = (bf16[1000,384]{1,0:T(8,128)(2,1)S(1)}, bf16[1000,128]{1,0:T(8,128)(2,1)S(1)}, bf16[1000,128]{1,0:T(8,128)(2,1)S(1)}, bf16[1000,128]{1,0:T(8,128...) custom-call(s32[1,6]{1,0:T(1,128)S(1)} %copy-done.1, ...), custom_call_target="tpu_custom_call" | custom-call | tf_op jit(solution)/shard_map/pallas_call | solution.py:268
  54.1 0.8 collective-permute-start.14
  54.9 1.9 %collective-permute-start.15 = (bf16[1000,128]{1,0:T(8,128)(2,1)S(1)}, bf16[1000,128]{1,0:T(8,128)(2,1)S(1)}, u32[]{:S(2)}, u32[]{:S(2)}) collective-permute-start(bf16[1000,128]{1,0:T(8,128)(2,1)S(1)} %get-tuple-element.53), channel_id=1, source_target_pairs={{3,4},{4,3},{7,8},{8,7},{11,12},{12,11},{15,16},{16,15},{19,20},{2... | collective-permute-start | bytes 768008 | tf_op jit(solution)/shard_map/ppermute | solution.py:253
  56.8 0.0 collective-permute-start.16
  56.9 2.7 %collective-permute-start.17 = (bf16[1000,128]{1,0:T(8,128)(2,1)S(1)}, bf16[1000,128]{1,0:T(8,128)(2,1)S(1)}, u32[]{:S(2)}, u32[]{:S(2)}) collective-permute-start(bf16[1000,128]{1,0:T(8,128)(2,1)S(1)} %get-tuple-element.55), channel_id=1, source_target_pairs={{0,2},{2,0},{1,3},{3,1},{4,6},{6,4},{5,7},{7,5},{8,10},{10,8},{9,1... | collective-permute-start | bytes 768008 | tf_op jit(solution)/shard_map/ppermute | solution.py:253
  59.6 7.1 %collective-permute-start.18 = (bf16[1000,128]{1,0:T(8,128)(2,1)S(1)}, bf16[1000,128]{1,0:T(8,128)(2,1)S(1)}, u32[]{:S(2)}, u32[]{:S(2)}) collective-permute-start(bf16[1000,128]{1,0:T(8,128)(2,1)S(1)} %get-tuple-element.56), channel_id=1, source_target_pairs={{2,4},{4,2},{3,5},{5,3},{6,8},{8,6},{7,9},{9,7},{10,12},{12,10},{1... | collective-permute-start | bytes 768008 | tf_op jit(solution)/shard_map/ppermute | solution.py:253
  66.6 0.0 collective-permute-start.19
  66.7 4.9 %collective-permute-done.15.refs_1_ = bf16[1000,128]{1,0:T(8,128)(2,1)S(1)} collective-permute-done((bf16[1000,128]{1,0:T(8,128)(2,1)S(1)}, bf16[1000,128]{1,0:T(8,128)(2,1)S(1)}, u32[]{:S(2)}, u32[]{:S(2)}) %collective-permute-start.15) | collective-permute-done | bytes 256032 | tf_op jit(solution)/shard_map/ppermute | solution.py:253
  71.5 1.6 %collective-permute-start.20 = (bf16[1000,128]{1,0:T(8,128)(2,1)S(1)}, bf16[1000,128]{1,0:T(8,128)(2,1)S(1)}, u32[]{:S(2)}, u32[]{:S(2)}) collective-permute-start(bf16[1000,128]{1,0:T(8,128)(2,1)S(1)} %get-tuple-element.58), channel_id=1, source_target_pairs={{0,720},{1,721},{2,722},{3,723},{4,724},{5,725},{6,726},{7,727},{8... | collective-permute-start | bytes 768008 | tf_op jit(solution)/shard_map/ppermute | solution.py:253
  73.2 1.0 %shard_map.79.sum_ref = f32[1000,384]{1,0:T(8,128)S(1)} custom-call(f32[1,384]{1,0:T(1,128)S(1)} %get-tuple-element.32.root_ref, s32[1,384]{1,0:T(1,128)S(1)} %get-tuple-element.33.seeds_ref, bf16[1000,384]{1,0:T(8,128)(2,1)S(1)} %get-tuple-element.34.prior_ref, bf16[1280,384]{1,0:T(8,128)(2,1)S(1)} %shard_map.74.weight_ref, ...), custom_call_target="tpu_custom_call" | custom-call | flops 589824000 | bytes 4000000 | tf_op jit(solution)/shard_map/pallas_call | solution.py:254
  74.2 3.7 %collective-permute-done.17.refs_0_ = bf16[1000,128]{1,0:T(8,128)(2,1)S(1)} collective-permute-done((bf16[1000,128]{1,0:T(8,128)(2,1)S(1)}, bf16[1000,128]{1,0:T(8,128)(2,1)S(1)}, u32[]{:S(2)}, u32[]{:S(2)}) %collective-permute-start.17) | collective-permute-done | bytes 256032 | tf_op jit(solution)/shard_map/ppermute | solution.py:253
  77.9 1.6 %collective-permute-done.20.refs_3_ = bf16[1000,128]{1,0:T(8,128)(2,1)S(1)} collective-permute-done((bf16[1000,128]{1,0:T(8,128)(2,1)S(1)}, bf16[1000,128]{1,0:T(8,128)(2,1)S(1)}, u32[]{:S(2)}, u32[]{:S(2)}) %collective-permute-start.20) | collective-permute-done | bytes 256032 | tf_op jit(solution)/shard_map/ppermute | solution.py:253
  79.5 1.5 %shard_map.80 = f32[1000,384]{1,0:T(8,128)} custom-call(f32[1,384]{1,0:T(1,128)S(1)} %get-tuple-element.32.root_ref, bf16[1280,384]{1,0:T(8,128)(2,1)S(1)} %shard_map.74.weight_ref, f32[1000,384]{1,0:T(8,128)S(1)} %shard_map.79.sum_ref, bf16[1000,128]{1,0:T(8,128)(2,1)S(1)} %collective-permute-done.17.refs_0_, ...), custom_call_target="tpu_custom_call" | custom-call | tf_op jit(solution)/shard_map/pallas_call | solution.py:275
  (8 shorter events, 0.0 us)
Async XLA Ops:
  1.7 12.4 %collective-permute-start = (bf16[1000,128]{1,0:T(8,128)(2,1)S(1)}, bf16[1000,128]{1,0:T(8,128)(2,1)S(1)}, u32[]{:S(2)}, u32[]{:S(2)}) collective-permute-start(bf16[1000,128]{1,0:T(8,128)(2,1)S(1)} %get-tuple-element.36), channel_id=1, source_target_pairs={{1,0},{2,1},{3,2},{51,3},{5,4},{6,5},{7,6},{55,7},{9,8},{10,9},{11... | collective-permute-start | bytes 768008 | tf_op jit(solution)/shard_map/ppermute | solution.py:253
  2.4 14.8 %collective-permute-start.1 = (bf16[1000,128]{1,0:T(8,128)(2,1)S(1)}, bf16[1000,128]{1,0:T(8,128)(2,1)S(1)}, u32[]{:S(2)}, u32[]{:S(2)}) collective-permute-start(bf16[1000,128]{1,0:T(8,128)(2,1)S(1)} %get-tuple-element.37), channel_id=1, source_target_pairs={{3,4},{4,3},{7,8},{8,7},{11,12},{12,11},{15,16},{16,15},{19,20},{2... | collective-permute-start | bytes 768008 | tf_op jit(solution)/shard_map/ppermute | solution.py:253
  6.0 16.9 %collective-permute-start.2 = (bf16[1000,128]{1,0:T(8,128)(2,1)S(1)}, bf16[1000,128]{1,0:T(8,128)(2,1)S(1)}, u32[]{:S(2)}, u32[]{:S(2)}) collective-permute-start(bf16[1000,128]{1,0:T(8,128)(2,1)S(1)} %get-tuple-element.38), channel_id=1, source_target_pairs={{0,1},{1,2},{2,3},{3,51},{4,5},{5,6},{6,7},{7,55},{8,9},{9,10},{10... | collective-permute-start | bytes 768008 | tf_op jit(solution)/shard_map/ppermute | solution.py:253
  6.0 19.8 %collective-permute-start.3 = (bf16[1000,128]{1,0:T(8,128)(2,1)S(1)}, bf16[1000,128]{1,0:T(8,128)(2,1)S(1)}, u32[]{:S(2)}, u32[]{:S(2)}) collective-permute-start(bf16[1000,128]{1,0:T(8,128)(2,1)S(1)} %get-tuple-element.39), channel_id=1, source_target_pairs={{0,2},{2,0},{1,3},{3,1},{4,6},{6,4},{5,7},{7,5},{8,10},{10,8},{9,1... | collective-permute-start | bytes 768008 | tf_op jit(solution)/shard_map/ppermute | solution.py:253
  9.5 16.3 %collective-permute-start.4 = (bf16[1000,128]{1,0:T(8,128)(2,1)S(1)}, bf16[1000,128]{1,0:T(8,128)(2,1)S(1)}, u32[]{:S(2)}, u32[]{:S(2)}) collective-permute-start(bf16[1000,128]{1,0:T(8,128)(2,1)S(1)} %get-tuple-element.40), channel_id=1, source_target_pairs={{2,4},{4,2},{3,5},{5,3},{6,8},{8,6},{7,9},{9,7},{10,12},{12,10},{1... | collective-permute-start | bytes 768008 | tf_op jit(solution)/shard_map/ppermute | solution.py:253
  14.1 11.7 %collective-permute-start.5 = (bf16[1000,128]{1,0:T(8,128)(2,1)S(1)}, bf16[1000,128]{1,0:T(8,128)(2,1)S(1)}, u32[]{:S(2)}, u32[]{:S(2)}) collective-permute-start(bf16[1000,128]{1,0:T(8,128)(2,1)S(1)} %get-tuple-element.41), channel_id=1, source_target_pairs={{0,48},{1,49},{2,50},{3,51},{4,52},{5,53},{6,54},{7,55},{8,56},{9,... | collective-permute-start | bytes 768008 | tf_op jit(solution)/shard_map/ppermute | solution.py:253
  17.2 8.6 %collective-permute-start.6 = (bf16[1000,128]{1,0:T(8,128)(2,1)S(1)}, bf16[1000,128]{1,0:T(8,128)(2,1)S(1)}, u32[]{:S(2)}, u32[]{:S(2)}) collective-permute-start(bf16[1000,128]{1,0:T(8,128)(2,1)S(1)} %get-tuple-element.42), channel_id=1, source_target_pairs={{0,720},{1,721},{2,722},{3,723},{4,724},{5,725},{6,726},{7,727},{8... | collective-permute-start | bytes 768008 | tf_op jit(solution)/shard_map/ppermute | solution.py:253
  19.5 1.1 %copy-start = (bf16[3,8,128,128]{3,2,1,0:T(8,128)(2,1)S(1)}, bf16[3,8,128,128]{3,2,1,0:T(8,128)(2,1)}, u32[]{:S(2)}) copy-start(bf16[3,8,128,128]{3,2,1,0:T(8,128)(2,1)} %tiles_ref.1) | copy-start | bytes 2359300
  20.7 0.7 copy-start.2
  22.9 2.9 %copy-start.1 = (s32[1,6]{1,0:T(1,128)S(1)}, s32[1,6]{1,0:T(1,128)}, u32[]{:S(2)}) copy-start(s32[1,6]{1,0:T(1,128)} %send_ref.3) | copy-start | bytes 76
  27.3 13.1 %collective-permute-start.7 = (bf16[1000,128]{1,0:T(8,128)(2,1)S(1)}, bf16[1000,128]{1,0:T(8,128)(2,1)S(1)}, u32[]{:S(2)}, u32[]{:S(2)}) collective-permute-start(bf16[1000,128]{1,0:T(8,128)(2,1)S(1)} %get-tuple-element.44), channel_id=1, source_target_pairs={{1,0},{2,1},{3,2},{51,3},{5,4},{6,5},{7,6},{55,7},{9,8},{10,9},{11... | collective-permute-start | bytes 768008 | tf_op jit(solution)/shard_map/ppermute | solution.py:253
  28.7 15.8 %collective-permute-start.8 = (bf16[1000,128]{1,0:T(8,128)(2,1)S(1)}, bf16[1000,128]{1,0:T(8,128)(2,1)S(1)}, u32[]{:S(2)}, u32[]{:S(2)}) collective-permute-start(bf16[1000,128]{1,0:T(8,128)(2,1)S(1)} %get-tuple-element.45), channel_id=1, source_target_pairs={{3,4},{4,3},{7,8},{8,7},{11,12},{12,11},{15,16},{16,15},{19,20},{2... | collective-permute-start | bytes 768008 | tf_op jit(solution)/shard_map/ppermute | solution.py:253
  31.3 14.7 %collective-permute-start.9 = (bf16[1000,128]{1,0:T(8,128)(2,1)S(1)}, bf16[1000,128]{1,0:T(8,128)(2,1)S(1)}, u32[]{:S(2)}, u32[]{:S(2)}) collective-permute-start(bf16[1000,128]{1,0:T(8,128)(2,1)S(1)} %get-tuple-element.46), channel_id=1, source_target_pairs={{0,1},{1,2},{2,3},{3,51},{4,5},{5,6},{6,7},{7,55},{8,9},{9,10},{10... | collective-permute-start | bytes 768008 | tf_op jit(solution)/shard_map/ppermute | solution.py:253
  31.4 20.2 %collective-permute-start.10 = (bf16[1000,128]{1,0:T(8,128)(2,1)S(1)}, bf16[1000,128]{1,0:T(8,128)(2,1)S(1)}, u32[]{:S(2)}, u32[]{:S(2)}) collective-permute-start(bf16[1000,128]{1,0:T(8,128)(2,1)S(1)} %get-tuple-element.47), channel_id=1, source_target_pairs={{0,2},{2,0},{1,3},{3,1},{4,6},{6,4},{5,7},{7,5},{8,10},{10,8},{9,1... | collective-permute-start | bytes 768008 | tf_op jit(solution)/shard_map/ppermute | solution.py:253
  34.5 17.1 %collective-permute-start.11 = (bf16[1000,128]{1,0:T(8,128)(2,1)S(1)}, bf16[1000,128]{1,0:T(8,128)(2,1)S(1)}, u32[]{:S(2)}, u32[]{:S(2)}) collective-permute-start(bf16[1000,128]{1,0:T(8,128)(2,1)S(1)} %get-tuple-element.48), channel_id=1, source_target_pairs={{2,4},{4,2},{3,5},{5,3},{6,8},{8,6},{7,9},{9,7},{10,12},{12,10},{1... | collective-permute-start | bytes 768008 | tf_op jit(solution)/shard_map/ppermute | solution.py:253
  40.4 11.2 %collective-permute-start.12 = (bf16[1000,128]{1,0:T(8,128)(2,1)S(1)}, bf16[1000,128]{1,0:T(8,128)(2,1)S(1)}, u32[]{:S(2)}, u32[]{:S(2)}) collective-permute-start(bf16[1000,128]{1,0:T(8,128)(2,1)S(1)} %get-tuple-element.49), channel_id=1, source_target_pairs={{0,48},{1,49},{2,50},{3,51},{4,52},{5,53},{6,54},{7,55},{8,56},{9,... | collective-permute-start | bytes 768008 | tf_op jit(solution)/shard_map/ppermute | solution.py:253
  44.4 8.2 %collective-permute-start.13 = (bf16[1000,128]{1,0:T(8,128)(2,1)S(1)}, bf16[1000,128]{1,0:T(8,128)(2,1)S(1)}, u32[]{:S(2)}, u32[]{:S(2)}) collective-permute-start(bf16[1000,128]{1,0:T(8,128)(2,1)S(1)} %get-tuple-element.50), channel_id=1, source_target_pairs={{0,720},{1,721},{2,722},{3,723},{4,724},{5,725},{6,726},{7,727},{8... | collective-permute-start | bytes 768008 | tf_op jit(solution)/shard_map/ppermute | solution.py:253
  54.1 12.5 %collective-permute-start.14 = (bf16[1000,128]{1,0:T(8,128)(2,1)S(1)}, bf16[1000,128]{1,0:T(8,128)(2,1)S(1)}, u32[]{:S(2)}, u32[]{:S(2)}) collective-permute-start(bf16[1000,128]{1,0:T(8,128)(2,1)S(1)} %get-tuple-element.52), channel_id=1, source_target_pairs={{1,0},{2,1},{3,2},{51,3},{5,4},{6,5},{7,6},{55,7},{9,8},{10,9},{11... | collective-permute-start | bytes 768008 | tf_op jit(solution)/shard_map/ppermute | solution.py:253
  54.9 16.6 %collective-permute-start.15 = (bf16[1000,128]{1,0:T(8,128)(2,1)S(1)}, bf16[1000,128]{1,0:T(8,128)(2,1)S(1)}, u32[]{:S(2)}, u32[]{:S(2)}) collective-permute-start(bf16[1000,128]{1,0:T(8,128)(2,1)S(1)} %get-tuple-element.53), channel_id=1, source_target_pairs={{3,4},{4,3},{7,8},{8,7},{11,12},{12,11},{15,16},{16,15},{19,20},{2... | collective-permute-start | bytes 768008 | tf_op jit(solution)/shard_map/ppermute | solution.py:253
  56.8 16.3 %collective-permute-start.16 = (bf16[1000,128]{1,0:T(8,128)(2,1)S(1)}, bf16[1000,128]{1,0:T(8,128)(2,1)S(1)}, u32[]{:S(2)}, u32[]{:S(2)}) collective-permute-start(bf16[1000,128]{1,0:T(8,128)(2,1)S(1)} %get-tuple-element.54), channel_id=1, source_target_pairs={{0,1},{1,2},{2,3},{3,51},{4,5},{5,6},{6,7},{7,55},{8,9},{9,10},{10... | collective-permute-start | bytes 768008 | tf_op jit(solution)/shard_map/ppermute | solution.py:253
  56.9 21.0 %collective-permute-start.17 = (bf16[1000,128]{1,0:T(8,128)(2,1)S(1)}, bf16[1000,128]{1,0:T(8,128)(2,1)S(1)}, u32[]{:S(2)}, u32[]{:S(2)}) collective-permute-start(bf16[1000,128]{1,0:T(8,128)(2,1)S(1)} %get-tuple-element.55), channel_id=1, source_target_pairs={{0,2},{2,0},{1,3},{3,1},{4,6},{6,4},{5,7},{7,5},{8,10},{10,8},{9,1... | collective-permute-start | bytes 768008 | tf_op jit(solution)/shard_map/ppermute | solution.py:253
  59.6 18.3 %collective-permute-start.18 = (bf16[1000,128]{1,0:T(8,128)(2,1)S(1)}, bf16[1000,128]{1,0:T(8,128)(2,1)S(1)}, u32[]{:S(2)}, u32[]{:S(2)}) collective-permute-start(bf16[1000,128]{1,0:T(8,128)(2,1)S(1)} %get-tuple-element.56), channel_id=1, source_target_pairs={{2,4},{4,2},{3,5},{5,3},{6,8},{8,6},{7,9},{9,7},{10,12},{12,10},{1... | collective-permute-start | bytes 768008 | tf_op jit(solution)/shard_map/ppermute | solution.py:253
  66.6 11.3 %collective-permute-start.19 = (bf16[1000,128]{1,0:T(8,128)(2,1)S(1)}, bf16[1000,128]{1,0:T(8,128)(2,1)S(1)}, u32[]{:S(2)}, u32[]{:S(2)}) collective-permute-start(bf16[1000,128]{1,0:T(8,128)(2,1)S(1)} %get-tuple-element.57), channel_id=1, source_target_pairs={{0,48},{1,49},{2,50},{3,51},{4,52},{5,53},{6,54},{7,55},{8,56},{9,... | collective-permute-start | bytes 768008 | tf_op jit(solution)/shard_map/ppermute | solution.py:253
  71.5 8.0 %collective-permute-start.20 = (bf16[1000,128]{1,0:T(8,128)(2,1)S(1)}, bf16[1000,128]{1,0:T(8,128)(2,1)S(1)}, u32[]{:S(2)}, u32[]{:S(2)}) collective-permute-start(bf16[1000,128]{1,0:T(8,128)(2,1)S(1)} %get-tuple-element.58), channel_id=1, source_target_pairs={{0,720},{1,721},{2,722},{3,723},{4,724},{5,725},{6,726},{7,727},{8... | collective-permute-start | bytes 768008 | tf_op jit(solution)/shard_map/ppermute | solution.py:253
